TPU v7x, 128 devices: a whole 4x4x4 slice. The times are simulated.
128 devices in a mesh: row: 8 (over x_lo, z), col: 16 (over y, x_hi, core).
Axes of the slice: x: 4 (x_hi: 2, x_lo: 2; x = x_hi * 2 + x_lo), y: 4, z: 4, core: 2. Of those that a mesh axis runs over, the one named last changes fastest.
Arguments:
- tokens: bfloat16 [1024, 8192], P('col', 'row'), may hold values from -6 to 6
- out_grad: bfloat16 [1024, 8192], P('col', 'row'), may hold values from -6 to 6
- gate_weight: bfloat16 [8192, 14336], P('row', 'col'), may hold values from -0.09375 to 0.09375
- up_weight: bfloat16 [8192, 14336], P('row', 'col'), may hold values from -0.09375 to 0.09375
- down_weight: bfloat16 [14336, 8192], P('col', 'row'), may hold values from -0.0625 to 0.0625
- gate_mask: int32 [64, 112], P('row', 'col'), may hold values 0 or 1
- up_mask: int32 [64, 112], P('row', 'col'), may hold values 0 or 1
- down_mask: int32 [112, 64], P('col', 'row'), may hold values 0 or 1
Outputs:
- output: bfloat16 [1024, 8192], P('col', 'row')
- token_grad: bfloat16 [1024, 8192], P('col', 'row')
- gate_grad: bfloat16 [8192, 14336], P('row', 'col')
- up_grad: bfloat16 [8192, 14336], P('row', 'col')
- down_grad: bfloat16 [14336, 8192], P('col', 'row')
All inputs are finite; a program needn't handle non-finite values. No bound on the sum of `gate_mask` or of `up_mask` or of `down_mask` on one device may be relied on, other than what follows from the above.
Results may differ from a plain program's by a relative error of at most 0.03.
Values may be sent and summed in bfloat16 or wider, within the bound.
No kernel may reach another device: no remote copies, remote signals or barrier semaphores. Data moves between devices by JAX's collectives and lax.ppermute only.
A program may use at most 128 MiB of HBM per device.

v0:
```python
import jax
import jax.numpy as jnp
from jax import lax
from jax.sharding import PartitionSpec as P


def widen(weight, keep_blocks):
    block_rows, block_cols = keep_blocks.shape
    block_size = weight.shape[0] // block_rows
    spread = jnp.broadcast_to(
        keep_blocks[:, None, :, None], (block_rows, block_size, block_cols, block_size)
    )
    return weight * spread.reshape(weight.shape).astype(jnp.bfloat16)


def contract_last(left, right):
    return lax.dot_general(
        left, right, (((1,), (1,)), ((), ())), preferred_element_type=jnp.float32
    )


def contract_first(left, right):
    return lax.dot_general(
        left, right, (((0,), (0,)), ((), ())), preferred_element_type=jnp.float32
    )


def elementwise(totals, hidden_width):
    gate = totals[:, :hidden_width]
    up_part = totals[:, hidden_width : 2 * hidden_width]
    hidden_grad = totals[:, 2 * hidden_width :]
    sigmoid_gate = jax.nn.sigmoid(gate)
    activated = gate * sigmoid_gate
    hidden = (activated * up_part).astype(jnp.bfloat16)
    gate_delta = (
        hidden_grad * up_part * sigmoid_gate * (1.0 + gate * (1.0 - sigmoid_gate))
    ).astype(jnp.bfloat16)
    up_delta = (hidden_grad * activated).astype(jnp.bfloat16)
    return (hidden, gate_delta, up_delta)


def shards(tokens, out_grad, gate_weight, up_weight, down_weight, gate_mask, up_mask, down_mask):
    gate_masked = widen(gate_weight, gate_mask)
    up_masked = widen(up_weight, up_mask)
    down_masked = widen(down_weight, down_mask)
    hidden_width = gate_masked.shape[1]
    full_tokens, full_grad = (
        lax.all_gather(tokens, "col", axis=0, tiled=True),
        lax.all_gather(out_grad, "col", axis=0, tiled=True),
    )
    gate_part = jnp.dot(full_tokens, gate_masked, preferred_element_type=jnp.float32)
    up_part = jnp.dot(full_tokens, up_masked, preferred_element_type=jnp.float32)
    back_part = contract_last(full_grad, down_masked)
    totals = lax.psum_scatter(
        jnp.concatenate([gate_part, up_part, back_part], axis=1).astype(jnp.bfloat16),
        "row",
        scatter_dimension=0,
        tiled=True,
    ).astype(jnp.float32)
    local_hidden, local_gate, local_up = elementwise(totals, hidden_width)
    hidden, gate_delta, up_delta = (
        lax.all_gather(local_hidden, "row", axis=0, tiled=True),
        lax.all_gather(local_gate, "row", axis=0, tiled=True),
        lax.all_gather(local_up, "row", axis=0, tiled=True),
    )
    down_grad = widen(contract_first(hidden, full_grad).astype(jnp.bfloat16), down_mask)
    gate_grad = widen(contract_first(full_tokens, gate_delta).astype(jnp.bfloat16), gate_mask)
    up_grad = widen(contract_first(full_tokens, up_delta).astype(jnp.bfloat16), up_mask)
    column_sums = lax.psum_scatter(
        jnp.concatenate(
            [
                jnp.dot(hidden, down_masked, preferred_element_type=jnp.float32),
                contract_last(gate_delta, gate_masked) + contract_last(up_delta, up_masked),
            ],
            axis=1,
        ).astype(jnp.bfloat16),
        "col",
        scatter_dimension=0,
        tiled=True,
    ).astype(jnp.float32)
    model_width = down_masked.shape[1]
    output = column_sums[:, :model_width].astype(jnp.bfloat16)
    token_grad = column_sums[:, model_width:].astype(jnp.bfloat16)
    return (output, token_grad, gate_grad, up_grad, down_grad)


def solution(mesh):
    in_specs = (
        P("col", "row"),
        P("col", "row"),
        P("row", "col"),
        P("row", "col"),
        P("col", "row"),
        P("row", "col"),
        P("row", "col"),
        P("col", "row"),
    )
    out_specs = (
        P("col", "row"),
        P("col", "row"),
        P("row", "col"),
        P("row", "col"),
        P("col", "row"),
    )
    return jax.shard_map(shards, mesh=mesh, in_specs=in_specs, out_specs=out_specs, check_vma=False)
```

profile of v0, /device:TPU:0, one launch (start us, length us, event | category | flops | bytes accessed | tf_op | source)
XLA Modules:
  0.0 441.1 jit_solution(11706960751799512838)
XLA Ops:
  7.2 0.7 all-gather.6.cloned.1.call-update
  7.9 0.7 all-gather.8.cloned.1.call-update
  8.7 0.7 convert_element_type.56
  9.4 0.1 copy.21
  9.5 0.7 convert_element_type.58
  10.2 0.1 copy.23
  10.3 0.7 convert_element_type.60
  11.0 3.9 copy.22
  14.9 2.4 copy.24
  17.3 43.1 %all-gather.6.cloned.1.call-done = bf16[1024,1024]{1,0:T(8,128)(2,1)} async-done(((bf16[64,1024]{1,0:T(8,128)(2,1)}), bf16[1024,1024]{1,0:T(8,128)(2,1)}) %all-gather.6.cloned.1.call-update) | async-done | bytes 2097168 | tf_op jit(solution)/shard_map/all_gather | solution.py:48
  60.4 0.3 broadcast_in_dim.7
  60.7 1.2 copy-done.3
  62.0 5.1 %convert_bitcast_fusion.1 = bf16[1024,896]{0,1:T(8,128)(2,1)} fusion(bf16[1024,1024]{1,0:T(8,128)(2,1)} %all-gather.6.cloned.1.call-done, bf16[1024,896]{0,1:T(8,128)(2,1)S(1)} %copy-done.1, bf16[112,8,8,128]{3,2,1,0:T(8,128)(2,1)S(1)} %bitcast.49), kind=kOutput, calls=%fused_computation.11 | convolution fusion | flops 1880883200 | bytes 7602176 | tf_op jit(solution)/shard_map/dot_general | solution.py:52
  67.0 0.3 broadcast_in_dim.6
  67.4 1.3 copy-done.5
  68.7 0.4 copy-done.2
  69.1 2.1 convert_bitcast_fusion.2
  71.2 38.0 %all-gather.8.cloned.1.call-done = bf16[1024,1024]{1,0:T(8,128)(2,1)} async-done(((bf16[64,1024]{1,0:T(8,128)(2,1)}), bf16[1024,1024]{1,0:T(8,128)(2,1)}) %all-gather.8.cloned.1.call-update) | async-done | bytes 2097168 | tf_op jit(solution)/shard_map/all_gather | solution.py:49
  109.2 0.3 broadcast_in_dim.8
  109.5 1.2 copy-done.4
  110.7 0.5 copy-done.8
  111.2 3.8 convert_bitcast_fusion
  115.1 11.4 %pad_maximum_fusion = bf16[1024,2688]{0,1:T(8,128)(2,1)} fusion(bf16[1024,896]{0,1:T(8,128)(2,1)S(1)} %convert_bitcast_fusion, bf16[1024,896]{0,1:T(8,128)(2,1)S(1)} %copy-done.6, bf16[1024,896]{0,1:T(8,128)(2,1)S(1)} %convert_bitcast_fusion.2), kind=kLoop, calls=%fused_computation | loop fusion | flops 16515072 | bytes 11010048 | tf_op jit(solution)/shard_map/concatenate | solution.py:55
  126.5 7.9 %copy.29 = bf16[1024,2688]{1,0:T(8,128)(2,1)} copy(bf16[1024,2688]{0,1:T(8,128)(2,1)} %pad_maximum_fusion) | data formatting | bytes 11010048
  134.4 0.0 all-gather.10.cloned.1.call-start
  134.5 64.6 %reduce-scatter.7.cloned.1.call-done = bf16[128,2688]{1,0:T(8,128)(2,1)} async-done(((bf16[1024,2688]{1,0:T(8,128)(2,1)}), bf16[128,2688]{1,0:T(8,128)(2,1)}) %reduce-scatter.7.cloned.1.call-update) | async-done | bytes 688144
  199.0 1.4 copy.30
  200.5 0.1 convert_element_type.62
  200.6 1.0 multiply_convert_fusion.2
  201.7 0.2 all-gather.12.cloned.1.call-start
  201.9 0.4 all-gather.12.cloned.1.call-update
  202.3 0.5 all-gather.14.cloned.1.call-update
  202.8 0.0 reduce-scatter.9.cloned.1.call-start
  202.9 40.8 %all-gather.10.cloned.1.call-done = bf16[1024,896]{0,1:T(8,128)(2,1)} async-done(((bf16[128,896]{0,1:T(8,128)(2,1)}), bf16[1024,896]{0,1:T(8,128)(2,1)}) %all-gather.10.cloned.1.call-update) | async-done | bytes 1835024 | tf_op jit(solution)/shard_map/all_gather | solution.py:62
  243.6 5.0 %convolution_convert_fusion = bf16[1024,1024]{0,1:T(8,128)(2,1)S(1)} fusion(bf16[1024,896]{0,1:T(8,128)(2,1)} %all-gather.10.cloned.1.call-done, bf16[896,1024]{1,0:T(8,128)(2,1)} %param.12, bf16[112,8,8,128]{3,2,1,0:T(8,128)(2,1)} %bitcast.53), kind=kOutput, calls=%fused_computation.3 | convolution fusion | flops 1881014272 | bytes 7602176 | tf_op jit(solution)/shard_map/dot_general | solution.py:72
  248.6 40.9 %all-gather.12.cloned.1.call-done = bf16[1024,896]{0,1:T(8,128)(2,1)} async-done(((bf16[128,896]{0,1:T(8,128)(2,1)}), bf16[1024,896]{0,1:T(8,128)(2,1)}) %all-gather.12.cloned.1.call-update) | async-done | bytes 1835024 | tf_op jit(solution)/shard_map/all_gather | solution.py:63
  289.5 7.1 %fusion = f32[1024,1024]{0,1:T(8,128)} fusion(bf16[1024,896]{0,1:T(8,128)(2,1)} %all-gather.12.cloned.1.call-done, bf16[1024,896]{0,1:T(8,128)(2,1)} %copy.22, bf16[112,8,8,128]{3,2,1,0:T(8,128)(2,1)} %bitcast.56), kind=kOutput, calls=%fused_computation.13 | convolution fusion | flops 1879965696 | bytes 9699328 | tf_op jit(solution)/shard_map/dot_general | solution.py:17
  296.6 38.8 %all-gather.14.cloned.1.call-done = bf16[1024,896]{0,1:T(8,128)(2,1)} async-done(((bf16[128,896]{0,1:T(8,128)(2,1)}), bf16[1024,896]{0,1:T(8,128)(2,1)}) %all-gather.14.cloned.1.call-update) | async-done | bytes 1835024 | tf_op jit(solution)/shard_map/all_gather | solution.py:64
  335.4 6.3 %add_convert_fusion = bf16[1024,1024]{0,1:T(8,128)(2,1)S(1)} fusion(f32[1024,1024]{0,1:T(8,128)} %fusion, bf16[1024,896]{0,1:T(8,128)(2,1)} %all-gather.14.cloned.1.call-done, bf16[1024,896]{0,1:T(8,128)(2,1)} %copy.24, bf16[112,8,8,128]{3,2,1,0:T(8,128)(2,1)} %bitcast.50), kind=kOutput, calls=%fused_computation.2 | convolution fusion | flops 1882062848 | bytes 11796480 | tf_op jit(solution)/shard_map/dot_general | solution.py:17
  341.6 2.5 pad_maximum_fusion.1
  344.1 6.5 %copy.31 = bf16[1024,2048]{1,0:T(8,128)(2,1)} copy(bf16[1024,2048]{0,1:T(8,128)(2,1)} %pad_maximum_fusion.1) | data formatting | bytes 8388608
  350.6 4.7 %bitcast_multiply_fusion.4 = bf16[1024,896]{0,1:T(8,128)(2,1)S(1)} fusion(bf16[1024,896]{0,1:T(8,128)(2,1)} %all-gather.12.cloned.1.call-done, bf16[1024,1024]{1,0:T(8,128)(2,1)} %all-gather.6.cloned.1.call-done, bf16[112,8,8,128]{3,2,1,0:T(8,128)(2,1)} %bitcast.57), kind=kOutput, calls=%fused_computation.8 | convolution fusion | flops 1880883200 | bytes 7602176 | tf_op jit(solution)/shard_map/dot_general | solution.py:23
  355.4 2.5 copy.27
  357.8 4.9 %bitcast_multiply_fusion.2 = bf16[1024,896]{0,1:T(8,128)(2,1)S(1)} fusion(bf16[1024,896]{0,1:T(8,128)(2,1)} %all-gather.14.cloned.1.call-done, bf16[1024,1024]{1,0:T(8,128)(2,1)} %all-gather.6.cloned.1.call-done, bf16[112,8,8,128]{3,2,1,0:T(8,128)(2,1)} %bitcast.51), kind=kOutput, calls=%fused_computation.6 | convolution fusion | flops 1880883200 | bytes 7602176 | tf_op jit(solution)/shard_map/dot_general | solution.py:23
  362.7 2.5 copy.28
  365.2 6.3 %bitcast_multiply_fusion = bf16[896,1024]{1,0:T(8,128)(2,1)} fusion(bf16[1024,896]{0,1:T(8,128)(2,1)} %all-gather.10.cloned.1.call-done, bf16[1024,1024]{1,0:T(8,128)(2,1)} %all-gather.8.cloned.1.call-done, bf16[112,8,8,128]{3,2,1,0:T(8,128)(2,1)} %bitcast.54), kind=kOutput, calls=%fused_computation.4 | convolution fusion | flops 1880883200 | bytes 7602176 | tf_op jit(solution)/shard_map/dot_general | solution.py:23
  371.5 61.1 %reduce-scatter.9.cloned.1.call-done = bf16[64,2048]{1,0:T(8,128)(2,1)} async-done(((bf16[1024,2048]{1,0:T(8,128)(2,1)}), bf16[64,2048]{1,0:T(8,128)(2,1)}) %reduce-scatter.9.cloned.1.call-update) | async-done | bytes 262160
  432.5 1.7 fusion.2
  (20 shorter events, 0.2 us)
Async XLA Ops:
  7.2 53.2 %all-gather.6.cloned.1.call-start = ((), (), s32[]{:S(2)}) async-start(), calls=%async_computation.2 | async-start | bytes 2228224 | tf_op jit(solution)/shard_map/all_gather | solution.py:48
  7.9 101.3 %all-gather.8.cloned.1.call-start = ((), (), s32[]{:S(2)}) async-start(), calls=%async_computation.3 | async-start | bytes 2228224 | tf_op jit(solution)/shard_map/all_gather | solution.py:49
  8.6 190.4 %reduce-scatter.7.cloned.1.call-start = ((), (), s32[]{:S(2)}) async-start(), calls=%async_computation.7 | async-start | bytes 6193152
  11.0 3.9 copy-start
  17.3 44.7 %copy-start.1 = (bf16[1024,896]{0,1:T(8,128)(2,1)S(1)}, bf16[1024,896]{0,1:T(8,128)(2,1)}, u32[]{:S(2)}) copy-start(bf16[1024,896]{0,1:T(8,128)(2,1)} %copy.24) | copy-start | bytes 5505028
  60.7 1.3 copy-start.3
  62.0 6.7 %copy-start.7 = (bf16[1024,1024]{1,0:T(8,128)(2,1)S(1)}, bf16[1024,1024]{1,0:T(8,128)(2,1)}, u32[]{:S(2)}) copy-start(bf16[1024,1024]{1,0:T(8,128)(2,1)} %all-gather.6.cloned.1.call-done) | copy-start | bytes 6291460
  67.0 2.0 copy-start.2
  67.4 1.3 copy-start.5
  109.2 2.0 copy-start.8
  109.5 1.3 copy-start.4
  111.2 3.8 copy-start.6
  134.4 109.2 %all-gather.10.cloned.1.call-start = ((), (), s32[]{:S(2)}) async-start(), calls=%async_computation.4 | async-start | bytes 2064384 | tf_op jit(solution)/shard_map/all_gather | solution.py:62
  201.7 87.8 %all-gather.12.cloned.1.call-start = ((), (), s32[]{:S(2)}) async-start(), calls=%async_computation.5 | async-start | bytes 2064384 | tf_op jit(solution)/shard_map/all_gather | solution.py:63
  202.2 133.1 %all-gather.14.cloned.1.call-start = ((), (), s32[]{:S(2)}) async-start(), calls=%async_computation.6 | async-start | bytes 2064384 | tf_op jit(solution)/shard_map/all_gather | solution.py:64
  202.8 229.7 %reduce-scatter.9.cloned.1.call-start = ((), (), s32[]{:S(2)}) async-start(), calls=%async_computation.8 | async-start | bytes 4456448
Sparse Core Ops, SparseCore 0:
  10.5 49.8 all-gather.5
  62.9 46.2 all-gather.7
  134.5 64.4 reduce-scatter.6
  201.8 41.8 all-gather.9
  245.0 44.4 all-gather.11
  290.9 44.4 all-gather.13
  350.7 81.7 reduce-scatter.8
where the time goes:
time: 442 us; the launch traced here: 441 us
  waiting for transfers between devices  329 us (74%)
  matrix products  45.2 us (10%)
  local copies, waits for them, and re-layouts  34.6 us (8%)
  other arithmetic  17.1 us (4%)
  between operations  14.2 us (3%)
    unnamed x9, waiting for transfers between devices  128 us
    all_gather x1, waiting for transfers between devices, shards(): lax.all_gather(tokens, 'col', axis=0, tiled=True)  43.1 us
    all_gather x1, waiting for transfers between devices, shards(): lax.all_gather(local_gate, 'row', axis=0, tiled=True)  40.9 us
    all_gather x1, waiting for transfers between devices, shards(): lax.all_gather(local_hidden, 'row', axis=0, tiled=True)  40.8 us
    all_gather x1, waiting for transfers between devices, shards(): lax.all_gather(local_up, 'row', axis=0, tiled=True)  38.8 us
    all_gather x1, waiting for transfers between devices, shards(): lax.all_gather(out_grad, 'col', axis=0, tiled=True)  38 us
    unnamed x25, local copies, waits for them, and re-layouts  31.8 us
    dot_general x3, matrix products, contract_last(): lax.dot_general(left, right, (((1,), (1,)), ((), ())), preferred_element_...  17.1 us
  transfers between devices with their start and end apart: 7, of which 7 were waited for; matrix products, arithmetic and copies ran while one was open for 11% of the time, Pallas kernels for 0%

commit v1 on v0

v1 whole, which is shorter than its diff:
```python
import functools

import jax
import jax.numpy as jnp
from jax import lax
from jax.experimental import pallas as pl
from jax.experimental.pallas import tpu as pltpu
from jax.sharding import PartitionSpec as P

BLK = 128
CHUNKS = ((32, True, True), (32, True, True))
SEND_UP = ((2, 0), (1, 1))
SEND_DOWN = ((2, 1), (3, 0))
NEXT_UP = ((1, 0),)
NEXT_DOWN = ((3, 1),)
OWN = ((0, 0), (0, 1))
GROUPS = (SEND_UP, SEND_DOWN, NEXT_UP, NEXT_DOWN, OWN)
GATHERED = tuple((dz, half) for dz in (0, 1, 3, 2) for half in range(2))
VMEM_LIMIT = 24 * 1024 * 1024


def move(array, dy=0, dxh=0, dcore=0, dxl=0, dz=0):
    pairs = []
    for device in range(128):
        row, col = divmod(device, 16)
        x_lo, z = divmod(row, 4)
        y, x_hi, core = col // 4, col // 2 % 2, col % 2
        to_row = (x_lo + dxl) % 2 * 4 + (z + dz) % 4
        to_col = ((y + dy) % 4 * 2 + (x_hi + dxh) % 2) * 2 + (core + dcore) % 2
        pairs.append((device, to_row * 16 + to_col))
    return lax.ppermute(array, ("row", "col"), pairs)


def nn(left, right):
    return lax.dot_general(
        left, right, (((1,), (0,)), ((), ())), preferred_element_type=jnp.float32
    )


def nt(left, right):
    return lax.dot_general(
        left, right, (((1,), (1,)), ((), ())), preferred_element_type=jnp.float32
    )


def tn(left, right):
    return lax.dot_general(
        left, right, (((0,), (0,)), ((), ())), preferred_element_type=jnp.float32
    )


def params():
    return pltpu.CompilerParams(vmem_limit_bytes=VMEM_LIMIT)


def cheap():
    return pl.CostEstimate(flops=1024, bytes_accessed=1024, transcendentals=0)


VMEM = pl.BlockSpec(memory_space=pltpu.VMEM)
ANY = pl.BlockSpec(memory_space=pl.ANY)
SMEM = pl.BlockSpec(memory_space=pltpu.SMEM)


def owner(dz):
    return lax.rem(lax.axis_index("row") + dz, 4)


def token_copies(gathered, pieces, held, first, sems):
    rows = held_rows = None
    copies = []
    if len(gathered) == 2:
        rows = gathered[0].shape[2]
        for at, (dz, half) in enumerate(pieces):
            to = held.at[:, pl.ds(first + at * rows, rows)]
            copies.append((gathered[half].at[owner(dz)], to))
    else:
        rows = gathered[0].shape[2]
        for at, (dz, half) in enumerate(pieces):
            for sub in range(2):
                to = held.at[:, pl.ds(first + (2 * at + sub) * rows, rows)]
                copies.append((gathered[0].at[owner(dz) * 4 + half * 2 + sub], to))
    return [
        pltpu.make_async_copy(source, to, sems.at[at]) for at, (source, to) in enumerate(copies)
    ]


def gathered_at(piece, arrays, rows):
    own, up, down, far_first, far_second = arrays
    dz, half = piece
    if dz == 2:
        return (far_first, far_second)[half]
    return {0: own, 1: up, 3: down}[dz].at[pl.ds(half * rows, rows)]


def mask_kernel(gate, up, down, gate_mask, up_mask, down_mask, out):
    step = pl.program_id(0)
    width = gate.shape[1]
    down_t = down[...].T
    for j in range(width // BLK):
        at = pl.ds(j * BLK, BLK)
        out[:, at] = gate[:, at] * gate_mask[step, j].astype(jnp.bfloat16)
        to = pl.ds(width + j * BLK, BLK)
        out[:, to] = up[:, at] * up_mask[step, j].astype(jnp.bfloat16)
        to = pl.ds(2 * width + j * BLK, BLK)
        out[:, to] = down_t[:, j * BLK : (j + 1) * BLK] * down_mask[j, step].astype(jnp.bfloat16)


def mask_weights(gate, up, down, gate_mask, up_mask, down_mask):
    depth, width = gate.shape
    return pl.pallas_call(
        mask_kernel,
        grid=(depth // BLK,),
        in_specs=[
            pl.BlockSpec((BLK, width), lambda i: (i, 0)),
            pl.BlockSpec((BLK, width), lambda i: (i, 0)),
            pl.BlockSpec((width, BLK), lambda i: (0, i)),
            SMEM,
            SMEM,
            SMEM,
        ],
        out_specs=pl.BlockSpec((BLK, 3 * width), lambda i: (i, 0)),
        out_shape=jax.ShapeDtypeStruct((depth, 3 * width), jnp.bfloat16),
        compiler_params=params(),
        cost_estimate=pl.CostEstimate(
            flops=3 * depth * width, bytes_accessed=12 * depth * width, transcendentals=0
        ),
        name="mask_weights",
    )(gate, up, down, gate_mask, up_mask, down_mask)


def weight_copies(source, target, sems, order):
    width = target.shape[1] // 3
    depth = target.shape[0] // 2
    copies = []
    for at in order:
        columns = pl.ds(at * width, width)
        copies.append(
            [
                pltpu.make_async_copy(
                    source.at[pl.ds(part * depth, depth), columns],
                    target.at[pl.ds(part * depth, depth), columns],
                    sems.at[at, part],
                )
                for part in range(2)
            ]
        )
    return copies


def start(copies):
    for copy in copies:
        copy.start()


def wait(copies):
    for copy in copies:
        copy.wait()


def forward_kernel(count, *refs):
    gathered, weights, outs = refs[:count], refs[count], refs[count + 1 : count + 6]
    held, held_weights, sems, weight_sems = refs[count + 6 :]
    pieces = [piece for group in GROUPS for piece in group]
    copies = token_copies(gathered, pieces, held, 0, sems)
    loads = weight_copies(weights, held_weights, weight_sems, range(3))
    start(loads[0])
    start(copies)
    start(loads[1])
    start(loads[2])
    wait(copies)
    width = weights.shape[1] // 3
    rows = held.shape[1] // 8
    for at in range(3):
        wait(loads[at])
        columns = slice(at * width, (at + 1) * width)
        part = nn(held[at // 2], held_weights[:, columns]).astype(jnp.bfloat16)
        first = 0
        for out, group in zip(outs, GROUPS):
            size = len(group) * rows
            out[:, columns] = part[first : first + size]
            first += size


def forward(gathered, weights):
    depth, total = weights.shape
    count = len(gathered)
    rows = gathered[0].shape[2] * count // 2 if count == 2 else gathered[0].shape[2] * 2
    return pl.pallas_call(
        functools.partial(forward_kernel, count),
        in_specs=[ANY] * (count + 1),
        out_specs=[VMEM] * len(GROUPS),
        out_shape=[
            jax.ShapeDtypeStruct((len(group) * rows, total), jnp.bfloat16) for group in GROUPS
        ],
        scratch_shapes=[
            pltpu.VMEM((2, 8 * rows, depth), jnp.bfloat16),
            pltpu.VMEM((depth, total), jnp.bfloat16),
            pltpu.SemaphoreType.DMA((16,)),
            pltpu.SemaphoreType.DMA((3, 2)),
        ],
        compiler_params=params(),
        cost_estimate=cheap(),
        name="forward",
    )(*gathered, weights)


def place(piece, sub, gather_hops, scatter_hops):
    dz, half = piece
    col = lax.axis_index("col")
    y_me, x_me, core_me = col // 4, lax.rem(col // 2, 2), lax.rem(col, 2)
    if gather_hops:
        y, x, core = owner(dz), sub, half
        if scatter_hops:
            return ((1 - core) * 4 + y) * 2 + x
        return (lax.rem(y + y_me, 4) * 2 + lax.rem(x + x_me, 2)) * 2 + lax.rem(core + core_me, 2)
    y, x, core = owner(dz), half, sub
    if not scatter_hops:
        return (y * 2 + x) * 2 + core
    other = lax.rem(core + core_me, 2)
    return ((1 - other) * 4 + lax.rem(y - y_me + 4, 4)) * 2 + lax.rem(x + x_me, 2)


def backward_kernel(gather_hops, scatter_hops, *refs):
    arrays, weights = refs[:5], refs[5]
    outs, (held, held_weights, sems, weight_sems) = refs[6:-4], refs[-4:]
    rows = arrays[3].shape[0]
    copies = []
    together = gather_hops == scatter_hops
    for piece in GATHERED:
        source = gathered_at(piece, arrays, rows)
        size = rows if together else rows // 2
        for sub in range(1 if together else 2):
            at = place(piece, sub, gather_hops, scatter_hops)
            to = pl.ds(pl.multiple_of(at * (rows // 2), rows // 2), size)
            copies.append(
                pltpu.make_async_copy(
                    source.at[pl.ds(sub * size, size)], held.at[to], sems.at[len(copies)]
                )
            )
    loads = weight_copies(weights, held_weights, weight_sems, (2, 0, 1))
    start(loads[0])
    start(copies)
    start(loads[1])
    start(loads[2])
    wait(copies)
    depth = held_weights.shape[0]
    width = held_weights.shape[1] // 3

    def term(at):
        columns = slice(at * width, (at + 1) * width)
        return nt(held[:, columns], held_weights[:, columns])

    def put(part, column):
        part = part.astype(jnp.bfloat16)
        size = part.shape[0] // len(outs)
        for at, out in enumerate(outs):
            out[:, column : column + depth] = part[at * size : (at + 1) * size]

    wait(loads[0])
    put(term(2), 0)
    wait(loads[1])
    wait(loads[2])
    columns = slice(0, 2 * width)
    put(nt(held[:, columns], held_weights[:, columns]), depth)


def backward(arrays, weights, gather_hops, scatter_hops):
    rows = arrays[3].shape[0]
    depth, total = weights.shape
    count = 2 if scatter_hops else 1
    return pl.pallas_call(
        functools.partial(backward_kernel, gather_hops, scatter_hops),
        in_specs=[ANY] * 6,
        out_specs=[VMEM] * count,
        out_shape=[jax.ShapeDtypeStruct((8 * rows // count, 2 * depth), jnp.bfloat16)] * count,
        scratch_shapes=[
            pltpu.VMEM((8 * rows, total), jnp.bfloat16),
            pltpu.VMEM((depth, total), jnp.bfloat16),
            pltpu.SemaphoreType.DMA((16,)),
            pltpu.SemaphoreType.DMA((3, 2)),
        ],
        compiler_params=params(),
        cost_estimate=cheap(),
        name="backward",
    )(*arrays, weights)


def weight_grad_kernel(counts, *refs):
    number = sum(counts) + 5 * len(counts)
    gate_mask, up_mask, down_mask, gate_grad, up_grad, down_grad = refs[number : number + 6]
    tokens, values, sems, value_sems = refs[number + 6 :]
    first = at = 0
    copies = []
    for which, count in enumerate(counts):
        gathered, arrays = refs[at : at + count], refs[at + count : at + count + 5]
        at += count + 5
        rows = arrays[3].shape[0]
        copies += token_copies(gathered, GATHERED, tokens, first, sems.at[which])
        for number, piece in enumerate(GATHERED):
            copies.append(
                pltpu.make_async_copy(
                    gathered_at(piece, arrays, rows),
                    values.at[pl.ds(first + number * rows, rows)],
                    value_sems.at[which, number],
                )
            )
        first += 8 * rows
    start(copies)
    wait(copies)
    width, depth = down_grad.shape

    def store(part, mask, row, out):
        for j in range(part.shape[1] // BLK):
            for i in range(part.shape[0] // BLK):
                block = part[i * BLK : (i + 1) * BLK, j * BLK : (j + 1) * BLK]
                keep = mask[row // BLK + i, j].astype(jnp.bfloat16)
                out[row + i * BLK : row + (i + 1) * BLK, j * BLK : (j + 1) * BLK] = (
                    block.astype(jnp.bfloat16) * keep
                )

    for row in range(0, depth, 256):
        left = tokens[0, :, row : row + 256]
        store(tn(left, values[:, :width]), gate_mask, row, gate_grad)
        store(tn(left, values[:, width : 2 * width]), up_mask, row, up_grad)
    for row in range(0, width, 256):
        size = min(256, width - row)
        left = values[:, 2 * width + row : 2 * width + row + size]
        store(tn(left, tokens[1]), down_mask, row, down_grad)


def weight_grads(chunks, gate_mask, up_mask, down_mask):
    depth = chunks[0][0][0].shape[-1]
    total = chunks[0][1][0].shape[-1]
    width = total // 3
    counts = tuple(len(gathered) for gathered, _ in chunks)
    count = sum(8 * arrays[3].shape[0] for _, arrays in chunks)
    inputs = [item for gathered, arrays in chunks for item in (*gathered, *arrays)]
    return pl.pallas_call(
        functools.partial(weight_grad_kernel, counts),
        in_specs=[ANY] * len(inputs) + [SMEM] * 3,
        out_specs=[VMEM] * 3,
        out_shape=[
            jax.ShapeDtypeStruct((depth, width), jnp.bfloat16),
            jax.ShapeDtypeStruct((depth, width), jnp.bfloat16),
            jax.ShapeDtypeStruct((width, depth), jnp.bfloat16),
        ],
        scratch_shapes=[
            pltpu.VMEM((2, count, depth), jnp.bfloat16),
            pltpu.VMEM((count, total), jnp.bfloat16),
            pltpu.SemaphoreType.DMA((len(chunks), 16)),
            pltpu.SemaphoreType.DMA((len(chunks), 8)),
        ],
        compiler_params=params(),
        cost_estimate=cheap(),
        name="weight_grads",
    )(*inputs, gate_mask, up_mask, down_mask)


def wide(array):
    return array.astype(jnp.float32)


def elementwise(totals):
    width = totals.shape[-1] // 3
    gate = totals[..., :width]
    up_part = totals[..., width : 2 * width]
    hidden_grad = totals[..., 2 * width :]
    sigmoid_gate = jax.nn.sigmoid(gate)
    activated = gate * sigmoid_gate
    hidden = activated * up_part
    gate_delta = hidden_grad * up_part * sigmoid_gate * (1.0 + gate * (1.0 - sigmoid_gate))
    up_delta = hidden_grad * activated
    return jnp.concatenate([gate_delta, up_delta, hidden], axis=-1).astype(jnp.bfloat16)


def after(value, *others):
    return lax.optimization_barrier((value, others))[0]


def chip_sum(for_own, received):
    return (wide(for_own) + wide(received)).astype(jnp.bfloat16)


def gather_pair(part):
    return jnp.concatenate([part, move(part, dxh=1)], axis=1)


def scatter_pairs(chip):
    rows = chip.shape[0] // 4
    total = wide(chip[:rows])
    for dy in range(1, 4):
        total = total + wide(move(chip[dy * rows : (dy + 1) * rows], dy=dy))
    return total.astype(jnp.bfloat16)


def scatter_pair(pair):
    rows = pair.shape[0] // 2
    return (wide(pair[:rows]) + wide(move(pair[rows:], dxh=1))).astype(jnp.bfloat16)


class Chunk:
    def __init__(self, part, gather_hops, scatter_hops):
        self.part, self.hops = part, (gather_hops, scatter_hops)

    def gather_near(self):
        self.pair = gather_pair(self.part)

    def gather_far(self, *others):
        self.pair = after(self.pair, *others)
        self.pairs = [self.pair] + [move(self.pair, dy=-dy) for dy in range(1, 4)]
        return self.pair

    def gather_core(self, *others):
        own = jnp.stack(after(self.pairs, *others))
        self.gathered = (own, move(own, dcore=1))
        return own

    def gather(self):
        self.gathered = (lax.all_gather(self.part, "col", axis=0),)

    def forward(self, weights):
        outs = forward(self.gathered, weights)
        self.late_up, self.late_down, self.kept = outs[2:]
        self.from_down = move(outs[0], dz=1)
        self.from_up = move(outs[1], dz=-1)
        return outs[0]

    def relay(self, *others):
        down, up = after((self.from_down, self.from_up), *others)
        rows = down.shape[0] // 2
        send_up = self.late_up + down[:rows]
        send_down = self.late_down + up[:rows]
        self.last_down = move(send_up, dz=1)
        self.last_up = move(send_down, dz=-1)
        self.direct = (up[rows:], down[rows:])
        return send_up, send_down

    def swap(self, *others):
        last_down, last_up = after((self.last_down, self.last_up), *others)
        rows = last_down.shape[0]
        self.sums = jnp.concatenate(
            [
                wide(self.kept[:rows]) + wide(last_down) + wide(self.direct[0]),
                wide(self.kept[rows:]) + wide(last_up) + wide(self.direct[1]),
            ]
        ).astype(jnp.bfloat16)
        self.partner = move(self.sums, dxl=1)
        return self.sums

    def spread(self, *others):
        partner = after(self.partner, *others)
        self.values = elementwise(wide(self.sums) + wide(partner))
        self.near = (move(self.values, dz=-1), move(self.values, dz=1))
        return self.values

    def far(self, *others):
        up, down = after(self.near, *others)
        rows = up.shape[0] // 2
        sent = down[:rows], up[rows:]
        self.arrays = (self.values, up, down, move(sent[0], dz=1), move(sent[1], dz=-1))
        return sent

    def backward(self, weights, *others):
        self.arrays = after(self.arrays, *others)
        outs = backward(self.arrays, weights, *self.hops)
        if self.hops[1]:
            self.for_own = outs[1]
            self.received = move(outs[0], dcore=1)
        else:
            self.result = lax.psum_scatter(outs[0], "col", scatter_dimension=0, tiled=True)
        return outs[0]

    def scatter(self, *others):
        if self.hops[1]:
            received = after(self.received, *others)
            chip = chip_sum(self.for_own, received)
            self.result = scatter_pair(scatter_pairs(chip))
            return chip
        return None


def shards(tokens, out_grad, gate_weight, up_weight, down_weight, gate_mask, up_mask, down_mask):
    depth = tokens.shape[1]
    chunks = []
    first = 0
    for rows, gather_hops, scatter_hops in CHUNKS:
        part = jnp.stack([tokens[first : first + rows], out_grad[first : first + rows]])
        chunks.append(Chunk(part, gather_hops, scatter_hops))
        first += rows
    a, b = chunks
    weights = mask_weights(gate_weight, up_weight, down_weight, gate_mask, up_mask, down_mask)
    a.gather_near()
    b.gather_near()
    a.pair, b.pair, weights = lax.optimization_barrier((a.pair, b.pair, weights))
    a.gather_far()
    own_a = a.gather_core()
    b.gather_far(own_a)
    up_a = a.forward(weights)
    own_b = b.gather_core(up_a)
    up_b = b.forward(weights)
    relay_a = a.relay(up_b)
    swap_a = a.swap(relay_a)
    relay_b = b.relay(swap_a)
    spread_a = a.spread(relay_b)
    swap_b = b.swap(spread_a)
    far_a = a.far(swap_b)
    spread_b = b.spread(far_a)
    back_a = a.backward(weights, spread_b)
    far_b = b.far(back_a)
    chip_a = a.scatter(far_b)
    back_b = b.backward(weights, chip_a)
    chip_b = b.scatter()
    inputs = after([(chunk.gathered, chunk.arrays) for chunk in chunks], chip_b)
    gate_grad, up_grad, down_grad = weight_grads(inputs, gate_mask, up_mask, down_mask)
    result = jnp.concatenate([chunk.result for chunk in chunks])
    return (result[:, :depth], result[:, depth:], gate_grad, up_grad, down_grad)


def solution(mesh):
    in_specs = (
        P("col", "row"),
        P("col", "row"),
        P("row", "col"),
        P("row", "col"),
        P("col", "row"),
        P("row", "col"),
        P("row", "col"),
        P("col", "row"),
    )
    out_specs = (
        P("col", "row"),
        P("col", "row"),
        P("row", "col"),
        P("row", "col"),
        P("col", "row"),
    )
    return jax.shard_map(shards, mesh=mesh, in_specs=in_specs, out_specs=out_specs, check_vma=False)
```

time: 442 us -> 218 us (0.49)
  waiting for transfers between devices: 329 us -> 116 us
  starting transfers between devices: 0.45 us -> 55.1 us
  matrix products: 45.2 us -> 0 us
  Pallas kernels: 0 us -> 34.2 us
  local copies, waits for them, and re-layouts: 34.6 us -> 7.77 us
  other arithmetic: 17.1 us -> 3.86 us
  between operations: 14.2 us -> 1.04 us
    all_gather x5 -> x0, waiting for transfers between devices: 202 us -> none  [the longest x1 43.1 us: shards(): lax.all_gather(tokens, 'col', axis=0, tiled=True)]
    unnamed x9 -> x0, waiting for transfers between devices: 128 us -> none
    ppermute x0 -> x38, waiting for transfers between devices: none -> 116 us  [move(): return lax.ppermute(array, ('row', 'col'), pairs)]
    ppermute x0 -> x38, starting transfers between devices: none -> 55.1 us  [move(): return lax.ppermute(array, ('row', 'col'), pairs)]
    dot_general x9 -> x0, matrix products: 45.2 us -> none  [the longest x3 17.1 us: contract_last(): lax.dot_general(left, right, (((1,), (1,)), ((), ())), preferred_element_...]
    pallas_call x0 -> x6, Pallas kernels: none -> 34.2 us  [the longest x1 12.2 us: weight_grads(): pl.pallas_call(functools.partial(weight_grad_kernel, counts), in_specs=[A...]
    unnamed x25 -> x18, local copies, waits for them, and re-layouts: 31.8 us -> 6.57 us
    concatenate x2 -> x7, other arithmetic: 13.9 us -> 0.96 us  [the longest x1 0.72 us: shards(): result = jnp.concatenate([chunk.result for chunk in chunks])]
  transfers between devices with their start and end apart: 7 -> 38, of which waited for: 7 -> 20; matrix products, arithmetic and copies ran while one was open for 11% -> 1% of each run, Pallas kernels for 0% -> 11%
where the time goes in v1:
time: 218 us
  waiting for transfers between devices  116 us (53%)
  starting transfers between devices  55.1 us (25%)
  Pallas kernels  34.2 us (16%)
  local copies, waits for them, and re-layouts  7.77 us (4%)
  other arithmetic  3.86 us (2%)
    ppermute x38, waiting for transfers between devices, move(): return lax.ppermute(array, ('row', 'col'), pairs)  116 us
    ppermute x38, starting transfers between devices, move(): return lax.ppermute(array, ('row', 'col'), pairs)  55.1 us
    pallas_call x1, Pallas kernels, weight_grads(): pl.pallas_call(functools.partial(weight_grad_kernel, counts), in_specs=[A...  12.2 us
    pallas_call x2, Pallas kernels, backward(): pl.pallas_call(functools.partial(backward_kernel, gather_hops, scatter_ho...  10.1 us
    pallas_call x2, Pallas kernels, forward(): pl.pallas_call(functools.partial(forward_kernel, count), in_specs=[ANY] *...  9.14 us
    unnamed x18, local copies, waits for them, and re-layouts  6.57 us
  transfers between devices with their start and end apart: 38, of which 20 were waited for; matrix products, arithmetic and copies ran while one was open for 1% of the time, Pallas kernels for 11%

profile of v1, /device:TPU:0, one launch (start us, length us, event | category | flops | bytes accessed | tf_op | source)
XLA Modules:
  0.0 217.6 jit_solution(13702126927869810867)
XLA Ops:
  0.6 1.0 slice_bitcast_fusion
  1.6 3.2 %collective-permute-start.1 = (bf16[2,32,1024]{2,1,0:T(8,128)(2,1)S(1)}, bf16[2,32,1024]{2,1,0:T(8,128)(2,1)S(1)}, u32[]{:S(2)}, u32[]{:S(2)}) collective-permute-start(bf16[2,32,1024]{2,1,0:T(8,128)(2,1)S(1)} %pad_maximum_fusion.10), channel_id=1, source_target_pairs={{0,2},{1,3},{2,0},{3,1},{4,6},{5,7},{6,4},{7,5},{8,10},{9,11},{10,... | collective-permute-start | bytes 393224 | tf_op jit(solution)/shard_map/ppermute | solution.py:31
  5.3 1.5 copy-done
  6.8 1.5 copy-done.1
  8.3 1.5 copy-done.2
  11.9 2.8 %mask_weights.1.refs_2_.refs_5_ = bf16[1024,2688]{1,0:T(8,128)(2,1)S(1)} custom-call(bf16[1024,896]{1,0:T(8,128)(2,1)S(1)} %copy-done, bf16[1024,896]{1,0:T(8,128)(2,1)S(1)} %copy-done.1, bf16[896,1024]{1,0:T(8,128)(2,1)S(1)} %copy-done.2, s32[8,7]{1,0:T(8,128)S(1)} %copy-done.3, s32[8,7]{1,0:T(8,128)S(1)} %copy-done.5, s32[7,8]{1,0:T(8,128)S(1)} %copy-done.7), custom_call_target="tpu_custom_call" | custom-call | flops 2752512 | bytes 11010048 | tf_op jit(solution)/shard_map/mask_weights/pallas_call | solution.py:111
  14.7 3.2 %collective-permute-start.2 = (bf16[2,64,1024]{2,1,0:T(8,128)(2,1)S(1)}, bf16[2,64,1024]{2,1,0:T(8,128)(2,1)S(1)}, u32[]{:S(2)}, u32[]{:S(2)}) collective-permute-start(bf16[2,64,1024]{2,1,0:T(8,128)(2,1)S(1)} %pad_maximum_fusion.6), channel_id=1, source_target_pairs={{0,12},{1,13},{2,14},{3,15},{4,0},{5,1},{6,2},{7,3},{8,4},{9,5},{1... | collective-permute-start | bytes 786440 | tf_op jit(solution)/shard_map/ppermute | solution.py:31
  18.5 1.0 collective-permute-start.4
  19.5 9.0 %collective-permute-done.2 = bf16[2,64,1024]{2,1,0:T(8,128)(2,1)S(1)} collective-permute-done((bf16[2,64,1024]{2,1,0:T(8,128)(2,1)S(1)}, bf16[2,64,1024]{2,1,0:T(8,128)(2,1)S(1)}, u32[]{:S(2)}, u32[]{:S(2)}) %collective-permute-start.2) | collective-permute-done | bytes 262176 | tf_op jit(solution)/shard_map/ppermute | solution.py:31
  28.7 3.6 %collective-permute-done.4 = bf16[2,64,1024]{2,1,0:T(8,128)(2,1)S(1)} collective-permute-done((bf16[2,64,1024]{2,1,0:T(8,128)(2,1)S(1)}, bf16[2,64,1024]{2,1,0:T(8,128)(2,1)S(1)}, u32[]{:S(2)}, u32[]{:S(2)}) %collective-permute-start.4) | collective-permute-done | bytes 262176 | tf_op jit(solution)/shard_map/ppermute | solution.py:31
  32.5 3.2 %collective-permute-start.8 = (bf16[2,64,1024]{2,1,0:T(8,128)(2,1)S(1)}, bf16[2,64,1024]{2,1,0:T(8,128)(2,1)S(1)}, u32[]{:S(2)}, u32[]{:S(2)}) collective-permute-start(bf16[2,64,1024]{2,1,0:T(8,128)(2,1)S(1)} %pad_maximum_fusion.7), channel_id=1, source_target_pairs={{0,12},{1,13},{2,14},{3,15},{4,0},{5,1},{6,2},{7,3},{8,4},{9,5},{1... | collective-permute-start | bytes 786440 | tf_op jit(solution)/shard_map/ppermute | solution.py:31
  35.8 4.6 %forward.2 = (bf16[128,2688]{1,0:T(8,128)(2,1)S(1)}, bf16[128,2688]{1,0:T(8,128)(2,1)S(1)}, bf16[64,2688]{1,0:T(8,128)(2,1)S(1)}, bf16[64,2688]{1,0:T(8,128)(2,1)S(1)}, bf16[128,2688]{1,0:T(8,128)(2,1)S(1)}) custom-call(bf16[4,2,64,1024]{3,2,1,0:T(8,128)(2,1)S(1)} %pad_maximum_fusion.refs_0_, bf16[4,2,64,1024]{3,2,1,0:T(8,128)(2,1)S(1)} %collective-permute-done.5.refs_1_, ...), custom_call_target="tpu_custom_call" | custom-call | flops 1024 | bytes 1024 | tf_op jit(solution)/shard_map/forward/pallas_call | solution.py:189
  40.4 7.7 %collective-permute-done.10 = bf16[2,64,1024]{2,1,0:T(8,128)(2,1)S(1)} collective-permute-done((bf16[2,64,1024]{2,1,0:T(8,128)(2,1)S(1)}, bf16[2,64,1024]{2,1,0:T(8,128)(2,1)S(1)}, u32[]{:S(2)}, u32[]{:S(2)}) %collective-permute-start.10) | collective-permute-done | bytes 262176 | tf_op jit(solution)/shard_map/ppermute | solution.py:31
  48.3 2.0 collective-permute-start.6
  50.2 2.2 %collective-permute-start.7 = (bf16[128,2688]{1,0:T(8,128)(2,1)S(1)}, bf16[128,2688]{1,0:T(8,128)(2,1)S(1)}, u32[]{:S(2)}, u32[]{:S(2)}) collective-permute-start(bf16[128,2688]{1,0:T(8,128)(2,1)S(1)} %get-tuple-element.82), channel_id=1, source_target_pairs={{0,48},{1,49},{2,50},{3,51},{4,52},{5,53},{6,54},{7,55},{8,56},{9,... | collective-permute-start | bytes 2064392 | tf_op jit(solution)/shard_map/ppermute | solution.py:31
  52.4 4.6 %forward.3 = (bf16[128,2688]{1,0:T(8,128)(2,1)S(1)}, bf16[128,2688]{1,0:T(8,128)(2,1)S(1)}, bf16[64,2688]{1,0:T(8,128)(2,1)S(1)}, bf16[64,2688]{1,0:T(8,128)(2,1)S(1)}, bf16[128,2688]{1,0:T(8,128)(2,1)S(1)}) custom-call(bf16[4,2,64,1024]{3,2,1,0:T(8,128)(2,1)S(1)} %pad_maximum_fusion.1.refs_0_.refs_7_, ...), custom_call_target="tpu_custom_call" | custom-call | flops 1024 | bytes 1024 | tf_op jit(solution)/shard_map/forward/pallas_call | solution.py:189
  57.0 11.4 %collective-permute-done.6 = bf16[128,2688]{1,0:T(8,128)(2,1)S(1)} collective-permute-done((bf16[128,2688]{1,0:T(8,128)(2,1)S(1)}, bf16[128,2688]{1,0:T(8,128)(2,1)S(1)}, u32[]{:S(2)}, u32[]{:S(2)}) %collective-permute-start.6) | collective-permute-done | bytes 688160 | tf_op jit(solution)/shard_map/ppermute | solution.py:31
  68.4 3.0 %collective-permute-start.13 = (bf16[64,2688]{1,0:T(8,128)(2,1)S(1)}, bf16[64,2688]{1,0:T(8,128)(2,1)S(1)}, u32[]{:S(2)}, u32[]{:S(2)}) collective-permute-start(bf16[64,2688]{1,0:T(8,128)(2,1)S(1)} %slice_add_fusion.2), channel_id=1, source_target_pairs={{0,48},{1,49},{2,50},{3,51},{4,52},{5,53},{6,54},{7,55},{8,56},{9,... | collective-permute-start | bytes 1032200 | tf_op jit(solution)/shard_map/ppermute | solution.py:31
  71.9 2.9 %collective-permute-start.16 = (bf16[128,2688]{1,0:T(8,128)(2,1)S(1)}, bf16[128,2688]{1,0:T(8,128)(2,1)S(1)}, u32[]{:S(2)}, u32[]{:S(2)}) collective-permute-start(bf16[128,2688]{1,0:T(8,128)(2,1)S(1)} %get-tuple-element.96), channel_id=1, source_target_pairs={{0,48},{1,49},{2,50},{3,51},{4,52},{5,53},{6,54},{7,55},{8,56},{9,... | collective-permute-start | bytes 2064392 | tf_op jit(solution)/shard_map/ppermute | solution.py:31
  74.9 5.1 %collective-permute-done.13 = bf16[64,2688]{1,0:T(8,128)(2,1)S(1)} collective-permute-done((bf16[64,2688]{1,0:T(8,128)(2,1)S(1)}, bf16[64,2688]{1,0:T(8,128)(2,1)S(1)}, u32[]{:S(2)}, u32[]{:S(2)}) %collective-permute-start.13) | collective-permute-done | bytes 344096 | tf_op jit(solution)/shard_map/ppermute | solution.py:31
  80.0 3.8 %collective-permute-done.12 = bf16[64,2688]{1,0:T(8,128)(2,1)S(1)} collective-permute-done((bf16[64,2688]{1,0:T(8,128)(2,1)S(1)}, bf16[64,2688]{1,0:T(8,128)(2,1)S(1)}, u32[]{:S(2)}, u32[]{:S(2)}) %collective-permute-start.12) | collective-permute-done | bytes 344096 | tf_op jit(solution)/shard_map/ppermute | solution.py:31
  84.1 1.6 collective-permute-start.14
  85.7 11.1 %collective-permute-done.15 = bf16[128,2688]{1,0:T(8,128)(2,1)S(1)} collective-permute-done((bf16[128,2688]{1,0:T(8,128)(2,1)S(1)}, bf16[128,2688]{1,0:T(8,128)(2,1)S(1)}, u32[]{:S(2)}, u32[]{:S(2)}) %collective-permute-start.15) | collective-permute-done | bytes 688160 | tf_op jit(solution)/shard_map/ppermute | solution.py:31
  97.1 1.9 collective-permute-start.19
  99.5 1.4 collective-permute-start.17
  101.6 6.3 %collective-permute-done.20 = bf16[64,2688]{1,0:T(8,128)(2,1)S(1)} collective-permute-done((bf16[64,2688]{1,0:T(8,128)(2,1)S(1)}, bf16[64,2688]{1,0:T(8,128)(2,1)S(1)}, u32[]{:S(2)}, u32[]{:S(2)}) %collective-permute-start.20) | collective-permute-done | bytes 344096 | tf_op jit(solution)/shard_map/ppermute | solution.py:31
  107.9 1.5 collective-permute-done.19
  109.7 1.6 collective-permute-start.23
  111.3 8.7 %collective-permute-done.17.refs_1_.refs_3_ = bf16[128,2688]{1,0:T(8,128)(2,1)S(1)} collective-permute-done((bf16[128,2688]{1,0:T(8,128)(2,1)S(1)}, bf16[128,2688]{1,0:T(8,128)(2,1)S(1)}, u32[]{:S(2)}, u32[]{:S(2)}) %collective-permute-start.17) | collective-permute-done | bytes 688160 | tf_op jit(solution)/shard_map/ppermute | solution.py:31
  119.9 1.5 collective-permute-done.18.refs_2_.refs_4_
  122.0 2.9 %collective-permute-start.22 = (bf16[64,2688]{1,0:T(8,128)(2,1)S(1)}, bf16[64,2688]{1,0:T(8,128)(2,1)S(1)}, u32[]{:S(2)}, u32[]{:S(2)}) collective-permute-start(bf16[64,2688]{1,0:T(8,128)(2,1)S(1)} %slice.140), channel_id=1, source_target_pairs={{0,48},{1,49},{2,50},{3,51},{4,52},{5,53},{6,54},{7,55},{8,56},{9,... | collective-permute-start | bytes 1032200 | tf_op jit(solution)/shard_map/ppermute | solution.py:31
  125.3 4.9 %collective-permute-done.21.refs_3_.refs_5_ = bf16[64,2688]{1,0:T(8,128)(2,1)S(1)} collective-permute-done((bf16[64,2688]{1,0:T(8,128)(2,1)S(1)}, bf16[64,2688]{1,0:T(8,128)(2,1)S(1)}, u32[]{:S(2)}, u32[]{:S(2)}) %collective-permute-start.21) | collective-permute-done | bytes 344096 | tf_op jit(solution)/shard_map/ppermute | solution.py:31
  130.2 5.0 %backward.2 = (bf16[256,2048]{1,0:T(8,128)(2,1)S(1)}, bf16[256,2048]{1,0:T(8,128)(2,1)S(1)}) custom-call(bf16[128,2688]{1,0:T(8,128)(2,1)S(1)} %pad_maximum_fusion.3.refs_0_.refs_2_, bf16[128,2688]{1,0:T(8,128)(2,1)S(1)} %collective-permute-done.17.refs_1_.refs_3_, bf16[128,2688]{1,0:T(8,128)(2,1)S(1)} %collective-permute-done.18.refs_2_.refs_4_, ...), custom_call_target="tpu_custom_call" | custom-call | flops 1024 | bytes 1024 | tf_op jit(solution)/shard_map/backward/pallas_call | solution.py:272
  135.3 3.2 %collective-permute-start.25 = (bf16[128,2688]{1,0:T(8,128)(2,1)S(1)}, bf16[128,2688]{1,0:T(8,128)(2,1)S(1)}, u32[]{:S(2)}, u32[]{:S(2)}) collective-permute-start(bf16[128,2688]{1,0:T(8,128)(2,1)S(1)} %pad_maximum_fusion.5.refs_0_.refs_9_), channel_id=1, source_target_pairs={{0,48},{1,49},{2,50},{3,51},{4,52},{5,53},{6,54},{7,55},{8,56},{9,... | collective-permute-start | bytes 2064392 | tf_op jit(solution)/shard_map/ppermute | solution.py:31
  138.5 15.3 %collective-permute-done.25.refs_1_.refs_10_ = bf16[128,2688]{1,0:T(8,128)(2,1)S(1)} collective-permute-done((bf16[128,2688]{1,0:T(8,128)(2,1)S(1)}, bf16[128,2688]{1,0:T(8,128)(2,1)S(1)}, u32[]{:S(2)}, u32[]{:S(2)}) %collective-permute-start.25) | collective-permute-done | bytes 688160 | tf_op jit(solution)/shard_map/ppermute | solution.py:31
  153.8 3.4 %collective-permute-done.26.refs_2_.refs_11_ = bf16[128,2688]{1,0:T(8,128)(2,1)S(1)} collective-permute-done((bf16[128,2688]{1,0:T(8,128)(2,1)S(1)}, bf16[128,2688]{1,0:T(8,128)(2,1)S(1)}, u32[]{:S(2)}, u32[]{:S(2)}) %collective-permute-start.26) | collective-permute-done | bytes 688160 | tf_op jit(solution)/shard_map/ppermute | solution.py:31
  157.3 3.2 %collective-permute-start.32 = (bf16[64,2688]{1,0:T(8,128)(2,1)S(1)}, bf16[64,2688]{1,0:T(8,128)(2,1)S(1)}, u32[]{:S(2)}, u32[]{:S(2)}) collective-permute-start(bf16[64,2688]{1,0:T(8,128)(2,1)S(1)} %slice.145), channel_id=1, source_target_pairs={{0,48},{1,49},{2,50},{3,51},{4,52},{5,53},{6,54},{7,55},{8,56},{9,... | collective-permute-start | bytes 1032200 | tf_op jit(solution)/shard_map/ppermute | solution.py:31
  161.0 6.9 %collective-permute-done.31.refs_3_.refs_12_ = bf16[64,2688]{1,0:T(8,128)(2,1)S(1)} collective-permute-done((bf16[64,2688]{1,0:T(8,128)(2,1)S(1)}, bf16[64,2688]{1,0:T(8,128)(2,1)S(1)}, u32[]{:S(2)}, u32[]{:S(2)}) %collective-permute-start.31) | collective-permute-done | bytes 344096 | tf_op jit(solution)/shard_map/ppermute | solution.py:31
  167.8 5.0 %backward.3 = (bf16[256,2048]{1,0:T(8,128)(2,1)S(1)}, bf16[256,2048]{1,0:T(8,128)(2,1)S(1)}) custom-call(bf16[128,2688]{1,0:T(8,128)(2,1)S(1)} %pad_maximum_fusion.5.refs_0_.refs_9_, bf16[128,2688]{1,0:T(8,128)(2,1)S(1)} %collective-permute-done.25.refs_1_.refs_10_, bf16[128,2688]{1,0:T(8,128)(2,1)S(1)} %collective-permute-done.26.refs_2_.refs_11_, ...), custom_call_target="tpu_custom_call" | custom-call | flops 1024 | bytes 1024 | tf_op jit(solution)/shard_map/backward/pallas_call | solution.py:272
  174.2 3.6 %collective-permute-start.28 = (bf16[64,2048]{1,0:T(8,128)(2,1)S(1)}, bf16[64,2048]{1,0:T(8,128)(2,1)S(1)}, u32[]{:S(2)}, u32[]{:S(2)}) collective-permute-start(bf16[64,2048]{1,0:T(8,128)(2,1)S(1)} %get-tuple-element.152), channel_id=1, source_target_pairs={{0,8},{1,9},{2,10},{3,11},{4,12},{5,13},{6,14},{7,15},{8,0},{9,1},... | collective-permute-start | bytes 786440 | tf_op jit(solution)/shard_map/ppermute | solution.py:31
  178.2 2.1 collective-permute-start.34
  180.8 2.9 %collective-permute-done.27 = bf16[64,2048]{1,0:T(8,128)(2,1)S(1)} collective-permute-done((bf16[64,2048]{1,0:T(8,128)(2,1)S(1)}, bf16[64,2048]{1,0:T(8,128)(2,1)S(1)}, u32[]{:S(2)}, u32[]{:S(2)}) %collective-permute-start.27) | collective-permute-done | bytes 262176 | tf_op jit(solution)/shard_map/ppermute | solution.py:31
  183.7 1.7 collective-permute-start.36
  185.4 5.1 %collective-permute-done.28 = bf16[64,2048]{1,0:T(8,128)(2,1)S(1)} collective-permute-done((bf16[64,2048]{1,0:T(8,128)(2,1)S(1)}, bf16[64,2048]{1,0:T(8,128)(2,1)S(1)}, u32[]{:S(2)}, u32[]{:S(2)}) %collective-permute-start.28) | collective-permute-done | bytes 262176 | tf_op jit(solution)/shard_map/ppermute | solution.py:31
  190.7 3.1 %collective-permute-start.30 = (bf16[32,2048]{1,0:T(8,128)(2,1)S(1)}, bf16[32,2048]{1,0:T(8,128)(2,1)S(1)}, u32[]{:S(2)}, u32[]{:S(2)}) collective-permute-start(bf16[32,2048]{1,0:T(8,128)(2,1)S(1)} %slice.171), channel_id=1, source_target_pairs={{0,2},{1,3},{2,0},{3,1},{4,6},{5,7},{6,4},{7,5},{8,10},{9,11},{10,... | collective-permute-start | bytes 393224 | tf_op jit(solution)/shard_map/ppermute | solution.py:31
  194.5 6.8 %collective-permute-done.35 = bf16[64,2048]{1,0:T(8,128)(2,1)S(1)} collective-permute-done((bf16[64,2048]{1,0:T(8,128)(2,1)S(1)}, bf16[64,2048]{1,0:T(8,128)(2,1)S(1)}, u32[]{:S(2)}, u32[]{:S(2)}) %collective-permute-start.35) | collective-permute-done | bytes 262176 | tf_op jit(solution)/shard_map/ppermute | solution.py:31
  201.5 3.1 %collective-permute-start.37 = (bf16[32,2048]{1,0:T(8,128)(2,1)S(1)}, bf16[32,2048]{1,0:T(8,128)(2,1)S(1)}, u32[]{:S(2)}, u32[]{:S(2)}) collective-permute-start(bf16[32,2048]{1,0:T(8,128)(2,1)S(1)} %slice.177), channel_id=1, source_target_pairs={{0,2},{1,3},{2,0},{3,1},{4,6},{5,7},{6,4},{7,5},{8,10},{9,11},{10,... | collective-permute-start | bytes 393224 | tf_op jit(solution)/shard_map/ppermute | solution.py:31
  204.7 12.2 %weight_grads.1 = (bf16[1024,896]{1,0:T(8,128)(2,1)}, bf16[1024,896]{1,0:T(8,128)(2,1)}, bf16[896,1024]{1,0:T(8,128)(2,1)}) custom-call(bf16[4,2,64,1024]{3,2,1,0:T(8,128)(2,1)S(1)} %pad_maximum_fusion.refs_0_, bf16[4,2,64,1024]{3,2,1,0:T(8,128)(2,1)S(1)} %collective-permute-done.5.refs_1_, bf16[128,2688]{1,0:T(8,128)(2,1)S(1)} %pad_maximum_fusion.3.refs_0_.refs_2_, ...), custom_call_target="tpu_custom_call" | custom-call | flops 1024 | bytes 1024 | tf_op jit(solution)/shard_map/weight_grads/pallas_call | solution.py:339
  (88 shorter events, 12.1 us)
Async XLA Ops:
  1.6 13.1 %collective-permute-start.1 = (bf16[2,32,1024]{2,1,0:T(8,128)(2,1)S(1)}, bf16[2,32,1024]{2,1,0:T(8,128)(2,1)S(1)}, u32[]{:S(2)}, u32[]{:S(2)}) collective-permute-start(bf16[2,32,1024]{2,1,0:T(8,128)(2,1)S(1)} %pad_maximum_fusion.10), channel_id=1, source_target_pairs={{0,2},{1,3},{2,0},{3,1},{4,6},{5,7},{6,4},{7,5},{8,10},{9,11},{10,... | collective-permute-start | bytes 393224 | tf_op jit(solution)/shard_map/ppermute | solution.py:31
  4.8 9.9 %collective-permute-start = (bf16[2,32,1024]{2,1,0:T(8,128)(2,1)S(1)}, bf16[2,32,1024]{2,1,0:T(8,128)(2,1)S(1)}, u32[]{:S(2)}, u32[]{:S(2)}) collective-permute-start(bf16[2,32,1024]{2,1,0:T(8,128)(2,1)S(1)} %pad_maximum_fusion.9), channel_id=1, source_target_pairs={{0,2},{1,3},{2,0},{3,1},{4,6},{5,7},{6,4},{7,5},{8,10},{9,11},{10,... | collective-permute-start | bytes 393224 | tf_op jit(solution)/shard_map/ppermute | solution.py:31
  5.3 1.5 copy-start
  6.8 1.5 copy-start.1
  8.3 1.5 copy-start.2
  9.8 0.7 copy-start.3
  10.5 0.7 copy-start.5
  11.2 0.7 copy-start.7
  14.7 13.8 %collective-permute-start.2 = (bf16[2,64,1024]{2,1,0:T(8,128)(2,1)S(1)}, bf16[2,64,1024]{2,1,0:T(8,128)(2,1)S(1)}, u32[]{:S(2)}, u32[]{:S(2)}) collective-permute-start(bf16[2,64,1024]{2,1,0:T(8,128)(2,1)S(1)} %pad_maximum_fusion.6), channel_id=1, source_target_pairs={{0,12},{1,13},{2,14},{3,15},{4,0},{5,1},{6,2},{7,3},{8,4},{9,5},{1... | collective-permute-start | bytes 786440 | tf_op jit(solution)/shard_map/ppermute | solution.py:31
  17.9 10.8 %collective-permute-start.3 = (bf16[2,64,1024]{2,1,0:T(8,128)(2,1)S(1)}, bf16[2,64,1024]{2,1,0:T(8,128)(2,1)S(1)}, u32[]{:S(2)}, u32[]{:S(2)}) collective-permute-start(bf16[2,64,1024]{2,1,0:T(8,128)(2,1)S(1)} %pad_maximum_fusion.6), channel_id=1, source_target_pairs={{0,8},{1,9},{2,10},{3,11},{4,12},{5,13},{6,14},{7,15},{8,0},{9,1},... | collective-permute-start | bytes 786440 | tf_op jit(solution)/shard_map/ppermute | solution.py:31
  18.5 13.7 %collective-permute-start.4 = (bf16[2,64,1024]{2,1,0:T(8,128)(2,1)S(1)}, bf16[2,64,1024]{2,1,0:T(8,128)(2,1)S(1)}, u32[]{:S(2)}, u32[]{:S(2)}) collective-permute-start(bf16[2,64,1024]{2,1,0:T(8,128)(2,1)S(1)} %pad_maximum_fusion.6), channel_id=1, source_target_pairs={{0,4},{1,5},{2,6},{3,7},{4,8},{5,9},{6,10},{7,11},{8,12},{9,13},{1... | collective-permute-start | bytes 786440 | tf_op jit(solution)/shard_map/ppermute | solution.py:31
  32.4 3.4 %collective-permute-start.5 = (bf16[4,2,64,1024]{3,2,1,0:T(8,128)(2,1)S(1)}, bf16[4,2,64,1024]{3,2,1,0:T(8,128)(2,1)S(1)}, u32[]{:S(2)}, u32[]{:S(2)}) collective-permute-start(bf16[4,2,64,1024]{3,2,1,0:T(8,128)(2,1)S(1)} %pad_maximum_fusion.refs_0_), channel_id=1, source_target_pairs={{0,1},{1,0},{2,3},{3,2},{4,5},{5,4},{6,7},{7,6},{8,9},{9,8},{10,11... | collective-permute-start | bytes 3145736 | tf_op jit(solution)/shard_map/ppermute | solution.py:31
  32.5 15.5 %collective-permute-start.10 = (bf16[2,64,1024]{2,1,0:T(8,128)(2,1)S(1)}, bf16[2,64,1024]{2,1,0:T(8,128)(2,1)S(1)}, u32[]{:S(2)}, u32[]{:S(2)}) collective-permute-start(bf16[2,64,1024]{2,1,0:T(8,128)(2,1)S(1)} %pad_maximum_fusion.7), channel_id=1, source_target_pairs={{0,4},{1,5},{2,6},{3,7},{4,8},{5,9},{6,10},{7,11},{8,12},{9,13},{1... | collective-permute-start | bytes 786440 | tf_op jit(solution)/shard_map/ppermute | solution.py:31
  32.5 15.5 %collective-permute-start.8 = (bf16[2,64,1024]{2,1,0:T(8,128)(2,1)S(1)}, bf16[2,64,1024]{2,1,0:T(8,128)(2,1)S(1)}, u32[]{:S(2)}, u32[]{:S(2)}) collective-permute-start(bf16[2,64,1024]{2,1,0:T(8,128)(2,1)S(1)} %pad_maximum_fusion.7), channel_id=1, source_target_pairs={{0,12},{1,13},{2,14},{3,15},{4,0},{5,1},{6,2},{7,3},{8,4},{9,5},{1... | collective-permute-start | bytes 786440 | tf_op jit(solution)/shard_map/ppermute | solution.py:31
  35.8 12.3 %collective-permute-start.9 = (bf16[2,64,1024]{2,1,0:T(8,128)(2,1)S(1)}, bf16[2,64,1024]{2,1,0:T(8,128)(2,1)S(1)}, u32[]{:S(2)}, u32[]{:S(2)}) collective-permute-start(bf16[2,64,1024]{2,1,0:T(8,128)(2,1)S(1)} %pad_maximum_fusion.7), channel_id=1, source_target_pairs={{0,8},{1,9},{2,10},{3,11},{4,12},{5,13},{6,14},{7,15},{8,0},{9,1},... | collective-permute-start | bytes 786440 | tf_op jit(solution)/shard_map/ppermute | solution.py:31
  48.2 4.3 %collective-permute-start.11 = (bf16[4,2,64,1024]{3,2,1,0:T(8,128)(2,1)S(1)}, bf16[4,2,64,1024]{3,2,1,0:T(8,128)(2,1)S(1)}, u32[]{:S(2)}, u32[]{:S(2)}) collective-permute-start(bf16[4,2,64,1024]{3,2,1,0:T(8,128)(2,1)S(1)} %pad_maximum_fusion.1.refs_0_.refs_7_), channel_id=1, source_target_pairs={{0,1},{1,0},{2,3},{3,2},{4,5},{5,4},{6,7},{7,6},{8,9},{9,8},{10,11... | collective-permute-start | bytes 3145736 | tf_op jit(solution)/shard_map/ppermute | solution.py:31
  48.3 20.1 %collective-permute-start.6 = (bf16[128,2688]{1,0:T(8,128)(2,1)S(1)}, bf16[128,2688]{1,0:T(8,128)(2,1)S(1)}, u32[]{:S(2)}, u32[]{:S(2)}) collective-permute-start(bf16[128,2688]{1,0:T(8,128)(2,1)S(1)} %get-tuple-element.81), channel_id=1, source_target_pairs={{0,16},{1,17},{2,18},{3,19},{4,20},{5,21},{6,22},{7,23},{8,24},{9,... | collective-permute-start | bytes 2064392 | tf_op jit(solution)/shard_map/ppermute | solution.py:31
  50.2 18.1 %collective-permute-start.7 = (bf16[128,2688]{1,0:T(8,128)(2,1)S(1)}, bf16[128,2688]{1,0:T(8,128)(2,1)S(1)}, u32[]{:S(2)}, u32[]{:S(2)}) collective-permute-start(bf16[128,2688]{1,0:T(8,128)(2,1)S(1)} %get-tuple-element.82), channel_id=1, source_target_pairs={{0,48},{1,49},{2,50},{3,51},{4,52},{5,53},{6,54},{7,55},{8,56},{9,... | collective-permute-start | bytes 2064392 | tf_op jit(solution)/shard_map/ppermute | solution.py:31
  68.4 11.5 %collective-permute-start.13 = (bf16[64,2688]{1,0:T(8,128)(2,1)S(1)}, bf16[64,2688]{1,0:T(8,128)(2,1)S(1)}, u32[]{:S(2)}, u32[]{:S(2)}) collective-permute-start(bf16[64,2688]{1,0:T(8,128)(2,1)S(1)} %slice_add_fusion.2), channel_id=1, source_target_pairs={{0,48},{1,49},{2,50},{3,51},{4,52},{5,53},{6,54},{7,55},{8,56},{9,... | collective-permute-start | bytes 1032200 | tf_op jit(solution)/shard_map/ppermute | solution.py:31
  71.5 12.3 %collective-permute-start.12 = (bf16[64,2688]{1,0:T(8,128)(2,1)S(1)}, bf16[64,2688]{1,0:T(8,128)(2,1)S(1)}, u32[]{:S(2)}, u32[]{:S(2)}) collective-permute-start(bf16[64,2688]{1,0:T(8,128)(2,1)S(1)} %slice_add_fusion.3), channel_id=1, source_target_pairs={{0,16},{1,17},{2,18},{3,19},{4,20},{5,21},{6,22},{7,23},{8,24},{9,... | collective-permute-start | bytes 1032200 | tf_op jit(solution)/shard_map/ppermute | solution.py:31
  71.6 25.2 %collective-permute-start.15 = (bf16[128,2688]{1,0:T(8,128)(2,1)S(1)}, bf16[128,2688]{1,0:T(8,128)(2,1)S(1)}, u32[]{:S(2)}, u32[]{:S(2)}) collective-permute-start(bf16[128,2688]{1,0:T(8,128)(2,1)S(1)} %get-tuple-element.89), channel_id=1, source_target_pairs={{0,16},{1,17},{2,18},{3,19},{4,20},{5,21},{6,22},{7,23},{8,24},{9,... | collective-permute-start | bytes 2064392 | tf_op jit(solution)/shard_map/ppermute | solution.py:31
  71.9 24.8 %collective-permute-start.16 = (bf16[128,2688]{1,0:T(8,128)(2,1)S(1)}, bf16[128,2688]{1,0:T(8,128)(2,1)S(1)}, u32[]{:S(2)}, u32[]{:S(2)}) collective-permute-start(bf16[128,2688]{1,0:T(8,128)(2,1)S(1)} %get-tuple-element.96), channel_id=1, source_target_pairs={{0,48},{1,49},{2,50},{3,51},{4,52},{5,53},{6,54},{7,55},{8,56},{9,... | collective-permute-start | bytes 2064392 | tf_op jit(solution)/shard_map/ppermute | solution.py:31
  84.1 15.0 %collective-permute-start.14 = (bf16[128,2688]{1,0:T(8,128)(2,1)S(1)}, bf16[128,2688]{1,0:T(8,128)(2,1)S(1)}, u32[]{:S(2)}, u32[]{:S(2)}) collective-permute-start(bf16[128,2688]{1,0:T(8,128)(2,1)S(1)} %pad_maximum_fusion.2), channel_id=1, source_target_pairs={{0,64},{1,65},{2,66},{3,67},{4,68},{5,69},{6,70},{7,71},{8,72},{9,... | collective-permute-start | bytes 2064392 | tf_op jit(solution)/shard_map/ppermute | solution.py:31
  96.8 11.1 %collective-permute-start.20 = (bf16[64,2688]{1,0:T(8,128)(2,1)S(1)}, bf16[64,2688]{1,0:T(8,128)(2,1)S(1)}, u32[]{:S(2)}, u32[]{:S(2)}) collective-permute-start(bf16[64,2688]{1,0:T(8,128)(2,1)S(1)} %slice_add_fusion), channel_id=1, source_target_pairs={{0,48},{1,49},{2,50},{3,51},{4,52},{5,53},{6,54},{7,55},{8,56},{9,... | collective-permute-start | bytes 1032200 | tf_op jit(solution)/shard_map/ppermute | solution.py:31
  97.1 12.3 %collective-permute-start.19 = (bf16[64,2688]{1,0:T(8,128)(2,1)S(1)}, bf16[64,2688]{1,0:T(8,128)(2,1)S(1)}, u32[]{:S(2)}, u32[]{:S(2)}) collective-permute-start(bf16[64,2688]{1,0:T(8,128)(2,1)S(1)} %slice_add_fusion.1), channel_id=1, source_target_pairs={{0,16},{1,17},{2,18},{3,19},{4,20},{5,21},{6,22},{7,23},{8,24},{9,... | collective-permute-start | bytes 1032200 | tf_op jit(solution)/shard_map/ppermute | solution.py:31
  99.5 20.4 %collective-permute-start.17 = (bf16[128,2688]{1,0:T(8,128)(2,1)S(1)}, bf16[128,2688]{1,0:T(8,128)(2,1)S(1)}, u32[]{:S(2)}, u32[]{:S(2)}) collective-permute-start(bf16[128,2688]{1,0:T(8,128)(2,1)S(1)} %pad_maximum_fusion.3.refs_0_.refs_2_), channel_id=1, source_target_pairs={{0,48},{1,49},{2,50},{3,51},{4,52},{5,53},{6,54},{7,55},{8,56},{9,... | collective-permute-start | bytes 2064392 | tf_op jit(solution)/shard_map/ppermute | solution.py:31
  101.0 20.5 %collective-permute-start.18 = (bf16[128,2688]{1,0:T(8,128)(2,1)S(1)}, bf16[128,2688]{1,0:T(8,128)(2,1)S(1)}, u32[]{:S(2)}, u32[]{:S(2)}) collective-permute-start(bf16[128,2688]{1,0:T(8,128)(2,1)S(1)} %pad_maximum_fusion.3.refs_0_.refs_2_), channel_id=1, source_target_pairs={{0,16},{1,17},{2,18},{3,19},{4,20},{5,21},{6,22},{7,23},{8,24},{9,... | collective-permute-start | bytes 2064392 | tf_op jit(solution)/shard_map/ppermute | solution.py:31
  109.7 15.1 %collective-permute-start.23 = (bf16[128,2688]{1,0:T(8,128)(2,1)S(1)}, bf16[128,2688]{1,0:T(8,128)(2,1)S(1)}, u32[]{:S(2)}, u32[]{:S(2)}) collective-permute-start(bf16[128,2688]{1,0:T(8,128)(2,1)S(1)} %pad_maximum_fusion.4), channel_id=1, source_target_pairs={{0,64},{1,65},{2,66},{3,67},{4,68},{5,69},{6,70},{7,71},{8,72},{9,... | collective-permute-start | bytes 2064392 | tf_op jit(solution)/shard_map/ppermute | solution.py:31
  121.5 8.7 %collective-permute-start.21 = (bf16[64,2688]{1,0:T(8,128)(2,1)S(1)}, bf16[64,2688]{1,0:T(8,128)(2,1)S(1)}, u32[]{:S(2)}, u32[]{:S(2)}) collective-permute-start(bf16[64,2688]{1,0:T(8,128)(2,1)S(1)} %slice.139), channel_id=1, source_target_pairs={{0,16},{1,17},{2,18},{3,19},{4,20},{5,21},{6,22},{7,23},{8,24},{9,... | collective-permute-start | bytes 1032200 | tf_op jit(solution)/shard_map/ppermute | solution.py:31
  122.0 8.3 %collective-permute-start.22 = (bf16[64,2688]{1,0:T(8,128)(2,1)S(1)}, bf16[64,2688]{1,0:T(8,128)(2,1)S(1)}, u32[]{:S(2)}, u32[]{:S(2)}) collective-permute-start(bf16[64,2688]{1,0:T(8,128)(2,1)S(1)} %slice.140), channel_id=1, source_target_pairs={{0,48},{1,49},{2,50},{3,51},{4,52},{5,53},{6,54},{7,55},{8,56},{9,... | collective-permute-start | bytes 1032200 | tf_op jit(solution)/shard_map/ppermute | solution.py:31
  135.2 25.3 %collective-permute-start.24 = (bf16[256,2048]{1,0:T(8,128)(2,1)S(1)}, bf16[256,2048]{1,0:T(8,128)(2,1)S(1)}, u32[]{:S(2)}, u32[]{:S(2)}) collective-permute-start(bf16[256,2048]{1,0:T(8,128)(2,1)S(1)} %get-tuple-element.113), channel_id=1, source_target_pairs={{0,1},{1,0},{2,3},{3,2},{4,5},{5,4},{6,7},{7,6},{8,9},{9,8},{10,11... | collective-permute-start | bytes 3145736 | tf_op jit(solution)/shard_map/ppermute | solution.py:31
  135.3 18.5 %collective-permute-start.25 = (bf16[128,2688]{1,0:T(8,128)(2,1)S(1)}, bf16[128,2688]{1,0:T(8,128)(2,1)S(1)}, u32[]{:S(2)}, u32[]{:S(2)}) collective-permute-start(bf16[128,2688]{1,0:T(8,128)(2,1)S(1)} %pad_maximum_fusion.5.refs_0_.refs_9_), channel_id=1, source_target_pairs={{0,48},{1,49},{2,50},{3,51},{4,52},{5,53},{6,54},{7,55},{8,56},{9,... | collective-permute-start | bytes 2064392 | tf_op jit(solution)/shard_map/ppermute | solution.py:31
  138.5 18.7 %collective-permute-start.26 = (bf16[128,2688]{1,0:T(8,128)(2,1)S(1)}, bf16[128,2688]{1,0:T(8,128)(2,1)S(1)}, u32[]{:S(2)}, u32[]{:S(2)}) collective-permute-start(bf16[128,2688]{1,0:T(8,128)(2,1)S(1)} %pad_maximum_fusion.5.refs_0_.refs_9_), channel_id=1, source_target_pairs={{0,16},{1,17},{2,18},{3,19},{4,20},{5,21},{6,22},{7,23},{8,24},{9,... | collective-permute-start | bytes 2064392 | tf_op jit(solution)/shard_map/ppermute | solution.py:31
  157.3 10.6 %collective-permute-start.31 = (bf16[64,2688]{1,0:T(8,128)(2,1)S(1)}, bf16[64,2688]{1,0:T(8,128)(2,1)S(1)}, u32[]{:S(2)}, u32[]{:S(2)}) collective-permute-start(bf16[64,2688]{1,0:T(8,128)(2,1)S(1)} %slice.144), channel_id=1, source_target_pairs={{0,16},{1,17},{2,18},{3,19},{4,20},{5,21},{6,22},{7,23},{8,24},{9,... | collective-permute-start | bytes 1032200 | tf_op jit(solution)/shard_map/ppermute | solution.py:31
  157.3 10.5 %collective-permute-start.32 = (bf16[64,2688]{1,0:T(8,128)(2,1)S(1)}, bf16[64,2688]{1,0:T(8,128)(2,1)S(1)}, u32[]{:S(2)}, u32[]{:S(2)}) collective-permute-start(bf16[64,2688]{1,0:T(8,128)(2,1)S(1)} %slice.145), channel_id=1, source_target_pairs={{0,48},{1,49},{2,50},{3,51},{4,52},{5,53},{6,54},{7,55},{8,56},{9,... | collective-permute-start | bytes 1032200 | tf_op jit(solution)/shard_map/ppermute | solution.py:31
  172.9 4.9 %collective-permute-start.33 = (bf16[256,2048]{1,0:T(8,128)(2,1)S(1)}, bf16[256,2048]{1,0:T(8,128)(2,1)S(1)}, u32[]{:S(2)}, u32[]{:S(2)}) collective-permute-start(bf16[256,2048]{1,0:T(8,128)(2,1)S(1)} %get-tuple-element.123), channel_id=1, source_target_pairs={{0,1},{1,0},{2,3},{3,2},{4,5},{5,4},{6,7},{7,6},{8,9},{9,8},{10,11... | collective-permute-start | bytes 3145736 | tf_op jit(solution)/shard_map/ppermute | solution.py:31
  173.3 10.4 %collective-permute-start.27 = (bf16[64,2048]{1,0:T(8,128)(2,1)S(1)}, bf16[64,2048]{1,0:T(8,128)(2,1)S(1)}, u32[]{:S(2)}, u32[]{:S(2)}) collective-permute-start(bf16[64,2048]{1,0:T(8,128)(2,1)S(1)} %get-tuple-element.150), channel_id=1, source_target_pairs={{0,4},{1,5},{2,6},{3,7},{4,8},{5,9},{6,10},{7,11},{8,12},{9,13},{1... | collective-permute-start | bytes 786440 | tf_op jit(solution)/shard_map/ppermute | solution.py:31
  174.2 16.3 %collective-permute-start.28 = (bf16[64,2048]{1,0:T(8,128)(2,1)S(1)}, bf16[64,2048]{1,0:T(8,128)(2,1)S(1)}, u32[]{:S(2)}, u32[]{:S(2)}) collective-permute-start(bf16[64,2048]{1,0:T(8,128)(2,1)S(1)} %get-tuple-element.152), channel_id=1, source_target_pairs={{0,8},{1,9},{2,10},{3,11},{4,12},{5,13},{6,14},{7,15},{8,0},{9,1},... | collective-permute-start | bytes 786440 | tf_op jit(solution)/shard_map/ppermute | solution.py:31
  177.8 12.7 %collective-permute-start.29 = (bf16[64,2048]{1,0:T(8,128)(2,1)S(1)}, bf16[64,2048]{1,0:T(8,128)(2,1)S(1)}, u32[]{:S(2)}, u32[]{:S(2)}) collective-permute-start(bf16[64,2048]{1,0:T(8,128)(2,1)S(1)} %get-tuple-element.151), channel_id=1, source_target_pairs={{0,12},{1,13},{2,14},{3,15},{4,0},{5,1},{6,2},{7,3},{8,4},{9,5},{1... | collective-permute-start | bytes 786440 | tf_op jit(solution)/shard_map/ppermute | solution.py:31
  178.2 16.3 %collective-permute-start.34 = (bf16[64,2048]{1,0:T(8,128)(2,1)S(1)}, bf16[64,2048]{1,0:T(8,128)(2,1)S(1)}, u32[]{:S(2)}, u32[]{:S(2)}) collective-permute-start(bf16[64,2048]{1,0:T(8,128)(2,1)S(1)} %get-tuple-element.147), channel_id=1, source_target_pairs={{0,4},{1,5},{2,6},{3,7},{4,8},{5,9},{6,10},{7,11},{8,12},{9,13},{1... | collective-permute-start | bytes 786440 | tf_op jit(solution)/shard_map/ppermute | solution.py:31
  180.3 21.0 %collective-permute-start.35 = (bf16[64,2048]{1,0:T(8,128)(2,1)S(1)}, bf16[64,2048]{1,0:T(8,128)(2,1)S(1)}, u32[]{:S(2)}, u32[]{:S(2)}) collective-permute-start(bf16[64,2048]{1,0:T(8,128)(2,1)S(1)} %get-tuple-element.149), channel_id=1, source_target_pairs={{0,8},{1,9},{2,10},{3,11},{4,12},{5,13},{6,14},{7,15},{8,0},{9,1},... | collective-permute-start | bytes 786440 | tf_op jit(solution)/shard_map/ppermute | solution.py:31
  183.7 17.7 %collective-permute-start.36 = (bf16[64,2048]{1,0:T(8,128)(2,1)S(1)}, bf16[64,2048]{1,0:T(8,128)(2,1)S(1)}, u32[]{:S(2)}, u32[]{:S(2)}) collective-permute-start(bf16[64,2048]{1,0:T(8,128)(2,1)S(1)} %get-tuple-element.148), channel_id=1, source_target_pairs={{0,12},{1,13},{2,14},{3,15},{4,0},{5,1},{6,2},{7,3},{8,4},{9,5},{1... | collective-permute-start | bytes 786440 | tf_op jit(solution)/shard_map/ppermute | solution.py:31
  190.6 14.0 %copy-start.4 = (s32[8,7]{1,0:T(8,128)S(1)}, s32[8,7]{1,0:T(8,128)}, u32[]{:S(2)}) copy-start(s32[8,7]{1,0:T(8,128)} %refs_14_.1) | copy-start | bytes 676
  190.7 14.0 %copy-start.6 = (s32[8,7]{1,0:T(8,128)S(1)}, s32[8,7]{1,0:T(8,128)}, u32[]{:S(2)}) copy-start(s32[8,7]{1,0:T(8,128)} %refs_15_.1) | copy-start | bytes 676
  190.7 14.0 %copy-start.8 = (s32[7,8]{1,0:T(8,128)S(1)}, s32[7,8]{1,0:T(8,128)}, u32[]{:S(2)}) copy-start(s32[7,8]{1,0:T(8,128)} %refs_16_.1) | copy-start | bytes 676
  190.7 13.9 %collective-permute-start.30 = (bf16[32,2048]{1,0:T(8,128)(2,1)S(1)}, bf16[32,2048]{1,0:T(8,128)(2,1)S(1)}, u32[]{:S(2)}, u32[]{:S(2)}) collective-permute-start(bf16[32,2048]{1,0:T(8,128)(2,1)S(1)} %slice.171), channel_id=1, source_target_pairs={{0,2},{1,3},{2,0},{3,1},{4,6},{5,7},{6,4},{7,5},{8,10},{9,11},{10,... | collective-permute-start | bytes 393224 | tf_op jit(solution)/shard_map/ppermute | solution.py:31
  201.5 15.4 %collective-permute-start.37 = (bf16[32,2048]{1,0:T(8,128)(2,1)S(1)}, bf16[32,2048]{1,0:T(8,128)(2,1)S(1)}, u32[]{:S(2)}, u32[]{:S(2)}) collective-permute-start(bf16[32,2048]{1,0:T(8,128)(2,1)S(1)} %slice.177), channel_id=1, source_target_pairs={{0,2},{1,3},{2,0},{3,1},{4,6},{5,7},{6,4},{7,5},{8,10},{9,11},{10,... | collective-permute-start | bytes 393224 | tf_op jit(solution)/shard_map/ppermute | solution.py:31

commit v2 on v1

--- a/solution.py
+++ b/solution.py
@@ -8,7 +8,30 @@
 from jax.sharding import PartitionSpec as P
 
 BLK = 128
-CHUNKS = ((32, True, True), (32, True, True))
+CHUNKS = (32, 32)
+GATHERS = ((0,), (1,))
+ORDER = (
+    "forward 0",
+    "core 1",
+    "relay 0",
+    "forward 1",
+    "swap 0",
+    "relay 1",
+    "spread 0",
+    "swap 1",
+    "far 0",
+    "spread 1",
+    "backward 0",
+    "far 1",
+    "send 0",
+    "chip 0",
+    "backward 1",
+    "send 1",
+    "chip 1",
+    "grads",
+    "last 0",
+    "last 1",
+)
 SEND_UP = ((2, 0), (1, 1))
 SEND_DOWN = ((2, 1), (3, 0))
 NEXT_UP = ((1, 0),)
@@ -66,23 +89,13 @@
     return lax.rem(lax.axis_index("row") + dz, 4)
 
 
-def token_copies(gathered, pieces, held, first, sems):
-    rows = held_rows = None
+def token_copies(gathered, offset, rows, pieces, held, first, sems):
     copies = []
-    if len(gathered) == 2:
-        rows = gathered[0].shape[2]
-        for at, (dz, half) in enumerate(pieces):
-            to = held.at[:, pl.ds(first + at * rows, rows)]
-            copies.append((gathered[half].at[owner(dz)], to))
-    else:
-        rows = gathered[0].shape[2]
-        for at, (dz, half) in enumerate(pieces):
-            for sub in range(2):
-                to = held.at[:, pl.ds(first + (2 * at + sub) * rows, rows)]
-                copies.append((gathered[0].at[owner(dz) * 4 + half * 2 + sub], to))
-    return [
-        pltpu.make_async_copy(source, to, sems.at[at]) for at, (source, to) in enumerate(copies)
-    ]
+    for at, (dz, half) in enumerate(pieces):
+        source = gathered[half].at[owner(dz), :, pl.ds(offset, rows)]
+        to = held.at[:, pl.ds(first + at * rows, rows)]
+        copies.append(pltpu.make_async_copy(source, to, sems.at[at]))
+    return copies
 
 
 def gathered_at(piece, arrays, rows):
@@ -158,11 +171,11 @@
         copy.wait()
 
 
-def forward_kernel(count, *refs):
-    gathered, weights, outs = refs[:count], refs[count], refs[count + 1 : count + 6]
-    held, held_weights, sems, weight_sems = refs[count + 6 :]
+def forward_kernel(offset, rows, *refs):
+    gathered, weights, outs = refs[:2], refs[2], refs[3:8]
+    held, held_weights, sems, weight_sems = refs[8:]
     pieces = [piece for group in GROUPS for piece in group]
-    copies = token_copies(gathered, pieces, held, 0, sems)
+    copies = token_copies(gathered, offset, rows, pieces, held, 0, sems)
     loads = weight_copies(weights, held_weights, weight_sems, range(3))
     start(loads[0])
     start(copies)
@@ -170,7 +183,6 @@
     start(loads[2])
     wait(copies)
     width = weights.shape[1] // 3
-    rows = held.shape[1] // 8
     for at in range(3):
         wait(loads[at])
         columns = slice(at * width, (at + 1) * width)
@@ -182,13 +194,11 @@
             first += size
 
 
-def forward(gathered, weights):
+def forward(gathered, offset, rows, weights):
     depth, total = weights.shape
-    count = len(gathered)
-    rows = gathered[0].shape[2] * count // 2 if count == 2 else gathered[0].shape[2] * 2
     return pl.pallas_call(
-        functools.partial(forward_kernel, count),
-        in_specs=[ANY] * (count + 1),
+        functools.partial(forward_kernel, offset, rows),
+        in_specs=[ANY] * 3,
         out_specs=[VMEM] * len(GROUPS),
         out_shape=[
             jax.ShapeDtypeStruct((len(group) * rows, total), jnp.bfloat16) for group in GROUPS
@@ -196,7 +206,7 @@
         scratch_shapes=[
             pltpu.VMEM((2, 8 * rows, depth), jnp.bfloat16),
             pltpu.VMEM((depth, total), jnp.bfloat16),
-            pltpu.SemaphoreType.DMA((16,)),
+            pltpu.SemaphoreType.DMA((8,)),
             pltpu.SemaphoreType.DMA((3, 2)),
         ],
         compiler_params=params(),
@@ -205,39 +215,15 @@
     )(*gathered, weights)
 
 
-def place(piece, sub, gather_hops, scatter_hops):
-    dz, half = piece
-    col = lax.axis_index("col")
-    y_me, x_me, core_me = col // 4, lax.rem(col // 2, 2), lax.rem(col, 2)
-    if gather_hops:
-        y, x, core = owner(dz), sub, half
-        if scatter_hops:
-            return ((1 - core) * 4 + y) * 2 + x
-        return (lax.rem(y + y_me, 4) * 2 + lax.rem(x + x_me, 2)) * 2 + lax.rem(core + core_me, 2)
-    y, x, core = owner(dz), half, sub
-    if not scatter_hops:
-        return (y * 2 + x) * 2 + core
-    other = lax.rem(core + core_me, 2)
-    return ((1 - other) * 4 + lax.rem(y - y_me + 4, 4)) * 2 + lax.rem(x + x_me, 2)
-
-
-def backward_kernel(gather_hops, scatter_hops, *refs):
+def backward_kernel(*refs):
     arrays, weights = refs[:5], refs[5]
-    outs, (held, held_weights, sems, weight_sems) = refs[6:-4], refs[-4:]
+    outs, (held, held_weights, sems, weight_sems) = refs[6:8], refs[8:]
     rows = arrays[3].shape[0]
     copies = []
-    together = gather_hops == scatter_hops
-    for piece in GATHERED:
-        source = gathered_at(piece, arrays, rows)
-        size = rows if together else rows // 2
-        for sub in range(1 if together else 2):
-            at = place(piece, sub, gather_hops, scatter_hops)
-            to = pl.ds(pl.multiple_of(at * (rows // 2), rows // 2), size)
-            copies.append(
-                pltpu.make_async_copy(
-                    source.at[pl.ds(sub * size, size)], held.at[to], sems.at[len(copies)]
-                )
-            )
+    for at, (dz, half) in enumerate(GATHERED):
+        source = gathered_at((dz, half), arrays, rows)
+        to = pl.ds(pl.multiple_of(((1 - half) * 4 + owner(dz)) * rows, rows), rows)
+        copies.append(pltpu.make_async_copy(source, held.at[to], sems.at[at]))
     loads = weight_copies(weights, held_weights, weight_sems, (2, 0, 1))
     start(loads[0])
     start(copies)
@@ -265,44 +251,44 @@
     put(nt(held[:, columns], held_weights[:, columns]), depth)
 
 
-def backward(arrays, weights, gather_hops, scatter_hops):
+def backward(arrays, weights):
     rows = arrays[3].shape[0]
     depth, total = weights.shape
-    count = 2 if scatter_hops else 1
     return pl.pallas_call(
-        functools.partial(backward_kernel, gather_hops, scatter_hops),
+        backward_kernel,
         in_specs=[ANY] * 6,
-        out_specs=[VMEM] * count,
-        out_shape=[jax.ShapeDtypeStruct((8 * rows // count, 2 * depth), jnp.bfloat16)] * count,
+        out_specs=[VMEM] * 2,
+        out_shape=[jax.ShapeDtypeStruct((4 * rows, 2 * depth), jnp.bfloat16)] * 2,
         scratch_shapes=[
             pltpu.VMEM((8 * rows, total), jnp.bfloat16),
             pltpu.VMEM((depth, total), jnp.bfloat16),
-            pltpu.SemaphoreType.DMA((16,)),
+            pltpu.SemaphoreType.DMA((8,)),
             pltpu.SemaphoreType.DMA((3, 2)),
         ],
         compiler_params=params(),
-        cost_estimate=cheap(),
+        cost_estimate=pl.CostEstimate(
+            flops=16 * rows * depth * total, bytes_accessed=8 * depth * total, transcendentals=0
+        ),
         name="backward",
     )(*arrays, weights)
 
 
-def weight_grad_kernel(counts, *refs):
-    number = sum(counts) + 5 * len(counts)
+def weight_grad_kernel(offsets, *refs):
+    number = 7 * len(offsets)
     gate_mask, up_mask, down_mask, gate_grad, up_grad, down_grad = refs[number : number + 6]
     tokens, values, sems, value_sems = refs[number + 6 :]
-    first = at = 0
+    first = 0
     copies = []
-    for which, count in enumerate(counts):
-        gathered, arrays = refs[at : at + count], refs[at + count : at + count + 5]
-        at += count + 5
+    for which, offset in enumerate(offsets):
+        gathered, arrays = refs[7 * which : 7 * which + 2], refs[7 * which + 2 : 7 * which + 7]
         rows = arrays[3].shape[0]
-        copies += token_copies(gathered, GATHERED, tokens, first, sems.at[which])
-        for number, piece in enumerate(GATHERED):
+        copies += token_copies(gathered, offset, rows, GATHERED, tokens, first, sems.at[which])
+        for at, piece in enumerate(GATHERED):
             copies.append(
                 pltpu.make_async_copy(
                     gathered_at(piece, arrays, rows),
-                    values.at[pl.ds(first + number * rows, rows)],
-                    value_sems.at[which, number],
+                    values.at[pl.ds(first + at * rows, rows)],
+                    value_sems.at[which, at],
                 )
             )
         first += 8 * rows
@@ -329,15 +315,14 @@
         store(tn(left, tokens[1]), down_mask, row, down_grad)
 
 
-def weight_grads(chunks, gate_mask, up_mask, down_mask):
+def weight_grads(offsets, chunks, gate_mask, up_mask, down_mask):
     depth = chunks[0][0][0].shape[-1]
     total = chunks[0][1][0].shape[-1]
     width = total // 3
-    counts = tuple(len(gathered) for gathered, _ in chunks)
     count = sum(8 * arrays[3].shape[0] for _, arrays in chunks)
     inputs = [item for gathered, arrays in chunks for item in (*gathered, *arrays)]
     return pl.pallas_call(
-        functools.partial(weight_grad_kernel, counts),
+        functools.partial(weight_grad_kernel, offsets),
         in_specs=[ANY] * len(inputs) + [SMEM] * 3,
         out_specs=[VMEM] * 3,
         out_shape=[
@@ -348,11 +333,13 @@
         scratch_shapes=[
             pltpu.VMEM((2, count, depth), jnp.bfloat16),
             pltpu.VMEM((count, total), jnp.bfloat16),
-            pltpu.SemaphoreType.DMA((len(chunks), 16)),
+            pltpu.SemaphoreType.DMA((len(chunks), 8)),
             pltpu.SemaphoreType.DMA((len(chunks), 8)),
         ],
         compiler_params=params(),
-        cost_estimate=cheap(),
+        cost_estimate=pl.CostEstimate(
+            flops=2 * count * depth * total, bytes_accessed=16 * depth * total, transcendentals=0
+        ),
         name="weight_grads",
     )(*inputs, gate_mask, up_mask, down_mask)
 
@@ -382,45 +369,29 @@
     return (wide(for_own) + wide(received)).astype(jnp.bfloat16)
 
 
-def gather_pair(part):
-    return jnp.concatenate([part, move(part, dxh=1)], axis=1)
-
-
-def scatter_pairs(chip):
-    rows = chip.shape[0] // 4
-    total = wide(chip[:rows])
-    for dy in range(1, 4):
-        total = total + wide(move(chip[dy * rows : (dy + 1) * rows], dy=dy))
-    return total.astype(jnp.bfloat16)
-
-
-def scatter_pair(pair):
-    rows = pair.shape[0] // 2
-    return (wide(pair[:rows]) + wide(move(pair[rows:], dxh=1))).astype(jnp.bfloat16)
-
-
-class Chunk:
-    def __init__(self, part, gather_hops, scatter_hops):
-        self.part, self.hops = part, (gather_hops, scatter_hops)
-
-    def gather_near(self):
-        self.pair = gather_pair(self.part)
-
-    def gather_far(self, *others):
+class Gather:
+    def __init__(self, pair):
+        self.pair = pair
+
+    def far(self, *others):
         self.pair = after(self.pair, *others)
         self.pairs = [self.pair] + [move(self.pair, dy=-dy) for dy in range(1, 4)]
-        return self.pair
-
-    def gather_core(self, *others):
+
+    def core(self, *others):
         own = jnp.stack(after(self.pairs, *others))
-        self.gathered = (own, move(own, dcore=1))
+        self.arrays = (own, move(own, dcore=1))
         return own
 
-    def gather(self):
-        self.gathered = (lax.all_gather(self.part, "col", axis=0),)
-
-    def forward(self, weights):
-        outs = forward(self.gathered, weights)
+
+class Chunk:
+    def __init__(self, gather, offset, rows, weights):
+        self.source, self.offset, self.rows = gather, offset, 2 * rows
+        self.weights = weights
+
+    def forward(self, *others):
+        self.gathered = self.source.arrays
+        gathered = after(self.gathered, *others)
+        outs = forward(gathered, self.offset, self.rows, self.weights)
         self.late_up, self.late_down, self.kept = outs[2:]
         self.from_down = move(outs[0], dz=1)
         self.from_up = move(outs[1], dz=-1)
@@ -428,7 +399,7 @@
 
     def relay(self, *others):
         down, up = after((self.from_down, self.from_up), *others)
-        rows = down.shape[0] // 2
+        rows = self.rows
         send_up = self.late_up + down[:rows]
         send_down = self.late_down + up[:rows]
         self.last_down = move(send_up, dz=1)
@@ -438,7 +409,7 @@
 
     def swap(self, *others):
         last_down, last_up = after((self.last_down, self.last_up), *others)
-        rows = last_down.shape[0]
+        rows = self.rows
         self.sums = jnp.concatenate(
             [
                 wide(self.kept[:rows]) + wide(last_down) + wide(self.direct[0]),
@@ -456,65 +427,68 @@
 
     def far(self, *others):
         up, down = after(self.near, *others)
-        rows = up.shape[0] // 2
-        sent = down[:rows], up[rows:]
+        sent = down[: self.rows], up[self.rows :]
         self.arrays = (self.values, up, down, move(sent[0], dz=1), move(sent[1], dz=-1))
         return sent
 
-    def backward(self, weights, *others):
+    def backward(self, *others):
         self.arrays = after(self.arrays, *others)
-        outs = backward(self.arrays, weights, *self.hops)
-        if self.hops[1]:
-            self.for_own = outs[1]
-            self.received = move(outs[0], dcore=1)
-        else:
-            self.result = lax.psum_scatter(outs[0], "col", scatter_dimension=0, tiled=True)
-        return outs[0]
-
-    def scatter(self, *others):
-        if self.hops[1]:
-            received = after(self.received, *others)
-            chip = chip_sum(self.for_own, received)
-            self.result = scatter_pair(scatter_pairs(chip))
-            return chip
-        return None
+        self.for_other, self.for_own = backward(self.arrays, self.weights)
+        return self.for_other
+
+    def send(self, *others):
+        for_other = after(self.for_other, *others)
+        self.received = move(for_other, dcore=1)
+        return for_other
+
+    def chip(self, *others):
+        received = after(self.received, *others)
+        chip = (wide(self.for_own) + wide(received)).astype(jnp.bfloat16)
+        rows = self.rows
+        self.parts = [chip[:rows]] + [
+            move(chip[dy * rows : (dy + 1) * rows], dy=dy) for dy in range(1, 4)
+        ]
+        return chip
+
+    def last(self, *others):
+        total = sum(wide(part) for part in after(self.parts, *others)).astype(jnp.bfloat16)
+        half = self.rows // 2
+        self.result = wide(total[:half]) + wide(move(total[half:], dxh=1))
+        return total
 
 
 def shards(tokens, out_grad, gate_weight, up_weight, down_weight, gate_mask, up_mask, down_mask):
     depth = tokens.shape[1]
-    chunks = []
-    first = 0
-    for rows, gather_hops, scatter_hops in CHUNKS:
-        part = jnp.stack([tokens[first : first + rows], out_grad[first : first + rows]])
-        chunks.append(Chunk(part, gather_hops, scatter_hops))
-        first += rows
-    a, b = chunks
+    starts = [sum(CHUNKS[:i]) for i in range(len(CHUNKS))]
+    part = jnp.stack([tokens, out_grad])
+    received = move(part, dxh=1)
     weights = mask_weights(gate_weight, up_weight, down_weight, gate_mask, up_mask, down_mask)
-    a.gather_near()
-    b.gather_near()
-    a.pair, b.pair, weights = lax.optimization_barrier((a.pair, b.pair, weights))
-    a.gather_far()
-    own_a = a.gather_core()
-    b.gather_far(own_a)
-    up_a = a.forward(weights)
-    own_b = b.gather_core(up_a)
-    up_b = b.forward(weights)
-    relay_a = a.relay(up_b)
-    swap_a = a.swap(relay_a)
-    relay_b = b.relay(swap_a)
-    spread_a = a.spread(relay_b)
-    swap_b = b.swap(spread_a)
-    far_a = a.far(swap_b)
-    spread_b = b.spread(far_a)
-    back_a = a.backward(weights, spread_b)
-    far_b = b.far(back_a)
-    chip_a = a.scatter(far_b)
-    back_b = b.backward(weights, chip_a)
-    chip_b = b.scatter()
-    inputs = after([(chunk.gathered, chunk.arrays) for chunk in chunks], chip_b)
-    gate_grad, up_grad, down_grad = weight_grads(inputs, gate_mask, up_mask, down_mask)
-    result = jnp.concatenate([chunk.result for chunk in chunks])
-    return (result[:, :depth], result[:, depth:], gate_grad, up_grad, down_grad)
+    gathers, chunks = [], []
+    for group in GATHERS:
+        slices = [slice(starts[i], starts[i] + CHUNKS[i]) for i in group]
+        gather = Gather(
+            jnp.concatenate([half[:, at] for at in slices for half in (part, received)], axis=1)
+        )
+        gathers.append(gather)
+        for i in group:
+            offset = 2 * (starts[i] - starts[group[0]])
+            chunks.append(Chunk(gather, offset, CHUNKS[i], weights))
+    gathers[0].far()
+    before = gathers[0].core()
+    gathers[1].far(before)
+    for step in ORDER:
+        name, _, which = step.partition(" ")
+        if name == "core":
+            before = gathers[int(which)].core(before)
+        elif name == "grads":
+            inputs = after([(chunk.gathered, chunk.arrays) for chunk in chunks], before)
+            offsets = tuple(chunk.offset for chunk in chunks)
+            grads = weight_grads(offsets, inputs, gate_mask, up_mask, down_mask)
+            before = grads[0]
+        else:
+            before = getattr(chunks[int(which)], name)(before)
+    result = jnp.concatenate([chunk.result for chunk in chunks]).astype(jnp.bfloat16)
+    return (result[:, :depth], result[:, depth:], *grads)
 
 
 def solution(mesh):

time: 218 us -> 204 us (0.936)
  waiting for transfers between devices: 116 us -> 109 us
  local copies, waits for them, and re-layouts: 7.77 us -> 1.82 us
  starting transfers between devices: 55.1 us -> 52.8 us
  other arithmetic: 3.86 us -> 6.05 us
    ppermute x38 -> x37, waiting for transfers between devices: 116 us -> 109 us  [move(): return lax.ppermute(array, ('row', 'col'), pairs)]
    unnamed x18 -> x12, local copies, waits for them, and re-layouts: 6.57 us -> 1.52 us
    ppermute x38 -> x37, starting transfers between devices: 55.1 us -> 52.8 us  [move(): return lax.ppermute(array, ('row', 'col'), pairs)]
  transfers between devices with their start and end apart: 38 -> 37, of which waited for: 20 -> 21; matrix products, arithmetic and copies ran while one was open for 1% -> 2% of each run, Pallas kernels for 11% -> 12%
where the time goes in v2:
time: 204 us
  waiting for transfers between devices  109 us (53%)
  starting transfers between devices  52.8 us (26%)
  Pallas kernels  33.8 us (17%)
  other arithmetic  6.05 us (3%)
    ppermute x37, waiting for transfers between devices, move(): return lax.ppermute(array, ('row', 'col'), pairs)  109 us
    ppermute x37, starting transfers between devices, move(): return lax.ppermute(array, ('row', 'col'), pairs)  52.8 us
    pallas_call x1, Pallas kernels, weight_grads(): pl.pallas_call(functools.partial(weight_grad_kernel, offsets), in_specs=[...  12 us
    pallas_call x2, Pallas kernels, backward(): pl.pallas_call(backward_kernel, in_specs=[ANY] * 6, out_specs=[VMEM] * 2,...  9.94 us
    pallas_call x2, Pallas kernels, forward(): pl.pallas_call(functools.partial(forward_kernel, offset, rows), in_specs=...  9.02 us
  transfers between devices with their start and end apart: 37, of which 21 were waited for; matrix products, arithmetic and copies ran while one was open for 2% of the time, Pallas kernels for 12%

profile of v2, /device:TPU:0, one launch (start us, length us, event | category | flops | bytes accessed | tf_op | source)
XLA Modules:
  0.0 204.1 jit_solution(18352509266413305269)
XLA Ops:
  1.6 3.2 %collective-permute-start = (bf16[2,64,1024]{2,1,0:T(8,128)(2,1)S(1)}, bf16[2,64,1024]{2,1,0:T(8,128)(2,1)S(1)}, u32[]{:S(2)}, u32[]{:S(2)}) collective-permute-start(bf16[2,64,1024]{2,1,0:T(8,128)(2,1)S(1)} %pad_maximum_fusion.6), channel_id=1, source_target_pairs={{0,2},{1,3},{2,0},{3,1},{4,6},{5,7},{6,4},{7,5},{8,10},{9,11},{10,... | collective-permute-start | bytes 786440 | tf_op jit(solution)/shard_map/ppermute | solution.py:54
  5.9 5.2 %collective-permute-done = bf16[2,64,1024]{2,1,0:T(8,128)(2,1)S(1)} collective-permute-done((bf16[2,64,1024]{2,1,0:T(8,128)(2,1)S(1)}, bf16[2,64,1024]{2,1,0:T(8,128)(2,1)S(1)}, u32[]{:S(2)}, u32[]{:S(2)}) %collective-permute-start) | collective-permute-done | bytes 262176 | tf_op jit(solution)/shard_map/ppermute | solution.py:54
  11.2 1.9 collective-permute-start.3
  13.1 2.9 %collective-permute-start.2 = (bf16[2,64,1024]{2,1,0:T(8,128)(2,1)S(1)}, bf16[2,64,1024]{2,1,0:T(8,128)(2,1)S(1)}, u32[]{:S(2)}, u32[]{:S(2)}) collective-permute-start(bf16[2,64,1024]{2,1,0:T(8,128)(2,1)S(1)} %pad_maximum_fusion.7), channel_id=1, source_target_pairs={{0,8},{1,9},{2,10},{3,11},{4,12},{5,13},{6,14},{7,15},{8,0},{9,1},... | collective-permute-start | bytes 786440 | tf_op jit(solution)/shard_map/ppermute | solution.py:54
  16.0 1.3 collective-permute-start.1
  17.3 3.5 %collective-permute-done.3 = bf16[2,64,1024]{2,1,0:T(8,128)(2,1)S(1)} collective-permute-done((bf16[2,64,1024]{2,1,0:T(8,128)(2,1)S(1)}, bf16[2,64,1024]{2,1,0:T(8,128)(2,1)S(1)}, u32[]{:S(2)}, u32[]{:S(2)}) %collective-permute-start.3) | collective-permute-done | bytes 262176 | tf_op jit(solution)/shard_map/ppermute | solution.py:54
  20.8 5.9 %collective-permute-done.2 = bf16[2,64,1024]{2,1,0:T(8,128)(2,1)S(1)} collective-permute-done((bf16[2,64,1024]{2,1,0:T(8,128)(2,1)S(1)}, bf16[2,64,1024]{2,1,0:T(8,128)(2,1)S(1)}, u32[]{:S(2)}, u32[]{:S(2)}) %collective-permute-start.2) | collective-permute-done | bytes 262176 | tf_op jit(solution)/shard_map/ppermute | solution.py:54
  27.0 1.5 copy-done.2
  28.5 2.8 %mask_weights.1.refs_2_.refs_5_ = bf16[1024,2688]{1,0:T(8,128)(2,1)S(1)} custom-call(bf16[1024,896]{1,0:T(8,128)(2,1)S(1)} %copy-done, bf16[1024,896]{1,0:T(8,128)(2,1)S(1)} %copy-done.1, bf16[896,1024]{1,0:T(8,128)(2,1)S(1)} %copy-done.2, s32[8,7]{1,0:T(8,128)S(1)} %copy-done.3, s32[8,7]{1,0:T(8,128)S(1)} %copy-done.4, s32[7,8]{1,0:T(8,128)S(1)} %copy-done.5), custom_call_target="tpu_custom_call" | custom-call | flops 2752512 | bytes 11010048 | tf_op jit(solution)/shard_map/mask_weights/pallas_call | solution.py:124
  31.3 4.5 %forward.2 = (bf16[128,2688]{1,0:T(8,128)(2,1)S(1)}, bf16[128,2688]{1,0:T(8,128)(2,1)S(1)}, bf16[64,2688]{1,0:T(8,128)(2,1)S(1)}, bf16[64,2688]{1,0:T(8,128)(2,1)S(1)}, bf16[128,2688]{1,0:T(8,128)(2,1)S(1)}) custom-call(bf16[4,2,64,1024]{3,2,1,0:T(8,128)(2,1)S(1)} %pad_maximum_fusion.refs_0_, bf16[4,2,64,1024]{3,2,1,0:T(8,128)(2,1)S(1)} %collective-permute-done.4.refs_1_, ...), custom_call_target="tpu_custom_call" | custom-call | flops 1024 | bytes 1024 | tf_op jit(solution)/shard_map/forward/pallas_call | solution.py:199
  35.9 4.1 %collective-permute-start.6 = (bf16[128,2688]{1,0:T(8,128)(2,1)S(1)}, bf16[128,2688]{1,0:T(8,128)(2,1)S(1)}, u32[]{:S(2)}, u32[]{:S(2)}) collective-permute-start(bf16[128,2688]{1,0:T(8,128)(2,1)S(1)} %get-tuple-element.93), channel_id=1, source_target_pairs={{0,48},{1,49},{2,50},{3,51},{4,52},{5,53},{6,54},{7,55},{8,56},{9,... | collective-permute-start | bytes 2064392 | tf_op jit(solution)/shard_map/ppermute | solution.py:54
  40.0 1.3 collective-permute-start.9
  41.3 2.4 %collective-permute-start.8 = (bf16[2,64,1024]{2,1,0:T(8,128)(2,1)S(1)}, bf16[2,64,1024]{2,1,0:T(8,128)(2,1)S(1)}, u32[]{:S(2)}, u32[]{:S(2)}) collective-permute-start(bf16[2,64,1024]{2,1,0:T(8,128)(2,1)S(1)} %pad_maximum_fusion.8), channel_id=1, source_target_pairs={{0,8},{1,9},{2,10},{3,11},{4,12},{5,13},{6,14},{7,15},{8,0},{9,1},... | collective-permute-start | bytes 786440 | tf_op jit(solution)/shard_map/ppermute | solution.py:54
  43.7 1.6 collective-permute-start.7
  45.3 4.8 %collective-permute-done.9 = bf16[2,64,1024]{2,1,0:T(8,128)(2,1)S(1)} collective-permute-done((bf16[2,64,1024]{2,1,0:T(8,128)(2,1)S(1)}, bf16[2,64,1024]{2,1,0:T(8,128)(2,1)S(1)}, u32[]{:S(2)}, u32[]{:S(2)}) %collective-permute-start.9) | collective-permute-done | bytes 262176 | tf_op jit(solution)/shard_map/ppermute | solution.py:54
  50.0 5.6 %collective-permute-done.8 = bf16[2,64,1024]{2,1,0:T(8,128)(2,1)S(1)} collective-permute-done((bf16[2,64,1024]{2,1,0:T(8,128)(2,1)S(1)}, bf16[2,64,1024]{2,1,0:T(8,128)(2,1)S(1)}, u32[]{:S(2)}, u32[]{:S(2)}) %collective-permute-start.8) | collective-permute-done | bytes 262176 | tf_op jit(solution)/shard_map/ppermute | solution.py:54
  56.2 2.6 %collective-permute-done.5 = bf16[128,2688]{1,0:T(8,128)(2,1)S(1)} collective-permute-done((bf16[128,2688]{1,0:T(8,128)(2,1)S(1)}, bf16[128,2688]{1,0:T(8,128)(2,1)S(1)}, u32[]{:S(2)}, u32[]{:S(2)}) %collective-permute-start.5) | collective-permute-done | bytes 688160 | tf_op jit(solution)/shard_map/ppermute | solution.py:54
  59.3 1.7 collective-permute-start.10
  61.0 4.5 %forward.3 = (bf16[128,2688]{1,0:T(8,128)(2,1)S(1)}, bf16[128,2688]{1,0:T(8,128)(2,1)S(1)}, bf16[64,2688]{1,0:T(8,128)(2,1)S(1)}, bf16[64,2688]{1,0:T(8,128)(2,1)S(1)}, bf16[128,2688]{1,0:T(8,128)(2,1)S(1)}) custom-call(bf16[4,2,64,1024]{3,2,1,0:T(8,128)(2,1)S(1)} %pad_maximum_fusion.1.refs_0_.refs_7_, ...), custom_call_target="tpu_custom_call" | custom-call | flops 1024 | bytes 1024 | tf_op jit(solution)/shard_map/forward/pallas_call | solution.py:199
  65.6 2.6 %collective-permute-done.11 = bf16[64,2688]{1,0:T(8,128)(2,1)S(1)} collective-permute-done((bf16[64,2688]{1,0:T(8,128)(2,1)S(1)}, bf16[64,2688]{1,0:T(8,128)(2,1)S(1)}, u32[]{:S(2)}, u32[]{:S(2)}) %collective-permute-start.11) | collective-permute-done | bytes 344096 | tf_op jit(solution)/shard_map/ppermute | solution.py:54
  68.2 3.3 %collective-permute-done.10 = bf16[64,2688]{1,0:T(8,128)(2,1)S(1)} collective-permute-done((bf16[64,2688]{1,0:T(8,128)(2,1)S(1)}, bf16[64,2688]{1,0:T(8,128)(2,1)S(1)}, u32[]{:S(2)}, u32[]{:S(2)}) %collective-permute-start.10) | collective-permute-done | bytes 344096 | tf_op jit(solution)/shard_map/ppermute | solution.py:54
  71.8 1.8 collective-permute-start.13
  73.6 13.9 %collective-permute-done.15 = bf16[128,2688]{1,0:T(8,128)(2,1)S(1)} collective-permute-done((bf16[128,2688]{1,0:T(8,128)(2,1)S(1)}, bf16[128,2688]{1,0:T(8,128)(2,1)S(1)}, u32[]{:S(2)}, u32[]{:S(2)}) %collective-permute-start.15) | collective-permute-done | bytes 688160 | tf_op jit(solution)/shard_map/ppermute | solution.py:54
  87.5 1.8 collective-permute-start.19
  90.3 3.2 %collective-permute-start.16 = (bf16[128,2688]{1,0:T(8,128)(2,1)S(1)}, bf16[128,2688]{1,0:T(8,128)(2,1)S(1)}, u32[]{:S(2)}, u32[]{:S(2)}) collective-permute-start(bf16[128,2688]{1,0:T(8,128)(2,1)S(1)} %pad_maximum_fusion.3.refs_0_.refs_2_), channel_id=1, source_target_pairs={{0,48},{1,49},{2,50},{3,51},{4,52},{5,53},{6,54},{7,55},{8,56},{9,... | collective-permute-start | bytes 2064392 | tf_op jit(solution)/shard_map/ppermute | solution.py:54
  93.6 5.1 %collective-permute-done.19 = bf16[64,2688]{1,0:T(8,128)(2,1)S(1)} collective-permute-done((bf16[64,2688]{1,0:T(8,128)(2,1)S(1)}, bf16[64,2688]{1,0:T(8,128)(2,1)S(1)}, u32[]{:S(2)}, u32[]{:S(2)}) %collective-permute-start.19) | collective-permute-done | bytes 344096 | tf_op jit(solution)/shard_map/ppermute | solution.py:54
  98.6 3.0 %collective-permute-done.18 = bf16[64,2688]{1,0:T(8,128)(2,1)S(1)} collective-permute-done((bf16[64,2688]{1,0:T(8,128)(2,1)S(1)}, bf16[64,2688]{1,0:T(8,128)(2,1)S(1)}, u32[]{:S(2)}, u32[]{:S(2)}) %collective-permute-start.18) | collective-permute-done | bytes 344096 | tf_op jit(solution)/shard_map/ppermute | solution.py:54
  102.0 1.6 collective-permute-start.22
  103.5 9.7 %collective-permute-done.17.refs_2_.refs_4_ = bf16[128,2688]{1,0:T(8,128)(2,1)S(1)} collective-permute-done((bf16[128,2688]{1,0:T(8,128)(2,1)S(1)}, bf16[128,2688]{1,0:T(8,128)(2,1)S(1)}, u32[]{:S(2)}, u32[]{:S(2)}) %collective-permute-start.17) | collective-permute-done | bytes 688160 | tf_op jit(solution)/shard_map/ppermute | solution.py:54
  114.0 3.2 %collective-permute-start.23 = (bf16[128,2688]{1,0:T(8,128)(2,1)S(1)}, bf16[128,2688]{1,0:T(8,128)(2,1)S(1)}, u32[]{:S(2)}, u32[]{:S(2)}) collective-permute-start(bf16[128,2688]{1,0:T(8,128)(2,1)S(1)} %pad_maximum_fusion.5.refs_0_.refs_9_), channel_id=1, source_target_pairs={{0,48},{1,49},{2,50},{3,51},{4,52},{5,53},{6,54},{7,55},{8,56},{9,... | collective-permute-start | bytes 2064392 | tf_op jit(solution)/shard_map/ppermute | solution.py:54
  117.2 3.2 %collective-permute-start.21 = (bf16[64,2688]{1,0:T(8,128)(2,1)S(1)}, bf16[64,2688]{1,0:T(8,128)(2,1)S(1)}, u32[]{:S(2)}, u32[]{:S(2)}) collective-permute-start(bf16[64,2688]{1,0:T(8,128)(2,1)S(1)} %slice.140), channel_id=1, source_target_pairs={{0,48},{1,49},{2,50},{3,51},{4,52},{5,53},{6,54},{7,55},{8,56},{9,... | collective-permute-start | bytes 1032200 | tf_op jit(solution)/shard_map/ppermute | solution.py:54
  120.4 16.4 %collective-permute-done.20.refs_3_.refs_5_ = bf16[64,2688]{1,0:T(8,128)(2,1)S(1)} collective-permute-done((bf16[64,2688]{1,0:T(8,128)(2,1)S(1)}, bf16[64,2688]{1,0:T(8,128)(2,1)S(1)}, u32[]{:S(2)}, u32[]{:S(2)}) %collective-permute-start.20) | collective-permute-done | bytes 344096 | tf_op jit(solution)/shard_map/ppermute | solution.py:54
  136.9 5.0 %backward.2 = (bf16[256,2048]{1,0:T(8,128)(2,1)S(1)}, bf16[256,2048]{1,0:T(8,128)(2,1)S(1)}) custom-call(bf16[128,2688]{1,0:T(8,128)(2,1)S(1)} %pad_maximum_fusion.3.refs_0_.refs_2_, bf16[128,2688]{1,0:T(8,128)(2,1)S(1)} %collective-permute-done.16.refs_1_.refs_3_, bf16[128,2688]{1,0:T(8,128)(2,1)S(1)} %collective-permute-done.17.refs_2_.refs_4_, ...), custom_call_target="tpu_custom_call" | custom-call | flops 2818572288 | bytes 22020096 | tf_op jit(solution)/shard_map/backward/pallas_call | solution.py:257
  142.0 3.0 %collective-permute-start.30 = (bf16[64,2688]{1,0:T(8,128)(2,1)S(1)}, bf16[64,2688]{1,0:T(8,128)(2,1)S(1)}, u32[]{:S(2)}, u32[]{:S(2)}) collective-permute-start(bf16[64,2688]{1,0:T(8,128)(2,1)S(1)} %slice.145), channel_id=1, source_target_pairs={{0,48},{1,49},{2,50},{3,51},{4,52},{5,53},{6,54},{7,55},{8,56},{9,... | collective-permute-start | bytes 1032200 | tf_op jit(solution)/shard_map/ppermute | solution.py:54
  145.4 7.5 %collective-permute-done.30.refs_4_.refs_13_ = bf16[64,2688]{1,0:T(8,128)(2,1)S(1)} collective-permute-done((bf16[64,2688]{1,0:T(8,128)(2,1)S(1)}, bf16[64,2688]{1,0:T(8,128)(2,1)S(1)}, u32[]{:S(2)}, u32[]{:S(2)}) %collective-permute-start.30) | collective-permute-done | bytes 344096 | tf_op jit(solution)/shard_map/ppermute | solution.py:54
  153.0 3.4 %collective-permute-done.29.refs_3_.refs_12_ = bf16[64,2688]{1,0:T(8,128)(2,1)S(1)} collective-permute-done((bf16[64,2688]{1,0:T(8,128)(2,1)S(1)}, bf16[64,2688]{1,0:T(8,128)(2,1)S(1)}, u32[]{:S(2)}, u32[]{:S(2)}) %collective-permute-start.29) | collective-permute-done | bytes 344096 | tf_op jit(solution)/shard_map/ppermute | solution.py:54
  156.4 5.0 %backward.3 = (bf16[256,2048]{1,0:T(8,128)(2,1)S(1)}, bf16[256,2048]{1,0:T(8,128)(2,1)S(1)}) custom-call(bf16[128,2688]{1,0:T(8,128)(2,1)S(1)} %pad_maximum_fusion.5.refs_0_.refs_9_, bf16[128,2688]{1,0:T(8,128)(2,1)S(1)} %collective-permute-done.23.refs_1_.refs_10_, bf16[128,2688]{1,0:T(8,128)(2,1)S(1)} %collective-permute-done.24.refs_2_.refs_11_, ...), custom_call_target="tpu_custom_call" | custom-call | flops 2818572288 | bytes 22020096 | tf_op jit(solution)/shard_map/backward/pallas_call | solution.py:257
  161.5 2.9 %collective-permute-start.28 = (bf16[64,2048]{1,0:T(8,128)(2,1)S(1)}, bf16[64,2048]{1,0:T(8,128)(2,1)S(1)}, u32[]{:S(2)}, u32[]{:S(2)}) collective-permute-start(bf16[64,2048]{1,0:T(8,128)(2,1)S(1)} %get-tuple-element.173), channel_id=1, source_target_pairs={{0,12},{1,13},{2,14},{3,15},{4,0},{5,1},{6,2},{7,3},{8,4},{9,5},{1... | collective-permute-start | bytes 786440 | tf_op jit(solution)/shard_map/ppermute | solution.py:54
  166.2 12.0 %weight_grads.1 = (bf16[1024,896]{1,0:T(8,128)(2,1)}, bf16[1024,896]{1,0:T(8,128)(2,1)}, bf16[896,1024]{1,0:T(8,128)(2,1)}) custom-call(bf16[4,2,64,1024]{3,2,1,0:T(8,128)(2,1)S(1)} %pad_maximum_fusion.refs_0_, bf16[4,2,64,1024]{3,2,1,0:T(8,128)(2,1)S(1)} %collective-permute-done.4.refs_1_, bf16[128,2688]{1,0:T(8,128)(2,1)S(1)} %pad_maximum_fusion.3.refs_0_.refs_2_, ...), custom_call_target="tpu_custom_call" | custom-call | flops 5637144576 | bytes 44040192 | tf_op jit(solution)/shard_map/weight_grads/pallas_call | solution.py:324
  178.4 1.6 collective-permute-done.26
  180.0 1.5 collective-permute-start.35
  181.4 1.2 collective-permute-start.34
  182.8 3.1 %collective-permute-start.32 = (bf16[32,2048]{1,0:T(8,128)(2,1)S(1)}, bf16[32,2048]{1,0:T(8,128)(2,1)S(1)}, u32[]{:S(2)}, u32[]{:S(2)}) collective-permute-start(bf16[32,2048]{1,0:T(8,128)(2,1)S(1)} %slice.177), channel_id=1, source_target_pairs={{0,2},{1,3},{2,0},{3,1},{4,6},{5,7},{6,4},{7,5},{8,10},{9,11},{10,... | collective-permute-start | bytes 393224 | tf_op jit(solution)/shard_map/ppermute | solution.py:54
  185.9 3.3 %collective-permute-done.35 = bf16[64,2048]{1,0:T(8,128)(2,1)S(1)} collective-permute-done((bf16[64,2048]{1,0:T(8,128)(2,1)S(1)}, bf16[64,2048]{1,0:T(8,128)(2,1)S(1)}, u32[]{:S(2)}, u32[]{:S(2)}) %collective-permute-start.35) | collective-permute-done | bytes 262176 | tf_op jit(solution)/shard_map/ppermute | solution.py:54
  189.2 3.1 %collective-permute-done.34 = bf16[64,2048]{1,0:T(8,128)(2,1)S(1)} collective-permute-done((bf16[64,2048]{1,0:T(8,128)(2,1)S(1)}, bf16[64,2048]{1,0:T(8,128)(2,1)S(1)}, u32[]{:S(2)}, u32[]{:S(2)}) %collective-permute-start.34) | collective-permute-done | bytes 262176 | tf_op jit(solution)/shard_map/ppermute | solution.py:54
  192.2 3.9 %collective-permute-done.33 = bf16[64,2048]{1,0:T(8,128)(2,1)S(1)} collective-permute-done((bf16[64,2048]{1,0:T(8,128)(2,1)S(1)}, bf16[64,2048]{1,0:T(8,128)(2,1)S(1)}, u32[]{:S(2)}, u32[]{:S(2)}) %collective-permute-start.33) | collective-permute-done | bytes 262176 | tf_op jit(solution)/shard_map/ppermute | solution.py:54
  196.3 3.1 %collective-permute-start.36 = (bf16[32,2048]{1,0:T(8,128)(2,1)S(1)}, bf16[32,2048]{1,0:T(8,128)(2,1)S(1)}, u32[]{:S(2)}, u32[]{:S(2)}) collective-permute-start(bf16[32,2048]{1,0:T(8,128)(2,1)S(1)} %slice.183), channel_id=1, source_target_pairs={{0,2},{1,3},{2,0},{3,1},{4,6},{5,7},{6,4},{7,5},{8,10},{9,11},{10,... | collective-permute-start | bytes 393224 | tf_op jit(solution)/shard_map/ppermute | solution.py:54
  199.5 3.9 %collective-permute-done.36 = bf16[32,2048]{1,0:T(8,128)(2,1)S(1)} collective-permute-done((bf16[32,2048]{1,0:T(8,128)(2,1)S(1)}, bf16[32,2048]{1,0:T(8,128)(2,1)S(1)}, u32[]{:S(2)}, u32[]{:S(2)}) %collective-permute-start.36) | collective-permute-done | bytes 131104 | tf_op jit(solution)/shard_map/ppermute | solution.py:54
  (80 shorter events, 9.6 us)
Async XLA Ops:
  0.6 26.4 %copy-start.5 = (s32[7,8]{1,0:T(8,128)S(1)}, s32[7,8]{1,0:T(8,128)}, u32[]{:S(2)}) copy-start(s32[7,8]{1,0:T(8,128)} %refs_16_.1) | copy-start | bytes 676
  1.6 9.5 %collective-permute-start = (bf16[2,64,1024]{2,1,0:T(8,128)(2,1)S(1)}, bf16[2,64,1024]{2,1,0:T(8,128)(2,1)S(1)}, u32[]{:S(2)}, u32[]{:S(2)}) collective-permute-start(bf16[2,64,1024]{2,1,0:T(8,128)(2,1)S(1)} %pad_maximum_fusion.6), channel_id=1, source_target_pairs={{0,2},{1,3},{2,0},{3,1},{4,6},{5,7},{6,4},{7,5},{8,10},{9,11},{10,... | collective-permute-start | bytes 786440 | tf_op jit(solution)/shard_map/ppermute | solution.py:54
  4.8 22.2 %copy-start.1 = (bf16[1024,896]{1,0:T(8,128)(2,1)S(1)}, bf16[1024,896]{1,0:T(8,128)(2,1)}, u32[]{:S(2)}) copy-start(bf16[1024,896]{1,0:T(8,128)(2,1)} %up.1) | copy-start | bytes 5505028
  11.2 15.9 %copy-start = (bf16[1024,896]{1,0:T(8,128)(2,1)S(1)}, bf16[1024,896]{1,0:T(8,128)(2,1)}, u32[]{:S(2)}) copy-start(bf16[1024,896]{1,0:T(8,128)(2,1)} %gate.1) | copy-start | bytes 5505028
  11.2 15.8 %copy-start.3 = (s32[8,7]{1,0:T(8,128)S(1)}, s32[8,7]{1,0:T(8,128)}, u32[]{:S(2)}) copy-start(s32[8,7]{1,0:T(8,128)} %refs_14_.1) | copy-start | bytes 676
  11.2 15.8 %copy-start.4 = (s32[8,7]{1,0:T(8,128)S(1)}, s32[8,7]{1,0:T(8,128)}, u32[]{:S(2)}) copy-start(s32[8,7]{1,0:T(8,128)} %refs_15_.1) | copy-start | bytes 676
  11.2 9.6 %collective-permute-start.3 = (bf16[2,64,1024]{2,1,0:T(8,128)(2,1)S(1)}, bf16[2,64,1024]{2,1,0:T(8,128)(2,1)S(1)}, u32[]{:S(2)}, u32[]{:S(2)}) collective-permute-start(bf16[2,64,1024]{2,1,0:T(8,128)(2,1)S(1)} %pad_maximum_fusion.7), channel_id=1, source_target_pairs={{0,4},{1,5},{2,6},{3,7},{4,8},{5,9},{6,10},{7,11},{8,12},{9,13},{1... | collective-permute-start | bytes 786440 | tf_op jit(solution)/shard_map/ppermute | solution.py:54
  13.1 13.7 %collective-permute-start.2 = (bf16[2,64,1024]{2,1,0:T(8,128)(2,1)S(1)}, bf16[2,64,1024]{2,1,0:T(8,128)(2,1)S(1)}, u32[]{:S(2)}, u32[]{:S(2)}) collective-permute-start(bf16[2,64,1024]{2,1,0:T(8,128)(2,1)S(1)} %pad_maximum_fusion.7), channel_id=1, source_target_pairs={{0,8},{1,9},{2,10},{3,11},{4,12},{5,13},{6,14},{7,15},{8,0},{9,1},... | collective-permute-start | bytes 786440 | tf_op jit(solution)/shard_map/ppermute | solution.py:54
  16.0 10.8 %collective-permute-start.1 = (bf16[2,64,1024]{2,1,0:T(8,128)(2,1)S(1)}, bf16[2,64,1024]{2,1,0:T(8,128)(2,1)S(1)}, u32[]{:S(2)}, u32[]{:S(2)}) collective-permute-start(bf16[2,64,1024]{2,1,0:T(8,128)(2,1)S(1)} %pad_maximum_fusion.7), channel_id=1, source_target_pairs={{0,12},{1,13},{2,14},{3,15},{4,0},{5,1},{6,2},{7,3},{8,4},{9,5},{1... | collective-permute-start | bytes 786440 | tf_op jit(solution)/shard_map/ppermute | solution.py:54
  26.9 4.4 %collective-permute-start.4 = (bf16[4,2,64,1024]{3,2,1,0:T(8,128)(2,1)S(1)}, bf16[4,2,64,1024]{3,2,1,0:T(8,128)(2,1)S(1)}, u32[]{:S(2)}, u32[]{:S(2)}) collective-permute-start(bf16[4,2,64,1024]{3,2,1,0:T(8,128)(2,1)S(1)} %pad_maximum_fusion.refs_0_), channel_id=1, source_target_pairs={{0,1},{1,0},{2,3},{3,2},{4,5},{5,4},{6,7},{7,6},{8,9},{9,8},{10,11... | collective-permute-start | bytes 3145736 | tf_op jit(solution)/shard_map/ppermute | solution.py:54
  27.0 1.5 copy-start.2
  35.9 20.3 %collective-permute-start.6 = (bf16[128,2688]{1,0:T(8,128)(2,1)S(1)}, bf16[128,2688]{1,0:T(8,128)(2,1)S(1)}, u32[]{:S(2)}, u32[]{:S(2)}) collective-permute-start(bf16[128,2688]{1,0:T(8,128)(2,1)S(1)} %get-tuple-element.93), channel_id=1, source_target_pairs={{0,48},{1,49},{2,50},{3,51},{4,52},{5,53},{6,54},{7,55},{8,56},{9,... | collective-permute-start | bytes 2064392 | tf_op jit(solution)/shard_map/ppermute | solution.py:54
  40.0 18.7 %collective-permute-start.5 = (bf16[128,2688]{1,0:T(8,128)(2,1)S(1)}, bf16[128,2688]{1,0:T(8,128)(2,1)S(1)}, u32[]{:S(2)}, u32[]{:S(2)}) collective-permute-start(bf16[128,2688]{1,0:T(8,128)(2,1)S(1)} %get-tuple-element.92), channel_id=1, source_target_pairs={{0,16},{1,17},{2,18},{3,19},{4,20},{5,21},{6,22},{7,23},{8,24},{9,... | collective-permute-start | bytes 2064392 | tf_op jit(solution)/shard_map/ppermute | solution.py:54
  40.0 10.0 %collective-permute-start.9 = (bf16[2,64,1024]{2,1,0:T(8,128)(2,1)S(1)}, bf16[2,64,1024]{2,1,0:T(8,128)(2,1)S(1)}, u32[]{:S(2)}, u32[]{:S(2)}) collective-permute-start(bf16[2,64,1024]{2,1,0:T(8,128)(2,1)S(1)} %pad_maximum_fusion.8), channel_id=1, source_target_pairs={{0,4},{1,5},{2,6},{3,7},{4,8},{5,9},{6,10},{7,11},{8,12},{9,13},{1... | collective-permute-start | bytes 786440 | tf_op jit(solution)/shard_map/ppermute | solution.py:54
  41.3 14.4 %collective-permute-start.8 = (bf16[2,64,1024]{2,1,0:T(8,128)(2,1)S(1)}, bf16[2,64,1024]{2,1,0:T(8,128)(2,1)S(1)}, u32[]{:S(2)}, u32[]{:S(2)}) collective-permute-start(bf16[2,64,1024]{2,1,0:T(8,128)(2,1)S(1)} %pad_maximum_fusion.8), channel_id=1, source_target_pairs={{0,8},{1,9},{2,10},{3,11},{4,12},{5,13},{6,14},{7,15},{8,0},{9,1},... | collective-permute-start | bytes 786440 | tf_op jit(solution)/shard_map/ppermute | solution.py:54
  43.7 12.2 %collective-permute-start.7 = (bf16[2,64,1024]{2,1,0:T(8,128)(2,1)S(1)}, bf16[2,64,1024]{2,1,0:T(8,128)(2,1)S(1)}, u32[]{:S(2)}, u32[]{:S(2)}) collective-permute-start(bf16[2,64,1024]{2,1,0:T(8,128)(2,1)S(1)} %pad_maximum_fusion.8), channel_id=1, source_target_pairs={{0,12},{1,13},{2,14},{3,15},{4,0},{5,1},{6,2},{7,3},{8,4},{9,5},{1... | collective-permute-start | bytes 786440 | tf_op jit(solution)/shard_map/ppermute | solution.py:54
  56.1 4.9 %collective-permute-start.12 = (bf16[4,2,64,1024]{3,2,1,0:T(8,128)(2,1)S(1)}, bf16[4,2,64,1024]{3,2,1,0:T(8,128)(2,1)S(1)}, u32[]{:S(2)}, u32[]{:S(2)}) collective-permute-start(bf16[4,2,64,1024]{3,2,1,0:T(8,128)(2,1)S(1)} %pad_maximum_fusion.1.refs_0_.refs_7_), channel_id=1, source_target_pairs={{0,1},{1,0},{2,3},{3,2},{4,5},{5,4},{6,7},{7,6},{8,9},{9,8},{10,11... | collective-permute-start | bytes 3145736 | tf_op jit(solution)/shard_map/ppermute | solution.py:54
  58.8 9.4 %collective-permute-start.11 = (bf16[64,2688]{1,0:T(8,128)(2,1)S(1)}, bf16[64,2688]{1,0:T(8,128)(2,1)S(1)}, u32[]{:S(2)}, u32[]{:S(2)}) collective-permute-start(bf16[64,2688]{1,0:T(8,128)(2,1)S(1)} %slice_add_fusion.2), channel_id=1, source_target_pairs={{0,48},{1,49},{2,50},{3,51},{4,52},{5,53},{6,54},{7,55},{8,56},{9,... | collective-permute-start | bytes 1032200 | tf_op jit(solution)/shard_map/ppermute | solution.py:54
  59.3 12.2 %collective-permute-start.10 = (bf16[64,2688]{1,0:T(8,128)(2,1)S(1)}, bf16[64,2688]{1,0:T(8,128)(2,1)S(1)}, u32[]{:S(2)}, u32[]{:S(2)}) collective-permute-start(bf16[64,2688]{1,0:T(8,128)(2,1)S(1)} %slice_add_fusion.3), channel_id=1, source_target_pairs={{0,16},{1,17},{2,18},{3,19},{4,20},{5,21},{6,22},{7,23},{8,24},{9,... | collective-permute-start | bytes 1032200 | tf_op jit(solution)/shard_map/ppermute | solution.py:54
  65.5 22.0 %collective-permute-start.14 = (bf16[128,2688]{1,0:T(8,128)(2,1)S(1)}, bf16[128,2688]{1,0:T(8,128)(2,1)S(1)}, u32[]{:S(2)}, u32[]{:S(2)}) collective-permute-start(bf16[128,2688]{1,0:T(8,128)(2,1)S(1)} %get-tuple-element.104), channel_id=1, source_target_pairs={{0,16},{1,17},{2,18},{3,19},{4,20},{5,21},{6,22},{7,23},{8,24},{9,... | collective-permute-start | bytes 2064392 | tf_op jit(solution)/shard_map/ppermute | solution.py:54
  71.5 16.0 %collective-permute-start.15 = (bf16[128,2688]{1,0:T(8,128)(2,1)S(1)}, bf16[128,2688]{1,0:T(8,128)(2,1)S(1)}, u32[]{:S(2)}, u32[]{:S(2)}) collective-permute-start(bf16[128,2688]{1,0:T(8,128)(2,1)S(1)} %get-tuple-element.108), channel_id=1, source_target_pairs={{0,48},{1,49},{2,50},{3,51},{4,52},{5,53},{6,54},{7,55},{8,56},{9,... | collective-permute-start | bytes 2064392 | tf_op jit(solution)/shard_map/ppermute | solution.py:54
  71.8 18.0 %collective-permute-start.13 = (bf16[128,2688]{1,0:T(8,128)(2,1)S(1)}, bf16[128,2688]{1,0:T(8,128)(2,1)S(1)}, u32[]{:S(2)}, u32[]{:S(2)}) collective-permute-start(bf16[128,2688]{1,0:T(8,128)(2,1)S(1)} %pad_maximum_fusion.2), channel_id=1, source_target_pairs={{0,64},{1,65},{2,66},{3,67},{4,68},{5,69},{6,70},{7,71},{8,72},{9,... | collective-permute-start | bytes 2064392 | tf_op jit(solution)/shard_map/ppermute | solution.py:54
  87.5 11.1 %collective-permute-start.19 = (bf16[64,2688]{1,0:T(8,128)(2,1)S(1)}, bf16[64,2688]{1,0:T(8,128)(2,1)S(1)}, u32[]{:S(2)}, u32[]{:S(2)}) collective-permute-start(bf16[64,2688]{1,0:T(8,128)(2,1)S(1)} %slice_add_fusion), channel_id=1, source_target_pairs={{0,48},{1,49},{2,50},{3,51},{4,52},{5,53},{6,54},{7,55},{8,56},{9,... | collective-permute-start | bytes 1032200 | tf_op jit(solution)/shard_map/ppermute | solution.py:54
  89.3 12.3 %collective-permute-start.18 = (bf16[64,2688]{1,0:T(8,128)(2,1)S(1)}, bf16[64,2688]{1,0:T(8,128)(2,1)S(1)}, u32[]{:S(2)}, u32[]{:S(2)}) collective-permute-start(bf16[64,2688]{1,0:T(8,128)(2,1)S(1)} %slice_add_fusion.1), channel_id=1, source_target_pairs={{0,16},{1,17},{2,18},{3,19},{4,20},{5,21},{6,22},{7,23},{8,24},{9,... | collective-permute-start | bytes 1032200 | tf_op jit(solution)/shard_map/ppermute | solution.py:54
  90.2 23.0 %collective-permute-start.17 = (bf16[128,2688]{1,0:T(8,128)(2,1)S(1)}, bf16[128,2688]{1,0:T(8,128)(2,1)S(1)}, u32[]{:S(2)}, u32[]{:S(2)}) collective-permute-start(bf16[128,2688]{1,0:T(8,128)(2,1)S(1)} %pad_maximum_fusion.3.refs_0_.refs_2_), channel_id=1, source_target_pairs={{0,16},{1,17},{2,18},{3,19},{4,20},{5,21},{6,22},{7,23},{8,24},{9,... | collective-permute-start | bytes 2064392 | tf_op jit(solution)/shard_map/ppermute | solution.py:54
  90.3 22.9 %collective-permute-start.16 = (bf16[128,2688]{1,0:T(8,128)(2,1)S(1)}, bf16[128,2688]{1,0:T(8,128)(2,1)S(1)}, u32[]{:S(2)}, u32[]{:S(2)}) collective-permute-start(bf16[128,2688]{1,0:T(8,128)(2,1)S(1)} %pad_maximum_fusion.3.refs_0_.refs_2_), channel_id=1, source_target_pairs={{0,48},{1,49},{2,50},{3,51},{4,52},{5,53},{6,54},{7,55},{8,56},{9,... | collective-permute-start | bytes 2064392 | tf_op jit(solution)/shard_map/ppermute | solution.py:54
  102.0 11.4 %collective-permute-start.22 = (bf16[128,2688]{1,0:T(8,128)(2,1)S(1)}, bf16[128,2688]{1,0:T(8,128)(2,1)S(1)}, u32[]{:S(2)}, u32[]{:S(2)}) collective-permute-start(bf16[128,2688]{1,0:T(8,128)(2,1)S(1)} %pad_maximum_fusion.4), channel_id=1, source_target_pairs={{0,64},{1,65},{2,66},{3,67},{4,68},{5,69},{6,70},{7,71},{8,72},{9,... | collective-permute-start | bytes 2064392 | tf_op jit(solution)/shard_map/ppermute | solution.py:54
  113.9 28.0 %collective-permute-start.24 = (bf16[128,2688]{1,0:T(8,128)(2,1)S(1)}, bf16[128,2688]{1,0:T(8,128)(2,1)S(1)}, u32[]{:S(2)}, u32[]{:S(2)}) collective-permute-start(bf16[128,2688]{1,0:T(8,128)(2,1)S(1)} %pad_maximum_fusion.5.refs_0_.refs_9_), channel_id=1, source_target_pairs={{0,16},{1,17},{2,18},{3,19},{4,20},{5,21},{6,22},{7,23},{8,24},{9,... | collective-permute-start | bytes 2064392 | tf_op jit(solution)/shard_map/ppermute | solution.py:54
  114.0 27.9 %collective-permute-start.23 = (bf16[128,2688]{1,0:T(8,128)(2,1)S(1)}, bf16[128,2688]{1,0:T(8,128)(2,1)S(1)}, u32[]{:S(2)}, u32[]{:S(2)}) collective-permute-start(bf16[128,2688]{1,0:T(8,128)(2,1)S(1)} %pad_maximum_fusion.5.refs_0_.refs_9_), channel_id=1, source_target_pairs={{0,48},{1,49},{2,50},{3,51},{4,52},{5,53},{6,54},{7,55},{8,56},{9,... | collective-permute-start | bytes 2064392 | tf_op jit(solution)/shard_map/ppermute | solution.py:54
  117.2 19.7 %collective-permute-start.20 = (bf16[64,2688]{1,0:T(8,128)(2,1)S(1)}, bf16[64,2688]{1,0:T(8,128)(2,1)S(1)}, u32[]{:S(2)}, u32[]{:S(2)}) collective-permute-start(bf16[64,2688]{1,0:T(8,128)(2,1)S(1)} %slice.139), channel_id=1, source_target_pairs={{0,16},{1,17},{2,18},{3,19},{4,20},{5,21},{6,22},{7,23},{8,24},{9,... | collective-permute-start | bytes 1032200 | tf_op jit(solution)/shard_map/ppermute | solution.py:54
  117.2 19.7 %collective-permute-start.21 = (bf16[64,2688]{1,0:T(8,128)(2,1)S(1)}, bf16[64,2688]{1,0:T(8,128)(2,1)S(1)}, u32[]{:S(2)}, u32[]{:S(2)}) collective-permute-start(bf16[64,2688]{1,0:T(8,128)(2,1)S(1)} %slice.140), channel_id=1, source_target_pairs={{0,48},{1,49},{2,50},{3,51},{4,52},{5,53},{6,54},{7,55},{8,56},{9,... | collective-permute-start | bytes 1032200 | tf_op jit(solution)/shard_map/ppermute | solution.py:54
  141.9 3.1 %collective-permute-start.25 = (bf16[256,2048]{1,0:T(8,128)(2,1)S(1)}, bf16[256,2048]{1,0:T(8,128)(2,1)S(1)}, u32[]{:S(2)}, u32[]{:S(2)}) collective-permute-start(bf16[256,2048]{1,0:T(8,128)(2,1)S(1)} %get-tuple-element.128), channel_id=1, source_target_pairs={{0,1},{1,0},{2,3},{3,2},{4,5},{5,4},{6,7},{7,6},{8,9},{9,8},{10,11... | collective-permute-start | bytes 3145736 | tf_op jit(solution)/shard_map/ppermute | solution.py:54
  142.0 10.9 %collective-permute-start.30 = (bf16[64,2688]{1,0:T(8,128)(2,1)S(1)}, bf16[64,2688]{1,0:T(8,128)(2,1)S(1)}, u32[]{:S(2)}, u32[]{:S(2)}) collective-permute-start(bf16[64,2688]{1,0:T(8,128)(2,1)S(1)} %slice.145), channel_id=1, source_target_pairs={{0,48},{1,49},{2,50},{3,51},{4,52},{5,53},{6,54},{7,55},{8,56},{9,... | collective-permute-start | bytes 1032200 | tf_op jit(solution)/shard_map/ppermute | solution.py:54
  145.0 11.3 %collective-permute-start.29 = (bf16[64,2688]{1,0:T(8,128)(2,1)S(1)}, bf16[64,2688]{1,0:T(8,128)(2,1)S(1)}, u32[]{:S(2)}, u32[]{:S(2)}) collective-permute-start(bf16[64,2688]{1,0:T(8,128)(2,1)S(1)} %slice.144), channel_id=1, source_target_pairs={{0,16},{1,17},{2,18},{3,19},{4,20},{5,21},{6,22},{7,23},{8,24},{9,... | collective-permute-start | bytes 1032200 | tf_op jit(solution)/shard_map/ppermute | solution.py:54
  161.4 4.5 %collective-permute-start.31 = (bf16[256,2048]{1,0:T(8,128)(2,1)S(1)}, bf16[256,2048]{1,0:T(8,128)(2,1)S(1)}, u32[]{:S(2)}, u32[]{:S(2)}) collective-permute-start(bf16[256,2048]{1,0:T(8,128)(2,1)S(1)} %get-tuple-element.136), channel_id=1, source_target_pairs={{0,1},{1,0},{2,3},{3,2},{4,5},{5,4},{6,7},{7,6},{8,9},{9,8},{10,11... | collective-permute-start | bytes 3145736 | tf_op jit(solution)/shard_map/ppermute | solution.py:54
  161.5 16.8 %collective-permute-start.28 = (bf16[64,2048]{1,0:T(8,128)(2,1)S(1)}, bf16[64,2048]{1,0:T(8,128)(2,1)S(1)}, u32[]{:S(2)}, u32[]{:S(2)}) collective-permute-start(bf16[64,2048]{1,0:T(8,128)(2,1)S(1)} %get-tuple-element.173), channel_id=1, source_target_pairs={{0,12},{1,13},{2,14},{3,15},{4,0},{5,1},{6,2},{7,3},{8,4},{9,5},{1... | collective-permute-start | bytes 786440 | tf_op jit(solution)/shard_map/ppermute | solution.py:54
  164.4 13.9 %collective-permute-start.27 = (bf16[64,2048]{1,0:T(8,128)(2,1)S(1)}, bf16[64,2048]{1,0:T(8,128)(2,1)S(1)}, u32[]{:S(2)}, u32[]{:S(2)}) collective-permute-start(bf16[64,2048]{1,0:T(8,128)(2,1)S(1)} %get-tuple-element.174), channel_id=1, source_target_pairs={{0,8},{1,9},{2,10},{3,11},{4,12},{5,13},{6,14},{7,15},{8,0},{9,1},... | collective-permute-start | bytes 786440 | tf_op jit(solution)/shard_map/ppermute | solution.py:54
  165.6 14.4 %collective-permute-start.26 = (bf16[64,2048]{1,0:T(8,128)(2,1)S(1)}, bf16[64,2048]{1,0:T(8,128)(2,1)S(1)}, u32[]{:S(2)}, u32[]{:S(2)}) collective-permute-start(bf16[64,2048]{1,0:T(8,128)(2,1)S(1)} %get-tuple-element.175), channel_id=1, source_target_pairs={{0,4},{1,5},{2,6},{3,7},{4,8},{5,9},{6,10},{7,11},{8,12},{9,13},{1... | collective-permute-start | bytes 786440 | tf_op jit(solution)/shard_map/ppermute | solution.py:54
  180.0 9.2 %collective-permute-start.35 = (bf16[64,2048]{1,0:T(8,128)(2,1)S(1)}, bf16[64,2048]{1,0:T(8,128)(2,1)S(1)}, u32[]{:S(2)}, u32[]{:S(2)}) collective-permute-start(bf16[64,2048]{1,0:T(8,128)(2,1)S(1)} %get-tuple-element.169), channel_id=1, source_target_pairs={{0,12},{1,13},{2,14},{3,15},{4,0},{5,1},{6,2},{7,3},{8,4},{9,5},{1... | collective-permute-start | bytes 786440 | tf_op jit(solution)/shard_map/ppermute | solution.py:54
  181.4 10.8 %collective-permute-start.34 = (bf16[64,2048]{1,0:T(8,128)(2,1)S(1)}, bf16[64,2048]{1,0:T(8,128)(2,1)S(1)}, u32[]{:S(2)}, u32[]{:S(2)}) collective-permute-start(bf16[64,2048]{1,0:T(8,128)(2,1)S(1)} %get-tuple-element.170), channel_id=1, source_target_pairs={{0,8},{1,9},{2,10},{3,11},{4,12},{5,13},{6,14},{7,15},{8,0},{9,1},... | collective-permute-start | bytes 786440 | tf_op jit(solution)/shard_map/ppermute | solution.py:54
  182.6 13.5 %collective-permute-start.33 = (bf16[64,2048]{1,0:T(8,128)(2,1)S(1)}, bf16[64,2048]{1,0:T(8,128)(2,1)S(1)}, u32[]{:S(2)}, u32[]{:S(2)}) collective-permute-start(bf16[64,2048]{1,0:T(8,128)(2,1)S(1)} %get-tuple-element.171), channel_id=1, source_target_pairs={{0,4},{1,5},{2,6},{3,7},{4,8},{5,9},{6,10},{7,11},{8,12},{9,13},{1... | collective-permute-start | bytes 786440 | tf_op jit(solution)/shard_map/ppermute | solution.py:54
  182.8 16.6 %collective-permute-start.32 = (bf16[32,2048]{1,0:T(8,128)(2,1)S(1)}, bf16[32,2048]{1,0:T(8,128)(2,1)S(1)}, u32[]{:S(2)}, u32[]{:S(2)}) collective-permute-start(bf16[32,2048]{1,0:T(8,128)(2,1)S(1)} %slice.177), channel_id=1, source_target_pairs={{0,2},{1,3},{2,0},{3,1},{4,6},{5,7},{6,4},{7,5},{8,10},{9,11},{10,... | collective-permute-start | bytes 393224 | tf_op jit(solution)/shard_map/ppermute | solution.py:54
  196.3 7.0 %collective-permute-start.36 = (bf16[32,2048]{1,0:T(8,128)(2,1)S(1)}, bf16[32,2048]{1,0:T(8,128)(2,1)S(1)}, u32[]{:S(2)}, u32[]{:S(2)}) collective-permute-start(bf16[32,2048]{1,0:T(8,128)(2,1)S(1)} %slice.183), channel_id=1, source_target_pairs={{0,2},{1,3},{2,0},{3,1},{4,6},{5,7},{6,4},{7,5},{8,10},{9,11},{10,... | collective-permute-start | bytes 393224 | tf_op jit(solution)/shard_map/ppermute | solution.py:54

commit v3 on v2

--- a/solution.py
+++ b/solution.py
@@ -13,8 +13,8 @@
 ORDER = (
     "forward 0",
     "core 1",
+    "forward 1",
     "relay 0",
-    "forward 1",
     "swap 0",
     "relay 1",
     "spread 0",
@@ -27,9 +27,9 @@
     "chip 0",
     "backward 1",
     "send 1",
+    "last 0",
     "chip 1",
     "grads",
-    "last 0",
     "last 1",
 )
 SEND_UP = ((2, 0), (1, 1))
@@ -92,9 +92,10 @@
 def token_copies(gathered, offset, rows, pieces, held, first, sems):
     copies = []
     for at, (dz, half) in enumerate(pieces):
-        source = gathered[half].at[owner(dz), :, pl.ds(offset, rows)]
-        to = held.at[:, pl.ds(first + at * rows, rows)]
-        copies.append(pltpu.make_async_copy(source, to, sems.at[at]))
+        to = pl.ds(first + at * rows, rows)
+        for kind in range(2):
+            source = gathered[2 * half + kind].at[owner(dz), pl.ds(offset, rows)]
+            copies.append(pltpu.make_async_copy(source, held.at[kind, to], sems.at[kind, at]))
     return copies
 
 
@@ -172,8 +173,8 @@
 
 
 def forward_kernel(offset, rows, *refs):
-    gathered, weights, outs = refs[:2], refs[2], refs[3:8]
-    held, held_weights, sems, weight_sems = refs[8:]
+    gathered, weights, outs = refs[:4], refs[4], refs[5:10]
+    held, held_weights, sems, weight_sems = refs[10:]
     pieces = [piece for group in GROUPS for piece in group]
     copies = token_copies(gathered, offset, rows, pieces, held, 0, sems)
     loads = weight_copies(weights, held_weights, weight_sems, range(3))
@@ -198,7 +199,7 @@
     depth, total = weights.shape
     return pl.pallas_call(
         functools.partial(forward_kernel, offset, rows),
-        in_specs=[ANY] * 3,
+        in_specs=[ANY] * 5,
         out_specs=[VMEM] * len(GROUPS),
         out_shape=[
             jax.ShapeDtypeStruct((len(group) * rows, total), jnp.bfloat16) for group in GROUPS
@@ -206,7 +207,7 @@
         scratch_shapes=[
             pltpu.VMEM((2, 8 * rows, depth), jnp.bfloat16),
             pltpu.VMEM((depth, total), jnp.bfloat16),
-            pltpu.SemaphoreType.DMA((8,)),
+            pltpu.SemaphoreType.DMA((2, 8)),
             pltpu.SemaphoreType.DMA((3, 2)),
         ],
         compiler_params=params(),
@@ -274,13 +275,13 @@
 
 
 def weight_grad_kernel(offsets, *refs):
-    number = 7 * len(offsets)
+    number = 9 * len(offsets)
     gate_mask, up_mask, down_mask, gate_grad, up_grad, down_grad = refs[number : number + 6]
     tokens, values, sems, value_sems = refs[number + 6 :]
     first = 0
     copies = []
     for which, offset in enumerate(offsets):
-        gathered, arrays = refs[7 * which : 7 * which + 2], refs[7 * which + 2 : 7 * which + 7]
+        gathered, arrays = refs[9 * which : 9 * which + 4], refs[9 * which + 4 : 9 * which + 9]
         rows = arrays[3].shape[0]
         copies += token_copies(gathered, offset, rows, GATHERED, tokens, first, sems.at[which])
         for at, piece in enumerate(GATHERED):
@@ -333,7 +334,7 @@
         scratch_shapes=[
             pltpu.VMEM((2, count, depth), jnp.bfloat16),
             pltpu.VMEM((count, total), jnp.bfloat16),
-            pltpu.SemaphoreType.DMA((len(chunks), 8)),
+            pltpu.SemaphoreType.DMA((len(chunks), 2, 8)),
             pltpu.SemaphoreType.DMA((len(chunks), 8)),
         ],
         compiler_params=params(),
@@ -378,8 +379,9 @@
         self.pairs = [self.pair] + [move(self.pair, dy=-dy) for dy in range(1, 4)]
 
     def core(self, *others):
-        own = jnp.stack(after(self.pairs, *others))
-        self.arrays = (own, move(own, dcore=1))
+        pairs = after(self.pairs, *others)
+        own = [jnp.stack([pair[kind] for pair in pairs]) for kind in range(2)]
+        self.arrays = (*own, *[move(array, dcore=1) for array in own])
         return own
 
 

time: 204 us -> 214 us (1.049)
  Pallas kernels: 33.8 us -> 44.4 us
  waiting for transfers between devices: 109 us -> 101 us
  starting transfers between devices: 52.8 us -> 59.4 us
    ppermute x37 -> x39, waiting for transfers between devices: 109 us -> 101 us  [move(): return lax.ppermute(array, ('row', 'col'), pairs)]
    ppermute x37 -> x39, starting transfers between devices: 52.8 us -> 59.4 us  [move(): return lax.ppermute(array, ('row', 'col'), pairs)]
    pallas_call x1, Pallas kernels: 12 us -> 17.4 us  [weight_grads(): pl.pallas_call(functools.partial(weight_grad_kernel, offsets), in_specs=[...]
    pallas_call x2, Pallas kernels: 9.02 us -> 14.3 us  [forward(): pl.pallas_call(functools.partial(forward_kernel, offset, rows), in_specs=...]
  transfers between devices with their start and end apart: 37 -> 39, of which waited for: 21 -> 21; matrix products, arithmetic and copies ran while one was open for 2% -> 2% of each run, Pallas kernels for 12% -> 19%
where the time goes in v3:
time: 214 us; the launch traced here: 213 us
  waiting for transfers between devices  101 us (47%)
  starting transfers between devices  59.4 us (28%)
  Pallas kernels  44.4 us (21%)
  other arithmetic  5.96 us (3%)
    ppermute x39, waiting for transfers between devices, move(): return lax.ppermute(array, ('row', 'col'), pairs)  101 us
    ppermute x39, starting transfers between devices, move(): return lax.ppermute(array, ('row', 'col'), pairs)  59.4 us
    pallas_call x1, Pallas kernels, weight_grads(): pl.pallas_call(functools.partial(weight_grad_kernel, offsets), in_specs=[...  17.4 us
    pallas_call x2, Pallas kernels, forward(): pl.pallas_call(functools.partial(forward_kernel, offset, rows), in_specs=...  14.3 us
    pallas_call x2, Pallas kernels, backward(): pl.pallas_call(backward_kernel, in_specs=[ANY] * 6, out_specs=[VMEM] * 2,...  9.93 us
  transfers between devices with their start and end apart: 39, of which 21 were waited for; matrix products, arithmetic and copies ran while one was open for 2% of the time, Pallas kernels for 19%

profile of v3, /device:TPU:0, one launch (start us, length us, event | category | flops | bytes accessed | tf_op | source)
XLA Modules:
  0.0 212.6 jit_solution(4528739139070904877)
XLA Ops:
  0.6 1.0 pad_maximum_fusion.8
  1.6 3.2 %collective-permute-start = (bf16[2,64,1024]{2,1,0:T(8,128)(2,1)S(1)}, bf16[2,64,1024]{2,1,0:T(8,128)(2,1)S(1)}, u32[]{:S(2)}, u32[]{:S(2)}) collective-permute-start(bf16[2,64,1024]{2,1,0:T(8,128)(2,1)S(1)} %pad_maximum_fusion.8), channel_id=1, source_target_pairs={{0,2},{1,3},{2,0},{3,1},{4,6},{5,7},{6,4},{7,5},{8,10},{9,11},{10,... | collective-permute-start | bytes 786440 | tf_op jit(solution)/shard_map/ppermute | solution.py:54
  4.8 1.0 fusion.4
  5.8 5.3 %collective-permute-done = bf16[2,64,1024]{2,1,0:T(8,128)(2,1)S(1)} collective-permute-done((bf16[2,64,1024]{2,1,0:T(8,128)(2,1)S(1)}, bf16[2,64,1024]{2,1,0:T(8,128)(2,1)S(1)}, u32[]{:S(2)}, u32[]{:S(2)}) %collective-permute-start) | collective-permute-done | bytes 262176 | tf_op jit(solution)/shard_map/ppermute | solution.py:54
  11.2 1.9 collective-permute-start.3
  13.0 2.9 %collective-permute-start.2 = (bf16[2,64,1024]{2,1,0:T(8,128)(2,1)S(1)}, bf16[2,64,1024]{2,1,0:T(8,128)(2,1)S(1)}, u32[]{:S(2)}, u32[]{:S(2)}) collective-permute-start(bf16[2,64,1024]{2,1,0:T(8,128)(2,1)S(1)} %pad_maximum_fusion.9), channel_id=1, source_target_pairs={{0,8},{1,9},{2,10},{3,11},{4,12},{5,13},{6,14},{7,15},{8,0},{9,1},... | collective-permute-start | bytes 786440 | tf_op jit(solution)/shard_map/ppermute | solution.py:54
  15.9 1.3 collective-permute-start.1
  17.3 3.5 %collective-permute-done.3 = bf16[2,64,1024]{2,1,0:T(8,128)(2,1)S(1)} collective-permute-done((bf16[2,64,1024]{2,1,0:T(8,128)(2,1)S(1)}, bf16[2,64,1024]{2,1,0:T(8,128)(2,1)S(1)}, u32[]{:S(2)}, u32[]{:S(2)}) %collective-permute-start.3) | collective-permute-done | bytes 262176 | tf_op jit(solution)/shard_map/ppermute | solution.py:54
  20.8 5.9 %collective-permute-done.2 = bf16[2,64,1024]{2,1,0:T(8,128)(2,1)S(1)} collective-permute-done((bf16[2,64,1024]{2,1,0:T(8,128)(2,1)S(1)}, bf16[2,64,1024]{2,1,0:T(8,128)(2,1)S(1)}, u32[]{:S(2)}, u32[]{:S(2)}) %collective-permute-start.2) | collective-permute-done | bytes 262176 | tf_op jit(solution)/shard_map/ppermute | solution.py:54
  27.7 1.3 collective-permute-start.10
  29.0 2.4 %collective-permute-start.9 = (bf16[2,64,1024]{2,1,0:T(8,128)(2,1)S(1)}, bf16[2,64,1024]{2,1,0:T(8,128)(2,1)S(1)}, u32[]{:S(2)}, u32[]{:S(2)}) collective-permute-start(bf16[2,64,1024]{2,1,0:T(8,128)(2,1)S(1)} %pad_maximum_fusion.10), channel_id=1, source_target_pairs={{0,8},{1,9},{2,10},{3,11},{4,12},{5,13},{6,14},{7,15},{8,0},{9,1},... | collective-permute-start | bytes 786440 | tf_op jit(solution)/shard_map/ppermute | solution.py:54
  31.4 1.6 collective-permute-start.8
  33.0 2.8 %mask_weights.1.refs_4_.refs_5_ = bf16[1024,2688]{1,0:T(8,128)(2,1)S(1)} custom-call(bf16[1024,896]{1,0:T(8,128)(2,1)S(1)} %copy-done, bf16[1024,896]{1,0:T(8,128)(2,1)S(1)} %copy-done.1, bf16[896,1024]{1,0:T(8,128)(2,1)S(1)} %copy-done.2, s32[8,7]{1,0:T(8,128)S(1)} %copy-done.3, s32[8,7]{1,0:T(8,128)S(1)} %copy-done.4, s32[7,8]{1,0:T(8,128)S(1)} %copy-done.5), custom_call_target="tpu_custom_call" | custom-call | flops 2752512 | bytes 11010048 | tf_op jit(solution)/shard_map/mask_weights/pallas_call | solution.py:125
  35.8 7.2 %forward.2 = (bf16[128,2688]{1,0:T(8,128)(2,1)S(1)}, bf16[128,2688]{1,0:T(8,128)(2,1)S(1)}, bf16[64,2688]{1,0:T(8,128)(2,1)S(1)}, bf16[64,2688]{1,0:T(8,128)(2,1)S(1)}, bf16[128,2688]{1,0:T(8,128)(2,1)S(1)}) custom-call(bf16[4,64,1024]{2,1,0:T(8,128)(2,1)S(1)} %pad_maximum_fusion.4.refs_0_, bf16[4,64,1024]{2,1,0:T(8,128)(2,1)S(1)} %pad_maximum_fusion.5.refs_1_, ...), custom_call_target="tpu_custom_call" | custom-call | flops 1024 | bytes 1024 | tf_op jit(solution)/shard_map/forward/pallas_call | solution.py:200
  43.0 2.0 collective-permute-start.6
  45.1 2.5 %collective-permute-start.7 = (bf16[128,2688]{1,0:T(8,128)(2,1)S(1)}, bf16[128,2688]{1,0:T(8,128)(2,1)S(1)}, u32[]{:S(2)}, u32[]{:S(2)}) collective-permute-start(bf16[128,2688]{1,0:T(8,128)(2,1)S(1)} %get-tuple-element.103), channel_id=1, source_target_pairs={{0,48},{1,49},{2,50},{3,51},{4,52},{5,53},{6,54},{7,55},{8,56},{9,... | collective-permute-start | bytes 2064392 | tf_op jit(solution)/shard_map/ppermute | solution.py:54
  48.5 1.2 collective-permute-done.11.refs_2_.refs_11_
  50.5 7.1 %forward.3 = (bf16[128,2688]{1,0:T(8,128)(2,1)S(1)}, bf16[128,2688]{1,0:T(8,128)(2,1)S(1)}, bf16[64,2688]{1,0:T(8,128)(2,1)S(1)}, bf16[64,2688]{1,0:T(8,128)(2,1)S(1)}, bf16[128,2688]{1,0:T(8,128)(2,1)S(1)}) custom-call(bf16[4,64,1024]{2,1,0:T(8,128)(2,1)S(1)} %pad_maximum_fusion.6.refs_0_.refs_9_, ...), custom_call_target="tpu_custom_call" | custom-call | flops 1024 | bytes 1024 | tf_op jit(solution)/shard_map/forward/pallas_call | solution.py:200
  57.6 4.0 %collective-permute-done.7 = bf16[128,2688]{1,0:T(8,128)(2,1)S(1)} collective-permute-done((bf16[128,2688]{1,0:T(8,128)(2,1)S(1)}, bf16[128,2688]{1,0:T(8,128)(2,1)S(1)}, u32[]{:S(2)}, u32[]{:S(2)}) %collective-permute-start.7) | collective-permute-done | bytes 688160 | tf_op jit(solution)/shard_map/ppermute | solution.py:54
  62.0 3.3 %collective-permute-start.14 = (bf16[64,2688]{1,0:T(8,128)(2,1)S(1)}, bf16[64,2688]{1,0:T(8,128)(2,1)S(1)}, u32[]{:S(2)}, u32[]{:S(2)}) collective-permute-start(bf16[64,2688]{1,0:T(8,128)(2,1)S(1)} %slice_add_fusion.2), channel_id=1, source_target_pairs={{0,48},{1,49},{2,50},{3,51},{4,52},{5,53},{6,54},{7,55},{8,56},{9,... | collective-permute-start | bytes 1032200 | tf_op jit(solution)/shard_map/ppermute | solution.py:54
  65.6 3.1 %collective-permute-start.17 = (bf16[128,2688]{1,0:T(8,128)(2,1)S(1)}, bf16[128,2688]{1,0:T(8,128)(2,1)S(1)}, u32[]{:S(2)}, u32[]{:S(2)}) collective-permute-start(bf16[128,2688]{1,0:T(8,128)(2,1)S(1)} %get-tuple-element.120), channel_id=1, source_target_pairs={{0,48},{1,49},{2,50},{3,51},{4,52},{5,53},{6,54},{7,55},{8,56},{9,... | collective-permute-start | bytes 2064392 | tf_op jit(solution)/shard_map/ppermute | solution.py:54
  68.7 5.1 %collective-permute-done.14 = bf16[64,2688]{1,0:T(8,128)(2,1)S(1)} collective-permute-done((bf16[64,2688]{1,0:T(8,128)(2,1)S(1)}, bf16[64,2688]{1,0:T(8,128)(2,1)S(1)}, u32[]{:S(2)}, u32[]{:S(2)}) %collective-permute-start.14) | collective-permute-done | bytes 344096 | tf_op jit(solution)/shard_map/ppermute | solution.py:54
  73.8 3.8 %collective-permute-done.13 = bf16[64,2688]{1,0:T(8,128)(2,1)S(1)} collective-permute-done((bf16[64,2688]{1,0:T(8,128)(2,1)S(1)}, bf16[64,2688]{1,0:T(8,128)(2,1)S(1)}, u32[]{:S(2)}, u32[]{:S(2)}) %collective-permute-start.13) | collective-permute-done | bytes 344096 | tf_op jit(solution)/shard_map/ppermute | solution.py:54
  78.0 1.6 collective-permute-start.15
  79.6 6.0 %collective-permute-done.17 = bf16[128,2688]{1,0:T(8,128)(2,1)S(1)} collective-permute-done((bf16[128,2688]{1,0:T(8,128)(2,1)S(1)}, bf16[128,2688]{1,0:T(8,128)(2,1)S(1)}, u32[]{:S(2)}, u32[]{:S(2)}) %collective-permute-start.17) | collective-permute-done | bytes 688160 | tf_op jit(solution)/shard_map/ppermute | solution.py:54
  85.6 3.5 %collective-permute-done.16 = bf16[128,2688]{1,0:T(8,128)(2,1)S(1)} collective-permute-done((bf16[128,2688]{1,0:T(8,128)(2,1)S(1)}, bf16[128,2688]{1,0:T(8,128)(2,1)S(1)}, u32[]{:S(2)}, u32[]{:S(2)}) %collective-permute-start.16) | collective-permute-done | bytes 688160 | tf_op jit(solution)/shard_map/ppermute | solution.py:54
  89.4 1.9 collective-permute-start.20
  91.9 3.2 %collective-permute-start.18 = (bf16[128,2688]{1,0:T(8,128)(2,1)S(1)}, bf16[128,2688]{1,0:T(8,128)(2,1)S(1)}, u32[]{:S(2)}, u32[]{:S(2)}) collective-permute-start(bf16[128,2688]{1,0:T(8,128)(2,1)S(1)} %pad_maximum_fusion.1.refs_0_.refs_4_), channel_id=1, source_target_pairs={{0,48},{1,49},{2,50},{3,51},{4,52},{5,53},{6,54},{7,55},{8,56},{9,... | collective-permute-start | bytes 2064392 | tf_op jit(solution)/shard_map/ppermute | solution.py:54
  95.2 5.1 %collective-permute-done.21 = bf16[64,2688]{1,0:T(8,128)(2,1)S(1)} collective-permute-done((bf16[64,2688]{1,0:T(8,128)(2,1)S(1)}, bf16[64,2688]{1,0:T(8,128)(2,1)S(1)}, u32[]{:S(2)}, u32[]{:S(2)}) %collective-permute-start.21) | collective-permute-done | bytes 344096 | tf_op jit(solution)/shard_map/ppermute | solution.py:54
  100.2 1.5 collective-permute-done.20
  102.1 1.6 collective-permute-start.24
  103.6 8.6 %collective-permute-done.19.refs_2_.refs_6_ = bf16[128,2688]{1,0:T(8,128)(2,1)S(1)} collective-permute-done((bf16[128,2688]{1,0:T(8,128)(2,1)S(1)}, bf16[128,2688]{1,0:T(8,128)(2,1)S(1)}, u32[]{:S(2)}, u32[]{:S(2)}) %collective-permute-start.19) | collective-permute-done | bytes 688160 | tf_op jit(solution)/shard_map/ppermute | solution.py:54
  114.3 2.6 %collective-permute-start.25 = (bf16[128,2688]{1,0:T(8,128)(2,1)S(1)}, bf16[128,2688]{1,0:T(8,128)(2,1)S(1)}, u32[]{:S(2)}, u32[]{:S(2)}) collective-permute-start(bf16[128,2688]{1,0:T(8,128)(2,1)S(1)} %pad_maximum_fusion.3.refs_0_.refs_13_), channel_id=1, source_target_pairs={{0,48},{1,49},{2,50},{3,51},{4,52},{5,53},{6,54},{7,55},{8,56},{9,... | collective-permute-start | bytes 2064392 | tf_op jit(solution)/shard_map/ppermute | solution.py:54
  116.9 3.2 %collective-permute-start.23 = (bf16[64,2688]{1,0:T(8,128)(2,1)S(1)}, bf16[64,2688]{1,0:T(8,128)(2,1)S(1)}, u32[]{:S(2)}, u32[]{:S(2)}) collective-permute-start(bf16[64,2688]{1,0:T(8,128)(2,1)S(1)} %slice.204), channel_id=1, source_target_pairs={{0,48},{1,49},{2,50},{3,51},{4,52},{5,53},{6,54},{7,55},{8,56},{9,... | collective-permute-start | bytes 1032200 | tf_op jit(solution)/shard_map/ppermute | solution.py:54
  120.2 14.6 %collective-permute-done.22.refs_3_.refs_7_ = bf16[64,2688]{1,0:T(8,128)(2,1)S(1)} collective-permute-done((bf16[64,2688]{1,0:T(8,128)(2,1)S(1)}, bf16[64,2688]{1,0:T(8,128)(2,1)S(1)}, u32[]{:S(2)}, u32[]{:S(2)}) %collective-permute-start.22) | collective-permute-done | bytes 344096 | tf_op jit(solution)/shard_map/ppermute | solution.py:54
  134.8 5.0 %backward.2 = (bf16[256,2048]{1,0:T(8,128)(2,1)S(1)}, bf16[256,2048]{1,0:T(8,128)(2,1)S(1)}) custom-call(bf16[128,2688]{1,0:T(8,128)(2,1)S(1)} %pad_maximum_fusion.1.refs_0_.refs_4_, bf16[128,2688]{1,0:T(8,128)(2,1)S(1)} %collective-permute-done.18.refs_1_.refs_5_, bf16[128,2688]{1,0:T(8,128)(2,1)S(1)} %collective-permute-done.19.refs_2_.refs_6_, ...), custom_call_target="tpu_custom_call" | custom-call | flops 2818572288 | bytes 22020096 | tf_op jit(solution)/shard_map/backward/pallas_call | solution.py:258
  139.9 3.0 %collective-permute-start.32 = (bf16[64,2688]{1,0:T(8,128)(2,1)S(1)}, bf16[64,2688]{1,0:T(8,128)(2,1)S(1)}, u32[]{:S(2)}, u32[]{:S(2)}) collective-permute-start(bf16[64,2688]{1,0:T(8,128)(2,1)S(1)} %slice.209), channel_id=1, source_target_pairs={{0,48},{1,49},{2,50},{3,51},{4,52},{5,53},{6,54},{7,55},{8,56},{9,... | collective-permute-start | bytes 1032200 | tf_op jit(solution)/shard_map/ppermute | solution.py:54
  143.4 7.5 %collective-permute-done.32.refs_4_.refs_17_ = bf16[64,2688]{1,0:T(8,128)(2,1)S(1)} collective-permute-done((bf16[64,2688]{1,0:T(8,128)(2,1)S(1)}, bf16[64,2688]{1,0:T(8,128)(2,1)S(1)}, u32[]{:S(2)}, u32[]{:S(2)}) %collective-permute-start.32) | collective-permute-done | bytes 344096 | tf_op jit(solution)/shard_map/ppermute | solution.py:54
  150.9 3.4 %collective-permute-done.31.refs_3_.refs_16_ = bf16[64,2688]{1,0:T(8,128)(2,1)S(1)} collective-permute-done((bf16[64,2688]{1,0:T(8,128)(2,1)S(1)}, bf16[64,2688]{1,0:T(8,128)(2,1)S(1)}, u32[]{:S(2)}, u32[]{:S(2)}) %collective-permute-start.31) | collective-permute-done | bytes 344096 | tf_op jit(solution)/shard_map/ppermute | solution.py:54
  154.3 5.0 %backward.3 = (bf16[256,2048]{1,0:T(8,128)(2,1)S(1)}, bf16[256,2048]{1,0:T(8,128)(2,1)S(1)}) custom-call(bf16[128,2688]{1,0:T(8,128)(2,1)S(1)} %pad_maximum_fusion.3.refs_0_.refs_13_, bf16[128,2688]{1,0:T(8,128)(2,1)S(1)} %collective-permute-done.25.refs_1_.refs_14_, bf16[128,2688]{1,0:T(8,128)(2,1)S(1)} %collective-permute-done.26.refs_2_.refs_15_, ...), custom_call_target="tpu_custom_call" | custom-call | flops 2818572288 | bytes 22020096 | tf_op jit(solution)/shard_map/backward/pallas_call | solution.py:258
  159.4 7.2 %collective-permute-start.30 = (bf16[64,2048]{1,0:T(8,128)(2,1)S(1)}, bf16[64,2048]{1,0:T(8,128)(2,1)S(1)}, u32[]{:S(2)}, u32[]{:S(2)}) collective-permute-start(bf16[64,2048]{1,0:T(8,128)(2,1)S(1)} %get-tuple-element.189), channel_id=1, source_target_pairs={{0,12},{1,13},{2,14},{3,15},{4,0},{5,1},{6,2},{7,3},{8,4},{9,5},{1... | collective-permute-start | bytes 786440 | tf_op jit(solution)/shard_map/ppermute | solution.py:54
  167.6 10.9 %collective-permute-done.30 = bf16[64,2048]{1,0:T(8,128)(2,1)S(1)} collective-permute-done((bf16[64,2048]{1,0:T(8,128)(2,1)S(1)}, bf16[64,2048]{1,0:T(8,128)(2,1)S(1)}, u32[]{:S(2)}, u32[]{:S(2)}) %collective-permute-start.30) | collective-permute-done | bytes 262176 | tf_op jit(solution)/shard_map/ppermute | solution.py:54
  178.5 3.4 %collective-permute-done.28 = bf16[64,2048]{1,0:T(8,128)(2,1)S(1)} collective-permute-done((bf16[64,2048]{1,0:T(8,128)(2,1)S(1)}, bf16[64,2048]{1,0:T(8,128)(2,1)S(1)}, u32[]{:S(2)}, u32[]{:S(2)}) %collective-permute-start.28) | collective-permute-done | bytes 262176 | tf_op jit(solution)/shard_map/ppermute | solution.py:54
  182.0 3.1 %collective-permute-start.33 = (bf16[32,2048]{1,0:T(8,128)(2,1)S(1)}, bf16[32,2048]{1,0:T(8,128)(2,1)S(1)}, u32[]{:S(2)}, u32[]{:S(2)}) collective-permute-start(bf16[32,2048]{1,0:T(8,128)(2,1)S(1)} %slice.241), channel_id=1, source_target_pairs={{0,2},{1,3},{2,0},{3,1},{4,6},{5,7},{6,4},{7,5},{8,10},{9,11},{10,... | collective-permute-start | bytes 393224 | tf_op jit(solution)/shard_map/ppermute | solution.py:54
  185.6 1.0 collective-permute-start.37
  186.9 0.8 collective-permute-start.35
  187.7 17.4 %weight_grads.1 = (bf16[1024,896]{1,0:T(8,128)(2,1)}, bf16[1024,896]{1,0:T(8,128)(2,1)}, bf16[896,1024]{1,0:T(8,128)(2,1)}) custom-call(bf16[4,64,1024]{2,1,0:T(8,128)(2,1)S(1)} %pad_maximum_fusion.4.refs_0_, bf16[4,64,1024]{2,1,0:T(8,128)(2,1)S(1)} %pad_maximum_fusion.5.refs_1_, bf16[4,64,1024]{2,1,0:T(8,128)(2,1)S(1)} %collective-permute-done.4.refs_2_, ...), custom_call_target="tpu_custom_call" | custom-call | flops 5637144576 | bytes 44040192 | tf_op jit(solution)/shard_map/weight_grads/pallas_call | solution.py:325
  206.0 5.9 %collective-permute-done.38 = bf16[32,2048]{1,0:T(8,128)(2,1)S(1)} collective-permute-done((bf16[32,2048]{1,0:T(8,128)(2,1)S(1)}, bf16[32,2048]{1,0:T(8,128)(2,1)S(1)}, u32[]{:S(2)}, u32[]{:S(2)}) %collective-permute-start.38) | collective-permute-done | bytes 131104 | tf_op jit(solution)/shard_map/ppermute | solution.py:54
  (92 shorter events, 11.0 us)
Async XLA Ops:
  1.6 9.5 %collective-permute-start = (bf16[2,64,1024]{2,1,0:T(8,128)(2,1)S(1)}, bf16[2,64,1024]{2,1,0:T(8,128)(2,1)S(1)}, u32[]{:S(2)}, u32[]{:S(2)}) collective-permute-start(bf16[2,64,1024]{2,1,0:T(8,128)(2,1)S(1)} %pad_maximum_fusion.8), channel_id=1, source_target_pairs={{0,2},{1,3},{2,0},{3,1},{4,6},{5,7},{6,4},{7,5},{8,10},{9,11},{10,... | collective-permute-start | bytes 786440 | tf_op jit(solution)/shard_map/ppermute | solution.py:54
  11.1 21.9 %copy-start.2 = (bf16[896,1024]{1,0:T(8,128)(2,1)S(1)}, bf16[896,1024]{1,0:T(8,128)(2,1)}, u32[]{:S(2)}) copy-start(bf16[896,1024]{1,0:T(8,128)(2,1)} %down.1) | copy-start | bytes 5505028
  11.2 9.6 %collective-permute-start.3 = (bf16[2,64,1024]{2,1,0:T(8,128)(2,1)S(1)}, bf16[2,64,1024]{2,1,0:T(8,128)(2,1)S(1)}, u32[]{:S(2)}, u32[]{:S(2)}) collective-permute-start(bf16[2,64,1024]{2,1,0:T(8,128)(2,1)S(1)} %pad_maximum_fusion.9), channel_id=1, source_target_pairs={{0,4},{1,5},{2,6},{3,7},{4,8},{5,9},{6,10},{7,11},{8,12},{9,13},{1... | collective-permute-start | bytes 786440 | tf_op jit(solution)/shard_map/ppermute | solution.py:54
  13.0 13.7 %collective-permute-start.2 = (bf16[2,64,1024]{2,1,0:T(8,128)(2,1)S(1)}, bf16[2,64,1024]{2,1,0:T(8,128)(2,1)S(1)}, u32[]{:S(2)}, u32[]{:S(2)}) collective-permute-start(bf16[2,64,1024]{2,1,0:T(8,128)(2,1)S(1)} %pad_maximum_fusion.9), channel_id=1, source_target_pairs={{0,8},{1,9},{2,10},{3,11},{4,12},{5,13},{6,14},{7,15},{8,0},{9,1},... | collective-permute-start | bytes 786440 | tf_op jit(solution)/shard_map/ppermute | solution.py:54
  15.9 10.8 %collective-permute-start.1 = (bf16[2,64,1024]{2,1,0:T(8,128)(2,1)S(1)}, bf16[2,64,1024]{2,1,0:T(8,128)(2,1)S(1)}, u32[]{:S(2)}, u32[]{:S(2)}) collective-permute-start(bf16[2,64,1024]{2,1,0:T(8,128)(2,1)S(1)} %pad_maximum_fusion.9), channel_id=1, source_target_pairs={{0,12},{1,13},{2,14},{3,15},{4,0},{5,1},{6,2},{7,3},{8,4},{9,5},{1... | collective-permute-start | bytes 786440 | tf_op jit(solution)/shard_map/ppermute | solution.py:54
  26.8 6.2 %copy-start.1 = (bf16[1024,896]{1,0:T(8,128)(2,1)S(1)}, bf16[1024,896]{1,0:T(8,128)(2,1)}, u32[]{:S(2)}) copy-start(bf16[1024,896]{1,0:T(8,128)(2,1)} %up.1) | copy-start | bytes 5505028
  26.8 6.2 %copy-start = (bf16[1024,896]{1,0:T(8,128)(2,1)S(1)}, bf16[1024,896]{1,0:T(8,128)(2,1)}, u32[]{:S(2)}) copy-start(bf16[1024,896]{1,0:T(8,128)(2,1)} %gate.1) | copy-start | bytes 5505028
  26.8 6.2 %copy-start.3 = (s32[8,7]{1,0:T(8,128)S(1)}, s32[8,7]{1,0:T(8,128)}, u32[]{:S(2)}) copy-start(s32[8,7]{1,0:T(8,128)} %refs_18_.1) | copy-start | bytes 676
  26.8 6.2 %copy-start.4 = (s32[8,7]{1,0:T(8,128)S(1)}, s32[8,7]{1,0:T(8,128)}, u32[]{:S(2)}) copy-start(s32[8,7]{1,0:T(8,128)} %refs_19_.1) | copy-start | bytes 676
  26.8 6.2 %copy-start.5 = (s32[7,8]{1,0:T(8,128)S(1)}, s32[7,8]{1,0:T(8,128)}, u32[]{:S(2)}) copy-start(s32[7,8]{1,0:T(8,128)} %refs_20_.1) | copy-start | bytes 676
  26.9 8.9 %collective-permute-start.4 = (bf16[4,64,1024]{2,1,0:T(8,128)(2,1)S(1)}, bf16[4,64,1024]{2,1,0:T(8,128)(2,1)S(1)}, u32[]{:S(2)}, u32[]{:S(2)}) collective-permute-start(bf16[4,64,1024]{2,1,0:T(8,128)(2,1)S(1)} %pad_maximum_fusion.4.refs_0_), channel_id=1, source_target_pairs={{0,1},{1,0},{2,3},{3,2},{4,5},{5,4},{6,7},{7,6},{8,9},{9,8},{10,11... | collective-permute-start | bytes 1572872 | tf_op jit(solution)/shard_map/ppermute | solution.py:54
  27.1 8.7 %collective-permute-start.5 = (bf16[4,64,1024]{2,1,0:T(8,128)(2,1)S(1)}, bf16[4,64,1024]{2,1,0:T(8,128)(2,1)S(1)}, u32[]{:S(2)}, u32[]{:S(2)}) collective-permute-start(bf16[4,64,1024]{2,1,0:T(8,128)(2,1)S(1)} %pad_maximum_fusion.5.refs_1_), channel_id=1, source_target_pairs={{0,1},{1,0},{2,3},{3,2},{4,5},{5,4},{6,7},{7,6},{8,9},{9,8},{10,11... | collective-permute-start | bytes 1572872 | tf_op jit(solution)/shard_map/ppermute | solution.py:54
  27.7 17.3 %collective-permute-start.10 = (bf16[2,64,1024]{2,1,0:T(8,128)(2,1)S(1)}, bf16[2,64,1024]{2,1,0:T(8,128)(2,1)S(1)}, u32[]{:S(2)}, u32[]{:S(2)}) collective-permute-start(bf16[2,64,1024]{2,1,0:T(8,128)(2,1)S(1)} %pad_maximum_fusion.10), channel_id=1, source_target_pairs={{0,4},{1,5},{2,6},{3,7},{4,8},{5,9},{6,10},{7,11},{8,12},{9,13},{1... | collective-permute-start | bytes 786440 | tf_op jit(solution)/shard_map/ppermute | solution.py:54
  29.0 16.0 %collective-permute-start.9 = (bf16[2,64,1024]{2,1,0:T(8,128)(2,1)S(1)}, bf16[2,64,1024]{2,1,0:T(8,128)(2,1)S(1)}, u32[]{:S(2)}, u32[]{:S(2)}) collective-permute-start(bf16[2,64,1024]{2,1,0:T(8,128)(2,1)S(1)} %pad_maximum_fusion.10), channel_id=1, source_target_pairs={{0,8},{1,9},{2,10},{3,11},{4,12},{5,13},{6,14},{7,15},{8,0},{9,1},... | collective-permute-start | bytes 786440 | tf_op jit(solution)/shard_map/ppermute | solution.py:54
  31.4 13.6 %collective-permute-start.8 = (bf16[2,64,1024]{2,1,0:T(8,128)(2,1)S(1)}, bf16[2,64,1024]{2,1,0:T(8,128)(2,1)S(1)}, u32[]{:S(2)}, u32[]{:S(2)}) collective-permute-start(bf16[2,64,1024]{2,1,0:T(8,128)(2,1)S(1)} %pad_maximum_fusion.10), channel_id=1, source_target_pairs={{0,12},{1,13},{2,14},{3,15},{4,0},{5,1},{6,2},{7,3},{8,4},{9,5},{1... | collective-permute-start | bytes 786440 | tf_op jit(solution)/shard_map/ppermute | solution.py:54
  43.0 18.9 %collective-permute-start.6 = (bf16[128,2688]{1,0:T(8,128)(2,1)S(1)}, bf16[128,2688]{1,0:T(8,128)(2,1)S(1)}, u32[]{:S(2)}, u32[]{:S(2)}) collective-permute-start(bf16[128,2688]{1,0:T(8,128)(2,1)S(1)} %get-tuple-element.102), channel_id=1, source_target_pairs={{0,16},{1,17},{2,18},{3,19},{4,20},{5,21},{6,22},{7,23},{8,24},{9,... | collective-permute-start | bytes 2064392 | tf_op jit(solution)/shard_map/ppermute | solution.py:54
  45.1 16.5 %collective-permute-start.7 = (bf16[128,2688]{1,0:T(8,128)(2,1)S(1)}, bf16[128,2688]{1,0:T(8,128)(2,1)S(1)}, u32[]{:S(2)}, u32[]{:S(2)}) collective-permute-start(bf16[128,2688]{1,0:T(8,128)(2,1)S(1)} %get-tuple-element.103), channel_id=1, source_target_pairs={{0,48},{1,49},{2,50},{3,51},{4,52},{5,53},{6,54},{7,55},{8,56},{9,... | collective-permute-start | bytes 2064392 | tf_op jit(solution)/shard_map/ppermute | solution.py:54
  47.7 2.0 collective-permute-start.11
  47.9 2.6 %collective-permute-start.12 = (bf16[4,64,1024]{2,1,0:T(8,128)(2,1)S(1)}, bf16[4,64,1024]{2,1,0:T(8,128)(2,1)S(1)}, u32[]{:S(2)}, u32[]{:S(2)}) collective-permute-start(bf16[4,64,1024]{2,1,0:T(8,128)(2,1)S(1)} %pad_maximum_fusion.7.refs_1_.refs_10_), channel_id=1, source_target_pairs={{0,1},{1,0},{2,3},{3,2},{4,5},{5,4},{6,7},{7,6},{8,9},{9,8},{10,11... | collective-permute-start | bytes 1572872 | tf_op jit(solution)/shard_map/ppermute | solution.py:54
  62.0 11.9 %collective-permute-start.14 = (bf16[64,2688]{1,0:T(8,128)(2,1)S(1)}, bf16[64,2688]{1,0:T(8,128)(2,1)S(1)}, u32[]{:S(2)}, u32[]{:S(2)}) collective-permute-start(bf16[64,2688]{1,0:T(8,128)(2,1)S(1)} %slice_add_fusion.2), channel_id=1, source_target_pairs={{0,48},{1,49},{2,50},{3,51},{4,52},{5,53},{6,54},{7,55},{8,56},{9,... | collective-permute-start | bytes 1032200 | tf_op jit(solution)/shard_map/ppermute | solution.py:54
  65.4 12.3 %collective-permute-start.13 = (bf16[64,2688]{1,0:T(8,128)(2,1)S(1)}, bf16[64,2688]{1,0:T(8,128)(2,1)S(1)}, u32[]{:S(2)}, u32[]{:S(2)}) collective-permute-start(bf16[64,2688]{1,0:T(8,128)(2,1)S(1)} %slice_add_fusion.3), channel_id=1, source_target_pairs={{0,16},{1,17},{2,18},{3,19},{4,20},{5,21},{6,22},{7,23},{8,24},{9,... | collective-permute-start | bytes 1032200 | tf_op jit(solution)/shard_map/ppermute | solution.py:54
  65.4 23.7 %collective-permute-start.16 = (bf16[128,2688]{1,0:T(8,128)(2,1)S(1)}, bf16[128,2688]{1,0:T(8,128)(2,1)S(1)}, u32[]{:S(2)}, u32[]{:S(2)}) collective-permute-start(bf16[128,2688]{1,0:T(8,128)(2,1)S(1)} %get-tuple-element.113), channel_id=1, source_target_pairs={{0,16},{1,17},{2,18},{3,19},{4,20},{5,21},{6,22},{7,23},{8,24},{9,... | collective-permute-start | bytes 2064392 | tf_op jit(solution)/shard_map/ppermute | solution.py:54
  65.6 19.9 %collective-permute-start.17 = (bf16[128,2688]{1,0:T(8,128)(2,1)S(1)}, bf16[128,2688]{1,0:T(8,128)(2,1)S(1)}, u32[]{:S(2)}, u32[]{:S(2)}) collective-permute-start(bf16[128,2688]{1,0:T(8,128)(2,1)S(1)} %get-tuple-element.120), channel_id=1, source_target_pairs={{0,48},{1,49},{2,50},{3,51},{4,52},{5,53},{6,54},{7,55},{8,56},{9,... | collective-permute-start | bytes 2064392 | tf_op jit(solution)/shard_map/ppermute | solution.py:54
  78.0 13.4 %collective-permute-start.15 = (bf16[128,2688]{1,0:T(8,128)(2,1)S(1)}, bf16[128,2688]{1,0:T(8,128)(2,1)S(1)}, u32[]{:S(2)}, u32[]{:S(2)}) collective-permute-start(bf16[128,2688]{1,0:T(8,128)(2,1)S(1)} %pad_maximum_fusion), channel_id=1, source_target_pairs={{0,64},{1,65},{2,66},{3,67},{4,68},{5,69},{6,70},{7,71},{8,72},{9,... | collective-permute-start | bytes 2064392 | tf_op jit(solution)/shard_map/ppermute | solution.py:54
  89.2 11.1 %collective-permute-start.21 = (bf16[64,2688]{1,0:T(8,128)(2,1)S(1)}, bf16[64,2688]{1,0:T(8,128)(2,1)S(1)}, u32[]{:S(2)}, u32[]{:S(2)}) collective-permute-start(bf16[64,2688]{1,0:T(8,128)(2,1)S(1)} %slice_add_fusion), channel_id=1, source_target_pairs={{0,48},{1,49},{2,50},{3,51},{4,52},{5,53},{6,54},{7,55},{8,56},{9,... | collective-permute-start | bytes 1032200 | tf_op jit(solution)/shard_map/ppermute | solution.py:54
  89.4 12.3 %collective-permute-start.20 = (bf16[64,2688]{1,0:T(8,128)(2,1)S(1)}, bf16[64,2688]{1,0:T(8,128)(2,1)S(1)}, u32[]{:S(2)}, u32[]{:S(2)}) collective-permute-start(bf16[64,2688]{1,0:T(8,128)(2,1)S(1)} %slice_add_fusion.1), channel_id=1, source_target_pairs={{0,16},{1,17},{2,18},{3,19},{4,20},{5,21},{6,22},{7,23},{8,24},{9,... | collective-permute-start | bytes 1032200 | tf_op jit(solution)/shard_map/ppermute | solution.py:54
  91.9 20.4 %collective-permute-start.19 = (bf16[128,2688]{1,0:T(8,128)(2,1)S(1)}, bf16[128,2688]{1,0:T(8,128)(2,1)S(1)}, u32[]{:S(2)}, u32[]{:S(2)}) collective-permute-start(bf16[128,2688]{1,0:T(8,128)(2,1)S(1)} %pad_maximum_fusion.1.refs_0_.refs_4_), channel_id=1, source_target_pairs={{0,16},{1,17},{2,18},{3,19},{4,20},{5,21},{6,22},{7,23},{8,24},{9,... | collective-permute-start | bytes 2064392 | tf_op jit(solution)/shard_map/ppermute | solution.py:54
  91.9 20.3 %collective-permute-start.18 = (bf16[128,2688]{1,0:T(8,128)(2,1)S(1)}, bf16[128,2688]{1,0:T(8,128)(2,1)S(1)}, u32[]{:S(2)}, u32[]{:S(2)}) collective-permute-start(bf16[128,2688]{1,0:T(8,128)(2,1)S(1)} %pad_maximum_fusion.1.refs_0_.refs_4_), channel_id=1, source_target_pairs={{0,48},{1,49},{2,50},{3,51},{4,52},{5,53},{6,54},{7,55},{8,56},{9,... | collective-permute-start | bytes 2064392 | tf_op jit(solution)/shard_map/ppermute | solution.py:54
  102.1 11.0 %collective-permute-start.24 = (bf16[128,2688]{1,0:T(8,128)(2,1)S(1)}, bf16[128,2688]{1,0:T(8,128)(2,1)S(1)}, u32[]{:S(2)}, u32[]{:S(2)}) collective-permute-start(bf16[128,2688]{1,0:T(8,128)(2,1)S(1)} %pad_maximum_fusion.2), channel_id=1, source_target_pairs={{0,64},{1,65},{2,66},{3,67},{4,68},{5,69},{6,70},{7,71},{8,72},{9,... | collective-permute-start | bytes 2064392 | tf_op jit(solution)/shard_map/ppermute | solution.py:54
  113.6 26.1 %collective-permute-start.26 = (bf16[128,2688]{1,0:T(8,128)(2,1)S(1)}, bf16[128,2688]{1,0:T(8,128)(2,1)S(1)}, u32[]{:S(2)}, u32[]{:S(2)}) collective-permute-start(bf16[128,2688]{1,0:T(8,128)(2,1)S(1)} %pad_maximum_fusion.3.refs_0_.refs_13_), channel_id=1, source_target_pairs={{0,16},{1,17},{2,18},{3,19},{4,20},{5,21},{6,22},{7,23},{8,24},{9,... | collective-permute-start | bytes 2064392 | tf_op jit(solution)/shard_map/ppermute | solution.py:54
  114.3 25.4 %collective-permute-start.25 = (bf16[128,2688]{1,0:T(8,128)(2,1)S(1)}, bf16[128,2688]{1,0:T(8,128)(2,1)S(1)}, u32[]{:S(2)}, u32[]{:S(2)}) collective-permute-start(bf16[128,2688]{1,0:T(8,128)(2,1)S(1)} %pad_maximum_fusion.3.refs_0_.refs_13_), channel_id=1, source_target_pairs={{0,48},{1,49},{2,50},{3,51},{4,52},{5,53},{6,54},{7,55},{8,56},{9,... | collective-permute-start | bytes 2064392 | tf_op jit(solution)/shard_map/ppermute | solution.py:54
  116.9 17.9 %collective-permute-start.22 = (bf16[64,2688]{1,0:T(8,128)(2,1)S(1)}, bf16[64,2688]{1,0:T(8,128)(2,1)S(1)}, u32[]{:S(2)}, u32[]{:S(2)}) collective-permute-start(bf16[64,2688]{1,0:T(8,128)(2,1)S(1)} %slice.203), channel_id=1, source_target_pairs={{0,16},{1,17},{2,18},{3,19},{4,20},{5,21},{6,22},{7,23},{8,24},{9,... | collective-permute-start | bytes 1032200 | tf_op jit(solution)/shard_map/ppermute | solution.py:54
  116.9 17.9 %collective-permute-start.23 = (bf16[64,2688]{1,0:T(8,128)(2,1)S(1)}, bf16[64,2688]{1,0:T(8,128)(2,1)S(1)}, u32[]{:S(2)}, u32[]{:S(2)}) collective-permute-start(bf16[64,2688]{1,0:T(8,128)(2,1)S(1)} %slice.204), channel_id=1, source_target_pairs={{0,48},{1,49},{2,50},{3,51},{4,52},{5,53},{6,54},{7,55},{8,56},{9,... | collective-permute-start | bytes 1032200 | tf_op jit(solution)/shard_map/ppermute | solution.py:54
  139.8 3.1 %collective-permute-start.27 = (bf16[256,2048]{1,0:T(8,128)(2,1)S(1)}, bf16[256,2048]{1,0:T(8,128)(2,1)S(1)}, u32[]{:S(2)}, u32[]{:S(2)}) collective-permute-start(bf16[256,2048]{1,0:T(8,128)(2,1)S(1)} %get-tuple-element.140), channel_id=1, source_target_pairs={{0,1},{1,0},{2,3},{3,2},{4,5},{5,4},{6,7},{7,6},{8,9},{9,8},{10,11... | collective-permute-start | bytes 3145736 | tf_op jit(solution)/shard_map/ppermute | solution.py:54
  139.9 10.9 %collective-permute-start.32 = (bf16[64,2688]{1,0:T(8,128)(2,1)S(1)}, bf16[64,2688]{1,0:T(8,128)(2,1)S(1)}, u32[]{:S(2)}, u32[]{:S(2)}) collective-permute-start(bf16[64,2688]{1,0:T(8,128)(2,1)S(1)} %slice.209), channel_id=1, source_target_pairs={{0,48},{1,49},{2,50},{3,51},{4,52},{5,53},{6,54},{7,55},{8,56},{9,... | collective-permute-start | bytes 1032200 | tf_op jit(solution)/shard_map/ppermute | solution.py:54
  143.0 11.3 %collective-permute-start.31 = (bf16[64,2688]{1,0:T(8,128)(2,1)S(1)}, bf16[64,2688]{1,0:T(8,128)(2,1)S(1)}, u32[]{:S(2)}, u32[]{:S(2)}) collective-permute-start(bf16[64,2688]{1,0:T(8,128)(2,1)S(1)} %slice.208), channel_id=1, source_target_pairs={{0,16},{1,17},{2,18},{3,19},{4,20},{5,21},{6,22},{7,23},{8,24},{9,... | collective-permute-start | bytes 1032200 | tf_op jit(solution)/shard_map/ppermute | solution.py:54
  159.3 25.9 %collective-permute-start.34 = (bf16[256,2048]{1,0:T(8,128)(2,1)S(1)}, bf16[256,2048]{1,0:T(8,128)(2,1)S(1)}, u32[]{:S(2)}, u32[]{:S(2)}) collective-permute-start(bf16[256,2048]{1,0:T(8,128)(2,1)S(1)} %get-tuple-element.147), channel_id=1, source_target_pairs={{0,1},{1,0},{2,3},{3,2},{4,5},{5,4},{6,7},{7,6},{8,9},{9,8},{10,11... | collective-permute-start | bytes 3145736 | tf_op jit(solution)/shard_map/ppermute | solution.py:54
  159.4 19.0 %collective-permute-start.30 = (bf16[64,2048]{1,0:T(8,128)(2,1)S(1)}, bf16[64,2048]{1,0:T(8,128)(2,1)S(1)}, u32[]{:S(2)}, u32[]{:S(2)}) collective-permute-start(bf16[64,2048]{1,0:T(8,128)(2,1)S(1)} %get-tuple-element.189), channel_id=1, source_target_pairs={{0,12},{1,13},{2,14},{3,15},{4,0},{5,1},{6,2},{7,3},{8,4},{9,5},{1... | collective-permute-start | bytes 786440 | tf_op jit(solution)/shard_map/ppermute | solution.py:54
  166.6 11.8 %collective-permute-start.29 = (bf16[64,2048]{1,0:T(8,128)(2,1)S(1)}, bf16[64,2048]{1,0:T(8,128)(2,1)S(1)}, u32[]{:S(2)}, u32[]{:S(2)}) collective-permute-start(bf16[64,2048]{1,0:T(8,128)(2,1)S(1)} %get-tuple-element.190), channel_id=1, source_target_pairs={{0,8},{1,9},{2,10},{3,11},{4,12},{5,13},{6,14},{7,15},{8,0},{9,1},... | collective-permute-start | bytes 786440 | tf_op jit(solution)/shard_map/ppermute | solution.py:54
  166.8 15.1 %collective-permute-start.28 = (bf16[64,2048]{1,0:T(8,128)(2,1)S(1)}, bf16[64,2048]{1,0:T(8,128)(2,1)S(1)}, u32[]{:S(2)}, u32[]{:S(2)}) collective-permute-start(bf16[64,2048]{1,0:T(8,128)(2,1)S(1)} %get-tuple-element.191), channel_id=1, source_target_pairs={{0,4},{1,5},{2,6},{3,7},{4,8},{5,9},{6,10},{7,11},{8,12},{9,13},{1... | collective-permute-start | bytes 786440 | tf_op jit(solution)/shard_map/ppermute | solution.py:54
  182.0 23.9 %collective-permute-start.33 = (bf16[32,2048]{1,0:T(8,128)(2,1)S(1)}, bf16[32,2048]{1,0:T(8,128)(2,1)S(1)}, u32[]{:S(2)}, u32[]{:S(2)}) collective-permute-start(bf16[32,2048]{1,0:T(8,128)(2,1)S(1)} %slice.241), channel_id=1, source_target_pairs={{0,2},{1,3},{2,0},{3,1},{4,6},{5,7},{6,4},{7,5},{8,10},{9,11},{10,... | collective-permute-start | bytes 393224 | tf_op jit(solution)/shard_map/ppermute | solution.py:54
  185.6 19.5 %collective-permute-start.37 = (bf16[64,2048]{1,0:T(8,128)(2,1)S(1)}, bf16[64,2048]{1,0:T(8,128)(2,1)S(1)}, u32[]{:S(2)}, u32[]{:S(2)}) collective-permute-start(bf16[64,2048]{1,0:T(8,128)(2,1)S(1)} %get-tuple-element.185), channel_id=1, source_target_pairs={{0,12},{1,13},{2,14},{3,15},{4,0},{5,1},{6,2},{7,3},{8,4},{9,5},{1... | collective-permute-start | bytes 786440 | tf_op jit(solution)/shard_map/ppermute | solution.py:54
  186.6 18.5 %collective-permute-start.36 = (bf16[64,2048]{1,0:T(8,128)(2,1)S(1)}, bf16[64,2048]{1,0:T(8,128)(2,1)S(1)}, u32[]{:S(2)}, u32[]{:S(2)}) collective-permute-start(bf16[64,2048]{1,0:T(8,128)(2,1)S(1)} %get-tuple-element.186), channel_id=1, source_target_pairs={{0,8},{1,9},{2,10},{3,11},{4,12},{5,13},{6,14},{7,15},{8,0},{9,1},... | collective-permute-start | bytes 786440 | tf_op jit(solution)/shard_map/ppermute | solution.py:54
  186.9 18.3 %collective-permute-start.35 = (bf16[64,2048]{1,0:T(8,128)(2,1)S(1)}, bf16[64,2048]{1,0:T(8,128)(2,1)S(1)}, u32[]{:S(2)}, u32[]{:S(2)}) collective-permute-start(bf16[64,2048]{1,0:T(8,128)(2,1)S(1)} %get-tuple-element.187), channel_id=1, source_target_pairs={{0,4},{1,5},{2,6},{3,7},{4,8},{5,9},{6,10},{7,11},{8,12},{9,13},{1... | collective-permute-start | bytes 786440 | tf_op jit(solution)/shard_map/ppermute | solution.py:54
  205.3 6.6 %collective-permute-start.38 = (bf16[32,2048]{1,0:T(8,128)(2,1)S(1)}, bf16[32,2048]{1,0:T(8,128)(2,1)S(1)}, u32[]{:S(2)}, u32[]{:S(2)}) collective-permute-start(bf16[32,2048]{1,0:T(8,128)(2,1)S(1)} %slice.247), channel_id=1, source_target_pairs={{0,2},{1,3},{2,0},{3,1},{4,6},{5,7},{6,4},{7,5},{8,10},{9,11},{10,... | collective-permute-start | bytes 393224 | tf_op jit(solution)/shard_map/ppermute | solution.py:54

commit v4 on v3

--- a/solution.py
+++ b/solution.py
@@ -26,8 +26,8 @@
     "send 0",
     "chip 0",
     "backward 1",
+    "last 0",
     "send 1",
-    "last 0",
     "chip 1",
     "grads",
     "last 1",
@@ -81,7 +81,6 @@
 
 
 VMEM = pl.BlockSpec(memory_space=pltpu.VMEM)
-ANY = pl.BlockSpec(memory_space=pl.ANY)
 SMEM = pl.BlockSpec(memory_space=pltpu.SMEM)
 
 
@@ -89,22 +88,16 @@
     return lax.rem(lax.axis_index("row") + dz, 4)
 
 
-def token_copies(gathered, offset, rows, pieces, held, first, sems):
-    copies = []
-    for at, (dz, half) in enumerate(pieces):
-        to = pl.ds(first + at * rows, rows)
-        for kind in range(2):
-            source = gathered[2 * half + kind].at[owner(dz), pl.ds(offset, rows)]
-            copies.append(pltpu.make_async_copy(source, held.at[kind, to], sems.at[kind, at]))
-    return copies
-
-
-def gathered_at(piece, arrays, rows):
+def tokens_of(kind, gathered, offset, rows, columns):
+    return [
+        gathered[2 * half + kind][owner(dz), offset : offset + rows, columns]
+        for dz, half in GATHERED
+    ]
+
+
+def values_of(arrays, columns):
     own, up, down, far_first, far_second = arrays
-    dz, half = piece
-    if dz == 2:
-        return (far_first, far_second)[half]
-    return {0: own, 1: up, 3: down}[dz].at[pl.ds(half * rows, rows)]
+    return [array[:, columns] for array in (own, up, down, far_first, far_second)]
 
 
 def mask_kernel(gate, up, down, gate_mask, up_mask, down_mask, out):
@@ -143,72 +136,29 @@
     )(gate, up, down, gate_mask, up_mask, down_mask)
 
 
-def weight_copies(source, target, sems, order):
-    width = target.shape[1] // 3
-    depth = target.shape[0] // 2
-    copies = []
-    for at in order:
-        columns = pl.ds(at * width, width)
-        copies.append(
-            [
-                pltpu.make_async_copy(
-                    source.at[pl.ds(part * depth, depth), columns],
-                    target.at[pl.ds(part * depth, depth), columns],
-                    sems.at[at, part],
-                )
-                for part in range(2)
-            ]
-        )
-    return copies
-
-
-def start(copies):
-    for copy in copies:
-        copy.start()
-
-
-def wait(copies):
-    for copy in copies:
-        copy.wait()
-
-
 def forward_kernel(offset, rows, *refs):
-    gathered, weights, outs = refs[:4], refs[4], refs[5:10]
-    held, held_weights, sems, weight_sems = refs[10:]
-    pieces = [piece for group in GROUPS for piece in group]
-    copies = token_copies(gathered, offset, rows, pieces, held, 0, sems)
-    loads = weight_copies(weights, held_weights, weight_sems, range(3))
-    start(loads[0])
-    start(copies)
-    start(loads[1])
-    start(loads[2])
-    wait(copies)
+    gathered, weights, outs = refs[:4], refs[4], refs[5:]
     width = weights.shape[1] // 3
+    every = slice(None)
     for at in range(3):
-        wait(loads[at])
         columns = slice(at * width, (at + 1) * width)
-        part = nn(held[at // 2], held_weights[:, columns]).astype(jnp.bfloat16)
-        first = 0
-        for out, group in zip(outs, GROUPS):
-            size = len(group) * rows
-            out[:, columns] = part[first : first + size]
-            first += size
+        left = jnp.concatenate(tokens_of(at // 2, gathered, offset, rows, every))
+        part = nn(left, weights[:, columns]).astype(jnp.bfloat16)
+        for number, piece in enumerate(GATHERED):
+            for out, group in zip(outs, GROUPS):
+                if piece in group:
+                    first = group.index(piece) * rows
+                    out[first : first + rows, columns] = part[number * rows : (number + 1) * rows]
 
 
 def forward(gathered, offset, rows, weights):
-    depth, total = weights.shape
+    total = weights.shape[1]
     return pl.pallas_call(
         functools.partial(forward_kernel, offset, rows),
-        in_specs=[ANY] * 5,
+        in_specs=[VMEM] * 5,
         out_specs=[VMEM] * len(GROUPS),
         out_shape=[
             jax.ShapeDtypeStruct((len(group) * rows, total), jnp.bfloat16) for group in GROUPS
-        ],
-        scratch_shapes=[
-            pltpu.VMEM((2, 8 * rows, depth), jnp.bfloat16),
-            pltpu.VMEM((depth, total), jnp.bfloat16),
-            pltpu.SemaphoreType.DMA((2, 8)),
-            pltpu.SemaphoreType.DMA((3, 2)),
         ],
         compiler_params=params(),
         cost_estimate=cheap(),
@@ -217,85 +167,53 @@
 
 
 def backward_kernel(*refs):
-    arrays, weights = refs[:5], refs[5]
-    outs, (held, held_weights, sems, weight_sems) = refs[6:8], refs[8:]
-    rows = arrays[3].shape[0]
-    copies = []
-    for at, (dz, half) in enumerate(GATHERED):
-        source = gathered_at((dz, half), arrays, rows)
-        to = pl.ds(pl.multiple_of(((1 - half) * 4 + owner(dz)) * rows, rows), rows)
-        copies.append(pltpu.make_async_copy(source, held.at[to], sems.at[at]))
-    loads = weight_copies(weights, held_weights, weight_sems, (2, 0, 1))
-    start(loads[0])
-    start(copies)
-    start(loads[1])
-    start(loads[2])
-    wait(copies)
-    depth = held_weights.shape[0]
-    width = held_weights.shape[1] // 3
-
-    def term(at):
-        columns = slice(at * width, (at + 1) * width)
-        return nt(held[:, columns], held_weights[:, columns])
-
-    def put(part, column):
-        part = part.astype(jnp.bfloat16)
-        size = part.shape[0] // len(outs)
-        for at, out in enumerate(outs):
-            out[:, column : column + depth] = part[at * size : (at + 1) * size]
-
-    wait(loads[0])
-    put(term(2), 0)
-    wait(loads[1])
-    wait(loads[2])
-    columns = slice(0, 2 * width)
-    put(nt(held[:, columns], held_weights[:, columns]), depth)
+    arrays, weights, for_other, for_own = refs[:5], *refs[5:]
+    depth, total = weights.shape
+    width = total // 3
+    rows = for_own.shape[1]
+    for columns, to in ((slice(2 * width, total), 0), (slice(0, 2 * width), depth)):
+        left = jnp.concatenate(values_of(arrays, columns))
+        part = nt(left, weights[:, columns]).astype(jnp.bfloat16)
+        for at, (dz, half) in enumerate(GATHERED):
+            out = (for_own, for_other)[half]
+            out[owner(dz), :, to : to + depth] = part[at * rows : (at + 1) * rows]
 
 
 def backward(arrays, weights):
     rows = arrays[3].shape[0]
     depth, total = weights.shape
-    return pl.pallas_call(
+    outs = pl.pallas_call(
         backward_kernel,
-        in_specs=[ANY] * 6,
+        in_specs=[VMEM] * 6,
         out_specs=[VMEM] * 2,
-        out_shape=[jax.ShapeDtypeStruct((4 * rows, 2 * depth), jnp.bfloat16)] * 2,
-        scratch_shapes=[
-            pltpu.VMEM((8 * rows, total), jnp.bfloat16),
-            pltpu.VMEM((depth, total), jnp.bfloat16),
-            pltpu.SemaphoreType.DMA((8,)),
-            pltpu.SemaphoreType.DMA((3, 2)),
-        ],
+        out_shape=[jax.ShapeDtypeStruct((4, rows, 2 * depth), jnp.bfloat16)] * 2,
         compiler_params=params(),
         cost_estimate=pl.CostEstimate(
             flops=16 * rows * depth * total, bytes_accessed=8 * depth * total, transcendentals=0
         ),
         name="backward",
     )(*arrays, weights)
+    return [out.reshape(4 * rows, 2 * depth) for out in outs]
 
 
 def weight_grad_kernel(offsets, *refs):
     number = 9 * len(offsets)
-    gate_mask, up_mask, down_mask, gate_grad, up_grad, down_grad = refs[number : number + 6]
-    tokens, values, sems, value_sems = refs[number + 6 :]
-    first = 0
-    copies = []
-    for which, offset in enumerate(offsets):
-        gathered, arrays = refs[9 * which : 9 * which + 4], refs[9 * which + 4 : 9 * which + 9]
-        rows = arrays[3].shape[0]
-        copies += token_copies(gathered, offset, rows, GATHERED, tokens, first, sems.at[which])
-        for at, piece in enumerate(GATHERED):
-            copies.append(
-                pltpu.make_async_copy(
-                    gathered_at(piece, arrays, rows),
-                    values.at[pl.ds(first + at * rows, rows)],
-                    value_sems.at[which, at],
-                )
-            )
-        first += 8 * rows
-    start(copies)
-    wait(copies)
+    gate_mask, up_mask, down_mask, gate_grad, up_grad, down_grad = refs[number:]
     width, depth = down_grad.shape
+    every = slice(None)
+
+    def tokens(kind, columns):
+        parts = []
+        for which, offset in enumerate(offsets):
+            chunk = refs[9 * which : 9 * which + 9]
+            parts += tokens_of(kind, chunk[:4], offset, chunk[7].shape[0], columns)
+        return jnp.concatenate(parts)
+
+    def values(columns):
+        parts = []
+        for which in range(len(offsets)):
+            parts += values_of(refs[9 * which + 4 : 9 * which + 9], columns)
+        return jnp.concatenate(parts)
 
     def store(part, mask, row, out):
         for j in range(part.shape[1] // BLK):
@@ -307,13 +225,13 @@
                 )
 
     for row in range(0, depth, 256):
-        left = tokens[0, :, row : row + 256]
-        store(tn(left, values[:, :width]), gate_mask, row, gate_grad)
-        store(tn(left, values[:, width : 2 * width]), up_mask, row, up_grad)
+        left = tokens(0, slice(row, row + 256))
+        store(tn(left, values(slice(0, width))), gate_mask, row, gate_grad)
+        store(tn(left, values(slice(width, 2 * width))), up_mask, row, up_grad)
     for row in range(0, width, 256):
         size = min(256, width - row)
-        left = values[:, 2 * width + row : 2 * width + row + size]
-        store(tn(left, tokens[1]), down_mask, row, down_grad)
+        left = values(slice(2 * width + row, 2 * width + row + size))
+        store(tn(left, tokens(1, every)), down_mask, row, down_grad)
 
 
 def weight_grads(offsets, chunks, gate_mask, up_mask, down_mask):
@@ -324,18 +242,12 @@
     inputs = [item for gathered, arrays in chunks for item in (*gathered, *arrays)]
     return pl.pallas_call(
         functools.partial(weight_grad_kernel, offsets),
-        in_specs=[ANY] * len(inputs) + [SMEM] * 3,
+        in_specs=[VMEM] * len(inputs) + [SMEM] * 3,
         out_specs=[VMEM] * 3,
         out_shape=[
             jax.ShapeDtypeStruct((depth, width), jnp.bfloat16),
             jax.ShapeDtypeStruct((depth, width), jnp.bfloat16),
             jax.ShapeDtypeStruct((width, depth), jnp.bfloat16),
-        ],
-        scratch_shapes=[
-            pltpu.VMEM((2, count, depth), jnp.bfloat16),
-            pltpu.VMEM((count, total), jnp.bfloat16),
-            pltpu.SemaphoreType.DMA((len(chunks), 2, 8)),
-            pltpu.SemaphoreType.DMA((len(chunks), 8)),
         ],
         compiler_params=params(),
         cost_estimate=pl.CostEstimate(
@@ -476,7 +388,7 @@
             offset = 2 * (starts[i] - starts[group[0]])
             chunks.append(Chunk(gather, offset, CHUNKS[i], weights))
     gathers[0].far()
-    before = gathers[0].core()
+    before = gathers[0].core(weights)
     gathers[1].far(before)
     for step in ORDER:
         name, _, which = step.partition(" ")

time: 214 us -> 203 us (0.949)
  Pallas kernels: 44.4 us -> 25.6 us
  starting transfers between devices: 59.4 us -> 63.4 us
  local copies, waits for them, and re-layouts: 0.5 us -> 3.47 us
    pallas_call x1, Pallas kernels: 17.4 us -> 9.6 us  [weight_grads(): pl.pallas_call(functools.partial(weight_grad_kernel, offsets), in_specs=[...]
    pallas_call x2, Pallas kernels: 14.3 us -> 6.85 us  [forward(): pl.pallas_call(functools.partial(forward_kernel, offset, rows), in_specs=...]
    ppermute x39, starting transfers between devices: 59.4 us -> 63.4 us  [move(): return lax.ppermute(array, ('row', 'col'), pairs)]
    pallas_call x2, Pallas kernels: 9.93 us -> 6.35 us  [backward(): pl.pallas_call(backward_kernel, in_specs=[VMEM] * 6, out_specs=[VMEM] * 2...]
    unnamed x12, local copies, waits for them, and re-layouts: 0.04 us -> 3.01 us
  transfers between devices with their start and end apart: 39 -> 39, of which waited for: 21 -> 23; matrix products, arithmetic and copies ran while one was open for 2% -> 2% of each run, Pallas kernels for 19% -> 13%
where the time goes in v4:
time: 203 us; the launch traced here: 202 us
  waiting for transfers between devices  103 us (51%)
  starting transfers between devices  63.4 us (31%)
  Pallas kernels  25.6 us (13%)
  other arithmetic  6.2 us (3%)
  local copies, waits for them, and re-layouts  3.47 us (2%)
    ppermute x39, waiting for transfers between devices, move(): return lax.ppermute(array, ('row', 'col'), pairs)  103 us
    ppermute x39, starting transfers between devices, move(): return lax.ppermute(array, ('row', 'col'), pairs)  63.4 us
    pallas_call x1, Pallas kernels, weight_grads(): pl.pallas_call(functools.partial(weight_grad_kernel, offsets), in_specs=[...  9.6 us
    pallas_call x2, Pallas kernels, forward(): pl.pallas_call(functools.partial(forward_kernel, offset, rows), in_specs=...  6.85 us
    pallas_call x2, Pallas kernels, backward(): pl.pallas_call(backward_kernel, in_specs=[VMEM] * 6, out_specs=[VMEM] * 2...  6.35 us
  transfers between devices with their start and end apart: 39, of which 23 were waited for; matrix products, arithmetic and copies ran while one was open for 2% of the time, Pallas kernels for 13%

profile of v4, /device:TPU:0, one launch (start us, length us, event | category | flops | bytes accessed | tf_op | source)
XLA Modules:
  0.0 202.3 jit_solution(10418412188222137548)
XLA Ops:
  1.8 3.2 %collective-permute-start = (bf16[2,64,1024]{2,1,0:T(8,128)(2,1)S(1)}, bf16[2,64,1024]{2,1,0:T(8,128)(2,1)S(1)}, u32[]{:S(2)}, u32[]{:S(2)}) collective-permute-start(bf16[2,64,1024]{2,1,0:T(8,128)(2,1)S(1)} %pad_maximum_fusion.8), channel_id=1, source_target_pairs={{0,2},{1,3},{2,0},{3,1},{4,6},{5,7},{6,4},{7,5},{8,10},{9,11},{10,... | collective-permute-start | bytes 786440 | tf_op jit(solution)/shard_map/ppermute | solution.py:54
  6.0 5.3 %collective-permute-done = bf16[2,64,1024]{2,1,0:T(8,128)(2,1)S(1)} collective-permute-done((bf16[2,64,1024]{2,1,0:T(8,128)(2,1)S(1)}, bf16[2,64,1024]{2,1,0:T(8,128)(2,1)S(1)}, u32[]{:S(2)}, u32[]{:S(2)}) %collective-permute-start) | collective-permute-done | bytes 262176 | tf_op jit(solution)/shard_map/ppermute | solution.py:54
  11.3 1.9 collective-permute-start.3
  13.2 2.9 %collective-permute-start.2 = (bf16[2,64,1024]{2,1,0:T(8,128)(2,1)S(1)}, bf16[2,64,1024]{2,1,0:T(8,128)(2,1)S(1)}, u32[]{:S(2)}, u32[]{:S(2)}) collective-permute-start(bf16[2,64,1024]{2,1,0:T(8,128)(2,1)S(1)} %pad_maximum_fusion.9), channel_id=1, source_target_pairs={{0,8},{1,9},{2,10},{3,11},{4,12},{5,13},{6,14},{7,15},{8,0},{9,1},... | collective-permute-start | bytes 786440 | tf_op jit(solution)/shard_map/ppermute | solution.py:54
  16.1 1.3 collective-permute-start.1
  17.5 1.5 copy-done.1
  19.0 1.5 copy-done.2
  20.5 2.8 %mask_weights.1.refs_4_.refs_5_ = bf16[1024,2688]{1,0:T(8,128)(2,1)S(1)} custom-call(bf16[1024,896]{1,0:T(8,128)(2,1)S(1)} %copy-done, bf16[1024,896]{1,0:T(8,128)(2,1)S(1)} %copy-done.1, bf16[896,1024]{1,0:T(8,128)(2,1)S(1)} %copy-done.2, s32[8,7]{1,0:T(8,128)S(1)} %copy-done.3, s32[8,7]{1,0:T(8,128)S(1)} %copy-done.4, s32[7,8]{1,0:T(8,128)S(1)} %copy-done.5), custom_call_target="tpu_custom_call" | custom-call | flops 2752512 | bytes 11010048 | tf_op jit(solution)/shard_map/mask_weights/pallas_call | solution.py:118
  23.3 3.6 %collective-permute-done.2 = bf16[2,64,1024]{2,1,0:T(8,128)(2,1)S(1)} collective-permute-done((bf16[2,64,1024]{2,1,0:T(8,128)(2,1)S(1)}, bf16[2,64,1024]{2,1,0:T(8,128)(2,1)S(1)}, u32[]{:S(2)}, u32[]{:S(2)}) %collective-permute-start.2) | collective-permute-done | bytes 262176 | tf_op jit(solution)/shard_map/ppermute | solution.py:54
  27.8 1.3 collective-permute-start.10
  29.1 2.4 %collective-permute-start.9 = (bf16[2,64,1024]{2,1,0:T(8,128)(2,1)S(1)}, bf16[2,64,1024]{2,1,0:T(8,128)(2,1)S(1)}, u32[]{:S(2)}, u32[]{:S(2)}) collective-permute-start(bf16[2,64,1024]{2,1,0:T(8,128)(2,1)S(1)} %pad_maximum_fusion.10), channel_id=1, source_target_pairs={{0,8},{1,9},{2,10},{3,11},{4,12},{5,13},{6,14},{7,15},{8,0},{9,1},... | collective-permute-start | bytes 786440 | tf_op jit(solution)/shard_map/ppermute | solution.py:54
  31.5 1.6 collective-permute-start.8
  33.1 3.4 %forward.2 = (bf16[128,2688]{1,0:T(8,128)(2,1)S(1)}, bf16[128,2688]{1,0:T(8,128)(2,1)S(1)}, bf16[64,2688]{1,0:T(8,128)(2,1)S(1)}, bf16[64,2688]{1,0:T(8,128)(2,1)S(1)}, bf16[128,2688]{1,0:T(8,128)(2,1)S(1)}) custom-call(bf16[4,64,1024]{2,1,0:T(8,128)(2,1)S(1)} %pad_maximum_fusion.4.refs_0_, bf16[4,64,1024]{2,1,0:T(8,128)(2,1)S(1)} %pad_maximum_fusion.5.refs_1_, ...), custom_call_target="tpu_custom_call" | custom-call | flops 1024 | bytes 1024 | tf_op jit(solution)/shard_map/forward/pallas_call | solution.py:156
  36.5 2.0 collective-permute-start.6
  38.5 4.8 %collective-permute-done.9 = bf16[2,64,1024]{2,1,0:T(8,128)(2,1)S(1)} collective-permute-done((bf16[2,64,1024]{2,1,0:T(8,128)(2,1)S(1)}, bf16[2,64,1024]{2,1,0:T(8,128)(2,1)S(1)}, u32[]{:S(2)}, u32[]{:S(2)}) %collective-permute-start.9) | collective-permute-done | bytes 262176 | tf_op jit(solution)/shard_map/ppermute | solution.py:54
  43.7 4.1 %collective-permute-start.7 = (bf16[128,2688]{1,0:T(8,128)(2,1)S(1)}, bf16[128,2688]{1,0:T(8,128)(2,1)S(1)}, u32[]{:S(2)}, u32[]{:S(2)}) collective-permute-start(bf16[128,2688]{1,0:T(8,128)(2,1)S(1)} %get-tuple-element.104), channel_id=1, source_target_pairs={{0,48},{1,49},{2,50},{3,51},{4,52},{5,53},{6,54},{7,55},{8,56},{9,... | collective-permute-start | bytes 2064392 | tf_op jit(solution)/shard_map/ppermute | solution.py:54
  48.6 1.2 collective-permute-done.11.refs_2_.refs_11_
  50.6 3.4 %forward.3 = (bf16[128,2688]{1,0:T(8,128)(2,1)S(1)}, bf16[128,2688]{1,0:T(8,128)(2,1)S(1)}, bf16[64,2688]{1,0:T(8,128)(2,1)S(1)}, bf16[64,2688]{1,0:T(8,128)(2,1)S(1)}, bf16[128,2688]{1,0:T(8,128)(2,1)S(1)}) custom-call(bf16[4,64,1024]{2,1,0:T(8,128)(2,1)S(1)} %pad_maximum_fusion.6.refs_0_.refs_9_, ...), custom_call_target="tpu_custom_call" | custom-call | flops 1024 | bytes 1024 | tf_op jit(solution)/shard_map/forward/pallas_call | solution.py:156
  54.0 7.6 %collective-permute-done.7 = bf16[128,2688]{1,0:T(8,128)(2,1)S(1)} collective-permute-done((bf16[128,2688]{1,0:T(8,128)(2,1)S(1)}, bf16[128,2688]{1,0:T(8,128)(2,1)S(1)}, u32[]{:S(2)}, u32[]{:S(2)}) %collective-permute-start.7) | collective-permute-done | bytes 688160 | tf_op jit(solution)/shard_map/ppermute | solution.py:54
  61.6 3.8 %collective-permute-start.14 = (bf16[64,2688]{1,0:T(8,128)(2,1)S(1)}, bf16[64,2688]{1,0:T(8,128)(2,1)S(1)}, u32[]{:S(2)}, u32[]{:S(2)}) collective-permute-start(bf16[64,2688]{1,0:T(8,128)(2,1)S(1)} %slice_add_fusion.2), channel_id=1, source_target_pairs={{0,48},{1,49},{2,50},{3,51},{4,52},{5,53},{6,54},{7,55},{8,56},{9,... | collective-permute-start | bytes 1032200 | tf_op jit(solution)/shard_map/ppermute | solution.py:54
  65.6 3.2 %collective-permute-start.17 = (bf16[128,2688]{1,0:T(8,128)(2,1)S(1)}, bf16[128,2688]{1,0:T(8,128)(2,1)S(1)}, u32[]{:S(2)}, u32[]{:S(2)}) collective-permute-start(bf16[128,2688]{1,0:T(8,128)(2,1)S(1)} %get-tuple-element.121), channel_id=1, source_target_pairs={{0,48},{1,49},{2,50},{3,51},{4,52},{5,53},{6,54},{7,55},{8,56},{9,... | collective-permute-start | bytes 2064392 | tf_op jit(solution)/shard_map/ppermute | solution.py:54
  68.9 5.1 %collective-permute-done.14 = bf16[64,2688]{1,0:T(8,128)(2,1)S(1)} collective-permute-done((bf16[64,2688]{1,0:T(8,128)(2,1)S(1)}, bf16[64,2688]{1,0:T(8,128)(2,1)S(1)}, u32[]{:S(2)}, u32[]{:S(2)}) %collective-permute-start.14) | collective-permute-done | bytes 344096 | tf_op jit(solution)/shard_map/ppermute | solution.py:54
  73.9 3.8 %collective-permute-done.13 = bf16[64,2688]{1,0:T(8,128)(2,1)S(1)} collective-permute-done((bf16[64,2688]{1,0:T(8,128)(2,1)S(1)}, bf16[64,2688]{1,0:T(8,128)(2,1)S(1)}, u32[]{:S(2)}, u32[]{:S(2)}) %collective-permute-start.13) | collective-permute-done | bytes 344096 | tf_op jit(solution)/shard_map/ppermute | solution.py:54
  78.1 1.6 collective-permute-start.15
  79.7 6.0 %collective-permute-done.17 = bf16[128,2688]{1,0:T(8,128)(2,1)S(1)} collective-permute-done((bf16[128,2688]{1,0:T(8,128)(2,1)S(1)}, bf16[128,2688]{1,0:T(8,128)(2,1)S(1)}, u32[]{:S(2)}, u32[]{:S(2)}) %collective-permute-start.17) | collective-permute-done | bytes 688160 | tf_op jit(solution)/shard_map/ppermute | solution.py:54
  85.7 3.5 %collective-permute-done.16 = bf16[128,2688]{1,0:T(8,128)(2,1)S(1)} collective-permute-done((bf16[128,2688]{1,0:T(8,128)(2,1)S(1)}, bf16[128,2688]{1,0:T(8,128)(2,1)S(1)}, u32[]{:S(2)}, u32[]{:S(2)}) %collective-permute-start.16) | collective-permute-done | bytes 688160 | tf_op jit(solution)/shard_map/ppermute | solution.py:54
  89.7 1.9 collective-permute-start.20
  92.2 3.2 %collective-permute-start.18 = (bf16[128,2688]{1,0:T(8,128)(2,1)S(1)}, bf16[128,2688]{1,0:T(8,128)(2,1)S(1)}, u32[]{:S(2)}, u32[]{:S(2)}) collective-permute-start(bf16[128,2688]{1,0:T(8,128)(2,1)S(1)} %pad_maximum_fusion.1.refs_0_.refs_4_), channel_id=1, source_target_pairs={{0,48},{1,49},{2,50},{3,51},{4,52},{5,53},{6,54},{7,55},{8,56},{9,... | collective-permute-start | bytes 2064392 | tf_op jit(solution)/shard_map/ppermute | solution.py:54
  95.5 5.1 %collective-permute-done.21 = bf16[64,2688]{1,0:T(8,128)(2,1)S(1)} collective-permute-done((bf16[64,2688]{1,0:T(8,128)(2,1)S(1)}, bf16[64,2688]{1,0:T(8,128)(2,1)S(1)}, u32[]{:S(2)}, u32[]{:S(2)}) %collective-permute-start.21) | collective-permute-done | bytes 344096 | tf_op jit(solution)/shard_map/ppermute | solution.py:54
  100.5 1.5 collective-permute-done.20
  102.4 1.6 collective-permute-start.24
  103.9 8.6 %collective-permute-done.19.refs_2_.refs_6_ = bf16[128,2688]{1,0:T(8,128)(2,1)S(1)} collective-permute-done((bf16[128,2688]{1,0:T(8,128)(2,1)S(1)}, bf16[128,2688]{1,0:T(8,128)(2,1)S(1)}, u32[]{:S(2)}, u32[]{:S(2)}) %collective-permute-start.19) | collective-permute-done | bytes 688160 | tf_op jit(solution)/shard_map/ppermute | solution.py:54
  114.6 2.6 %collective-permute-start.25 = (bf16[128,2688]{1,0:T(8,128)(2,1)S(1)}, bf16[128,2688]{1,0:T(8,128)(2,1)S(1)}, u32[]{:S(2)}, u32[]{:S(2)}) collective-permute-start(bf16[128,2688]{1,0:T(8,128)(2,1)S(1)} %pad_maximum_fusion.3.refs_0_.refs_13_), channel_id=1, source_target_pairs={{0,48},{1,49},{2,50},{3,51},{4,52},{5,53},{6,54},{7,55},{8,56},{9,... | collective-permute-start | bytes 2064392 | tf_op jit(solution)/shard_map/ppermute | solution.py:54
  117.2 3.2 %collective-permute-start.23 = (bf16[64,2688]{1,0:T(8,128)(2,1)S(1)}, bf16[64,2688]{1,0:T(8,128)(2,1)S(1)}, u32[]{:S(2)}, u32[]{:S(2)}) collective-permute-start(bf16[64,2688]{1,0:T(8,128)(2,1)S(1)} %slice.204), channel_id=1, source_target_pairs={{0,48},{1,49},{2,50},{3,51},{4,52},{5,53},{6,54},{7,55},{8,56},{9,... | collective-permute-start | bytes 1032200 | tf_op jit(solution)/shard_map/ppermute | solution.py:54
  120.4 14.6 %collective-permute-done.22.refs_3_.refs_7_ = bf16[64,2688]{1,0:T(8,128)(2,1)S(1)} collective-permute-done((bf16[64,2688]{1,0:T(8,128)(2,1)S(1)}, bf16[64,2688]{1,0:T(8,128)(2,1)S(1)}, u32[]{:S(2)}, u32[]{:S(2)}) %collective-permute-start.22) | collective-permute-done | bytes 344096 | tf_op jit(solution)/shard_map/ppermute | solution.py:54
  135.0 3.2 %backward.2 = (bf16[4,64,2048]{2,1,0:T(8,128)(2,1)S(1)}, bf16[4,64,2048]{2,1,0:T(8,128)(2,1)S(1)}) custom-call(bf16[128,2688]{1,0:T(8,128)(2,1)S(1)} %pad_maximum_fusion.1.refs_0_.refs_4_, bf16[128,2688]{1,0:T(8,128)(2,1)S(1)} %collective-permute-done.18.refs_1_.refs_5_, bf16[128,2688]{1,0:T(8,128)(2,1)S(1)} %collective-permute-done.19.refs_2_.refs_6_, ...), custom_call_target="tpu_custom_call" | custom-call | flops 2818572288 | bytes 22020096 | tf_op jit(solution)/shard_map/backward/pallas_call | solution.py:185
  138.4 3.0 %collective-permute-start.32 = (bf16[64,2688]{1,0:T(8,128)(2,1)S(1)}, bf16[64,2688]{1,0:T(8,128)(2,1)S(1)}, u32[]{:S(2)}, u32[]{:S(2)}) collective-permute-start(bf16[64,2688]{1,0:T(8,128)(2,1)S(1)} %slice.209), channel_id=1, source_target_pairs={{0,48},{1,49},{2,50},{3,51},{4,52},{5,53},{6,54},{7,55},{8,56},{9,... | collective-permute-start | bytes 1032200 | tf_op jit(solution)/shard_map/ppermute | solution.py:54
  142.0 7.4 %collective-permute-done.32.refs_4_.refs_17_ = bf16[64,2688]{1,0:T(8,128)(2,1)S(1)} collective-permute-done((bf16[64,2688]{1,0:T(8,128)(2,1)S(1)}, bf16[64,2688]{1,0:T(8,128)(2,1)S(1)}, u32[]{:S(2)}, u32[]{:S(2)}) %collective-permute-start.32) | collective-permute-done | bytes 344096 | tf_op jit(solution)/shard_map/ppermute | solution.py:54
  149.4 3.4 %collective-permute-done.31.refs_3_.refs_16_ = bf16[64,2688]{1,0:T(8,128)(2,1)S(1)} collective-permute-done((bf16[64,2688]{1,0:T(8,128)(2,1)S(1)}, bf16[64,2688]{1,0:T(8,128)(2,1)S(1)}, u32[]{:S(2)}, u32[]{:S(2)}) %collective-permute-start.31) | collective-permute-done | bytes 344096 | tf_op jit(solution)/shard_map/ppermute | solution.py:54
  152.8 7.1 %collective-permute-start.30 = (bf16[64,2048]{1,0:T(8,128)(2,1)S(1)}, bf16[64,2048]{1,0:T(8,128)(2,1)S(1)}, u32[]{:S(2)}, u32[]{:S(2)}) collective-permute-start(bf16[64,2048]{1,0:T(8,128)(2,1)S(1)} %get-tuple-element.191), channel_id=1, source_target_pairs={{0,12},{1,13},{2,14},{3,15},{4,0},{5,1},{6,2},{7,3},{8,4},{9,5},{1... | collective-permute-start | bytes 786440 | tf_op jit(solution)/shard_map/ppermute | solution.py:54
  160.7 3.2 %backward.3 = (bf16[4,64,2048]{2,1,0:T(8,128)(2,1)S(1)}, bf16[4,64,2048]{2,1,0:T(8,128)(2,1)S(1)}) custom-call(bf16[128,2688]{1,0:T(8,128)(2,1)S(1)} %pad_maximum_fusion.3.refs_0_.refs_13_, bf16[128,2688]{1,0:T(8,128)(2,1)S(1)} %collective-permute-done.25.refs_1_.refs_14_, bf16[128,2688]{1,0:T(8,128)(2,1)S(1)} %collective-permute-done.26.refs_2_.refs_15_, ...), custom_call_target="tpu_custom_call" | custom-call | flops 2818572288 | bytes 22020096 | tf_op jit(solution)/shard_map/backward/pallas_call | solution.py:185
  163.9 6.6 %collective-permute-done.30 = bf16[64,2048]{1,0:T(8,128)(2,1)S(1)} collective-permute-done((bf16[64,2048]{1,0:T(8,128)(2,1)S(1)}, bf16[64,2048]{1,0:T(8,128)(2,1)S(1)}, u32[]{:S(2)}, u32[]{:S(2)}) %collective-permute-start.30) | collective-permute-done | bytes 262176 | tf_op jit(solution)/shard_map/ppermute | solution.py:54
  170.6 3.3 %collective-permute-done.28 = bf16[64,2048]{1,0:T(8,128)(2,1)S(1)} collective-permute-done((bf16[64,2048]{1,0:T(8,128)(2,1)S(1)}, bf16[64,2048]{1,0:T(8,128)(2,1)S(1)}, u32[]{:S(2)}, u32[]{:S(2)}) %collective-permute-start.28) | collective-permute-done | bytes 262176 | tf_op jit(solution)/shard_map/ppermute | solution.py:54
  174.2 3.3 %collective-permute-start.33 = (bf16[32,2048]{1,0:T(8,128)(2,1)S(1)}, bf16[32,2048]{1,0:T(8,128)(2,1)S(1)}, u32[]{:S(2)}, u32[]{:S(2)}) collective-permute-start(bf16[32,2048]{1,0:T(8,128)(2,1)S(1)} %slice.241), channel_id=1, source_target_pairs={{0,2},{1,3},{2,0},{3,1},{4,6},{5,7},{6,4},{7,5},{8,10},{9,11},{10,... | collective-permute-start | bytes 393224 | tf_op jit(solution)/shard_map/ppermute | solution.py:54
  180.2 9.6 %weight_grads.1 = (bf16[1024,896]{1,0:T(8,128)(2,1)}, bf16[1024,896]{1,0:T(8,128)(2,1)}, bf16[896,1024]{1,0:T(8,128)(2,1)}) custom-call(bf16[4,64,1024]{2,1,0:T(8,128)(2,1)S(1)} %pad_maximum_fusion.4.refs_0_, bf16[4,64,1024]{2,1,0:T(8,128)(2,1)S(1)} %pad_maximum_fusion.5.refs_1_, bf16[4,64,1024]{2,1,0:T(8,128)(2,1)S(1)} %collective-permute-done.4.refs_2_, ...), custom_call_target="tpu_custom_call" | custom-call | flops 5637144576 | bytes 44040192 | tf_op jit(solution)/shard_map/weight_grads/pallas_call | solution.py:243
  189.8 4.5 %collective-permute-done.35 = bf16[64,2048]{1,0:T(8,128)(2,1)S(1)} collective-permute-done((bf16[64,2048]{1,0:T(8,128)(2,1)S(1)}, bf16[64,2048]{1,0:T(8,128)(2,1)S(1)}, u32[]{:S(2)}, u32[]{:S(2)}) %collective-permute-start.35) | collective-permute-done | bytes 262176 | tf_op jit(solution)/shard_map/ppermute | solution.py:54
  194.5 2.3 %collective-permute-start.38 = (bf16[32,2048]{1,0:T(8,128)(2,1)S(1)}, bf16[32,2048]{1,0:T(8,128)(2,1)S(1)}, u32[]{:S(2)}, u32[]{:S(2)}) collective-permute-start(bf16[32,2048]{1,0:T(8,128)(2,1)S(1)} %slice.247), channel_id=1, source_target_pairs={{0,2},{1,3},{2,0},{3,1},{4,6},{5,7},{6,4},{7,5},{8,10},{9,11},{10,... | collective-permute-start | bytes 393224 | tf_op jit(solution)/shard_map/ppermute | solution.py:54
  196.9 4.6 %collective-permute-done.38 = bf16[32,2048]{1,0:T(8,128)(2,1)S(1)} collective-permute-done((bf16[32,2048]{1,0:T(8,128)(2,1)S(1)}, bf16[32,2048]{1,0:T(8,128)(2,1)S(1)}, u32[]{:S(2)}, u32[]{:S(2)}) %collective-permute-start.38) | collective-permute-done | bytes 131104 | tf_op jit(solution)/shard_map/ppermute | solution.py:54
  (92 shorter events, 14.3 us)
Async XLA Ops:
  0.6 16.8 %copy-start.5 = (s32[7,8]{1,0:T(8,128)S(1)}, s32[7,8]{1,0:T(8,128)}, u32[]{:S(2)}) copy-start(s32[7,8]{1,0:T(8,128)} %refs_20_.1) | copy-start | bytes 676
  0.6 16.8 %copy-start.4 = (s32[8,7]{1,0:T(8,128)S(1)}, s32[8,7]{1,0:T(8,128)}, u32[]{:S(2)}) copy-start(s32[8,7]{1,0:T(8,128)} %refs_19_.1) | copy-start | bytes 676
  0.7 16.8 %copy-start.3 = (s32[8,7]{1,0:T(8,128)S(1)}, s32[8,7]{1,0:T(8,128)}, u32[]{:S(2)}) copy-start(s32[8,7]{1,0:T(8,128)} %refs_18_.1) | copy-start | bytes 676
  0.7 16.8 %copy-start = (bf16[1024,896]{1,0:T(8,128)(2,1)S(1)}, bf16[1024,896]{1,0:T(8,128)(2,1)}, u32[]{:S(2)}) copy-start(bf16[1024,896]{1,0:T(8,128)(2,1)} %gate.1) | copy-start | bytes 5505028
  1.8 9.5 %collective-permute-start = (bf16[2,64,1024]{2,1,0:T(8,128)(2,1)S(1)}, bf16[2,64,1024]{2,1,0:T(8,128)(2,1)S(1)}, u32[]{:S(2)}, u32[]{:S(2)}) collective-permute-start(bf16[2,64,1024]{2,1,0:T(8,128)(2,1)S(1)} %pad_maximum_fusion.8), channel_id=1, source_target_pairs={{0,2},{1,3},{2,0},{3,1},{4,6},{5,7},{6,4},{7,5},{8,10},{9,11},{10,... | collective-permute-start | bytes 786440 | tf_op jit(solution)/shard_map/ppermute | solution.py:54
  11.3 11.9 %collective-permute-start.3 = (bf16[2,64,1024]{2,1,0:T(8,128)(2,1)S(1)}, bf16[2,64,1024]{2,1,0:T(8,128)(2,1)S(1)}, u32[]{:S(2)}, u32[]{:S(2)}) collective-permute-start(bf16[2,64,1024]{2,1,0:T(8,128)(2,1)S(1)} %pad_maximum_fusion.9), channel_id=1, source_target_pairs={{0,4},{1,5},{2,6},{3,7},{4,8},{5,9},{6,10},{7,11},{8,12},{9,13},{1... | collective-permute-start | bytes 786440 | tf_op jit(solution)/shard_map/ppermute | solution.py:54
  13.2 13.7 %collective-permute-start.2 = (bf16[2,64,1024]{2,1,0:T(8,128)(2,1)S(1)}, bf16[2,64,1024]{2,1,0:T(8,128)(2,1)S(1)}, u32[]{:S(2)}, u32[]{:S(2)}) collective-permute-start(bf16[2,64,1024]{2,1,0:T(8,128)(2,1)S(1)} %pad_maximum_fusion.9), channel_id=1, source_target_pairs={{0,8},{1,9},{2,10},{3,11},{4,12},{5,13},{6,14},{7,15},{8,0},{9,1},... | collective-permute-start | bytes 786440 | tf_op jit(solution)/shard_map/ppermute | solution.py:54
  16.1 10.8 %collective-permute-start.1 = (bf16[2,64,1024]{2,1,0:T(8,128)(2,1)S(1)}, bf16[2,64,1024]{2,1,0:T(8,128)(2,1)S(1)}, u32[]{:S(2)}, u32[]{:S(2)}) collective-permute-start(bf16[2,64,1024]{2,1,0:T(8,128)(2,1)S(1)} %pad_maximum_fusion.9), channel_id=1, source_target_pairs={{0,12},{1,13},{2,14},{3,15},{4,0},{5,1},{6,2},{7,3},{8,4},{9,5},{1... | collective-permute-start | bytes 786440 | tf_op jit(solution)/shard_map/ppermute | solution.py:54
  17.5 1.5 copy-start.1
  19.0 1.5 copy-start.2
  27.0 6.0 %collective-permute-start.4 = (bf16[4,64,1024]{2,1,0:T(8,128)(2,1)S(1)}, bf16[4,64,1024]{2,1,0:T(8,128)(2,1)S(1)}, u32[]{:S(2)}, u32[]{:S(2)}) collective-permute-start(bf16[4,64,1024]{2,1,0:T(8,128)(2,1)S(1)} %pad_maximum_fusion.4.refs_0_), channel_id=1, source_target_pairs={{0,1},{1,0},{2,3},{3,2},{4,5},{5,4},{6,7},{7,6},{8,9},{9,8},{10,11... | collective-permute-start | bytes 1572872 | tf_op jit(solution)/shard_map/ppermute | solution.py:54
  27.2 5.9 %collective-permute-start.5 = (bf16[4,64,1024]{2,1,0:T(8,128)(2,1)S(1)}, bf16[4,64,1024]{2,1,0:T(8,128)(2,1)S(1)}, u32[]{:S(2)}, u32[]{:S(2)}) collective-permute-start(bf16[4,64,1024]{2,1,0:T(8,128)(2,1)S(1)} %pad_maximum_fusion.5.refs_1_), channel_id=1, source_target_pairs={{0,1},{1,0},{2,3},{3,2},{4,5},{5,4},{6,7},{7,6},{8,9},{9,8},{10,11... | collective-permute-start | bytes 1572872 | tf_op jit(solution)/shard_map/ppermute | solution.py:54
  27.8 10.7 %collective-permute-start.10 = (bf16[2,64,1024]{2,1,0:T(8,128)(2,1)S(1)}, bf16[2,64,1024]{2,1,0:T(8,128)(2,1)S(1)}, u32[]{:S(2)}, u32[]{:S(2)}) collective-permute-start(bf16[2,64,1024]{2,1,0:T(8,128)(2,1)S(1)} %pad_maximum_fusion.10), channel_id=1, source_target_pairs={{0,4},{1,5},{2,6},{3,7},{4,8},{5,9},{6,10},{7,11},{8,12},{9,13},{1... | collective-permute-start | bytes 786440 | tf_op jit(solution)/shard_map/ppermute | solution.py:54
  29.1 14.2 %collective-permute-start.9 = (bf16[2,64,1024]{2,1,0:T(8,128)(2,1)S(1)}, bf16[2,64,1024]{2,1,0:T(8,128)(2,1)S(1)}, u32[]{:S(2)}, u32[]{:S(2)}) collective-permute-start(bf16[2,64,1024]{2,1,0:T(8,128)(2,1)S(1)} %pad_maximum_fusion.10), channel_id=1, source_target_pairs={{0,8},{1,9},{2,10},{3,11},{4,12},{5,13},{6,14},{7,15},{8,0},{9,1},... | collective-permute-start | bytes 786440 | tf_op jit(solution)/shard_map/ppermute | solution.py:54
  31.5 12.1 %collective-permute-start.8 = (bf16[2,64,1024]{2,1,0:T(8,128)(2,1)S(1)}, bf16[2,64,1024]{2,1,0:T(8,128)(2,1)S(1)}, u32[]{:S(2)}, u32[]{:S(2)}) collective-permute-start(bf16[2,64,1024]{2,1,0:T(8,128)(2,1)S(1)} %pad_maximum_fusion.10), channel_id=1, source_target_pairs={{0,12},{1,13},{2,14},{3,15},{4,0},{5,1},{6,2},{7,3},{8,4},{9,5},{1... | collective-permute-start | bytes 786440 | tf_op jit(solution)/shard_map/ppermute | solution.py:54
  36.5 25.1 %collective-permute-start.6 = (bf16[128,2688]{1,0:T(8,128)(2,1)S(1)}, bf16[128,2688]{1,0:T(8,128)(2,1)S(1)}, u32[]{:S(2)}, u32[]{:S(2)}) collective-permute-start(bf16[128,2688]{1,0:T(8,128)(2,1)S(1)} %get-tuple-element.103), channel_id=1, source_target_pairs={{0,16},{1,17},{2,18},{3,19},{4,20},{5,21},{6,22},{7,23},{8,24},{9,... | collective-permute-start | bytes 2064392 | tf_op jit(solution)/shard_map/ppermute | solution.py:54
  43.7 17.9 %collective-permute-start.7 = (bf16[128,2688]{1,0:T(8,128)(2,1)S(1)}, bf16[128,2688]{1,0:T(8,128)(2,1)S(1)}, u32[]{:S(2)}, u32[]{:S(2)}) collective-permute-start(bf16[128,2688]{1,0:T(8,128)(2,1)S(1)} %get-tuple-element.104), channel_id=1, source_target_pairs={{0,48},{1,49},{2,50},{3,51},{4,52},{5,53},{6,54},{7,55},{8,56},{9,... | collective-permute-start | bytes 2064392 | tf_op jit(solution)/shard_map/ppermute | solution.py:54
  47.8 2.0 collective-permute-start.11
  48.0 2.6 %collective-permute-start.12 = (bf16[4,64,1024]{2,1,0:T(8,128)(2,1)S(1)}, bf16[4,64,1024]{2,1,0:T(8,128)(2,1)S(1)}, u32[]{:S(2)}, u32[]{:S(2)}) collective-permute-start(bf16[4,64,1024]{2,1,0:T(8,128)(2,1)S(1)} %pad_maximum_fusion.7.refs_1_.refs_10_), channel_id=1, source_target_pairs={{0,1},{1,0},{2,3},{3,2},{4,5},{5,4},{6,7},{7,6},{8,9},{9,8},{10,11... | collective-permute-start | bytes 1572872 | tf_op jit(solution)/shard_map/ppermute | solution.py:54
  61.6 12.3 %collective-permute-start.14 = (bf16[64,2688]{1,0:T(8,128)(2,1)S(1)}, bf16[64,2688]{1,0:T(8,128)(2,1)S(1)}, u32[]{:S(2)}, u32[]{:S(2)}) collective-permute-start(bf16[64,2688]{1,0:T(8,128)(2,1)S(1)} %slice_add_fusion.2), channel_id=1, source_target_pairs={{0,48},{1,49},{2,50},{3,51},{4,52},{5,53},{6,54},{7,55},{8,56},{9,... | collective-permute-start | bytes 1032200 | tf_op jit(solution)/shard_map/ppermute | solution.py:54
  65.5 12.3 %collective-permute-start.13 = (bf16[64,2688]{1,0:T(8,128)(2,1)S(1)}, bf16[64,2688]{1,0:T(8,128)(2,1)S(1)}, u32[]{:S(2)}, u32[]{:S(2)}) collective-permute-start(bf16[64,2688]{1,0:T(8,128)(2,1)S(1)} %slice_add_fusion.3), channel_id=1, source_target_pairs={{0,16},{1,17},{2,18},{3,19},{4,20},{5,21},{6,22},{7,23},{8,24},{9,... | collective-permute-start | bytes 1032200 | tf_op jit(solution)/shard_map/ppermute | solution.py:54
  65.5 23.7 %collective-permute-start.16 = (bf16[128,2688]{1,0:T(8,128)(2,1)S(1)}, bf16[128,2688]{1,0:T(8,128)(2,1)S(1)}, u32[]{:S(2)}, u32[]{:S(2)}) collective-permute-start(bf16[128,2688]{1,0:T(8,128)(2,1)S(1)} %get-tuple-element.114), channel_id=1, source_target_pairs={{0,16},{1,17},{2,18},{3,19},{4,20},{5,21},{6,22},{7,23},{8,24},{9,... | collective-permute-start | bytes 2064392 | tf_op jit(solution)/shard_map/ppermute | solution.py:54
  65.6 20.0 %collective-permute-start.17 = (bf16[128,2688]{1,0:T(8,128)(2,1)S(1)}, bf16[128,2688]{1,0:T(8,128)(2,1)S(1)}, u32[]{:S(2)}, u32[]{:S(2)}) collective-permute-start(bf16[128,2688]{1,0:T(8,128)(2,1)S(1)} %get-tuple-element.121), channel_id=1, source_target_pairs={{0,48},{1,49},{2,50},{3,51},{4,52},{5,53},{6,54},{7,55},{8,56},{9,... | collective-permute-start | bytes 2064392 | tf_op jit(solution)/shard_map/ppermute | solution.py:54
  78.1 13.6 %collective-permute-start.15 = (bf16[128,2688]{1,0:T(8,128)(2,1)S(1)}, bf16[128,2688]{1,0:T(8,128)(2,1)S(1)}, u32[]{:S(2)}, u32[]{:S(2)}) collective-permute-start(bf16[128,2688]{1,0:T(8,128)(2,1)S(1)} %pad_maximum_fusion), channel_id=1, source_target_pairs={{0,64},{1,65},{2,66},{3,67},{4,68},{5,69},{6,70},{7,71},{8,72},{9,... | collective-permute-start | bytes 2064392 | tf_op jit(solution)/shard_map/ppermute | solution.py:54
  89.3 11.2 %collective-permute-start.21 = (bf16[64,2688]{1,0:T(8,128)(2,1)S(1)}, bf16[64,2688]{1,0:T(8,128)(2,1)S(1)}, u32[]{:S(2)}, u32[]{:S(2)}) collective-permute-start(bf16[64,2688]{1,0:T(8,128)(2,1)S(1)} %slice_add_fusion), channel_id=1, source_target_pairs={{0,48},{1,49},{2,50},{3,51},{4,52},{5,53},{6,54},{7,55},{8,56},{9,... | collective-permute-start | bytes 1032200 | tf_op jit(solution)/shard_map/ppermute | solution.py:54
  89.7 12.3 %collective-permute-start.20 = (bf16[64,2688]{1,0:T(8,128)(2,1)S(1)}, bf16[64,2688]{1,0:T(8,128)(2,1)S(1)}, u32[]{:S(2)}, u32[]{:S(2)}) collective-permute-start(bf16[64,2688]{1,0:T(8,128)(2,1)S(1)} %slice_add_fusion.1), channel_id=1, source_target_pairs={{0,16},{1,17},{2,18},{3,19},{4,20},{5,21},{6,22},{7,23},{8,24},{9,... | collective-permute-start | bytes 1032200 | tf_op jit(solution)/shard_map/ppermute | solution.py:54
  92.1 20.4 %collective-permute-start.19 = (bf16[128,2688]{1,0:T(8,128)(2,1)S(1)}, bf16[128,2688]{1,0:T(8,128)(2,1)S(1)}, u32[]{:S(2)}, u32[]{:S(2)}) collective-permute-start(bf16[128,2688]{1,0:T(8,128)(2,1)S(1)} %pad_maximum_fusion.1.refs_0_.refs_4_), channel_id=1, source_target_pairs={{0,16},{1,17},{2,18},{3,19},{4,20},{5,21},{6,22},{7,23},{8,24},{9,... | collective-permute-start | bytes 2064392 | tf_op jit(solution)/shard_map/ppermute | solution.py:54
  92.2 20.3 %collective-permute-start.18 = (bf16[128,2688]{1,0:T(8,128)(2,1)S(1)}, bf16[128,2688]{1,0:T(8,128)(2,1)S(1)}, u32[]{:S(2)}, u32[]{:S(2)}) collective-permute-start(bf16[128,2688]{1,0:T(8,128)(2,1)S(1)} %pad_maximum_fusion.1.refs_0_.refs_4_), channel_id=1, source_target_pairs={{0,48},{1,49},{2,50},{3,51},{4,52},{5,53},{6,54},{7,55},{8,56},{9,... | collective-permute-start | bytes 2064392 | tf_op jit(solution)/shard_map/ppermute | solution.py:54
  102.4 11.0 %collective-permute-start.24 = (bf16[128,2688]{1,0:T(8,128)(2,1)S(1)}, bf16[128,2688]{1,0:T(8,128)(2,1)S(1)}, u32[]{:S(2)}, u32[]{:S(2)}) collective-permute-start(bf16[128,2688]{1,0:T(8,128)(2,1)S(1)} %pad_maximum_fusion.2), channel_id=1, source_target_pairs={{0,64},{1,65},{2,66},{3,67},{4,68},{5,69},{6,70},{7,71},{8,72},{9,... | collective-permute-start | bytes 2064392 | tf_op jit(solution)/shard_map/ppermute | solution.py:54
  113.9 24.4 %collective-permute-start.26 = (bf16[128,2688]{1,0:T(8,128)(2,1)S(1)}, bf16[128,2688]{1,0:T(8,128)(2,1)S(1)}, u32[]{:S(2)}, u32[]{:S(2)}) collective-permute-start(bf16[128,2688]{1,0:T(8,128)(2,1)S(1)} %pad_maximum_fusion.3.refs_0_.refs_13_), channel_id=1, source_target_pairs={{0,16},{1,17},{2,18},{3,19},{4,20},{5,21},{6,22},{7,23},{8,24},{9,... | collective-permute-start | bytes 2064392 | tf_op jit(solution)/shard_map/ppermute | solution.py:54
  114.6 23.6 %collective-permute-start.25 = (bf16[128,2688]{1,0:T(8,128)(2,1)S(1)}, bf16[128,2688]{1,0:T(8,128)(2,1)S(1)}, u32[]{:S(2)}, u32[]{:S(2)}) collective-permute-start(bf16[128,2688]{1,0:T(8,128)(2,1)S(1)} %pad_maximum_fusion.3.refs_0_.refs_13_), channel_id=1, source_target_pairs={{0,48},{1,49},{2,50},{3,51},{4,52},{5,53},{6,54},{7,55},{8,56},{9,... | collective-permute-start | bytes 2064392 | tf_op jit(solution)/shard_map/ppermute | solution.py:54
  117.2 17.9 %collective-permute-start.22 = (bf16[64,2688]{1,0:T(8,128)(2,1)S(1)}, bf16[64,2688]{1,0:T(8,128)(2,1)S(1)}, u32[]{:S(2)}, u32[]{:S(2)}) collective-permute-start(bf16[64,2688]{1,0:T(8,128)(2,1)S(1)} %slice.203), channel_id=1, source_target_pairs={{0,16},{1,17},{2,18},{3,19},{4,20},{5,21},{6,22},{7,23},{8,24},{9,... | collective-permute-start | bytes 1032200 | tf_op jit(solution)/shard_map/ppermute | solution.py:54
  117.2 17.9 %collective-permute-start.23 = (bf16[64,2688]{1,0:T(8,128)(2,1)S(1)}, bf16[64,2688]{1,0:T(8,128)(2,1)S(1)}, u32[]{:S(2)}, u32[]{:S(2)}) collective-permute-start(bf16[64,2688]{1,0:T(8,128)(2,1)S(1)} %slice.204), channel_id=1, source_target_pairs={{0,48},{1,49},{2,50},{3,51},{4,52},{5,53},{6,54},{7,55},{8,56},{9,... | collective-permute-start | bytes 1032200 | tf_op jit(solution)/shard_map/ppermute | solution.py:54
  138.3 3.1 %collective-permute-start.27 = (bf16[256,2048]{1,0:T(8,128)(2,1)S(1)}, bf16[256,2048]{1,0:T(8,128)(2,1)S(1)}, u32[]{:S(2)}, u32[]{:S(2)}) collective-permute-start(bf16[256,2048]{1,0:T(8,128)(2,1)S(1)} %bitcast.11), channel_id=1, source_target_pairs={{0,1},{1,0},{2,3},{3,2},{4,5},{5,4},{6,7},{7,6},{8,9},{9,8},{10,11... | collective-permute-start | bytes 3145736 | tf_op jit(solution)/shard_map/ppermute | solution.py:54
  138.4 10.9 %collective-permute-start.32 = (bf16[64,2688]{1,0:T(8,128)(2,1)S(1)}, bf16[64,2688]{1,0:T(8,128)(2,1)S(1)}, u32[]{:S(2)}, u32[]{:S(2)}) collective-permute-start(bf16[64,2688]{1,0:T(8,128)(2,1)S(1)} %slice.209), channel_id=1, source_target_pairs={{0,48},{1,49},{2,50},{3,51},{4,52},{5,53},{6,54},{7,55},{8,56},{9,... | collective-permute-start | bytes 1032200 | tf_op jit(solution)/shard_map/ppermute | solution.py:54
  141.4 11.3 %collective-permute-start.31 = (bf16[64,2688]{1,0:T(8,128)(2,1)S(1)}, bf16[64,2688]{1,0:T(8,128)(2,1)S(1)}, u32[]{:S(2)}, u32[]{:S(2)}) collective-permute-start(bf16[64,2688]{1,0:T(8,128)(2,1)S(1)} %slice.208), channel_id=1, source_target_pairs={{0,16},{1,17},{2,18},{3,19},{4,20},{5,21},{6,22},{7,23},{8,24},{9,... | collective-permute-start | bytes 1032200 | tf_op jit(solution)/shard_map/ppermute | solution.py:54
  152.8 17.8 %collective-permute-start.30 = (bf16[64,2048]{1,0:T(8,128)(2,1)S(1)}, bf16[64,2048]{1,0:T(8,128)(2,1)S(1)}, u32[]{:S(2)}, u32[]{:S(2)}) collective-permute-start(bf16[64,2048]{1,0:T(8,128)(2,1)S(1)} %get-tuple-element.191), channel_id=1, source_target_pairs={{0,12},{1,13},{2,14},{3,15},{4,0},{5,1},{6,2},{7,3},{8,4},{9,5},{1... | collective-permute-start | bytes 786440 | tf_op jit(solution)/shard_map/ppermute | solution.py:54
  159.9 10.7 %collective-permute-start.29 = (bf16[64,2048]{1,0:T(8,128)(2,1)S(1)}, bf16[64,2048]{1,0:T(8,128)(2,1)S(1)}, u32[]{:S(2)}, u32[]{:S(2)}) collective-permute-start(bf16[64,2048]{1,0:T(8,128)(2,1)S(1)} %get-tuple-element.192), channel_id=1, source_target_pairs={{0,8},{1,9},{2,10},{3,11},{4,12},{5,13},{6,14},{7,15},{8,0},{9,1},... | collective-permute-start | bytes 786440 | tf_op jit(solution)/shard_map/ppermute | solution.py:54
  160.0 14.0 %collective-permute-start.28 = (bf16[64,2048]{1,0:T(8,128)(2,1)S(1)}, bf16[64,2048]{1,0:T(8,128)(2,1)S(1)}, u32[]{:S(2)}, u32[]{:S(2)}) collective-permute-start(bf16[64,2048]{1,0:T(8,128)(2,1)S(1)} %get-tuple-element.193), channel_id=1, source_target_pairs={{0,4},{1,5},{2,6},{3,7},{4,8},{5,9},{6,10},{7,11},{8,12},{9,13},{1... | collective-permute-start | bytes 786440 | tf_op jit(solution)/shard_map/ppermute | solution.py:54
  174.1 3.4 %collective-permute-start.34 = (bf16[256,2048]{1,0:T(8,128)(2,1)S(1)}, bf16[256,2048]{1,0:T(8,128)(2,1)S(1)}, u32[]{:S(2)}, u32[]{:S(2)}) collective-permute-start(bf16[256,2048]{1,0:T(8,128)(2,1)S(1)} %bitcast.10), channel_id=1, source_target_pairs={{0,1},{1,0},{2,3},{3,2},{4,5},{5,4},{6,7},{7,6},{8,9},{9,8},{10,11... | collective-permute-start | bytes 3145736 | tf_op jit(solution)/shard_map/ppermute | solution.py:54
  174.2 22.6 %collective-permute-start.33 = (bf16[32,2048]{1,0:T(8,128)(2,1)S(1)}, bf16[32,2048]{1,0:T(8,128)(2,1)S(1)}, u32[]{:S(2)}, u32[]{:S(2)}) collective-permute-start(bf16[32,2048]{1,0:T(8,128)(2,1)S(1)} %slice.241), channel_id=1, source_target_pairs={{0,2},{1,3},{2,0},{3,1},{4,6},{5,7},{6,4},{7,5},{8,10},{9,11},{10,... | collective-permute-start | bytes 393224 | tf_op jit(solution)/shard_map/ppermute | solution.py:54
  178.1 11.7 %collective-permute-start.37 = (bf16[64,2048]{1,0:T(8,128)(2,1)S(1)}, bf16[64,2048]{1,0:T(8,128)(2,1)S(1)}, u32[]{:S(2)}, u32[]{:S(2)}) collective-permute-start(bf16[64,2048]{1,0:T(8,128)(2,1)S(1)} %get-tuple-element.187), channel_id=1, source_target_pairs={{0,12},{1,13},{2,14},{3,15},{4,0},{5,1},{6,2},{7,3},{8,4},{9,5},{1... | collective-permute-start | bytes 786440 | tf_op jit(solution)/shard_map/ppermute | solution.py:54
  179.1 10.7 %collective-permute-start.36 = (bf16[64,2048]{1,0:T(8,128)(2,1)S(1)}, bf16[64,2048]{1,0:T(8,128)(2,1)S(1)}, u32[]{:S(2)}, u32[]{:S(2)}) collective-permute-start(bf16[64,2048]{1,0:T(8,128)(2,1)S(1)} %get-tuple-element.188), channel_id=1, source_target_pairs={{0,8},{1,9},{2,10},{3,11},{4,12},{5,13},{6,14},{7,15},{8,0},{9,1},... | collective-permute-start | bytes 786440 | tf_op jit(solution)/shard_map/ppermute | solution.py:54
  179.4 15.0 %collective-permute-start.35 = (bf16[64,2048]{1,0:T(8,128)(2,1)S(1)}, bf16[64,2048]{1,0:T(8,128)(2,1)S(1)}, u32[]{:S(2)}, u32[]{:S(2)}) collective-permute-start(bf16[64,2048]{1,0:T(8,128)(2,1)S(1)} %get-tuple-element.189), channel_id=1, source_target_pairs={{0,4},{1,5},{2,6},{3,7},{4,8},{5,9},{6,10},{7,11},{8,12},{9,13},{1... | collective-permute-start | bytes 786440 | tf_op jit(solution)/shard_map/ppermute | solution.py:54
  194.5 7.0 %collective-permute-start.38 = (bf16[32,2048]{1,0:T(8,128)(2,1)S(1)}, bf16[32,2048]{1,0:T(8,128)(2,1)S(1)}, u32[]{:S(2)}, u32[]{:S(2)}) collective-permute-start(bf16[32,2048]{1,0:T(8,128)(2,1)S(1)} %slice.247), channel_id=1, source_target_pairs={{0,2},{1,3},{2,0},{3,1},{4,6},{5,7},{6,4},{7,5},{8,10},{9,11},{10,... | collective-permute-start | bytes 393224 | tf_op jit(solution)/shard_map/ppermute | solution.py:54

commit v5 on v4

--- a/solution.py
+++ b/solution.py
@@ -12,9 +12,9 @@
 GATHERS = ((0,), (1,))
 ORDER = (
     "forward 0",
+    "relay 0",
     "core 1",
     "forward 1",
-    "relay 0",
     "swap 0",
     "relay 1",
     "spread 0",
@@ -22,9 +22,9 @@
     "far 0",
     "spread 1",
     "backward 0",
-    "far 1",
     "send 0",
     "chip 0",
+    "far 1",
     "backward 1",
     "last 0",
     "send 1",

time: 203 us -> 189 us (0.931)
  starting transfers between devices: 63.4 us -> 53.4 us
  waiting for transfers between devices: 103 us -> 99.3 us
    ppermute x39, starting transfers between devices: 63.4 us -> 53.4 us  [move(): return lax.ppermute(array, ('row', 'col'), pairs)]
    ppermute x39, waiting for transfers between devices: 103 us -> 99.3 us  [move(): return lax.ppermute(array, ('row', 'col'), pairs)]
  transfers between devices with their start and end apart: 39 -> 39, of which waited for: 23 -> 20; matrix products, arithmetic and copies ran while one was open for 2% -> 2% of each run, Pallas kernels for 13% -> 10%
where the time goes in v5:
time: 189 us
  waiting for transfers between devices  99.3 us (53%)
  starting transfers between devices  53.4 us (28%)
  Pallas kernels  25.6 us (14%)
  other arithmetic  6.22 us (3%)
  local copies, waits for them, and re-layouts  3.47 us (2%)
    ppermute x39, waiting for transfers between devices, move(): return lax.ppermute(array, ('row', 'col'), pairs)  99.3 us
    ppermute x39, starting transfers between devices, move(): return lax.ppermute(array, ('row', 'col'), pairs)  53.4 us
    pallas_call x1, Pallas kernels, weight_grads(): pl.pallas_call(functools.partial(weight_grad_kernel, offsets), in_specs=[...  9.6 us
    pallas_call x2, Pallas kernels, forward(): pl.pallas_call(functools.partial(forward_kernel, offset, rows), in_specs=...  6.85 us
    pallas_call x2, Pallas kernels, backward(): pl.pallas_call(backward_kernel, in_specs=[VMEM] * 6, out_specs=[VMEM] * 2...  6.34 us
  transfers between devices with their start and end apart: 39, of which 20 were waited for; matrix products, arithmetic and copies ran while one was open for 2% of the time, Pallas kernels for 10%

profile of v5, /device:TPU:0, one launch (start us, length us, event | category | flops | bytes accessed | tf_op | source)
XLA Modules:
  0.0 189.0 jit_solution(11656956303659737704)
XLA Ops:
  1.8 3.2 %collective-permute-start = (bf16[2,64,1024]{2,1,0:T(8,128)(2,1)S(1)}, bf16[2,64,1024]{2,1,0:T(8,128)(2,1)S(1)}, u32[]{:S(2)}, u32[]{:S(2)}) collective-permute-start(bf16[2,64,1024]{2,1,0:T(8,128)(2,1)S(1)} %pad_maximum_fusion.8), channel_id=1, source_target_pairs={{0,2},{1,3},{2,0},{3,1},{4,6},{5,7},{6,4},{7,5},{8,10},{9,11},{10,... | collective-permute-start | bytes 786440 | tf_op jit(solution)/shard_map/ppermute | solution.py:54
  6.0 5.3 %collective-permute-done = bf16[2,64,1024]{2,1,0:T(8,128)(2,1)S(1)} collective-permute-done((bf16[2,64,1024]{2,1,0:T(8,128)(2,1)S(1)}, bf16[2,64,1024]{2,1,0:T(8,128)(2,1)S(1)}, u32[]{:S(2)}, u32[]{:S(2)}) %collective-permute-start) | collective-permute-done | bytes 262176 | tf_op jit(solution)/shard_map/ppermute | solution.py:54
  11.3 1.9 collective-permute-start.3
  13.2 2.9 %collective-permute-start.2 = (bf16[2,64,1024]{2,1,0:T(8,128)(2,1)S(1)}, bf16[2,64,1024]{2,1,0:T(8,128)(2,1)S(1)}, u32[]{:S(2)}, u32[]{:S(2)}) collective-permute-start(bf16[2,64,1024]{2,1,0:T(8,128)(2,1)S(1)} %pad_maximum_fusion.9), channel_id=1, source_target_pairs={{0,8},{1,9},{2,10},{3,11},{4,12},{5,13},{6,14},{7,15},{8,0},{9,1},... | collective-permute-start | bytes 786440 | tf_op jit(solution)/shard_map/ppermute | solution.py:54
  16.1 1.3 collective-permute-start.1
  17.5 1.5 copy-done.1
  19.0 1.5 copy-done.2
  20.5 2.8 %mask_weights.1.refs_4_.refs_5_ = bf16[1024,2688]{1,0:T(8,128)(2,1)S(1)} custom-call(bf16[1024,896]{1,0:T(8,128)(2,1)S(1)} %copy-done, bf16[1024,896]{1,0:T(8,128)(2,1)S(1)} %copy-done.1, bf16[896,1024]{1,0:T(8,128)(2,1)S(1)} %copy-done.2, s32[8,7]{1,0:T(8,128)S(1)} %copy-done.3, s32[8,7]{1,0:T(8,128)S(1)} %copy-done.4, s32[7,8]{1,0:T(8,128)S(1)} %copy-done.5), custom_call_target="tpu_custom_call" | custom-call | flops 2752512 | bytes 11010048 | tf_op jit(solution)/shard_map/mask_weights/pallas_call | solution.py:118
  23.3 3.6 %collective-permute-done.2 = bf16[2,64,1024]{2,1,0:T(8,128)(2,1)S(1)} collective-permute-done((bf16[2,64,1024]{2,1,0:T(8,128)(2,1)S(1)}, bf16[2,64,1024]{2,1,0:T(8,128)(2,1)S(1)}, u32[]{:S(2)}, u32[]{:S(2)}) %collective-permute-start.2) | collective-permute-done | bytes 262176 | tf_op jit(solution)/shard_map/ppermute | solution.py:54
  27.8 1.2 collective-permute-done.4.refs_2_
  29.8 3.4 %forward.2 = (bf16[128,2688]{1,0:T(8,128)(2,1)S(1)}, bf16[128,2688]{1,0:T(8,128)(2,1)S(1)}, bf16[64,2688]{1,0:T(8,128)(2,1)S(1)}, bf16[64,2688]{1,0:T(8,128)(2,1)S(1)}, bf16[128,2688]{1,0:T(8,128)(2,1)S(1)}) custom-call(bf16[4,64,1024]{2,1,0:T(8,128)(2,1)S(1)} %pad_maximum_fusion.4.refs_0_, bf16[4,64,1024]{2,1,0:T(8,128)(2,1)S(1)} %pad_maximum_fusion.5.refs_1_, ...), custom_call_target="tpu_custom_call" | custom-call | flops 1024 | bytes 1024 | tf_op jit(solution)/shard_map/forward/pallas_call | solution.py:156
  33.2 4.1 %collective-permute-start.7 = (bf16[128,2688]{1,0:T(8,128)(2,1)S(1)}, bf16[128,2688]{1,0:T(8,128)(2,1)S(1)}, u32[]{:S(2)}, u32[]{:S(2)}) collective-permute-start(bf16[128,2688]{1,0:T(8,128)(2,1)S(1)} %get-tuple-element.103), channel_id=1, source_target_pairs={{0,48},{1,49},{2,50},{3,51},{4,52},{5,53},{6,54},{7,55},{8,56},{9,... | collective-permute-start | bytes 2064392 | tf_op jit(solution)/shard_map/ppermute | solution.py:54
  37.4 1.3 collective-permute-start.12
  38.7 2.4 %collective-permute-start.11 = (bf16[2,64,1024]{2,1,0:T(8,128)(2,1)S(1)}, bf16[2,64,1024]{2,1,0:T(8,128)(2,1)S(1)}, u32[]{:S(2)}, u32[]{:S(2)}) collective-permute-start(bf16[2,64,1024]{2,1,0:T(8,128)(2,1)S(1)} %pad_maximum_fusion.10), channel_id=1, source_target_pairs={{0,8},{1,9},{2,10},{3,11},{4,12},{5,13},{6,14},{7,15},{8,0},{9,1},... | collective-permute-start | bytes 786440 | tf_op jit(solution)/shard_map/ppermute | solution.py:54
  41.0 1.6 collective-permute-start.10
  42.6 9.7 %collective-permute-done.7 = bf16[128,2688]{1,0:T(8,128)(2,1)S(1)} collective-permute-done((bf16[128,2688]{1,0:T(8,128)(2,1)S(1)}, bf16[128,2688]{1,0:T(8,128)(2,1)S(1)}, u32[]{:S(2)}, u32[]{:S(2)}) %collective-permute-start.7) | collective-permute-done | bytes 688160 | tf_op jit(solution)/shard_map/ppermute | solution.py:54
  52.3 3.4 %collective-permute-done.6 = bf16[128,2688]{1,0:T(8,128)(2,1)S(1)} collective-permute-done((bf16[128,2688]{1,0:T(8,128)(2,1)S(1)}, bf16[128,2688]{1,0:T(8,128)(2,1)S(1)}, u32[]{:S(2)}, u32[]{:S(2)}) %collective-permute-start.6) | collective-permute-done | bytes 688160 | tf_op jit(solution)/shard_map/ppermute | solution.py:54
  57.1 1.7 collective-permute-start.8
  58.9 3.4 %forward.3 = (bf16[128,2688]{1,0:T(8,128)(2,1)S(1)}, bf16[128,2688]{1,0:T(8,128)(2,1)S(1)}, bf16[64,2688]{1,0:T(8,128)(2,1)S(1)}, bf16[64,2688]{1,0:T(8,128)(2,1)S(1)}, bf16[128,2688]{1,0:T(8,128)(2,1)S(1)}) custom-call(bf16[4,64,1024]{2,1,0:T(8,128)(2,1)S(1)} %pad_maximum_fusion.6.refs_0_.refs_9_, ...), custom_call_target="tpu_custom_call" | custom-call | flops 1024 | bytes 1024 | tf_op jit(solution)/shard_map/forward/pallas_call | solution.py:156
  62.4 4.5 %collective-permute-done.9 = bf16[64,2688]{1,0:T(8,128)(2,1)S(1)} collective-permute-done((bf16[64,2688]{1,0:T(8,128)(2,1)S(1)}, bf16[64,2688]{1,0:T(8,128)(2,1)S(1)}, u32[]{:S(2)}, u32[]{:S(2)}) %collective-permute-start.9) | collective-permute-done | bytes 344096 | tf_op jit(solution)/shard_map/ppermute | solution.py:54
  66.9 2.4 %collective-permute-done.8 = bf16[64,2688]{1,0:T(8,128)(2,1)S(1)} collective-permute-done((bf16[64,2688]{1,0:T(8,128)(2,1)S(1)}, bf16[64,2688]{1,0:T(8,128)(2,1)S(1)}, u32[]{:S(2)}, u32[]{:S(2)}) %collective-permute-start.8) | collective-permute-done | bytes 344096 | tf_op jit(solution)/shard_map/ppermute | solution.py:54
  69.6 1.6 collective-permute-start.15
  71.2 13.3 %collective-permute-done.17 = bf16[128,2688]{1,0:T(8,128)(2,1)S(1)} collective-permute-done((bf16[128,2688]{1,0:T(8,128)(2,1)S(1)}, bf16[128,2688]{1,0:T(8,128)(2,1)S(1)}, u32[]{:S(2)}, u32[]{:S(2)}) %collective-permute-start.17) | collective-permute-done | bytes 688160 | tf_op jit(solution)/shard_map/ppermute | solution.py:54
  84.6 1.9 %collective-permute-start.21 = (bf16[64,2688]{1,0:T(8,128)(2,1)S(1)}, bf16[64,2688]{1,0:T(8,128)(2,1)S(1)}, u32[]{:S(2)}, u32[]{:S(2)}) collective-permute-start(bf16[64,2688]{1,0:T(8,128)(2,1)S(1)} %slice_add_fusion), channel_id=1, source_target_pairs={{0,48},{1,49},{2,50},{3,51},{4,52},{5,53},{6,54},{7,55},{8,56},{9,... | collective-permute-start | bytes 1032200 | tf_op jit(solution)/shard_map/ppermute | solution.py:54
  87.9 2.9 %collective-permute-start.18 = (bf16[128,2688]{1,0:T(8,128)(2,1)S(1)}, bf16[128,2688]{1,0:T(8,128)(2,1)S(1)}, u32[]{:S(2)}, u32[]{:S(2)}) collective-permute-start(bf16[128,2688]{1,0:T(8,128)(2,1)S(1)} %pad_maximum_fusion.1.refs_0_.refs_4_), channel_id=1, source_target_pairs={{0,48},{1,49},{2,50},{3,51},{4,52},{5,53},{6,54},{7,55},{8,56},{9,... | collective-permute-start | bytes 2064392 | tf_op jit(solution)/shard_map/ppermute | solution.py:54
  90.7 5.1 %collective-permute-done.21 = bf16[64,2688]{1,0:T(8,128)(2,1)S(1)} collective-permute-done((bf16[64,2688]{1,0:T(8,128)(2,1)S(1)}, bf16[64,2688]{1,0:T(8,128)(2,1)S(1)}, u32[]{:S(2)}, u32[]{:S(2)}) %collective-permute-start.21) | collective-permute-done | bytes 344096 | tf_op jit(solution)/shard_map/ppermute | solution.py:54
  95.8 3.0 %collective-permute-done.20 = bf16[64,2688]{1,0:T(8,128)(2,1)S(1)} collective-permute-done((bf16[64,2688]{1,0:T(8,128)(2,1)S(1)}, bf16[64,2688]{1,0:T(8,128)(2,1)S(1)}, u32[]{:S(2)}, u32[]{:S(2)}) %collective-permute-start.20) | collective-permute-done | bytes 344096 | tf_op jit(solution)/shard_map/ppermute | solution.py:54
  99.2 1.6 collective-permute-start.24
  100.7 8.9 %collective-permute-done.19.refs_2_.refs_6_ = bf16[128,2688]{1,0:T(8,128)(2,1)S(1)} collective-permute-done((bf16[128,2688]{1,0:T(8,128)(2,1)S(1)}, bf16[128,2688]{1,0:T(8,128)(2,1)S(1)}, u32[]{:S(2)}, u32[]{:S(2)}) %collective-permute-start.19) | collective-permute-done | bytes 688160 | tf_op jit(solution)/shard_map/ppermute | solution.py:54
  109.8 3.2 %collective-permute-start.23 = (bf16[64,2688]{1,0:T(8,128)(2,1)S(1)}, bf16[64,2688]{1,0:T(8,128)(2,1)S(1)}, u32[]{:S(2)}, u32[]{:S(2)}) collective-permute-start(bf16[64,2688]{1,0:T(8,128)(2,1)S(1)} %slice.204), channel_id=1, source_target_pairs={{0,48},{1,49},{2,50},{3,51},{4,52},{5,53},{6,54},{7,55},{8,56},{9,... | collective-permute-start | bytes 1032200 | tf_op jit(solution)/shard_map/ppermute | solution.py:54
  113.6 4.7 %collective-permute-done.22.refs_3_.refs_7_ = bf16[64,2688]{1,0:T(8,128)(2,1)S(1)} collective-permute-done((bf16[64,2688]{1,0:T(8,128)(2,1)S(1)}, bf16[64,2688]{1,0:T(8,128)(2,1)S(1)}, u32[]{:S(2)}, u32[]{:S(2)}) %collective-permute-start.22) | collective-permute-done | bytes 344096 | tf_op jit(solution)/shard_map/ppermute | solution.py:54
  118.3 3.2 %backward.2 = (bf16[4,64,2048]{2,1,0:T(8,128)(2,1)S(1)}, bf16[4,64,2048]{2,1,0:T(8,128)(2,1)S(1)}) custom-call(bf16[128,2688]{1,0:T(8,128)(2,1)S(1)} %pad_maximum_fusion.1.refs_0_.refs_4_, bf16[128,2688]{1,0:T(8,128)(2,1)S(1)} %collective-permute-done.18.refs_1_.refs_5_, bf16[128,2688]{1,0:T(8,128)(2,1)S(1)} %collective-permute-done.19.refs_2_.refs_6_, ...), custom_call_target="tpu_custom_call" | custom-call | flops 2818572288 | bytes 22020096 | tf_op jit(solution)/shard_map/backward/pallas_call | solution.py:185
  121.6 3.3 %collective-permute-start.29 = (bf16[128,2688]{1,0:T(8,128)(2,1)S(1)}, bf16[128,2688]{1,0:T(8,128)(2,1)S(1)}, u32[]{:S(2)}, u32[]{:S(2)}) collective-permute-start(bf16[128,2688]{1,0:T(8,128)(2,1)S(1)} %pad_maximum_fusion.3.refs_0_.refs_13_), channel_id=1, source_target_pairs={{0,48},{1,49},{2,50},{3,51},{4,52},{5,53},{6,54},{7,55},{8,56},{9,... | collective-permute-start | bytes 2064392 | tf_op jit(solution)/shard_map/ppermute | solution.py:54
  125.4 15.5 %collective-permute-done.30.refs_2_.refs_15_ = bf16[128,2688]{1,0:T(8,128)(2,1)S(1)} collective-permute-done((bf16[128,2688]{1,0:T(8,128)(2,1)S(1)}, bf16[128,2688]{1,0:T(8,128)(2,1)S(1)}, u32[]{:S(2)}, u32[]{:S(2)}) %collective-permute-start.30) | collective-permute-done | bytes 688160 | tf_op jit(solution)/shard_map/ppermute | solution.py:54
  140.9 1.2 collective-permute-start.31
  142.2 2.1 %collective-permute-start.32 = (bf16[64,2688]{1,0:T(8,128)(2,1)S(1)}, bf16[64,2688]{1,0:T(8,128)(2,1)S(1)}, u32[]{:S(2)}, u32[]{:S(2)}) collective-permute-start(bf16[64,2688]{1,0:T(8,128)(2,1)S(1)} %slice.213), channel_id=1, source_target_pairs={{0,48},{1,49},{2,50},{3,51},{4,52},{5,53},{6,54},{7,55},{8,56},{9,... | collective-permute-start | bytes 1032200 | tf_op jit(solution)/shard_map/ppermute | solution.py:54
  144.3 2.4 %collective-permute-start.28 = (bf16[64,2048]{1,0:T(8,128)(2,1)S(1)}, bf16[64,2048]{1,0:T(8,128)(2,1)S(1)}, u32[]{:S(2)}, u32[]{:S(2)}) collective-permute-start(bf16[64,2048]{1,0:T(8,128)(2,1)S(1)} %get-tuple-element.189), channel_id=1, source_target_pairs={{0,12},{1,13},{2,14},{3,15},{4,0},{5,1},{6,2},{7,3},{8,4},{9,5},{1... | collective-permute-start | bytes 786440 | tf_op jit(solution)/shard_map/ppermute | solution.py:54
  146.7 1.1 collective-permute-start.27
  148.4 3.6 %collective-permute-done.31.refs_3_.refs_16_ = bf16[64,2688]{1,0:T(8,128)(2,1)S(1)} collective-permute-done((bf16[64,2688]{1,0:T(8,128)(2,1)S(1)}, bf16[64,2688]{1,0:T(8,128)(2,1)S(1)}, u32[]{:S(2)}, u32[]{:S(2)}) %collective-permute-start.31) | collective-permute-done | bytes 344096 | tf_op jit(solution)/shard_map/ppermute | solution.py:54
  152.0 3.2 %backward.3 = (bf16[4,64,2048]{2,1,0:T(8,128)(2,1)S(1)}, bf16[4,64,2048]{2,1,0:T(8,128)(2,1)S(1)}) custom-call(bf16[128,2688]{1,0:T(8,128)(2,1)S(1)} %pad_maximum_fusion.3.refs_0_.refs_13_, bf16[128,2688]{1,0:T(8,128)(2,1)S(1)} %collective-permute-done.29.refs_1_.refs_14_, bf16[128,2688]{1,0:T(8,128)(2,1)S(1)} %collective-permute-done.30.refs_2_.refs_15_, ...), custom_call_target="tpu_custom_call" | custom-call | flops 2818572288 | bytes 22020096 | tf_op jit(solution)/shard_map/backward/pallas_call | solution.py:185
  155.2 2.2 %collective-permute-done.28 = bf16[64,2048]{1,0:T(8,128)(2,1)S(1)} collective-permute-done((bf16[64,2048]{1,0:T(8,128)(2,1)S(1)}, bf16[64,2048]{1,0:T(8,128)(2,1)S(1)}, u32[]{:S(2)}, u32[]{:S(2)}) %collective-permute-start.28) | collective-permute-done | bytes 262176 | tf_op jit(solution)/shard_map/ppermute | solution.py:54
  157.5 3.5 %collective-permute-done.26 = bf16[64,2048]{1,0:T(8,128)(2,1)S(1)} collective-permute-done((bf16[64,2048]{1,0:T(8,128)(2,1)S(1)}, bf16[64,2048]{1,0:T(8,128)(2,1)S(1)}, u32[]{:S(2)}, u32[]{:S(2)}) %collective-permute-start.26) | collective-permute-done | bytes 262176 | tf_op jit(solution)/shard_map/ppermute | solution.py:54
  161.3 3.3 %collective-permute-start.33 = (bf16[32,2048]{1,0:T(8,128)(2,1)S(1)}, bf16[32,2048]{1,0:T(8,128)(2,1)S(1)}, u32[]{:S(2)}, u32[]{:S(2)}) collective-permute-start(bf16[32,2048]{1,0:T(8,128)(2,1)S(1)} %slice.241), channel_id=1, source_target_pairs={{0,2},{1,3},{2,0},{3,1},{4,6},{5,7},{6,4},{7,5},{8,10},{9,11},{10,... | collective-permute-start | bytes 393224 | tf_op jit(solution)/shard_map/ppermute | solution.py:54
  165.9 1.1 collective-permute-start.36
  167.8 9.6 %weight_grads.1 = (bf16[1024,896]{1,0:T(8,128)(2,1)}, bf16[1024,896]{1,0:T(8,128)(2,1)}, bf16[896,1024]{1,0:T(8,128)(2,1)}) custom-call(bf16[4,64,1024]{2,1,0:T(8,128)(2,1)S(1)} %pad_maximum_fusion.4.refs_0_, bf16[4,64,1024]{2,1,0:T(8,128)(2,1)S(1)} %pad_maximum_fusion.5.refs_1_, bf16[4,64,1024]{2,1,0:T(8,128)(2,1)S(1)} %collective-permute-done.4.refs_2_, ...), custom_call_target="tpu_custom_call" | custom-call | flops 5637144576 | bytes 44040192 | tf_op jit(solution)/shard_map/weight_grads/pallas_call | solution.py:243
  177.4 3.7 %collective-permute-done.35 = bf16[64,2048]{1,0:T(8,128)(2,1)S(1)} collective-permute-done((bf16[64,2048]{1,0:T(8,128)(2,1)S(1)}, bf16[64,2048]{1,0:T(8,128)(2,1)S(1)}, u32[]{:S(2)}, u32[]{:S(2)}) %collective-permute-start.35) | collective-permute-done | bytes 262176 | tf_op jit(solution)/shard_map/ppermute | solution.py:54
  181.3 2.3 %collective-permute-start.38 = (bf16[32,2048]{1,0:T(8,128)(2,1)S(1)}, bf16[32,2048]{1,0:T(8,128)(2,1)S(1)}, u32[]{:S(2)}, u32[]{:S(2)}) collective-permute-start(bf16[32,2048]{1,0:T(8,128)(2,1)S(1)} %slice.247), channel_id=1, source_target_pairs={{0,2},{1,3},{2,0},{3,1},{4,6},{5,7},{6,4},{7,5},{8,10},{9,11},{10,... | collective-permute-start | bytes 393224 | tf_op jit(solution)/shard_map/ppermute | solution.py:54
  183.7 4.6 %collective-permute-done.38 = bf16[32,2048]{1,0:T(8,128)(2,1)S(1)} collective-permute-done((bf16[32,2048]{1,0:T(8,128)(2,1)S(1)}, bf16[32,2048]{1,0:T(8,128)(2,1)S(1)}, u32[]{:S(2)}, u32[]{:S(2)}) %collective-permute-start.38) | collective-permute-done | bytes 131104 | tf_op jit(solution)/shard_map/ppermute | solution.py:54
  (92 shorter events, 12.5 us)
Async XLA Ops:
  0.6 16.8 %copy-start.5 = (s32[7,8]{1,0:T(8,128)S(1)}, s32[7,8]{1,0:T(8,128)}, u32[]{:S(2)}) copy-start(s32[7,8]{1,0:T(8,128)} %refs_20_.1) | copy-start | bytes 676
  0.6 16.8 %copy-start.4 = (s32[8,7]{1,0:T(8,128)S(1)}, s32[8,7]{1,0:T(8,128)}, u32[]{:S(2)}) copy-start(s32[8,7]{1,0:T(8,128)} %refs_19_.1) | copy-start | bytes 676
  0.7 16.8 %copy-start.3 = (s32[8,7]{1,0:T(8,128)S(1)}, s32[8,7]{1,0:T(8,128)}, u32[]{:S(2)}) copy-start(s32[8,7]{1,0:T(8,128)} %refs_18_.1) | copy-start | bytes 676
  0.7 16.8 %copy-start = (bf16[1024,896]{1,0:T(8,128)(2,1)S(1)}, bf16[1024,896]{1,0:T(8,128)(2,1)}, u32[]{:S(2)}) copy-start(bf16[1024,896]{1,0:T(8,128)(2,1)} %gate.1) | copy-start | bytes 5505028
  1.8 9.5 %collective-permute-start = (bf16[2,64,1024]{2,1,0:T(8,128)(2,1)S(1)}, bf16[2,64,1024]{2,1,0:T(8,128)(2,1)S(1)}, u32[]{:S(2)}, u32[]{:S(2)}) collective-permute-start(bf16[2,64,1024]{2,1,0:T(8,128)(2,1)S(1)} %pad_maximum_fusion.8), channel_id=1, source_target_pairs={{0,2},{1,3},{2,0},{3,1},{4,6},{5,7},{6,4},{7,5},{8,10},{9,11},{10,... | collective-permute-start | bytes 786440 | tf_op jit(solution)/shard_map/ppermute | solution.py:54
  11.3 11.9 %collective-permute-start.3 = (bf16[2,64,1024]{2,1,0:T(8,128)(2,1)S(1)}, bf16[2,64,1024]{2,1,0:T(8,128)(2,1)S(1)}, u32[]{:S(2)}, u32[]{:S(2)}) collective-permute-start(bf16[2,64,1024]{2,1,0:T(8,128)(2,1)S(1)} %pad_maximum_fusion.9), channel_id=1, source_target_pairs={{0,4},{1,5},{2,6},{3,7},{4,8},{5,9},{6,10},{7,11},{8,12},{9,13},{1... | collective-permute-start | bytes 786440 | tf_op jit(solution)/shard_map/ppermute | solution.py:54
  13.2 13.7 %collective-permute-start.2 = (bf16[2,64,1024]{2,1,0:T(8,128)(2,1)S(1)}, bf16[2,64,1024]{2,1,0:T(8,128)(2,1)S(1)}, u32[]{:S(2)}, u32[]{:S(2)}) collective-permute-start(bf16[2,64,1024]{2,1,0:T(8,128)(2,1)S(1)} %pad_maximum_fusion.9), channel_id=1, source_target_pairs={{0,8},{1,9},{2,10},{3,11},{4,12},{5,13},{6,14},{7,15},{8,0},{9,1},... | collective-permute-start | bytes 786440 | tf_op jit(solution)/shard_map/ppermute | solution.py:54
  16.1 10.8 %collective-permute-start.1 = (bf16[2,64,1024]{2,1,0:T(8,128)(2,1)S(1)}, bf16[2,64,1024]{2,1,0:T(8,128)(2,1)S(1)}, u32[]{:S(2)}, u32[]{:S(2)}) collective-permute-start(bf16[2,64,1024]{2,1,0:T(8,128)(2,1)S(1)} %pad_maximum_fusion.9), channel_id=1, source_target_pairs={{0,12},{1,13},{2,14},{3,15},{4,0},{5,1},{6,2},{7,3},{8,4},{9,5},{1... | collective-permute-start | bytes 786440 | tf_op jit(solution)/shard_map/ppermute | solution.py:54
  17.5 1.5 copy-start.1
  19.0 1.5 copy-start.2
  27.0 2.0 %collective-permute-start.4 = (bf16[4,64,1024]{2,1,0:T(8,128)(2,1)S(1)}, bf16[4,64,1024]{2,1,0:T(8,128)(2,1)S(1)}, u32[]{:S(2)}, u32[]{:S(2)}) collective-permute-start(bf16[4,64,1024]{2,1,0:T(8,128)(2,1)S(1)} %pad_maximum_fusion.4.refs_0_), channel_id=1, source_target_pairs={{0,1},{1,0},{2,3},{3,2},{4,5},{5,4},{6,7},{7,6},{8,9},{9,8},{10,11... | collective-permute-start | bytes 1572872 | tf_op jit(solution)/shard_map/ppermute | solution.py:54
  27.2 2.6 %collective-permute-start.5 = (bf16[4,64,1024]{2,1,0:T(8,128)(2,1)S(1)}, bf16[4,64,1024]{2,1,0:T(8,128)(2,1)S(1)}, u32[]{:S(2)}, u32[]{:S(2)}) collective-permute-start(bf16[4,64,1024]{2,1,0:T(8,128)(2,1)S(1)} %pad_maximum_fusion.5.refs_1_), channel_id=1, source_target_pairs={{0,1},{1,0},{2,3},{3,2},{4,5},{5,4},{6,7},{7,6},{8,9},{9,8},{10,11... | collective-permute-start | bytes 1572872 | tf_op jit(solution)/shard_map/ppermute | solution.py:54
  33.2 19.1 %collective-permute-start.7 = (bf16[128,2688]{1,0:T(8,128)(2,1)S(1)}, bf16[128,2688]{1,0:T(8,128)(2,1)S(1)}, u32[]{:S(2)}, u32[]{:S(2)}) collective-permute-start(bf16[128,2688]{1,0:T(8,128)(2,1)S(1)} %get-tuple-element.103), channel_id=1, source_target_pairs={{0,48},{1,49},{2,50},{3,51},{4,52},{5,53},{6,54},{7,55},{8,56},{9,... | collective-permute-start | bytes 2064392 | tf_op jit(solution)/shard_map/ppermute | solution.py:54
  37.3 18.4 %collective-permute-start.6 = (bf16[128,2688]{1,0:T(8,128)(2,1)S(1)}, bf16[128,2688]{1,0:T(8,128)(2,1)S(1)}, u32[]{:S(2)}, u32[]{:S(2)}) collective-permute-start(bf16[128,2688]{1,0:T(8,128)(2,1)S(1)} %get-tuple-element.102), channel_id=1, source_target_pairs={{0,16},{1,17},{2,18},{3,19},{4,20},{5,21},{6,22},{7,23},{8,24},{9,... | collective-permute-start | bytes 2064392 | tf_op jit(solution)/shard_map/ppermute | solution.py:54
  37.4 18.5 %collective-permute-start.12 = (bf16[2,64,1024]{2,1,0:T(8,128)(2,1)S(1)}, bf16[2,64,1024]{2,1,0:T(8,128)(2,1)S(1)}, u32[]{:S(2)}, u32[]{:S(2)}) collective-permute-start(bf16[2,64,1024]{2,1,0:T(8,128)(2,1)S(1)} %pad_maximum_fusion.10), channel_id=1, source_target_pairs={{0,4},{1,5},{2,6},{3,7},{4,8},{5,9},{6,10},{7,11},{8,12},{9,13},{1... | collective-permute-start | bytes 786440 | tf_op jit(solution)/shard_map/ppermute | solution.py:54
  38.7 17.2 %collective-permute-start.11 = (bf16[2,64,1024]{2,1,0:T(8,128)(2,1)S(1)}, bf16[2,64,1024]{2,1,0:T(8,128)(2,1)S(1)}, u32[]{:S(2)}, u32[]{:S(2)}) collective-permute-start(bf16[2,64,1024]{2,1,0:T(8,128)(2,1)S(1)} %pad_maximum_fusion.10), channel_id=1, source_target_pairs={{0,8},{1,9},{2,10},{3,11},{4,12},{5,13},{6,14},{7,15},{8,0},{9,1},... | collective-permute-start | bytes 786440 | tf_op jit(solution)/shard_map/ppermute | solution.py:54
  41.0 14.8 %collective-permute-start.10 = (bf16[2,64,1024]{2,1,0:T(8,128)(2,1)S(1)}, bf16[2,64,1024]{2,1,0:T(8,128)(2,1)S(1)}, u32[]{:S(2)}, u32[]{:S(2)}) collective-permute-start(bf16[2,64,1024]{2,1,0:T(8,128)(2,1)S(1)} %pad_maximum_fusion.10), channel_id=1, source_target_pairs={{0,12},{1,13},{2,14},{3,15},{4,0},{5,1},{6,2},{7,3},{8,4},{9,5},{1... | collective-permute-start | bytes 786440 | tf_op jit(solution)/shard_map/ppermute | solution.py:54
  56.1 2.8 %collective-permute-start.13 = (bf16[4,64,1024]{2,1,0:T(8,128)(2,1)S(1)}, bf16[4,64,1024]{2,1,0:T(8,128)(2,1)S(1)}, u32[]{:S(2)}, u32[]{:S(2)}) collective-permute-start(bf16[4,64,1024]{2,1,0:T(8,128)(2,1)S(1)} %pad_maximum_fusion.6.refs_0_.refs_9_), channel_id=1, source_target_pairs={{0,1},{1,0},{2,3},{3,2},{4,5},{5,4},{6,7},{7,6},{8,9},{9,8},{10,11... | collective-permute-start | bytes 1572872 | tf_op jit(solution)/shard_map/ppermute | solution.py:54
  56.2 2.6 %collective-permute-start.14 = (bf16[4,64,1024]{2,1,0:T(8,128)(2,1)S(1)}, bf16[4,64,1024]{2,1,0:T(8,128)(2,1)S(1)}, u32[]{:S(2)}, u32[]{:S(2)}) collective-permute-start(bf16[4,64,1024]{2,1,0:T(8,128)(2,1)S(1)} %pad_maximum_fusion.7.refs_1_.refs_10_), channel_id=1, source_target_pairs={{0,1},{1,0},{2,3},{3,2},{4,5},{5,4},{6,7},{7,6},{8,9},{9,8},{10,11... | collective-permute-start | bytes 1572872 | tf_op jit(solution)/shard_map/ppermute | solution.py:54
  56.8 10.0 %collective-permute-start.9 = (bf16[64,2688]{1,0:T(8,128)(2,1)S(1)}, bf16[64,2688]{1,0:T(8,128)(2,1)S(1)}, u32[]{:S(2)}, u32[]{:S(2)}) collective-permute-start(bf16[64,2688]{1,0:T(8,128)(2,1)S(1)} %slice_add_fusion.2), channel_id=1, source_target_pairs={{0,48},{1,49},{2,50},{3,51},{4,52},{5,53},{6,54},{7,55},{8,56},{9,... | collective-permute-start | bytes 1032200 | tf_op jit(solution)/shard_map/ppermute | solution.py:54
  57.1 12.2 %collective-permute-start.8 = (bf16[64,2688]{1,0:T(8,128)(2,1)S(1)}, bf16[64,2688]{1,0:T(8,128)(2,1)S(1)}, u32[]{:S(2)}, u32[]{:S(2)}) collective-permute-start(bf16[64,2688]{1,0:T(8,128)(2,1)S(1)} %slice_add_fusion.3), channel_id=1, source_target_pairs={{0,16},{1,17},{2,18},{3,19},{4,20},{5,21},{6,22},{7,23},{8,24},{9,... | collective-permute-start | bytes 1032200 | tf_op jit(solution)/shard_map/ppermute | solution.py:54
  62.3 22.2 %collective-permute-start.16 = (bf16[128,2688]{1,0:T(8,128)(2,1)S(1)}, bf16[128,2688]{1,0:T(8,128)(2,1)S(1)}, u32[]{:S(2)}, u32[]{:S(2)}) collective-permute-start(bf16[128,2688]{1,0:T(8,128)(2,1)S(1)} %get-tuple-element.116), channel_id=1, source_target_pairs={{0,16},{1,17},{2,18},{3,19},{4,20},{5,21},{6,22},{7,23},{8,24},{9,... | collective-permute-start | bytes 2064392 | tf_op jit(solution)/shard_map/ppermute | solution.py:54
  69.3 15.3 %collective-permute-start.17 = (bf16[128,2688]{1,0:T(8,128)(2,1)S(1)}, bf16[128,2688]{1,0:T(8,128)(2,1)S(1)}, u32[]{:S(2)}, u32[]{:S(2)}) collective-permute-start(bf16[128,2688]{1,0:T(8,128)(2,1)S(1)} %get-tuple-element.120), channel_id=1, source_target_pairs={{0,48},{1,49},{2,50},{3,51},{4,52},{5,53},{6,54},{7,55},{8,56},{9,... | collective-permute-start | bytes 2064392 | tf_op jit(solution)/shard_map/ppermute | solution.py:54
  69.6 17.4 %collective-permute-start.15 = (bf16[128,2688]{1,0:T(8,128)(2,1)S(1)}, bf16[128,2688]{1,0:T(8,128)(2,1)S(1)}, u32[]{:S(2)}, u32[]{:S(2)}) collective-permute-start(bf16[128,2688]{1,0:T(8,128)(2,1)S(1)} %pad_maximum_fusion), channel_id=1, source_target_pairs={{0,64},{1,65},{2,66},{3,67},{4,68},{5,69},{6,70},{7,71},{8,72},{9,... | collective-permute-start | bytes 2064392 | tf_op jit(solution)/shard_map/ppermute | solution.py:54
  84.6 11.2 %collective-permute-start.21 = (bf16[64,2688]{1,0:T(8,128)(2,1)S(1)}, bf16[64,2688]{1,0:T(8,128)(2,1)S(1)}, u32[]{:S(2)}, u32[]{:S(2)}) collective-permute-start(bf16[64,2688]{1,0:T(8,128)(2,1)S(1)} %slice_add_fusion), channel_id=1, source_target_pairs={{0,48},{1,49},{2,50},{3,51},{4,52},{5,53},{6,54},{7,55},{8,56},{9,... | collective-permute-start | bytes 1032200 | tf_op jit(solution)/shard_map/ppermute | solution.py:54
  86.5 12.3 %collective-permute-start.20 = (bf16[64,2688]{1,0:T(8,128)(2,1)S(1)}, bf16[64,2688]{1,0:T(8,128)(2,1)S(1)}, u32[]{:S(2)}, u32[]{:S(2)}) collective-permute-start(bf16[64,2688]{1,0:T(8,128)(2,1)S(1)} %slice_add_fusion.1), channel_id=1, source_target_pairs={{0,16},{1,17},{2,18},{3,19},{4,20},{5,21},{6,22},{7,23},{8,24},{9,... | collective-permute-start | bytes 1032200 | tf_op jit(solution)/shard_map/ppermute | solution.py:54
  87.4 22.2 %collective-permute-start.19 = (bf16[128,2688]{1,0:T(8,128)(2,1)S(1)}, bf16[128,2688]{1,0:T(8,128)(2,1)S(1)}, u32[]{:S(2)}, u32[]{:S(2)}) collective-permute-start(bf16[128,2688]{1,0:T(8,128)(2,1)S(1)} %pad_maximum_fusion.1.refs_0_.refs_4_), channel_id=1, source_target_pairs={{0,16},{1,17},{2,18},{3,19},{4,20},{5,21},{6,22},{7,23},{8,24},{9,... | collective-permute-start | bytes 2064392 | tf_op jit(solution)/shard_map/ppermute | solution.py:54
  87.9 21.8 %collective-permute-start.18 = (bf16[128,2688]{1,0:T(8,128)(2,1)S(1)}, bf16[128,2688]{1,0:T(8,128)(2,1)S(1)}, u32[]{:S(2)}, u32[]{:S(2)}) collective-permute-start(bf16[128,2688]{1,0:T(8,128)(2,1)S(1)} %pad_maximum_fusion.1.refs_0_.refs_4_), channel_id=1, source_target_pairs={{0,48},{1,49},{2,50},{3,51},{4,52},{5,53},{6,54},{7,55},{8,56},{9,... | collective-permute-start | bytes 2064392 | tf_op jit(solution)/shard_map/ppermute | solution.py:54
  99.2 13.9 %collective-permute-start.24 = (bf16[128,2688]{1,0:T(8,128)(2,1)S(1)}, bf16[128,2688]{1,0:T(8,128)(2,1)S(1)}, u32[]{:S(2)}, u32[]{:S(2)}) collective-permute-start(bf16[128,2688]{1,0:T(8,128)(2,1)S(1)} %pad_maximum_fusion.2), channel_id=1, source_target_pairs={{0,64},{1,65},{2,66},{3,67},{4,68},{5,69},{6,70},{7,71},{8,72},{9,... | collective-permute-start | bytes 2064392 | tf_op jit(solution)/shard_map/ppermute | solution.py:54
  109.7 8.5 %collective-permute-start.22 = (bf16[64,2688]{1,0:T(8,128)(2,1)S(1)}, bf16[64,2688]{1,0:T(8,128)(2,1)S(1)}, u32[]{:S(2)}, u32[]{:S(2)}) collective-permute-start(bf16[64,2688]{1,0:T(8,128)(2,1)S(1)} %slice.203), channel_id=1, source_target_pairs={{0,16},{1,17},{2,18},{3,19},{4,20},{5,21},{6,22},{7,23},{8,24},{9,... | collective-permute-start | bytes 1032200 | tf_op jit(solution)/shard_map/ppermute | solution.py:54
  109.8 8.4 %collective-permute-start.23 = (bf16[64,2688]{1,0:T(8,128)(2,1)S(1)}, bf16[64,2688]{1,0:T(8,128)(2,1)S(1)}, u32[]{:S(2)}, u32[]{:S(2)}) collective-permute-start(bf16[64,2688]{1,0:T(8,128)(2,1)S(1)} %slice.204), channel_id=1, source_target_pairs={{0,48},{1,49},{2,50},{3,51},{4,52},{5,53},{6,54},{7,55},{8,56},{9,... | collective-permute-start | bytes 1032200 | tf_op jit(solution)/shard_map/ppermute | solution.py:54
  121.4 3.5 %collective-permute-start.25 = (bf16[256,2048]{1,0:T(8,128)(2,1)S(1)}, bf16[256,2048]{1,0:T(8,128)(2,1)S(1)}, u32[]{:S(2)}, u32[]{:S(2)}) collective-permute-start(bf16[256,2048]{1,0:T(8,128)(2,1)S(1)} %bitcast.11), channel_id=1, source_target_pairs={{0,1},{1,0},{2,3},{3,2},{4,5},{5,4},{6,7},{7,6},{8,9},{9,8},{10,11... | collective-permute-start | bytes 3145736 | tf_op jit(solution)/shard_map/ppermute | solution.py:54
  121.5 19.3 %collective-permute-start.30 = (bf16[128,2688]{1,0:T(8,128)(2,1)S(1)}, bf16[128,2688]{1,0:T(8,128)(2,1)S(1)}, u32[]{:S(2)}, u32[]{:S(2)}) collective-permute-start(bf16[128,2688]{1,0:T(8,128)(2,1)S(1)} %pad_maximum_fusion.3.refs_0_.refs_13_), channel_id=1, source_target_pairs={{0,16},{1,17},{2,18},{3,19},{4,20},{5,21},{6,22},{7,23},{8,24},{9,... | collective-permute-start | bytes 2064392 | tf_op jit(solution)/shard_map/ppermute | solution.py:54
  121.6 19.3 %collective-permute-start.29 = (bf16[128,2688]{1,0:T(8,128)(2,1)S(1)}, bf16[128,2688]{1,0:T(8,128)(2,1)S(1)}, u32[]{:S(2)}, u32[]{:S(2)}) collective-permute-start(bf16[128,2688]{1,0:T(8,128)(2,1)S(1)} %pad_maximum_fusion.3.refs_0_.refs_13_), channel_id=1, source_target_pairs={{0,48},{1,49},{2,50},{3,51},{4,52},{5,53},{6,54},{7,55},{8,56},{9,... | collective-permute-start | bytes 2064392 | tf_op jit(solution)/shard_map/ppermute | solution.py:54
  140.9 11.1 %collective-permute-start.31 = (bf16[64,2688]{1,0:T(8,128)(2,1)S(1)}, bf16[64,2688]{1,0:T(8,128)(2,1)S(1)}, u32[]{:S(2)}, u32[]{:S(2)}) collective-permute-start(bf16[64,2688]{1,0:T(8,128)(2,1)S(1)} %slice.212), channel_id=1, source_target_pairs={{0,16},{1,17},{2,18},{3,19},{4,20},{5,21},{6,22},{7,23},{8,24},{9,... | collective-permute-start | bytes 1032200 | tf_op jit(solution)/shard_map/ppermute | solution.py:54
  142.2 9.9 %collective-permute-start.32 = (bf16[64,2688]{1,0:T(8,128)(2,1)S(1)}, bf16[64,2688]{1,0:T(8,128)(2,1)S(1)}, u32[]{:S(2)}, u32[]{:S(2)}) collective-permute-start(bf16[64,2688]{1,0:T(8,128)(2,1)S(1)} %slice.213), channel_id=1, source_target_pairs={{0,48},{1,49},{2,50},{3,51},{4,52},{5,53},{6,54},{7,55},{8,56},{9,... | collective-permute-start | bytes 1032200 | tf_op jit(solution)/shard_map/ppermute | solution.py:54
  144.3 13.1 %collective-permute-start.28 = (bf16[64,2048]{1,0:T(8,128)(2,1)S(1)}, bf16[64,2048]{1,0:T(8,128)(2,1)S(1)}, u32[]{:S(2)}, u32[]{:S(2)}) collective-permute-start(bf16[64,2048]{1,0:T(8,128)(2,1)S(1)} %get-tuple-element.189), channel_id=1, source_target_pairs={{0,12},{1,13},{2,14},{3,15},{4,0},{5,1},{6,2},{7,3},{8,4},{9,5},{1... | collective-permute-start | bytes 786440 | tf_op jit(solution)/shard_map/ppermute | solution.py:54
  146.7 10.8 %collective-permute-start.27 = (bf16[64,2048]{1,0:T(8,128)(2,1)S(1)}, bf16[64,2048]{1,0:T(8,128)(2,1)S(1)}, u32[]{:S(2)}, u32[]{:S(2)}) collective-permute-start(bf16[64,2048]{1,0:T(8,128)(2,1)S(1)} %get-tuple-element.190), channel_id=1, source_target_pairs={{0,8},{1,9},{2,10},{3,11},{4,12},{5,13},{6,14},{7,15},{8,0},{9,1},... | collective-permute-start | bytes 786440 | tf_op jit(solution)/shard_map/ppermute | solution.py:54
  147.9 13.2 %collective-permute-start.26 = (bf16[64,2048]{1,0:T(8,128)(2,1)S(1)}, bf16[64,2048]{1,0:T(8,128)(2,1)S(1)}, u32[]{:S(2)}, u32[]{:S(2)}) collective-permute-start(bf16[64,2048]{1,0:T(8,128)(2,1)S(1)} %get-tuple-element.191), channel_id=1, source_target_pairs={{0,4},{1,5},{2,6},{3,7},{4,8},{5,9},{6,10},{7,11},{8,12},{9,13},{1... | collective-permute-start | bytes 786440 | tf_op jit(solution)/shard_map/ppermute | solution.py:54
  161.2 3.4 %collective-permute-start.34 = (bf16[256,2048]{1,0:T(8,128)(2,1)S(1)}, bf16[256,2048]{1,0:T(8,128)(2,1)S(1)}, u32[]{:S(2)}, u32[]{:S(2)}) collective-permute-start(bf16[256,2048]{1,0:T(8,128)(2,1)S(1)} %bitcast.10), channel_id=1, source_target_pairs={{0,1},{1,0},{2,3},{3,2},{4,5},{5,4},{6,7},{7,6},{8,9},{9,8},{10,11... | collective-permute-start | bytes 3145736 | tf_op jit(solution)/shard_map/ppermute | solution.py:54
  161.3 22.3 %collective-permute-start.33 = (bf16[32,2048]{1,0:T(8,128)(2,1)S(1)}, bf16[32,2048]{1,0:T(8,128)(2,1)S(1)}, u32[]{:S(2)}, u32[]{:S(2)}) collective-permute-start(bf16[32,2048]{1,0:T(8,128)(2,1)S(1)} %slice.241), channel_id=1, source_target_pairs={{0,2},{1,3},{2,0},{3,1},{4,6},{5,7},{6,4},{7,5},{8,10},{9,11},{10,... | collective-permute-start | bytes 393224 | tf_op jit(solution)/shard_map/ppermute | solution.py:54
  165.2 12.2 %collective-permute-start.37 = (bf16[64,2048]{1,0:T(8,128)(2,1)S(1)}, bf16[64,2048]{1,0:T(8,128)(2,1)S(1)}, u32[]{:S(2)}, u32[]{:S(2)}) collective-permute-start(bf16[64,2048]{1,0:T(8,128)(2,1)S(1)} %get-tuple-element.185), channel_id=1, source_target_pairs={{0,12},{1,13},{2,14},{3,15},{4,0},{5,1},{6,2},{7,3},{8,4},{9,5},{1... | collective-permute-start | bytes 786440 | tf_op jit(solution)/shard_map/ppermute | solution.py:54
  165.9 11.6 %collective-permute-start.36 = (bf16[64,2048]{1,0:T(8,128)(2,1)S(1)}, bf16[64,2048]{1,0:T(8,128)(2,1)S(1)}, u32[]{:S(2)}, u32[]{:S(2)}) collective-permute-start(bf16[64,2048]{1,0:T(8,128)(2,1)S(1)} %get-tuple-element.186), channel_id=1, source_target_pairs={{0,8},{1,9},{2,10},{3,11},{4,12},{5,13},{6,14},{7,15},{8,0},{9,1},... | collective-permute-start | bytes 786440 | tf_op jit(solution)/shard_map/ppermute | solution.py:54
  167.0 14.1 %collective-permute-start.35 = (bf16[64,2048]{1,0:T(8,128)(2,1)S(1)}, bf16[64,2048]{1,0:T(8,128)(2,1)S(1)}, u32[]{:S(2)}, u32[]{:S(2)}) collective-permute-start(bf16[64,2048]{1,0:T(8,128)(2,1)S(1)} %get-tuple-element.187), channel_id=1, source_target_pairs={{0,4},{1,5},{2,6},{3,7},{4,8},{5,9},{6,10},{7,11},{8,12},{9,13},{1... | collective-permute-start | bytes 786440 | tf_op jit(solution)/shard_map/ppermute | solution.py:54
  181.3 7.0 %collective-permute-start.38 = (bf16[32,2048]{1,0:T(8,128)(2,1)S(1)}, bf16[32,2048]{1,0:T(8,128)(2,1)S(1)}, u32[]{:S(2)}, u32[]{:S(2)}) collective-permute-start(bf16[32,2048]{1,0:T(8,128)(2,1)S(1)} %slice.247), channel_id=1, source_target_pairs={{0,2},{1,3},{2,0},{3,1},{4,6},{5,7},{6,4},{7,5},{8,10},{9,11},{10,... | collective-permute-start | bytes 393224 | tf_op jit(solution)/shard_map/ppermute | solution.py:54

commit v6 on v5

--- a/solution.py
+++ b/solution.py
@@ -23,8 +23,8 @@
     "spread 1",
     "backward 0",
     "send 0",
+    "far 1",
     "chip 0",
-    "far 1",
     "backward 1",
     "last 0",
     "send 1",
@@ -167,16 +167,15 @@
 
 
 def backward_kernel(*refs):
-    arrays, weights, for_other, for_own = refs[:5], *refs[5:]
-    depth, total = weights.shape
+    arrays, weights, outs = refs[:5], refs[5], refs[6:]
+    total = weights.shape[1]
     width = total // 3
-    rows = for_own.shape[1]
-    for columns, to in ((slice(2 * width, total), 0), (slice(0, 2 * width), depth)):
+    rows = arrays[3].shape[0]
+    for which, columns in enumerate((slice(2 * width, total), slice(0, 2 * width))):
         left = jnp.concatenate(values_of(arrays, columns))
         part = nt(left, weights[:, columns]).astype(jnp.bfloat16)
         for at, (dz, half) in enumerate(GATHERED):
-            out = (for_own, for_other)[half]
-            out[owner(dz), :, to : to + depth] = part[at * rows : (at + 1) * rows]
+            outs[2 * half + which][owner(dz)] = part[at * rows : (at + 1) * rows]
 
 
 def backward(arrays, weights):
@@ -185,15 +184,16 @@
     outs = pl.pallas_call(
         backward_kernel,
         in_specs=[VMEM] * 6,
-        out_specs=[VMEM] * 2,
-        out_shape=[jax.ShapeDtypeStruct((4, rows, 2 * depth), jnp.bfloat16)] * 2,
+        out_specs=[VMEM] * 4,
+        out_shape=[jax.ShapeDtypeStruct((4, rows, depth), jnp.bfloat16)] * 4,
         compiler_params=params(),
         cost_estimate=pl.CostEstimate(
             flops=16 * rows * depth * total, bytes_accessed=8 * depth * total, transcendentals=0
         ),
         name="backward",
     )(*arrays, weights)
-    return [out.reshape(4 * rows, 2 * depth) for out in outs]
+    outs = [out.reshape(4 * rows, depth) for out in outs]
+    return outs[2:], outs[:2]
 
 
 def weight_grad_kernel(offsets, *refs):
@@ -352,12 +352,14 @@
 
     def send(self, *others):
         for_other = after(self.for_other, *others)
-        self.received = move(for_other, dcore=1)
+        self.received = [move(part, dcore=1) for part in for_other]
         return for_other
 
     def chip(self, *others):
         received = after(self.received, *others)
-        chip = (wide(self.for_own) + wide(received)).astype(jnp.bfloat16)
+        chip = jnp.concatenate(
+            [wide(mine) + wide(theirs) for mine, theirs in zip(self.for_own, received)], axis=1
+        ).astype(jnp.bfloat16)
         rows = self.rows
         self.parts = [chip[:rows]] + [
             move(chip[dy * rows : (dy + 1) * rows], dy=dy) for dy in range(1, 4)
@@ -374,21 +376,21 @@
 def shards(tokens, out_grad, gate_weight, up_weight, down_weight, gate_mask, up_mask, down_mask):
     depth = tokens.shape[1]
     starts = [sum(CHUNKS[:i]) for i in range(len(CHUNKS))]
-    part = jnp.stack([tokens, out_grad])
-    received = move(part, dxh=1)
     weights = mask_weights(gate_weight, up_weight, down_weight, gate_mask, up_mask, down_mask)
     gathers, chunks = [], []
     for group in GATHERS:
-        slices = [slice(starts[i], starts[i] + CHUNKS[i]) for i in group]
+        first, last = starts[group[0]], starts[group[-1]] + CHUNKS[group[-1]]
+        part = jnp.stack([tokens[first:last], out_grad[first:last]])
+        received = move(part, dxh=1)
+        slices = [slice(starts[i] - first, starts[i] - first + CHUNKS[i]) for i in group]
         gather = Gather(
             jnp.concatenate([half[:, at] for at in slices for half in (part, received)], axis=1)
         )
         gathers.append(gather)
         for i in group:
-            offset = 2 * (starts[i] - starts[group[0]])
-            chunks.append(Chunk(gather, offset, CHUNKS[i], weights))
+            chunks.append(Chunk(gather, 2 * (starts[i] - first), CHUNKS[i], weights))
     gathers[0].far()
-    before = gathers[0].core(weights)
+    before = gathers[0].core(weights, *[gather.pair for gather in gathers[1:]])
     gathers[1].far(before)
     for step in ORDER:
         name, _, which = step.partition(" ")

time: 189 us -> 174 us (0.921)
  waiting for transfers between devices: 99.3 us -> 84 us
  local copies, waits for them, and re-layouts: 3.47 us -> 5.75 us
  other arithmetic: 6.22 us -> 4.31 us
    ppermute x39 -> x42, waiting for transfers between devices: 99.3 us -> 84 us  [move(): return lax.ppermute(array, ('row', 'col'), pairs)]
    ppermute x39 -> x42, starting transfers between devices: 53.4 us -> 53.5 us  [move(): return lax.ppermute(array, ('row', 'col'), pairs)]
  transfers between devices with their start and end apart: 39 -> 42, of which waited for: 20 -> 21; matrix products, arithmetic and copies ran while one was open for 2% -> 2% of each run, Pallas kernels for 10% -> 13%
where the time goes in v6:
time: 174 us
  waiting for transfers between devices  84 us (48%)
  starting transfers between devices  53.5 us (31%)
  Pallas kernels  25.6 us (15%)
  local copies, waits for them, and re-layouts  5.75 us (3%)
  other arithmetic  4.31 us (2%)
    ppermute x42, waiting for transfers between devices, move(): return lax.ppermute(array, ('row', 'col'), pairs)  84 us
    ppermute x42, starting transfers between devices, move(): return lax.ppermute(array, ('row', 'col'), pairs)  53.5 us
    pallas_call x1, Pallas kernels, weight_grads(): pl.pallas_call(functools.partial(weight_grad_kernel, offsets), in_specs=[...  9.61 us
    pallas_call x2, Pallas kernels, forward(): pl.pallas_call(functools.partial(forward_kernel, offset, rows), in_specs=...  6.86 us
    pallas_call x2, Pallas kernels, backward(): pl.pallas_call(backward_kernel, in_specs=[VMEM] * 6, out_specs=[VMEM] * 4...  6.34 us
    unnamed x12, local copies, waits for them, and re-layouts  4.51 us
  transfers between devices with their start and end apart: 42, of which 21 were waited for; matrix products, arithmetic and copies ran while one was open for 2% of the time, Pallas kernels for 13%

profile of v6, /device:TPU:0, one launch (start us, length us, event | category | flops | bytes accessed | tf_op | source)
XLA Modules:
  0.0 174.2 jit_solution(1521418698578865135)
XLA Ops:
  0.7 1.0 slice_bitcast_fusion
  1.7 3.2 %collective-permute-start = (bf16[2,32,1024]{2,1,0:T(8,128)(2,1)S(1)}, bf16[2,32,1024]{2,1,0:T(8,128)(2,1)S(1)}, u32[]{:S(2)}, u32[]{:S(2)}) collective-permute-start(bf16[2,32,1024]{2,1,0:T(8,128)(2,1)S(1)} %pad_maximum_fusion.13), channel_id=1, source_target_pairs={{0,2},{1,3},{2,0},{3,1},{4,6},{5,7},{6,4},{7,5},{8,10},{9,11},{10,... | collective-permute-start | bytes 393224 | tf_op jit(solution)/shard_map/ppermute | solution.py:54
  4.8 3.5 %collective-permute-done = bf16[2,32,1024]{2,1,0:T(8,128)(2,1)S(1)} collective-permute-done((bf16[2,32,1024]{2,1,0:T(8,128)(2,1)S(1)}, bf16[2,32,1024]{2,1,0:T(8,128)(2,1)S(1)}, u32[]{:S(2)}, u32[]{:S(2)}) %collective-permute-start) | collective-permute-done | bytes 131104 | tf_op jit(solution)/shard_map/ppermute | solution.py:54
  8.4 3.3 %collective-permute-start.1 = (bf16[2,64,1024]{2,1,0:T(8,128)(2,1)S(1)}, bf16[2,64,1024]{2,1,0:T(8,128)(2,1)S(1)}, u32[]{:S(2)}, u32[]{:S(2)}) collective-permute-start(bf16[2,64,1024]{2,1,0:T(8,128)(2,1)S(1)} %pad_maximum_fusion.10), channel_id=1, source_target_pairs={{0,12},{1,13},{2,14},{3,15},{4,0},{5,1},{6,2},{7,3},{8,4},{9,5},{1... | collective-permute-start | bytes 786440 | tf_op jit(solution)/shard_map/ppermute | solution.py:54
  12.3 1.0 collective-permute-start.3
  13.3 3.1 %collective-permute-start.4 = (bf16[2,32,1024]{2,1,0:T(8,128)(2,1)S(1)}, bf16[2,32,1024]{2,1,0:T(8,128)(2,1)S(1)}, u32[]{:S(2)}, u32[]{:S(2)}) collective-permute-start(bf16[2,32,1024]{2,1,0:T(8,128)(2,1)S(1)} %pad_maximum_fusion.14), channel_id=1, source_target_pairs={{0,2},{1,3},{2,0},{3,1},{4,6},{5,7},{6,4},{7,5},{8,10},{9,11},{10,... | collective-permute-start | bytes 393224 | tf_op jit(solution)/shard_map/ppermute | solution.py:54
  16.4 1.5 copy-done
  17.9 1.5 copy-done.1
  19.4 1.5 copy-done.2
  20.9 2.8 %mask_weights.1.refs_4_.refs_5_ = bf16[1024,2688]{1,0:T(8,128)(2,1)S(1)} custom-call(bf16[1024,896]{1,0:T(8,128)(2,1)S(1)} %copy-done, bf16[1024,896]{1,0:T(8,128)(2,1)S(1)} %copy-done.1, bf16[896,1024]{1,0:T(8,128)(2,1)S(1)} %copy-done.2, s32[8,7]{1,0:T(8,128)S(1)} %copy-done.3, s32[8,7]{1,0:T(8,128)S(1)} %copy-done.4, s32[7,8]{1,0:T(8,128)S(1)} %copy-done.5), custom_call_target="tpu_custom_call" | custom-call | flops 2752512 | bytes 11010048 | tf_op jit(solution)/shard_map/mask_weights/pallas_call | solution.py:118
  23.7 1.9 %collective-permute-done.3 = bf16[2,64,1024]{2,1,0:T(8,128)(2,1)S(1)} collective-permute-done((bf16[2,64,1024]{2,1,0:T(8,128)(2,1)S(1)}, bf16[2,64,1024]{2,1,0:T(8,128)(2,1)S(1)}, u32[]{:S(2)}, u32[]{:S(2)}) %collective-permute-start.3) | collective-permute-done | bytes 262176 | tf_op jit(solution)/shard_map/ppermute | solution.py:54
  26.6 1.2 collective-permute-done.6.refs_3_
  28.6 3.4 %forward.2 = (bf16[128,2688]{1,0:T(8,128)(2,1)S(1)}, bf16[128,2688]{1,0:T(8,128)(2,1)S(1)}, bf16[64,2688]{1,0:T(8,128)(2,1)S(1)}, bf16[64,2688]{1,0:T(8,128)(2,1)S(1)}, bf16[128,2688]{1,0:T(8,128)(2,1)S(1)}) custom-call(bf16[4,64,1024]{2,1,0:T(8,128)(2,1)S(1)} %pad_maximum_fusion.6.refs_0_, bf16[4,64,1024]{2,1,0:T(8,128)(2,1)S(1)} %pad_maximum_fusion.7.refs_1_, ...), custom_call_target="tpu_custom_call" | custom-call | flops 1024 | bytes 1024 | tf_op jit(solution)/shard_map/forward/pallas_call | solution.py:156
  32.0 2.0 %collective-permute-start.7 = (bf16[128,2688]{1,0:T(8,128)(2,1)S(1)}, bf16[128,2688]{1,0:T(8,128)(2,1)S(1)}, u32[]{:S(2)}, u32[]{:S(2)}) collective-permute-start(bf16[128,2688]{1,0:T(8,128)(2,1)S(1)} %get-tuple-element.111), channel_id=1, source_target_pairs={{0,16},{1,17},{2,18},{3,19},{4,20},{5,21},{6,22},{7,23},{8,24},{9,... | collective-permute-start | bytes 2064392 | tf_op jit(solution)/shard_map/ppermute | solution.py:54
  34.0 2.2 %collective-permute-start.8 = (bf16[128,2688]{1,0:T(8,128)(2,1)S(1)}, bf16[128,2688]{1,0:T(8,128)(2,1)S(1)}, u32[]{:S(2)}, u32[]{:S(2)}) collective-permute-start(bf16[128,2688]{1,0:T(8,128)(2,1)S(1)} %get-tuple-element.112), channel_id=1, source_target_pairs={{0,48},{1,49},{2,50},{3,51},{4,52},{5,53},{6,54},{7,55},{8,56},{9,... | collective-permute-start | bytes 2064392 | tf_op jit(solution)/shard_map/ppermute | solution.py:54
  36.8 1.4 collective-permute-start.12
  38.3 13.6 %collective-permute-done.7 = bf16[128,2688]{1,0:T(8,128)(2,1)S(1)} collective-permute-done((bf16[128,2688]{1,0:T(8,128)(2,1)S(1)}, bf16[128,2688]{1,0:T(8,128)(2,1)S(1)}, u32[]{:S(2)}, u32[]{:S(2)}) %collective-permute-start.7) | collective-permute-done | bytes 688160 | tf_op jit(solution)/shard_map/ppermute | solution.py:54
  53.0 3.0 %collective-permute-start.10 = (bf16[64,2688]{1,0:T(8,128)(2,1)S(1)}, bf16[64,2688]{1,0:T(8,128)(2,1)S(1)}, u32[]{:S(2)}, u32[]{:S(2)}) collective-permute-start(bf16[64,2688]{1,0:T(8,128)(2,1)S(1)} %slice_add_fusion.2), channel_id=1, source_target_pairs={{0,48},{1,49},{2,50},{3,51},{4,52},{5,53},{6,54},{7,55},{8,56},{9,... | collective-permute-start | bytes 1032200 | tf_op jit(solution)/shard_map/ppermute | solution.py:54
  56.0 3.4 %forward.3 = (bf16[128,2688]{1,0:T(8,128)(2,1)S(1)}, bf16[128,2688]{1,0:T(8,128)(2,1)S(1)}, bf16[64,2688]{1,0:T(8,128)(2,1)S(1)}, bf16[64,2688]{1,0:T(8,128)(2,1)S(1)}, bf16[128,2688]{1,0:T(8,128)(2,1)S(1)}) custom-call(bf16[4,64,1024]{2,1,0:T(8,128)(2,1)S(1)} %pad_maximum_fusion.8.refs_0_.refs_9_, ...), custom_call_target="tpu_custom_call" | custom-call | flops 1024 | bytes 1024 | tf_op jit(solution)/shard_map/forward/pallas_call | solution.py:156
  59.8 3.8 %collective-permute-done.10 = bf16[64,2688]{1,0:T(8,128)(2,1)S(1)} collective-permute-done((bf16[64,2688]{1,0:T(8,128)(2,1)S(1)}, bf16[64,2688]{1,0:T(8,128)(2,1)S(1)}, u32[]{:S(2)}, u32[]{:S(2)}) %collective-permute-start.10) | collective-permute-done | bytes 344096 | tf_op jit(solution)/shard_map/ppermute | solution.py:54
  63.6 4.6 %collective-permute-done.9 = bf16[64,2688]{1,0:T(8,128)(2,1)S(1)} collective-permute-done((bf16[64,2688]{1,0:T(8,128)(2,1)S(1)}, bf16[64,2688]{1,0:T(8,128)(2,1)S(1)}, u32[]{:S(2)}, u32[]{:S(2)}) %collective-permute-start.9) | collective-permute-done | bytes 344096 | tf_op jit(solution)/shard_map/ppermute | solution.py:54
  68.5 1.8 %collective-permute-start.16 = (bf16[128,2688]{1,0:T(8,128)(2,1)S(1)}, bf16[128,2688]{1,0:T(8,128)(2,1)S(1)}, u32[]{:S(2)}, u32[]{:S(2)}) collective-permute-start(bf16[128,2688]{1,0:T(8,128)(2,1)S(1)} %pad_maximum_fusion.2), channel_id=1, source_target_pairs={{0,64},{1,65},{2,66},{3,67},{4,68},{5,69},{6,70},{7,71},{8,72},{9,... | collective-permute-start | bytes 2064392 | tf_op jit(solution)/shard_map/ppermute | solution.py:54
  70.3 11.5 %collective-permute-done.17 = bf16[128,2688]{1,0:T(8,128)(2,1)S(1)} collective-permute-done((bf16[128,2688]{1,0:T(8,128)(2,1)S(1)}, bf16[128,2688]{1,0:T(8,128)(2,1)S(1)}, u32[]{:S(2)}, u32[]{:S(2)}) %collective-permute-start.17) | collective-permute-done | bytes 688160 | tf_op jit(solution)/shard_map/ppermute | solution.py:54
  81.7 1.5 collective-permute-done.18
  83.3 1.9 %collective-permute-start.22 = (bf16[64,2688]{1,0:T(8,128)(2,1)S(1)}, bf16[64,2688]{1,0:T(8,128)(2,1)S(1)}, u32[]{:S(2)}, u32[]{:S(2)}) collective-permute-start(bf16[64,2688]{1,0:T(8,128)(2,1)S(1)} %slice_add_fusion), channel_id=1, source_target_pairs={{0,48},{1,49},{2,50},{3,51},{4,52},{5,53},{6,54},{7,55},{8,56},{9,... | collective-permute-start | bytes 1032200 | tf_op jit(solution)/shard_map/ppermute | solution.py:54
  86.0 3.1 %collective-permute-start.19 = (bf16[128,2688]{1,0:T(8,128)(2,1)S(1)}, bf16[128,2688]{1,0:T(8,128)(2,1)S(1)}, u32[]{:S(2)}, u32[]{:S(2)}) collective-permute-start(bf16[128,2688]{1,0:T(8,128)(2,1)S(1)} %pad_maximum_fusion.3.refs_0_.refs_4_), channel_id=1, source_target_pairs={{0,48},{1,49},{2,50},{3,51},{4,52},{5,53},{6,54},{7,55},{8,56},{9,... | collective-permute-start | bytes 2064392 | tf_op jit(solution)/shard_map/ppermute | solution.py:54
  89.1 5.2 %collective-permute-done.22 = bf16[64,2688]{1,0:T(8,128)(2,1)S(1)} collective-permute-done((bf16[64,2688]{1,0:T(8,128)(2,1)S(1)}, bf16[64,2688]{1,0:T(8,128)(2,1)S(1)}, u32[]{:S(2)}, u32[]{:S(2)}) %collective-permute-start.22) | collective-permute-done | bytes 344096 | tf_op jit(solution)/shard_map/ppermute | solution.py:54
  94.4 3.1 %collective-permute-done.21 = bf16[64,2688]{1,0:T(8,128)(2,1)S(1)} collective-permute-done((bf16[64,2688]{1,0:T(8,128)(2,1)S(1)}, bf16[64,2688]{1,0:T(8,128)(2,1)S(1)}, u32[]{:S(2)}, u32[]{:S(2)}) %collective-permute-start.21) | collective-permute-done | bytes 344096 | tf_op jit(solution)/shard_map/ppermute | solution.py:54
  97.9 1.6 collective-permute-start.25
  99.4 6.0 %collective-permute-done.19.refs_1_.refs_5_ = bf16[128,2688]{1,0:T(8,128)(2,1)S(1)} collective-permute-done((bf16[128,2688]{1,0:T(8,128)(2,1)S(1)}, bf16[128,2688]{1,0:T(8,128)(2,1)S(1)}, u32[]{:S(2)}, u32[]{:S(2)}) %collective-permute-start.19) | collective-permute-done | bytes 688160 | tf_op jit(solution)/shard_map/ppermute | solution.py:54
  105.5 2.9 %collective-permute-done.20.refs_2_.refs_6_ = bf16[128,2688]{1,0:T(8,128)(2,1)S(1)} collective-permute-done((bf16[128,2688]{1,0:T(8,128)(2,1)S(1)}, bf16[128,2688]{1,0:T(8,128)(2,1)S(1)}, u32[]{:S(2)}, u32[]{:S(2)}) %collective-permute-start.20) | collective-permute-done | bytes 688160 | tf_op jit(solution)/shard_map/ppermute | solution.py:54
  108.5 3.2 %collective-permute-start.24 = (bf16[64,2688]{1,0:T(8,128)(2,1)S(1)}, bf16[64,2688]{1,0:T(8,128)(2,1)S(1)}, u32[]{:S(2)}, u32[]{:S(2)}) collective-permute-start(bf16[64,2688]{1,0:T(8,128)(2,1)S(1)} %slice.204), channel_id=1, source_target_pairs={{0,48},{1,49},{2,50},{3,51},{4,52},{5,53},{6,54},{7,55},{8,56},{9,... | collective-permute-start | bytes 1032200 | tf_op jit(solution)/shard_map/ppermute | solution.py:54
  112.3 2.0 %collective-permute-start.29 = (bf16[128,2688]{1,0:T(8,128)(2,1)S(1)}, bf16[128,2688]{1,0:T(8,128)(2,1)S(1)}, u32[]{:S(2)}, u32[]{:S(2)}) collective-permute-start(bf16[128,2688]{1,0:T(8,128)(2,1)S(1)} %pad_maximum_fusion.5.refs_0_.refs_13_), channel_id=1, source_target_pairs={{0,16},{1,17},{2,18},{3,19},{4,20},{5,21},{6,22},{7,23},{8,24},{9,... | collective-permute-start | bytes 2064392 | tf_op jit(solution)/shard_map/ppermute | solution.py:54
  114.3 6.4 %collective-permute-done.23.refs_3_.refs_7_ = bf16[64,2688]{1,0:T(8,128)(2,1)S(1)} collective-permute-done((bf16[64,2688]{1,0:T(8,128)(2,1)S(1)}, bf16[64,2688]{1,0:T(8,128)(2,1)S(1)}, u32[]{:S(2)}, u32[]{:S(2)}) %collective-permute-start.23) | collective-permute-done | bytes 344096 | tf_op jit(solution)/shard_map/ppermute | solution.py:54
  120.7 3.2 %backward.2 = (bf16[4,64,1024]{2,1,0:T(8,128)(2,1)S(1)}, bf16[4,64,1024]{2,1,0:T(8,128)(2,1)S(1)}, bf16[4,64,1024]{2,1,0:T(8,128)(2,1)S(1)}, bf16[4,64,1024]{2,1,0:T(8,128)(2,1)S(1)}) custom-call(bf16[128,2688]{1,0:T(8,128)(2,1)S(1)} %pad_maximum_fusion.3.refs_0_.refs_4_, bf16[128,2688]{1,0:T(8,128)(2,1)S(1)} %collective-permute-done.19.refs_1_.refs_5_, ...), custom_call_target="tpu_custom_call" | custom-call | flops 2818572288 | bytes 22020096 | tf_op jit(solution)/shard_map/backward/pallas_call | solution.py:184
  124.5 6.1 %collective-permute-done.28.refs_1_.refs_14_ = bf16[128,2688]{1,0:T(8,128)(2,1)S(1)} collective-permute-done((bf16[128,2688]{1,0:T(8,128)(2,1)S(1)}, bf16[128,2688]{1,0:T(8,128)(2,1)S(1)}, u32[]{:S(2)}, u32[]{:S(2)}) %collective-permute-start.28) | collective-permute-done | bytes 688160 | tf_op jit(solution)/shard_map/ppermute | solution.py:54
  131.5 3.2 %collective-permute-start.34 = (bf16[64,2688]{1,0:T(8,128)(2,1)S(1)}, bf16[64,2688]{1,0:T(8,128)(2,1)S(1)}, u32[]{:S(2)}, u32[]{:S(2)}) collective-permute-start(bf16[64,2688]{1,0:T(8,128)(2,1)S(1)} %slice.209), channel_id=1, source_target_pairs={{0,48},{1,49},{2,50},{3,51},{4,52},{5,53},{6,54},{7,55},{8,56},{9,... | collective-permute-start | bytes 1032200 | tf_op jit(solution)/shard_map/ppermute | solution.py:54
  135.3 2.1 %collective-permute-start.31 = (bf16[64,2048]{1,0:T(8,128)(2,1)S(1)}, bf16[64,2048]{1,0:T(8,128)(2,1)S(1)}, u32[]{:S(2)}, u32[]{:S(2)}) collective-permute-start(bf16[64,2048]{1,0:T(8,128)(2,1)S(1)} %get-tuple-element.209), channel_id=1, source_target_pairs={{0,8},{1,9},{2,10},{3,11},{4,12},{5,13},{6,14},{7,15},{8,0},{9,1},... | collective-permute-start | bytes 786440 | tf_op jit(solution)/shard_map/ppermute | solution.py:54
  137.4 1.2 collective-permute-start.32
  138.6 1.4 collective-permute-done.33.refs_3_.refs_16_
  139.9 3.2 %backward.3 = (bf16[4,64,1024]{2,1,0:T(8,128)(2,1)S(1)}, bf16[4,64,1024]{2,1,0:T(8,128)(2,1)S(1)}, bf16[4,64,1024]{2,1,0:T(8,128)(2,1)S(1)}, bf16[4,64,1024]{2,1,0:T(8,128)(2,1)S(1)}) custom-call(bf16[128,2688]{1,0:T(8,128)(2,1)S(1)} %pad_maximum_fusion.5.refs_0_.refs_13_, bf16[128,2688]{1,0:T(8,128)(2,1)S(1)} %collective-permute-done.28.refs_1_.refs_14_, ...), custom_call_target="tpu_custom_call" | custom-call | flops 2818572288 | bytes 22020096 | tf_op jit(solution)/shard_map/backward/pallas_call | solution.py:184
  143.1 2.6 %collective-permute-done.30 = bf16[64,2048]{1,0:T(8,128)(2,1)S(1)} collective-permute-done((bf16[64,2048]{1,0:T(8,128)(2,1)S(1)}, bf16[64,2048]{1,0:T(8,128)(2,1)S(1)}, u32[]{:S(2)}, u32[]{:S(2)}) %collective-permute-start.30) | collective-permute-done | bytes 262176 | tf_op jit(solution)/shard_map/ppermute | solution.py:54
  147.6 3.1 %collective-permute-start.35 = (bf16[32,2048]{1,0:T(8,128)(2,1)S(1)}, bf16[32,2048]{1,0:T(8,128)(2,1)S(1)}, u32[]{:S(2)}, u32[]{:S(2)}) collective-permute-start(bf16[32,2048]{1,0:T(8,128)(2,1)S(1)} %slice.239), channel_id=1, source_target_pairs={{0,2},{1,3},{2,0},{3,1},{4,6},{5,7},{6,4},{7,5},{8,10},{9,11},{10,... | collective-permute-start | bytes 393224 | tf_op jit(solution)/shard_map/ppermute | solution.py:54
  151.3 3.8 %collective-permute-start.39 = (bf16[64,2048]{1,0:T(8,128)(2,1)S(1)}, bf16[64,2048]{1,0:T(8,128)(2,1)S(1)}, u32[]{:S(2)}, u32[]{:S(2)}) collective-permute-start(bf16[64,2048]{1,0:T(8,128)(2,1)S(1)} %get-tuple-element.205), channel_id=1, source_target_pairs={{0,8},{1,9},{2,10},{3,11},{4,12},{5,13},{6,14},{7,15},{8,0},{9,1},... | collective-permute-start | bytes 786440 | tf_op jit(solution)/shard_map/ppermute | solution.py:54
  155.1 9.6 %weight_grads.1 = (bf16[1024,896]{1,0:T(8,128)(2,1)}, bf16[1024,896]{1,0:T(8,128)(2,1)}, bf16[896,1024]{1,0:T(8,128)(2,1)}) custom-call(bf16[4,64,1024]{2,1,0:T(8,128)(2,1)S(1)} %pad_maximum_fusion.6.refs_0_, bf16[4,64,1024]{2,1,0:T(8,128)(2,1)S(1)} %pad_maximum_fusion.7.refs_1_, bf16[4,64,1024]{2,1,0:T(8,128)(2,1)S(1)} %collective-permute-done.5.refs_2_, ...), custom_call_target="tpu_custom_call" | custom-call | flops 5637144576 | bytes 44040192 | tf_op jit(solution)/shard_map/weight_grads/pallas_call | solution.py:243
  164.7 2.0 %collective-permute-done.39 = bf16[64,2048]{1,0:T(8,128)(2,1)S(1)} collective-permute-done((bf16[64,2048]{1,0:T(8,128)(2,1)S(1)}, bf16[64,2048]{1,0:T(8,128)(2,1)S(1)}, u32[]{:S(2)}, u32[]{:S(2)}) %collective-permute-start.39) | collective-permute-done | bytes 262176 | tf_op jit(solution)/shard_map/ppermute | solution.py:54
  166.9 2.5 %collective-permute-start.41 = (bf16[32,2048]{1,0:T(8,128)(2,1)S(1)}, bf16[32,2048]{1,0:T(8,128)(2,1)S(1)}, u32[]{:S(2)}, u32[]{:S(2)}) collective-permute-start(bf16[32,2048]{1,0:T(8,128)(2,1)S(1)} %slice.249), channel_id=1, source_target_pairs={{0,2},{1,3},{2,0},{3,1},{4,6},{5,7},{6,4},{7,5},{8,10},{9,11},{10,... | collective-permute-start | bytes 393224 | tf_op jit(solution)/shard_map/ppermute | solution.py:54
  169.4 4.1 %collective-permute-done.41 = bf16[32,2048]{1,0:T(8,128)(2,1)S(1)} collective-permute-done((bf16[32,2048]{1,0:T(8,128)(2,1)S(1)}, bf16[32,2048]{1,0:T(8,128)(2,1)S(1)}, u32[]{:S(2)}, u32[]{:S(2)}) %collective-permute-start.41) | collective-permute-done | bytes 131104 | tf_op jit(solution)/shard_map/ppermute | solution.py:54
  (102 shorter events, 12.0 us)
Async XLA Ops:
  0.6 15.8 %copy-start.3 = (s32[8,7]{1,0:T(8,128)S(1)}, s32[8,7]{1,0:T(8,128)}, u32[]{:S(2)}) copy-start(s32[8,7]{1,0:T(8,128)} %refs_18_.1) | copy-start | bytes 676
  0.6 15.8 %copy-start.4 = (s32[8,7]{1,0:T(8,128)S(1)}, s32[8,7]{1,0:T(8,128)}, u32[]{:S(2)}) copy-start(s32[8,7]{1,0:T(8,128)} %refs_19_.1) | copy-start | bytes 676
  0.7 15.7 %copy-start.5 = (s32[7,8]{1,0:T(8,128)S(1)}, s32[7,8]{1,0:T(8,128)}, u32[]{:S(2)}) copy-start(s32[7,8]{1,0:T(8,128)} %refs_20_.1) | copy-start | bytes 676
  1.7 6.7 %collective-permute-start = (bf16[2,32,1024]{2,1,0:T(8,128)(2,1)S(1)}, bf16[2,32,1024]{2,1,0:T(8,128)(2,1)S(1)}, u32[]{:S(2)}, u32[]{:S(2)}) collective-permute-start(bf16[2,32,1024]{2,1,0:T(8,128)(2,1)S(1)} %pad_maximum_fusion.13), channel_id=1, source_target_pairs={{0,2},{1,3},{2,0},{3,1},{4,6},{5,7},{6,4},{7,5},{8,10},{9,11},{10,... | collective-permute-start | bytes 393224 | tf_op jit(solution)/shard_map/ppermute | solution.py:54
  8.4 15.4 %collective-permute-start.1 = (bf16[2,64,1024]{2,1,0:T(8,128)(2,1)S(1)}, bf16[2,64,1024]{2,1,0:T(8,128)(2,1)S(1)}, u32[]{:S(2)}, u32[]{:S(2)}) collective-permute-start(bf16[2,64,1024]{2,1,0:T(8,128)(2,1)S(1)} %pad_maximum_fusion.10), channel_id=1, source_target_pairs={{0,12},{1,13},{2,14},{3,15},{4,0},{5,1},{6,2},{7,3},{8,4},{9,5},{1... | collective-permute-start | bytes 786440 | tf_op jit(solution)/shard_map/ppermute | solution.py:54
  11.7 12.1 %collective-permute-start.2 = (bf16[2,64,1024]{2,1,0:T(8,128)(2,1)S(1)}, bf16[2,64,1024]{2,1,0:T(8,128)(2,1)S(1)}, u32[]{:S(2)}, u32[]{:S(2)}) collective-permute-start(bf16[2,64,1024]{2,1,0:T(8,128)(2,1)S(1)} %pad_maximum_fusion.10), channel_id=1, source_target_pairs={{0,8},{1,9},{2,10},{3,11},{4,12},{5,13},{6,14},{7,15},{8,0},{9,1},... | collective-permute-start | bytes 786440 | tf_op jit(solution)/shard_map/ppermute | solution.py:54
  12.3 13.4 %collective-permute-start.3 = (bf16[2,64,1024]{2,1,0:T(8,128)(2,1)S(1)}, bf16[2,64,1024]{2,1,0:T(8,128)(2,1)S(1)}, u32[]{:S(2)}, u32[]{:S(2)}) collective-permute-start(bf16[2,64,1024]{2,1,0:T(8,128)(2,1)S(1)} %pad_maximum_fusion.10), channel_id=1, source_target_pairs={{0,4},{1,5},{2,6},{3,7},{4,8},{5,9},{6,10},{7,11},{8,12},{9,13},{1... | collective-permute-start | bytes 786440 | tf_op jit(solution)/shard_map/ppermute | solution.py:54
  13.3 10.4 %collective-permute-start.4 = (bf16[2,32,1024]{2,1,0:T(8,128)(2,1)S(1)}, bf16[2,32,1024]{2,1,0:T(8,128)(2,1)S(1)}, u32[]{:S(2)}, u32[]{:S(2)}) collective-permute-start(bf16[2,32,1024]{2,1,0:T(8,128)(2,1)S(1)} %pad_maximum_fusion.14), channel_id=1, source_target_pairs={{0,2},{1,3},{2,0},{3,1},{4,6},{5,7},{6,4},{7,5},{8,10},{9,11},{10,... | collective-permute-start | bytes 393224 | tf_op jit(solution)/shard_map/ppermute | solution.py:54
  16.4 1.5 copy-start
  17.9 1.5 copy-start.1
  19.4 1.5 copy-start.2
  25.9 2.0 %collective-permute-start.6 = (bf16[4,64,1024]{2,1,0:T(8,128)(2,1)S(1)}, bf16[4,64,1024]{2,1,0:T(8,128)(2,1)S(1)}, u32[]{:S(2)}, u32[]{:S(2)}) collective-permute-start(bf16[4,64,1024]{2,1,0:T(8,128)(2,1)S(1)} %pad_maximum_fusion.7.refs_1_), channel_id=1, source_target_pairs={{0,1},{1,0},{2,3},{3,2},{4,5},{5,4},{6,7},{7,6},{8,9},{9,8},{10,11... | collective-permute-start | bytes 1572872 | tf_op jit(solution)/shard_map/ppermute | solution.py:54
  26.0 2.6 %collective-permute-start.5 = (bf16[4,64,1024]{2,1,0:T(8,128)(2,1)S(1)}, bf16[4,64,1024]{2,1,0:T(8,128)(2,1)S(1)}, u32[]{:S(2)}, u32[]{:S(2)}) collective-permute-start(bf16[4,64,1024]{2,1,0:T(8,128)(2,1)S(1)} %pad_maximum_fusion.6.refs_0_), channel_id=1, source_target_pairs={{0,1},{1,0},{2,3},{3,2},{4,5},{5,4},{6,7},{7,6},{8,9},{9,8},{10,11... | collective-permute-start | bytes 1572872 | tf_op jit(solution)/shard_map/ppermute | solution.py:54
  32.0 19.8 %collective-permute-start.7 = (bf16[128,2688]{1,0:T(8,128)(2,1)S(1)}, bf16[128,2688]{1,0:T(8,128)(2,1)S(1)}, u32[]{:S(2)}, u32[]{:S(2)}) collective-permute-start(bf16[128,2688]{1,0:T(8,128)(2,1)S(1)} %get-tuple-element.111), channel_id=1, source_target_pairs={{0,16},{1,17},{2,18},{3,19},{4,20},{5,21},{6,22},{7,23},{8,24},{9,... | collective-permute-start | bytes 2064392 | tf_op jit(solution)/shard_map/ppermute | solution.py:54
  34.0 17.9 %collective-permute-start.8 = (bf16[128,2688]{1,0:T(8,128)(2,1)S(1)}, bf16[128,2688]{1,0:T(8,128)(2,1)S(1)}, u32[]{:S(2)}, u32[]{:S(2)}) collective-permute-start(bf16[128,2688]{1,0:T(8,128)(2,1)S(1)} %get-tuple-element.112), channel_id=1, source_target_pairs={{0,48},{1,49},{2,50},{3,51},{4,52},{5,53},{6,54},{7,55},{8,56},{9,... | collective-permute-start | bytes 2064392 | tf_op jit(solution)/shard_map/ppermute | solution.py:54
  36.2 15.8 %collective-permute-start.11 = (bf16[2,64,1024]{2,1,0:T(8,128)(2,1)S(1)}, bf16[2,64,1024]{2,1,0:T(8,128)(2,1)S(1)}, u32[]{:S(2)}, u32[]{:S(2)}) collective-permute-start(bf16[2,64,1024]{2,1,0:T(8,128)(2,1)S(1)} %pad_maximum_fusion.11), channel_id=1, source_target_pairs={{0,12},{1,13},{2,14},{3,15},{4,0},{5,1},{6,2},{7,3},{8,4},{9,5},{1... | collective-permute-start | bytes 786440 | tf_op jit(solution)/shard_map/ppermute | solution.py:54
  36.8 15.2 %collective-permute-start.12 = (bf16[2,64,1024]{2,1,0:T(8,128)(2,1)S(1)}, bf16[2,64,1024]{2,1,0:T(8,128)(2,1)S(1)}, u32[]{:S(2)}, u32[]{:S(2)}) collective-permute-start(bf16[2,64,1024]{2,1,0:T(8,128)(2,1)S(1)} %pad_maximum_fusion.11), channel_id=1, source_target_pairs={{0,8},{1,9},{2,10},{3,11},{4,12},{5,13},{6,14},{7,15},{8,0},{9,1},... | collective-permute-start | bytes 786440 | tf_op jit(solution)/shard_map/ppermute | solution.py:54
  38.3 13.8 %collective-permute-start.13 = (bf16[2,64,1024]{2,1,0:T(8,128)(2,1)S(1)}, bf16[2,64,1024]{2,1,0:T(8,128)(2,1)S(1)}, u32[]{:S(2)}, u32[]{:S(2)}) collective-permute-start(bf16[2,64,1024]{2,1,0:T(8,128)(2,1)S(1)} %pad_maximum_fusion.11), channel_id=1, source_target_pairs={{0,4},{1,5},{2,6},{3,7},{4,8},{5,9},{6,10},{7,11},{8,12},{9,13},{1... | collective-permute-start | bytes 786440 | tf_op jit(solution)/shard_map/ppermute | solution.py:54
  52.2 3.8 %collective-permute-start.15 = (bf16[4,64,1024]{2,1,0:T(8,128)(2,1)S(1)}, bf16[4,64,1024]{2,1,0:T(8,128)(2,1)S(1)}, u32[]{:S(2)}, u32[]{:S(2)}) collective-permute-start(bf16[4,64,1024]{2,1,0:T(8,128)(2,1)S(1)} %pad_maximum_fusion.9.refs_1_.refs_10_), channel_id=1, source_target_pairs={{0,1},{1,0},{2,3},{3,2},{4,5},{5,4},{6,7},{7,6},{8,9},{9,8},{10,11... | collective-permute-start | bytes 1572872 | tf_op jit(solution)/shard_map/ppermute | solution.py:54
  52.4 3.6 %collective-permute-start.14 = (bf16[4,64,1024]{2,1,0:T(8,128)(2,1)S(1)}, bf16[4,64,1024]{2,1,0:T(8,128)(2,1)S(1)}, u32[]{:S(2)}, u32[]{:S(2)}) collective-permute-start(bf16[4,64,1024]{2,1,0:T(8,128)(2,1)S(1)} %pad_maximum_fusion.8.refs_0_.refs_9_), channel_id=1, source_target_pairs={{0,1},{1,0},{2,3},{3,2},{4,5},{5,4},{6,7},{7,6},{8,9},{9,8},{10,11... | collective-permute-start | bytes 1572872 | tf_op jit(solution)/shard_map/ppermute | solution.py:54
  53.0 10.6 %collective-permute-start.10 = (bf16[64,2688]{1,0:T(8,128)(2,1)S(1)}, bf16[64,2688]{1,0:T(8,128)(2,1)S(1)}, u32[]{:S(2)}, u32[]{:S(2)}) collective-permute-start(bf16[64,2688]{1,0:T(8,128)(2,1)S(1)} %slice_add_fusion.2), channel_id=1, source_target_pairs={{0,48},{1,49},{2,50},{3,51},{4,52},{5,53},{6,54},{7,55},{8,56},{9,... | collective-permute-start | bytes 1032200 | tf_op jit(solution)/shard_map/ppermute | solution.py:54
  56.0 12.2 %collective-permute-start.9 = (bf16[64,2688]{1,0:T(8,128)(2,1)S(1)}, bf16[64,2688]{1,0:T(8,128)(2,1)S(1)}, u32[]{:S(2)}, u32[]{:S(2)}) collective-permute-start(bf16[64,2688]{1,0:T(8,128)(2,1)S(1)} %slice_add_fusion.3), channel_id=1, source_target_pairs={{0,16},{1,17},{2,18},{3,19},{4,20},{5,21},{6,22},{7,23},{8,24},{9,... | collective-permute-start | bytes 1032200 | tf_op jit(solution)/shard_map/ppermute | solution.py:54
  59.4 22.3 %collective-permute-start.17 = (bf16[128,2688]{1,0:T(8,128)(2,1)S(1)}, bf16[128,2688]{1,0:T(8,128)(2,1)S(1)}, u32[]{:S(2)}, u32[]{:S(2)}) collective-permute-start(bf16[128,2688]{1,0:T(8,128)(2,1)S(1)} %get-tuple-element.125), channel_id=1, source_target_pairs={{0,16},{1,17},{2,18},{3,19},{4,20},{5,21},{6,22},{7,23},{8,24},{9,... | collective-permute-start | bytes 2064392 | tf_op jit(solution)/shard_map/ppermute | solution.py:54
  68.2 15.1 %collective-permute-start.18 = (bf16[128,2688]{1,0:T(8,128)(2,1)S(1)}, bf16[128,2688]{1,0:T(8,128)(2,1)S(1)}, u32[]{:S(2)}, u32[]{:S(2)}) collective-permute-start(bf16[128,2688]{1,0:T(8,128)(2,1)S(1)} %get-tuple-element.129), channel_id=1, source_target_pairs={{0,48},{1,49},{2,50},{3,51},{4,52},{5,53},{6,54},{7,55},{8,56},{9,... | collective-permute-start | bytes 2064392 | tf_op jit(solution)/shard_map/ppermute | solution.py:54
  68.5 17.0 %collective-permute-start.16 = (bf16[128,2688]{1,0:T(8,128)(2,1)S(1)}, bf16[128,2688]{1,0:T(8,128)(2,1)S(1)}, u32[]{:S(2)}, u32[]{:S(2)}) collective-permute-start(bf16[128,2688]{1,0:T(8,128)(2,1)S(1)} %pad_maximum_fusion.2), channel_id=1, source_target_pairs={{0,64},{1,65},{2,66},{3,67},{4,68},{5,69},{6,70},{7,71},{8,72},{9,... | collective-permute-start | bytes 2064392 | tf_op jit(solution)/shard_map/ppermute | solution.py:54
  83.3 11.1 %collective-permute-start.22 = (bf16[64,2688]{1,0:T(8,128)(2,1)S(1)}, bf16[64,2688]{1,0:T(8,128)(2,1)S(1)}, u32[]{:S(2)}, u32[]{:S(2)}) collective-permute-start(bf16[64,2688]{1,0:T(8,128)(2,1)S(1)} %slice_add_fusion), channel_id=1, source_target_pairs={{0,48},{1,49},{2,50},{3,51},{4,52},{5,53},{6,54},{7,55},{8,56},{9,... | collective-permute-start | bytes 1032200 | tf_op jit(solution)/shard_map/ppermute | solution.py:54
  85.2 12.3 %collective-permute-start.21 = (bf16[64,2688]{1,0:T(8,128)(2,1)S(1)}, bf16[64,2688]{1,0:T(8,128)(2,1)S(1)}, u32[]{:S(2)}, u32[]{:S(2)}) collective-permute-start(bf16[64,2688]{1,0:T(8,128)(2,1)S(1)} %slice_add_fusion.1), channel_id=1, source_target_pairs={{0,16},{1,17},{2,18},{3,19},{4,20},{5,21},{6,22},{7,23},{8,24},{9,... | collective-permute-start | bytes 1032200 | tf_op jit(solution)/shard_map/ppermute | solution.py:54
  86.0 19.4 %collective-permute-start.19 = (bf16[128,2688]{1,0:T(8,128)(2,1)S(1)}, bf16[128,2688]{1,0:T(8,128)(2,1)S(1)}, u32[]{:S(2)}, u32[]{:S(2)}) collective-permute-start(bf16[128,2688]{1,0:T(8,128)(2,1)S(1)} %pad_maximum_fusion.3.refs_0_.refs_4_), channel_id=1, source_target_pairs={{0,48},{1,49},{2,50},{3,51},{4,52},{5,53},{6,54},{7,55},{8,56},{9,... | collective-permute-start | bytes 2064392 | tf_op jit(solution)/shard_map/ppermute | solution.py:54
  89.1 19.2 %collective-permute-start.20 = (bf16[128,2688]{1,0:T(8,128)(2,1)S(1)}, bf16[128,2688]{1,0:T(8,128)(2,1)S(1)}, u32[]{:S(2)}, u32[]{:S(2)}) collective-permute-start(bf16[128,2688]{1,0:T(8,128)(2,1)S(1)} %pad_maximum_fusion.3.refs_0_.refs_4_), channel_id=1, source_target_pairs={{0,16},{1,17},{2,18},{3,19},{4,20},{5,21},{6,22},{7,23},{8,24},{9,... | collective-permute-start | bytes 2064392 | tf_op jit(solution)/shard_map/ppermute | solution.py:54
  97.9 13.9 %collective-permute-start.25 = (bf16[128,2688]{1,0:T(8,128)(2,1)S(1)}, bf16[128,2688]{1,0:T(8,128)(2,1)S(1)}, u32[]{:S(2)}, u32[]{:S(2)}) collective-permute-start(bf16[128,2688]{1,0:T(8,128)(2,1)S(1)} %pad_maximum_fusion.4), channel_id=1, source_target_pairs={{0,64},{1,65},{2,66},{3,67},{4,68},{5,69},{6,70},{7,71},{8,72},{9,... | collective-permute-start | bytes 2064392 | tf_op jit(solution)/shard_map/ppermute | solution.py:54
  108.4 12.3 %collective-permute-start.23 = (bf16[64,2688]{1,0:T(8,128)(2,1)S(1)}, bf16[64,2688]{1,0:T(8,128)(2,1)S(1)}, u32[]{:S(2)}, u32[]{:S(2)}) collective-permute-start(bf16[64,2688]{1,0:T(8,128)(2,1)S(1)} %slice.203), channel_id=1, source_target_pairs={{0,16},{1,17},{2,18},{3,19},{4,20},{5,21},{6,22},{7,23},{8,24},{9,... | collective-permute-start | bytes 1032200 | tf_op jit(solution)/shard_map/ppermute | solution.py:54
  108.5 12.2 %collective-permute-start.24 = (bf16[64,2688]{1,0:T(8,128)(2,1)S(1)}, bf16[64,2688]{1,0:T(8,128)(2,1)S(1)}, u32[]{:S(2)}, u32[]{:S(2)}) collective-permute-start(bf16[64,2688]{1,0:T(8,128)(2,1)S(1)} %slice.204), channel_id=1, source_target_pairs={{0,48},{1,49},{2,50},{3,51},{4,52},{5,53},{6,54},{7,55},{8,56},{9,... | collective-permute-start | bytes 1032200 | tf_op jit(solution)/shard_map/ppermute | solution.py:54
  112.2 18.4 %collective-permute-start.28 = (bf16[128,2688]{1,0:T(8,128)(2,1)S(1)}, bf16[128,2688]{1,0:T(8,128)(2,1)S(1)}, u32[]{:S(2)}, u32[]{:S(2)}) collective-permute-start(bf16[128,2688]{1,0:T(8,128)(2,1)S(1)} %pad_maximum_fusion.5.refs_0_.refs_13_), channel_id=1, source_target_pairs={{0,48},{1,49},{2,50},{3,51},{4,52},{5,53},{6,54},{7,55},{8,56},{9,... | collective-permute-start | bytes 2064392 | tf_op jit(solution)/shard_map/ppermute | solution.py:54
  112.3 19.0 %collective-permute-start.29 = (bf16[128,2688]{1,0:T(8,128)(2,1)S(1)}, bf16[128,2688]{1,0:T(8,128)(2,1)S(1)}, u32[]{:S(2)}, u32[]{:S(2)}) collective-permute-start(bf16[128,2688]{1,0:T(8,128)(2,1)S(1)} %pad_maximum_fusion.5.refs_0_.refs_13_), channel_id=1, source_target_pairs={{0,16},{1,17},{2,18},{3,19},{4,20},{5,21},{6,22},{7,23},{8,24},{9,... | collective-permute-start | bytes 2064392 | tf_op jit(solution)/shard_map/ppermute | solution.py:54
  123.9 10.8 %collective-permute-start.26 = (bf16[256,1024]{1,0:T(8,128)(2,1)S(1)}, bf16[256,1024]{1,0:T(8,128)(2,1)S(1)}, u32[]{:S(2)}, u32[]{:S(2)}) collective-permute-start(bf16[256,1024]{1,0:T(8,128)(2,1)S(1)} %bitcast.27), channel_id=1, source_target_pairs={{0,1},{1,0},{2,3},{3,2},{4,5},{5,4},{6,7},{7,6},{8,9},{9,8},{10,11... | collective-permute-start | bytes 1572872 | tf_op jit(solution)/shard_map/ppermute | solution.py:54
  124.0 10.7 %collective-permute-start.27 = (bf16[256,1024]{1,0:T(8,128)(2,1)S(1)}, bf16[256,1024]{1,0:T(8,128)(2,1)S(1)}, u32[]{:S(2)}, u32[]{:S(2)}) collective-permute-start(bf16[256,1024]{1,0:T(8,128)(2,1)S(1)} %bitcast.26), channel_id=1, source_target_pairs={{0,1},{1,0},{2,3},{3,2},{4,5},{5,4},{6,7},{7,6},{8,9},{9,8},{10,11... | collective-permute-start | bytes 1572872 | tf_op jit(solution)/shard_map/ppermute | solution.py:54
  131.4 8.5 %collective-permute-start.33 = (bf16[64,2688]{1,0:T(8,128)(2,1)S(1)}, bf16[64,2688]{1,0:T(8,128)(2,1)S(1)}, u32[]{:S(2)}, u32[]{:S(2)}) collective-permute-start(bf16[64,2688]{1,0:T(8,128)(2,1)S(1)} %slice.208), channel_id=1, source_target_pairs={{0,16},{1,17},{2,18},{3,19},{4,20},{5,21},{6,22},{7,23},{8,24},{9,... | collective-permute-start | bytes 1032200 | tf_op jit(solution)/shard_map/ppermute | solution.py:54
  131.5 8.4 %collective-permute-start.34 = (bf16[64,2688]{1,0:T(8,128)(2,1)S(1)}, bf16[64,2688]{1,0:T(8,128)(2,1)S(1)}, u32[]{:S(2)}, u32[]{:S(2)}) collective-permute-start(bf16[64,2688]{1,0:T(8,128)(2,1)S(1)} %slice.209), channel_id=1, source_target_pairs={{0,48},{1,49},{2,50},{3,51},{4,52},{5,53},{6,54},{7,55},{8,56},{9,... | collective-permute-start | bytes 1032200 | tf_op jit(solution)/shard_map/ppermute | solution.py:54
  135.2 10.5 %collective-permute-start.30 = (bf16[64,2048]{1,0:T(8,128)(2,1)S(1)}, bf16[64,2048]{1,0:T(8,128)(2,1)S(1)}, u32[]{:S(2)}, u32[]{:S(2)}) collective-permute-start(bf16[64,2048]{1,0:T(8,128)(2,1)S(1)} %get-tuple-element.208), channel_id=1, source_target_pairs={{0,4},{1,5},{2,6},{3,7},{4,8},{5,9},{6,10},{7,11},{8,12},{9,13},{1... | collective-permute-start | bytes 786440 | tf_op jit(solution)/shard_map/ppermute | solution.py:54
  135.3 10.4 %collective-permute-start.31 = (bf16[64,2048]{1,0:T(8,128)(2,1)S(1)}, bf16[64,2048]{1,0:T(8,128)(2,1)S(1)}, u32[]{:S(2)}, u32[]{:S(2)}) collective-permute-start(bf16[64,2048]{1,0:T(8,128)(2,1)S(1)} %get-tuple-element.209), channel_id=1, source_target_pairs={{0,8},{1,9},{2,10},{3,11},{4,12},{5,13},{6,14},{7,15},{8,0},{9,1},... | collective-permute-start | bytes 786440 | tf_op jit(solution)/shard_map/ppermute | solution.py:54
  137.4 9.2 %collective-permute-start.32 = (bf16[64,2048]{1,0:T(8,128)(2,1)S(1)}, bf16[64,2048]{1,0:T(8,128)(2,1)S(1)}, u32[]{:S(2)}, u32[]{:S(2)}) collective-permute-start(bf16[64,2048]{1,0:T(8,128)(2,1)S(1)} %get-tuple-element.207), channel_id=1, source_target_pairs={{0,12},{1,13},{2,14},{3,15},{4,0},{5,1},{6,2},{7,3},{8,4},{9,5},{1... | collective-permute-start | bytes 786440 | tf_op jit(solution)/shard_map/ppermute | solution.py:54
  146.7 3.9 %collective-permute-start.36 = (bf16[256,1024]{1,0:T(8,128)(2,1)S(1)}, bf16[256,1024]{1,0:T(8,128)(2,1)S(1)}, u32[]{:S(2)}, u32[]{:S(2)}) collective-permute-start(bf16[256,1024]{1,0:T(8,128)(2,1)S(1)} %bitcast.25), channel_id=1, source_target_pairs={{0,1},{1,0},{2,3},{3,2},{4,5},{5,4},{6,7},{7,6},{8,9},{9,8},{10,11... | collective-permute-start | bytes 1572872 | tf_op jit(solution)/shard_map/ppermute | solution.py:54
  147.1 3.6 %collective-permute-start.37 = (bf16[256,1024]{1,0:T(8,128)(2,1)S(1)}, bf16[256,1024]{1,0:T(8,128)(2,1)S(1)}, u32[]{:S(2)}, u32[]{:S(2)}) collective-permute-start(bf16[256,1024]{1,0:T(8,128)(2,1)S(1)} %bitcast.24), channel_id=1, source_target_pairs={{0,1},{1,0},{2,3},{3,2},{4,5},{5,4},{6,7},{7,6},{8,9},{9,8},{10,11... | collective-permute-start | bytes 1572872 | tf_op jit(solution)/shard_map/ppermute | solution.py:54
  147.6 21.8 %collective-permute-start.35 = (bf16[32,2048]{1,0:T(8,128)(2,1)S(1)}, bf16[32,2048]{1,0:T(8,128)(2,1)S(1)}, u32[]{:S(2)}, u32[]{:S(2)}) collective-permute-start(bf16[32,2048]{1,0:T(8,128)(2,1)S(1)} %slice.239), channel_id=1, source_target_pairs={{0,2},{1,3},{2,0},{3,1},{4,6},{5,7},{6,4},{7,5},{8,10},{9,11},{10,... | collective-permute-start | bytes 393224 | tf_op jit(solution)/shard_map/ppermute | solution.py:54
  151.2 13.5 %collective-permute-start.38 = (bf16[64,2048]{1,0:T(8,128)(2,1)S(1)}, bf16[64,2048]{1,0:T(8,128)(2,1)S(1)}, u32[]{:S(2)}, u32[]{:S(2)}) collective-permute-start(bf16[64,2048]{1,0:T(8,128)(2,1)S(1)} %get-tuple-element.204), channel_id=1, source_target_pairs={{0,4},{1,5},{2,6},{3,7},{4,8},{5,9},{6,10},{7,11},{8,12},{9,13},{1... | collective-permute-start | bytes 786440 | tf_op jit(solution)/shard_map/ppermute | solution.py:54
  151.3 15.4 %collective-permute-start.39 = (bf16[64,2048]{1,0:T(8,128)(2,1)S(1)}, bf16[64,2048]{1,0:T(8,128)(2,1)S(1)}, u32[]{:S(2)}, u32[]{:S(2)}) collective-permute-start(bf16[64,2048]{1,0:T(8,128)(2,1)S(1)} %get-tuple-element.205), channel_id=1, source_target_pairs={{0,8},{1,9},{2,10},{3,11},{4,12},{5,13},{6,14},{7,15},{8,0},{9,1},... | collective-permute-start | bytes 786440 | tf_op jit(solution)/shard_map/ppermute | solution.py:54
  155.1 11.7 %collective-permute-start.40 = (bf16[64,2048]{1,0:T(8,128)(2,1)S(1)}, bf16[64,2048]{1,0:T(8,128)(2,1)S(1)}, u32[]{:S(2)}, u32[]{:S(2)}) collective-permute-start(bf16[64,2048]{1,0:T(8,128)(2,1)S(1)} %get-tuple-element.203), channel_id=1, source_target_pairs={{0,12},{1,13},{2,14},{3,15},{4,0},{5,1},{6,2},{7,3},{8,4},{9,5},{1... | collective-permute-start | bytes 786440 | tf_op jit(solution)/shard_map/ppermute | solution.py:54
  166.9 6.6 %collective-permute-start.41 = (bf16[32,2048]{1,0:T(8,128)(2,1)S(1)}, bf16[32,2048]{1,0:T(8,128)(2,1)S(1)}, u32[]{:S(2)}, u32[]{:S(2)}) collective-permute-start(bf16[32,2048]{1,0:T(8,128)(2,1)S(1)} %slice.249), channel_id=1, source_target_pairs={{0,2},{1,3},{2,0},{3,1},{4,6},{5,7},{6,4},{7,5},{8,10},{9,11},{10,... | collective-permute-start | bytes 393224 | tf_op jit(solution)/shard_map/ppermute | solution.py:54

commit v7 on v6

--- a/solution.py
+++ b/solution.py
@@ -48,7 +48,7 @@
         row, col = divmod(device, 16)
         x_lo, z = divmod(row, 4)
         y, x_hi, core = col // 4, col // 2 % 2, col % 2
-        to_row = (x_lo + dxl) % 2 * 4 + (z + dz) % 4
+        to_row = (x_lo + dxl) % 2 * 4 + (z + dz * (1 - 2 * core)) % 4
         to_col = ((y + dy) % 4 * 2 + (x_hi + dxh) % 2) * 2 + (core + dcore) % 2
         pairs.append((device, to_row * 16 + to_col))
     return lax.ppermute(array, ("row", "col"), pairs)
@@ -85,7 +85,9 @@
 
 
 def owner(dz):
-    return lax.rem(lax.axis_index("row") + dz, 4)
+    z = lax.rem(lax.axis_index("row"), 4)
+    odd = lax.rem(lax.axis_index("col"), 2)
+    return lax.rem(z + dz + odd * ((4 - 2 * dz) % 4), 4)
 
 
 def tokens_of(kind, gathered, offset, rows, columns):
@@ -312,11 +314,12 @@
         return outs[0]
 
     def relay(self, *others):
-        down, up = after((self.from_down, self.from_up), *others)
         rows = self.rows
+        down = after(self.from_down, *others)
         send_up = self.late_up + down[:rows]
+        self.last_down = move(send_up, dz=1)
+        up = after(self.from_up, send_up)
         send_down = self.late_down + up[:rows]
-        self.last_down = move(send_up, dz=1)
         self.last_up = move(send_down, dz=-1)
         self.direct = (up[rows:], down[rows:])
         return send_up, send_down
@@ -336,14 +339,17 @@
     def spread(self, *others):
         partner = after(self.partner, *others)
         self.values = elementwise(wide(self.sums) + wide(partner))
-        self.near = (move(self.values, dz=-1), move(self.values, dz=1))
+        from_down = move(self.values, dz=1)
+        self.near = (move(self.values, dz=-1), from_down)
         return self.values
 
     def far(self, *others):
-        up, down = after(self.near, *others)
-        sent = down[: self.rows], up[self.rows :]
-        self.arrays = (self.values, up, down, move(sent[0], dz=1), move(sent[1], dz=-1))
-        return sent
+        down = after(self.near[1], *others)
+        sent_up = down[: self.rows]
+        up = after(self.near[0], sent_up)
+        sent_down = up[self.rows :]
+        self.arrays = (self.values, up, down, move(sent_up, dz=1), move(sent_down, dz=-1))
+        return sent_up, sent_down
 
     def backward(self, *others):
         self.arrays = after(self.arrays, *others)

time: 174 us -> 171 us (0.983)
  waiting for transfers between devices: 84 us -> 73.5 us
  starting transfers between devices: 53.5 us -> 60.8 us
    ppermute x42, waiting for transfers between devices: 84 us -> 73.5 us  [move(): return lax.ppermute(array, ('row', 'col'), pairs)]
    ppermute x42, starting transfers between devices: 53.5 us -> 60.8 us  [move(): return lax.ppermute(array, ('row', 'col'), pairs)]
where the time goes in v7:
time: 171 us
  waiting for transfers between devices  73.5 us (43%)
  starting transfers between devices  60.8 us (36%)
  Pallas kernels  25.6 us (15%)
  local copies, waits for them, and re-layouts  5.75 us (3%)
  other arithmetic  4.19 us (2%)
    ppermute x42, waiting for transfers between devices, move(): return lax.ppermute(array, ('row', 'col'), pairs)  73.5 us
    ppermute x42, starting transfers between devices, move(): return lax.ppermute(array, ('row', 'col'), pairs)  60.8 us
    pallas_call x1, Pallas kernels, weight_grads(): pl.pallas_call(functools.partial(weight_grad_kernel, offsets), in_specs=[...  9.6 us
    pallas_call x2, Pallas kernels, forward(): pl.pallas_call(functools.partial(forward_kernel, offset, rows), in_specs=...  6.86 us
    pallas_call x2, Pallas kernels, backward(): pl.pallas_call(backward_kernel, in_specs=[VMEM] * 6, out_specs=[VMEM] * 4...  6.35 us
    unnamed x12, local copies, waits for them, and re-layouts  4.51 us
  transfers between devices with their start and end apart: 42, of which 21 were waited for; matrix products, arithmetic and copies ran while one was open for 2% of the time, Pallas kernels for 13%

profile of v7, /device:TPU:0, one launch (start us, length us, event | category | flops | bytes accessed | tf_op | source)
XLA Modules:
  0.0 170.9 jit_solution(6047194568073779369)
XLA Ops:
  0.7 1.0 slice_bitcast_fusion
  1.7 3.2 %collective-permute-start = (bf16[2,32,1024]{2,1,0:T(8,128)(2,1)S(1)}, bf16[2,32,1024]{2,1,0:T(8,128)(2,1)S(1)}, u32[]{:S(2)}, u32[]{:S(2)}) collective-permute-start(bf16[2,32,1024]{2,1,0:T(8,128)(2,1)S(1)} %pad_maximum_fusion.13), channel_id=1, source_target_pairs={{0,2},{1,3},{2,0},{3,1},{4,6},{5,7},{6,4},{7,5},{8,10},{9,11},{10,... | collective-permute-start | bytes 393224 | tf_op jit(solution)/shard_map/ppermute | solution.py:54
  4.8 3.5 %collective-permute-done = bf16[2,32,1024]{2,1,0:T(8,128)(2,1)S(1)} collective-permute-done((bf16[2,32,1024]{2,1,0:T(8,128)(2,1)S(1)}, bf16[2,32,1024]{2,1,0:T(8,128)(2,1)S(1)}, u32[]{:S(2)}, u32[]{:S(2)}) %collective-permute-start) | collective-permute-done | bytes 131104 | tf_op jit(solution)/shard_map/ppermute | solution.py:54
  8.4 3.3 %collective-permute-start.1 = (bf16[2,64,1024]{2,1,0:T(8,128)(2,1)S(1)}, bf16[2,64,1024]{2,1,0:T(8,128)(2,1)S(1)}, u32[]{:S(2)}, u32[]{:S(2)}) collective-permute-start(bf16[2,64,1024]{2,1,0:T(8,128)(2,1)S(1)} %pad_maximum_fusion.10), channel_id=1, source_target_pairs={{0,12},{1,13},{2,14},{3,15},{4,0},{5,1},{6,2},{7,3},{8,4},{9,5},{1... | collective-permute-start | bytes 786440 | tf_op jit(solution)/shard_map/ppermute | solution.py:54
  12.3 1.0 collective-permute-start.3
  13.3 3.1 %collective-permute-start.4 = (bf16[2,32,1024]{2,1,0:T(8,128)(2,1)S(1)}, bf16[2,32,1024]{2,1,0:T(8,128)(2,1)S(1)}, u32[]{:S(2)}, u32[]{:S(2)}) collective-permute-start(bf16[2,32,1024]{2,1,0:T(8,128)(2,1)S(1)} %pad_maximum_fusion.14), channel_id=1, source_target_pairs={{0,2},{1,3},{2,0},{3,1},{4,6},{5,7},{6,4},{7,5},{8,10},{9,11},{10,... | collective-permute-start | bytes 393224 | tf_op jit(solution)/shard_map/ppermute | solution.py:54
  16.4 1.5 copy-done
  17.9 1.5 copy-done.1
  19.4 1.5 copy-done.2
  20.9 2.8 %mask_weights.1.refs_4_.refs_5_ = bf16[1024,2688]{1,0:T(8,128)(2,1)S(1)} custom-call(bf16[1024,896]{1,0:T(8,128)(2,1)S(1)} %copy-done, bf16[1024,896]{1,0:T(8,128)(2,1)S(1)} %copy-done.1, bf16[896,1024]{1,0:T(8,128)(2,1)S(1)} %copy-done.2, s32[8,7]{1,0:T(8,128)S(1)} %copy-done.3, s32[8,7]{1,0:T(8,128)S(1)} %copy-done.4, s32[7,8]{1,0:T(8,128)S(1)} %copy-done.5), custom_call_target="tpu_custom_call" | custom-call | flops 2752512 | bytes 11010048 | tf_op jit(solution)/shard_map/mask_weights/pallas_call | solution.py:120
  23.7 1.9 %collective-permute-done.3 = bf16[2,64,1024]{2,1,0:T(8,128)(2,1)S(1)} collective-permute-done((bf16[2,64,1024]{2,1,0:T(8,128)(2,1)S(1)}, bf16[2,64,1024]{2,1,0:T(8,128)(2,1)S(1)}, u32[]{:S(2)}, u32[]{:S(2)}) %collective-permute-start.3) | collective-permute-done | bytes 262176 | tf_op jit(solution)/shard_map/ppermute | solution.py:54
  26.6 1.2 collective-permute-done.6.refs_3_
  28.6 3.4 %forward.2 = (bf16[128,2688]{1,0:T(8,128)(2,1)S(1)}, bf16[128,2688]{1,0:T(8,128)(2,1)S(1)}, bf16[64,2688]{1,0:T(8,128)(2,1)S(1)}, bf16[64,2688]{1,0:T(8,128)(2,1)S(1)}, bf16[128,2688]{1,0:T(8,128)(2,1)S(1)}) custom-call(bf16[4,64,1024]{2,1,0:T(8,128)(2,1)S(1)} %pad_maximum_fusion.6.refs_0_, bf16[4,64,1024]{2,1,0:T(8,128)(2,1)S(1)} %pad_maximum_fusion.7.refs_1_, ...), custom_call_target="tpu_custom_call" | custom-call | flops 1024 | bytes 1024 | tf_op jit(solution)/shard_map/forward/pallas_call | solution.py:158
  32.0 2.0 %collective-permute-start.7 = (bf16[128,2688]{1,0:T(8,128)(2,1)S(1)}, bf16[128,2688]{1,0:T(8,128)(2,1)S(1)}, u32[]{:S(2)}, u32[]{:S(2)}) collective-permute-start(bf16[128,2688]{1,0:T(8,128)(2,1)S(1)} %get-tuple-element.111), channel_id=1, source_target_pairs={{0,16},{1,49},{2,18},{3,51},{4,20},{5,53},{6,22},{7,55},{8,24},{9,... | collective-permute-start | bytes 2064392 | tf_op jit(solution)/shard_map/ppermute | solution.py:54
  34.6 1.4 collective-permute-start.12
  36.1 2.2 %collective-permute-start.9 = (bf16[128,2688]{1,0:T(8,128)(2,1)S(1)}, bf16[128,2688]{1,0:T(8,128)(2,1)S(1)}, u32[]{:S(2)}, u32[]{:S(2)}) collective-permute-start(bf16[128,2688]{1,0:T(8,128)(2,1)S(1)} %get-tuple-element.114), channel_id=1, source_target_pairs={{0,48},{1,17},{2,50},{3,19},{4,52},{5,21},{6,54},{7,23},{8,56},{9,... | collective-permute-start | bytes 2064392 | tf_op jit(solution)/shard_map/ppermute | solution.py:54
  38.3 10.5 %collective-permute-done.7 = bf16[128,2688]{1,0:T(8,128)(2,1)S(1)} collective-permute-done((bf16[128,2688]{1,0:T(8,128)(2,1)S(1)}, bf16[128,2688]{1,0:T(8,128)(2,1)S(1)}, u32[]{:S(2)}, u32[]{:S(2)}) %collective-permute-start.7) | collective-permute-done | bytes 688160 | tf_op jit(solution)/shard_map/ppermute | solution.py:54
  48.8 2.3 %collective-permute-done.9 = bf16[128,2688]{1,0:T(8,128)(2,1)S(1)} collective-permute-done((bf16[128,2688]{1,0:T(8,128)(2,1)S(1)}, bf16[128,2688]{1,0:T(8,128)(2,1)S(1)}, u32[]{:S(2)}, u32[]{:S(2)}) %collective-permute-start.9) | collective-permute-done | bytes 688160 | tf_op jit(solution)/shard_map/ppermute | solution.py:54
  51.4 1.2 collective-permute-start.15
  52.8 3.1 %collective-permute-start.10 = (bf16[64,2688]{1,0:T(8,128)(2,1)S(1)}, bf16[64,2688]{1,0:T(8,128)(2,1)S(1)}, u32[]{:S(2)}, u32[]{:S(2)}) collective-permute-start(bf16[64,2688]{1,0:T(8,128)(2,1)S(1)} %slice_add_fusion.2), channel_id=1, source_target_pairs={{0,48},{1,17},{2,50},{3,19},{4,52},{5,21},{6,54},{7,23},{8,56},{9,... | collective-permute-start | bytes 1032200 | tf_op jit(solution)/shard_map/ppermute | solution.py:54
  55.9 3.4 %forward.3 = (bf16[128,2688]{1,0:T(8,128)(2,1)S(1)}, bf16[128,2688]{1,0:T(8,128)(2,1)S(1)}, bf16[64,2688]{1,0:T(8,128)(2,1)S(1)}, bf16[64,2688]{1,0:T(8,128)(2,1)S(1)}, bf16[128,2688]{1,0:T(8,128)(2,1)S(1)}) custom-call(bf16[4,64,1024]{2,1,0:T(8,128)(2,1)S(1)} %pad_maximum_fusion.8.refs_0_.refs_9_, ...), custom_call_target="tpu_custom_call" | custom-call | flops 1024 | bytes 1024 | tf_op jit(solution)/shard_map/forward/pallas_call | solution.py:158
  59.4 4.9 %collective-permute-done.10 = bf16[64,2688]{1,0:T(8,128)(2,1)S(1)} collective-permute-done((bf16[64,2688]{1,0:T(8,128)(2,1)S(1)}, bf16[64,2688]{1,0:T(8,128)(2,1)S(1)}, u32[]{:S(2)}, u32[]{:S(2)}) %collective-permute-start.10) | collective-permute-done | bytes 344096 | tf_op jit(solution)/shard_map/ppermute | solution.py:54
  64.4 3.5 %collective-permute-start.18 = (bf16[128,2688]{1,0:T(8,128)(2,1)S(1)}, bf16[128,2688]{1,0:T(8,128)(2,1)S(1)}, u32[]{:S(2)}, u32[]{:S(2)}) collective-permute-start(bf16[128,2688]{1,0:T(8,128)(2,1)S(1)} %get-tuple-element.131), channel_id=1, source_target_pairs={{0,48},{1,17},{2,50},{3,19},{4,52},{5,21},{6,54},{7,23},{8,56},{9,... | collective-permute-start | bytes 2064392 | tf_op jit(solution)/shard_map/ppermute | solution.py:54
  68.3 1.8 %collective-permute-start.16 = (bf16[128,2688]{1,0:T(8,128)(2,1)S(1)}, bf16[128,2688]{1,0:T(8,128)(2,1)S(1)}, u32[]{:S(2)}, u32[]{:S(2)}) collective-permute-start(bf16[128,2688]{1,0:T(8,128)(2,1)S(1)} %pad_maximum_fusion.2), channel_id=1, source_target_pairs={{0,64},{1,65},{2,66},{3,67},{4,68},{5,69},{6,70},{7,71},{8,72},{9,... | collective-permute-start | bytes 2064392 | tf_op jit(solution)/shard_map/ppermute | solution.py:54
  70.0 5.7 %collective-permute-done.17 = bf16[128,2688]{1,0:T(8,128)(2,1)S(1)} collective-permute-done((bf16[128,2688]{1,0:T(8,128)(2,1)S(1)}, bf16[128,2688]{1,0:T(8,128)(2,1)S(1)}, u32[]{:S(2)}, u32[]{:S(2)}) %collective-permute-start.17) | collective-permute-done | bytes 688160 | tf_op jit(solution)/shard_map/ppermute | solution.py:54
  75.9 4.0 %collective-permute-done.18 = bf16[128,2688]{1,0:T(8,128)(2,1)S(1)} collective-permute-done((bf16[128,2688]{1,0:T(8,128)(2,1)S(1)}, bf16[128,2688]{1,0:T(8,128)(2,1)S(1)}, u32[]{:S(2)}, u32[]{:S(2)}) %collective-permute-start.18) | collective-permute-done | bytes 688160 | tf_op jit(solution)/shard_map/ppermute | solution.py:54
  79.9 3.6 %collective-permute-start.22 = (bf16[64,2688]{1,0:T(8,128)(2,1)S(1)}, bf16[64,2688]{1,0:T(8,128)(2,1)S(1)}, u32[]{:S(2)}, u32[]{:S(2)}) collective-permute-start(bf16[64,2688]{1,0:T(8,128)(2,1)S(1)} %slice_add_fusion), channel_id=1, source_target_pairs={{0,48},{1,17},{2,50},{3,19},{4,52},{5,21},{6,54},{7,23},{8,56},{9,... | collective-permute-start | bytes 1032200 | tf_op jit(solution)/shard_map/ppermute | solution.py:54
  84.5 2.9 %collective-permute-start.19 = (bf16[128,2688]{1,0:T(8,128)(2,1)S(1)}, bf16[128,2688]{1,0:T(8,128)(2,1)S(1)}, u32[]{:S(2)}, u32[]{:S(2)}) collective-permute-start(bf16[128,2688]{1,0:T(8,128)(2,1)S(1)} %pad_maximum_fusion.3.refs_0_.refs_4_), channel_id=1, source_target_pairs={{0,48},{1,17},{2,50},{3,19},{4,52},{5,21},{6,54},{7,23},{8,56},{9,... | collective-permute-start | bytes 2064392 | tf_op jit(solution)/shard_map/ppermute | solution.py:54
  87.3 4.7 %collective-permute-done.22 = bf16[64,2688]{1,0:T(8,128)(2,1)S(1)} collective-permute-done((bf16[64,2688]{1,0:T(8,128)(2,1)S(1)}, bf16[64,2688]{1,0:T(8,128)(2,1)S(1)}, u32[]{:S(2)}, u32[]{:S(2)}) %collective-permute-start.22) | collective-permute-done | bytes 344096 | tf_op jit(solution)/shard_map/ppermute | solution.py:54
  92.4 1.6 collective-permute-start.25
  93.9 8.8 %collective-permute-done.20.refs_2_.refs_6_ = bf16[128,2688]{1,0:T(8,128)(2,1)S(1)} collective-permute-done((bf16[128,2688]{1,0:T(8,128)(2,1)S(1)}, bf16[128,2688]{1,0:T(8,128)(2,1)S(1)}, u32[]{:S(2)}, u32[]{:S(2)}) %collective-permute-start.20) | collective-permute-done | bytes 688160 | tf_op jit(solution)/shard_map/ppermute | solution.py:54
  102.9 3.5 %collective-permute-start.24 = (bf16[64,2688]{1,0:T(8,128)(2,1)S(1)}, bf16[64,2688]{1,0:T(8,128)(2,1)S(1)}, u32[]{:S(2)}, u32[]{:S(2)}) collective-permute-start(bf16[64,2688]{1,0:T(8,128)(2,1)S(1)} %slice.204), channel_id=1, source_target_pairs={{0,48},{1,17},{2,50},{3,19},{4,52},{5,21},{6,54},{7,23},{8,56},{9,... | collective-permute-start | bytes 1032200 | tf_op jit(solution)/shard_map/ppermute | solution.py:54
  107.0 3.2 %collective-permute-start.29 = (bf16[128,2688]{1,0:T(8,128)(2,1)S(1)}, bf16[128,2688]{1,0:T(8,128)(2,1)S(1)}, u32[]{:S(2)}, u32[]{:S(2)}) collective-permute-start(bf16[128,2688]{1,0:T(8,128)(2,1)S(1)} %pad_maximum_fusion.5.refs_0_.refs_13_), channel_id=1, source_target_pairs={{0,48},{1,17},{2,50},{3,19},{4,52},{5,21},{6,54},{7,23},{8,56},{9,... | collective-permute-start | bytes 2064392 | tf_op jit(solution)/shard_map/ppermute | solution.py:54
  110.3 4.7 %collective-permute-done.24.refs_4_.refs_8_ = bf16[64,2688]{1,0:T(8,128)(2,1)S(1)} collective-permute-done((bf16[64,2688]{1,0:T(8,128)(2,1)S(1)}, bf16[64,2688]{1,0:T(8,128)(2,1)S(1)}, u32[]{:S(2)}, u32[]{:S(2)}) %collective-permute-start.24) | collective-permute-done | bytes 344096 | tf_op jit(solution)/shard_map/ppermute | solution.py:54
  115.1 3.2 %backward.2 = (bf16[4,64,1024]{2,1,0:T(8,128)(2,1)S(1)}, bf16[4,64,1024]{2,1,0:T(8,128)(2,1)S(1)}, bf16[4,64,1024]{2,1,0:T(8,128)(2,1)S(1)}, bf16[4,64,1024]{2,1,0:T(8,128)(2,1)S(1)}) custom-call(bf16[128,2688]{1,0:T(8,128)(2,1)S(1)} %pad_maximum_fusion.3.refs_0_.refs_4_, bf16[128,2688]{1,0:T(8,128)(2,1)S(1)} %collective-permute-done.19.refs_1_.refs_5_, ...), custom_call_target="tpu_custom_call" | custom-call | flops 2818572288 | bytes 22020096 | tf_op jit(solution)/shard_map/backward/pallas_call | solution.py:186
  118.9 9.1 %collective-permute-done.28.refs_2_.refs_15_ = bf16[128,2688]{1,0:T(8,128)(2,1)S(1)} collective-permute-done((bf16[128,2688]{1,0:T(8,128)(2,1)S(1)}, bf16[128,2688]{1,0:T(8,128)(2,1)S(1)}, u32[]{:S(2)}, u32[]{:S(2)}) %collective-permute-start.28) | collective-permute-done | bytes 688160 | tf_op jit(solution)/shard_map/ppermute | solution.py:54
  128.1 3.3 %collective-permute-start.34 = (bf16[64,2688]{1,0:T(8,128)(2,1)S(1)}, bf16[64,2688]{1,0:T(8,128)(2,1)S(1)}, u32[]{:S(2)}, u32[]{:S(2)}) collective-permute-start(bf16[64,2688]{1,0:T(8,128)(2,1)S(1)} %slice.209), channel_id=1, source_target_pairs={{0,48},{1,17},{2,50},{3,19},{4,52},{5,21},{6,54},{7,23},{8,56},{9,... | collective-permute-start | bytes 1032200 | tf_op jit(solution)/shard_map/ppermute | solution.py:54
  132.0 2.1 %collective-permute-start.31 = (bf16[64,2048]{1,0:T(8,128)(2,1)S(1)}, bf16[64,2048]{1,0:T(8,128)(2,1)S(1)}, u32[]{:S(2)}, u32[]{:S(2)}) collective-permute-start(bf16[64,2048]{1,0:T(8,128)(2,1)S(1)} %get-tuple-element.209), channel_id=1, source_target_pairs={{0,8},{1,9},{2,10},{3,11},{4,12},{5,13},{6,14},{7,15},{8,0},{9,1},... | collective-permute-start | bytes 786440 | tf_op jit(solution)/shard_map/ppermute | solution.py:54
  134.1 1.2 collective-permute-start.32
  136.2 1.3 collective-permute-done.33.refs_3_.refs_16_
  137.5 3.2 %backward.3 = (bf16[4,64,1024]{2,1,0:T(8,128)(2,1)S(1)}, bf16[4,64,1024]{2,1,0:T(8,128)(2,1)S(1)}, bf16[4,64,1024]{2,1,0:T(8,128)(2,1)S(1)}, bf16[4,64,1024]{2,1,0:T(8,128)(2,1)S(1)}) custom-call(bf16[128,2688]{1,0:T(8,128)(2,1)S(1)} %pad_maximum_fusion.5.refs_0_.refs_13_, bf16[128,2688]{1,0:T(8,128)(2,1)S(1)} %collective-permute-done.29.refs_1_.refs_14_, ...), custom_call_target="tpu_custom_call" | custom-call | flops 2818572288 | bytes 22020096 | tf_op jit(solution)/shard_map/backward/pallas_call | solution.py:186
  140.7 1.7 %collective-permute-done.30 = bf16[64,2048]{1,0:T(8,128)(2,1)S(1)} collective-permute-done((bf16[64,2048]{1,0:T(8,128)(2,1)S(1)}, bf16[64,2048]{1,0:T(8,128)(2,1)S(1)}, u32[]{:S(2)}, u32[]{:S(2)}) %collective-permute-start.30) | collective-permute-done | bytes 262176 | tf_op jit(solution)/shard_map/ppermute | solution.py:54
  144.3 3.1 %collective-permute-start.35 = (bf16[32,2048]{1,0:T(8,128)(2,1)S(1)}, bf16[32,2048]{1,0:T(8,128)(2,1)S(1)}, u32[]{:S(2)}, u32[]{:S(2)}) collective-permute-start(bf16[32,2048]{1,0:T(8,128)(2,1)S(1)} %slice.239), channel_id=1, source_target_pairs={{0,2},{1,3},{2,0},{3,1},{4,6},{5,7},{6,4},{7,5},{8,10},{9,11},{10,... | collective-permute-start | bytes 393224 | tf_op jit(solution)/shard_map/ppermute | solution.py:54
  148.0 3.8 %collective-permute-start.39 = (bf16[64,2048]{1,0:T(8,128)(2,1)S(1)}, bf16[64,2048]{1,0:T(8,128)(2,1)S(1)}, u32[]{:S(2)}, u32[]{:S(2)}) collective-permute-start(bf16[64,2048]{1,0:T(8,128)(2,1)S(1)} %get-tuple-element.205), channel_id=1, source_target_pairs={{0,8},{1,9},{2,10},{3,11},{4,12},{5,13},{6,14},{7,15},{8,0},{9,1},... | collective-permute-start | bytes 786440 | tf_op jit(solution)/shard_map/ppermute | solution.py:54
  151.8 9.6 %weight_grads.1 = (bf16[1024,896]{1,0:T(8,128)(2,1)}, bf16[1024,896]{1,0:T(8,128)(2,1)}, bf16[896,1024]{1,0:T(8,128)(2,1)}) custom-call(bf16[4,64,1024]{2,1,0:T(8,128)(2,1)S(1)} %pad_maximum_fusion.6.refs_0_, bf16[4,64,1024]{2,1,0:T(8,128)(2,1)S(1)} %pad_maximum_fusion.7.refs_1_, bf16[4,64,1024]{2,1,0:T(8,128)(2,1)S(1)} %collective-permute-done.5.refs_2_, ...), custom_call_target="tpu_custom_call" | custom-call | flops 5637144576 | bytes 44040192 | tf_op jit(solution)/shard_map/weight_grads/pallas_call | solution.py:245
  161.4 2.0 %collective-permute-done.39 = bf16[64,2048]{1,0:T(8,128)(2,1)S(1)} collective-permute-done((bf16[64,2048]{1,0:T(8,128)(2,1)S(1)}, bf16[64,2048]{1,0:T(8,128)(2,1)S(1)}, u32[]{:S(2)}, u32[]{:S(2)}) %collective-permute-start.39) | collective-permute-done | bytes 262176 | tf_op jit(solution)/shard_map/ppermute | solution.py:54
  163.6 2.5 %collective-permute-start.41 = (bf16[32,2048]{1,0:T(8,128)(2,1)S(1)}, bf16[32,2048]{1,0:T(8,128)(2,1)S(1)}, u32[]{:S(2)}, u32[]{:S(2)}) collective-permute-start(bf16[32,2048]{1,0:T(8,128)(2,1)S(1)} %slice.249), channel_id=1, source_target_pairs={{0,2},{1,3},{2,0},{3,1},{4,6},{5,7},{6,4},{7,5},{8,10},{9,11},{10,... | collective-permute-start | bytes 393224 | tf_op jit(solution)/shard_map/ppermute | solution.py:54
  166.1 4.1 %collective-permute-done.41 = bf16[32,2048]{1,0:T(8,128)(2,1)S(1)} collective-permute-done((bf16[32,2048]{1,0:T(8,128)(2,1)S(1)}, bf16[32,2048]{1,0:T(8,128)(2,1)S(1)}, u32[]{:S(2)}, u32[]{:S(2)}) %collective-permute-start.41) | collective-permute-done | bytes 131104 | tf_op jit(solution)/shard_map/ppermute | solution.py:54
  (102 shorter events, 11.8 us)
Async XLA Ops:
  0.6 15.8 %copy-start.3 = (s32[8,7]{1,0:T(8,128)S(1)}, s32[8,7]{1,0:T(8,128)}, u32[]{:S(2)}) copy-start(s32[8,7]{1,0:T(8,128)} %refs_18_.1) | copy-start | bytes 676
  0.6 15.8 %copy-start.4 = (s32[8,7]{1,0:T(8,128)S(1)}, s32[8,7]{1,0:T(8,128)}, u32[]{:S(2)}) copy-start(s32[8,7]{1,0:T(8,128)} %refs_19_.1) | copy-start | bytes 676
  0.7 15.7 %copy-start.5 = (s32[7,8]{1,0:T(8,128)S(1)}, s32[7,8]{1,0:T(8,128)}, u32[]{:S(2)}) copy-start(s32[7,8]{1,0:T(8,128)} %refs_20_.1) | copy-start | bytes 676
  1.7 6.7 %collective-permute-start = (bf16[2,32,1024]{2,1,0:T(8,128)(2,1)S(1)}, bf16[2,32,1024]{2,1,0:T(8,128)(2,1)S(1)}, u32[]{:S(2)}, u32[]{:S(2)}) collective-permute-start(bf16[2,32,1024]{2,1,0:T(8,128)(2,1)S(1)} %pad_maximum_fusion.13), channel_id=1, source_target_pairs={{0,2},{1,3},{2,0},{3,1},{4,6},{5,7},{6,4},{7,5},{8,10},{9,11},{10,... | collective-permute-start | bytes 393224 | tf_op jit(solution)/shard_map/ppermute | solution.py:54
  8.4 15.4 %collective-permute-start.1 = (bf16[2,64,1024]{2,1,0:T(8,128)(2,1)S(1)}, bf16[2,64,1024]{2,1,0:T(8,128)(2,1)S(1)}, u32[]{:S(2)}, u32[]{:S(2)}) collective-permute-start(bf16[2,64,1024]{2,1,0:T(8,128)(2,1)S(1)} %pad_maximum_fusion.10), channel_id=1, source_target_pairs={{0,12},{1,13},{2,14},{3,15},{4,0},{5,1},{6,2},{7,3},{8,4},{9,5},{1... | collective-permute-start | bytes 786440 | tf_op jit(solution)/shard_map/ppermute | solution.py:54
  11.7 12.1 %collective-permute-start.2 = (bf16[2,64,1024]{2,1,0:T(8,128)(2,1)S(1)}, bf16[2,64,1024]{2,1,0:T(8,128)(2,1)S(1)}, u32[]{:S(2)}, u32[]{:S(2)}) collective-permute-start(bf16[2,64,1024]{2,1,0:T(8,128)(2,1)S(1)} %pad_maximum_fusion.10), channel_id=1, source_target_pairs={{0,8},{1,9},{2,10},{3,11},{4,12},{5,13},{6,14},{7,15},{8,0},{9,1},... | collective-permute-start | bytes 786440 | tf_op jit(solution)/shard_map/ppermute | solution.py:54
  12.3 13.4 %collective-permute-start.3 = (bf16[2,64,1024]{2,1,0:T(8,128)(2,1)S(1)}, bf16[2,64,1024]{2,1,0:T(8,128)(2,1)S(1)}, u32[]{:S(2)}, u32[]{:S(2)}) collective-permute-start(bf16[2,64,1024]{2,1,0:T(8,128)(2,1)S(1)} %pad_maximum_fusion.10), channel_id=1, source_target_pairs={{0,4},{1,5},{2,6},{3,7},{4,8},{5,9},{6,10},{7,11},{8,12},{9,13},{1... | collective-permute-start | bytes 786440 | tf_op jit(solution)/shard_map/ppermute | solution.py:54
  13.3 10.4 %collective-permute-start.4 = (bf16[2,32,1024]{2,1,0:T(8,128)(2,1)S(1)}, bf16[2,32,1024]{2,1,0:T(8,128)(2,1)S(1)}, u32[]{:S(2)}, u32[]{:S(2)}) collective-permute-start(bf16[2,32,1024]{2,1,0:T(8,128)(2,1)S(1)} %pad_maximum_fusion.14), channel_id=1, source_target_pairs={{0,2},{1,3},{2,0},{3,1},{4,6},{5,7},{6,4},{7,5},{8,10},{9,11},{10,... | collective-permute-start | bytes 393224 | tf_op jit(solution)/shard_map/ppermute | solution.py:54
  16.4 1.5 copy-start
  17.9 1.5 copy-start.1
  19.4 1.5 copy-start.2
  25.9 2.0 %collective-permute-start.6 = (bf16[4,64,1024]{2,1,0:T(8,128)(2,1)S(1)}, bf16[4,64,1024]{2,1,0:T(8,128)(2,1)S(1)}, u32[]{:S(2)}, u32[]{:S(2)}) collective-permute-start(bf16[4,64,1024]{2,1,0:T(8,128)(2,1)S(1)} %pad_maximum_fusion.7.refs_1_), channel_id=1, source_target_pairs={{0,1},{1,0},{2,3},{3,2},{4,5},{5,4},{6,7},{7,6},{8,9},{9,8},{10,11... | collective-permute-start | bytes 1572872 | tf_op jit(solution)/shard_map/ppermute | solution.py:54
  26.0 2.6 %collective-permute-start.5 = (bf16[4,64,1024]{2,1,0:T(8,128)(2,1)S(1)}, bf16[4,64,1024]{2,1,0:T(8,128)(2,1)S(1)}, u32[]{:S(2)}, u32[]{:S(2)}) collective-permute-start(bf16[4,64,1024]{2,1,0:T(8,128)(2,1)S(1)} %pad_maximum_fusion.6.refs_0_), channel_id=1, source_target_pairs={{0,1},{1,0},{2,3},{3,2},{4,5},{5,4},{6,7},{7,6},{8,9},{9,8},{10,11... | collective-permute-start | bytes 1572872 | tf_op jit(solution)/shard_map/ppermute | solution.py:54
  32.0 16.7 %collective-permute-start.7 = (bf16[128,2688]{1,0:T(8,128)(2,1)S(1)}, bf16[128,2688]{1,0:T(8,128)(2,1)S(1)}, u32[]{:S(2)}, u32[]{:S(2)}) collective-permute-start(bf16[128,2688]{1,0:T(8,128)(2,1)S(1)} %get-tuple-element.111), channel_id=1, source_target_pairs={{0,16},{1,49},{2,18},{3,51},{4,20},{5,53},{6,22},{7,55},{8,24},{9,... | collective-permute-start | bytes 2064392 | tf_op jit(solution)/shard_map/ppermute | solution.py:54
  34.0 17.2 %collective-permute-start.11 = (bf16[2,64,1024]{2,1,0:T(8,128)(2,1)S(1)}, bf16[2,64,1024]{2,1,0:T(8,128)(2,1)S(1)}, u32[]{:S(2)}, u32[]{:S(2)}) collective-permute-start(bf16[2,64,1024]{2,1,0:T(8,128)(2,1)S(1)} %pad_maximum_fusion.11), channel_id=1, source_target_pairs={{0,12},{1,13},{2,14},{3,15},{4,0},{5,1},{6,2},{7,3},{8,4},{9,5},{1... | collective-permute-start | bytes 786440 | tf_op jit(solution)/shard_map/ppermute | solution.py:54
  34.6 16.6 %collective-permute-start.12 = (bf16[2,64,1024]{2,1,0:T(8,128)(2,1)S(1)}, bf16[2,64,1024]{2,1,0:T(8,128)(2,1)S(1)}, u32[]{:S(2)}, u32[]{:S(2)}) collective-permute-start(bf16[2,64,1024]{2,1,0:T(8,128)(2,1)S(1)} %pad_maximum_fusion.11), channel_id=1, source_target_pairs={{0,8},{1,9},{2,10},{3,11},{4,12},{5,13},{6,14},{7,15},{8,0},{9,1},... | collective-permute-start | bytes 786440 | tf_op jit(solution)/shard_map/ppermute | solution.py:54
  36.1 15.2 %collective-permute-start.13 = (bf16[2,64,1024]{2,1,0:T(8,128)(2,1)S(1)}, bf16[2,64,1024]{2,1,0:T(8,128)(2,1)S(1)}, u32[]{:S(2)}, u32[]{:S(2)}) collective-permute-start(bf16[2,64,1024]{2,1,0:T(8,128)(2,1)S(1)} %pad_maximum_fusion.11), channel_id=1, source_target_pairs={{0,4},{1,5},{2,6},{3,7},{4,8},{5,9},{6,10},{7,11},{8,12},{9,13},{1... | collective-permute-start | bytes 786440 | tf_op jit(solution)/shard_map/ppermute | solution.py:54
  36.1 15.1 %collective-permute-start.9 = (bf16[128,2688]{1,0:T(8,128)(2,1)S(1)}, bf16[128,2688]{1,0:T(8,128)(2,1)S(1)}, u32[]{:S(2)}, u32[]{:S(2)}) collective-permute-start(bf16[128,2688]{1,0:T(8,128)(2,1)S(1)} %get-tuple-element.114), channel_id=1, source_target_pairs={{0,48},{1,17},{2,50},{3,19},{4,52},{5,21},{6,54},{7,23},{8,56},{9,... | collective-permute-start | bytes 2064392 | tf_op jit(solution)/shard_map/ppermute | solution.py:54
  51.4 4.5 %collective-permute-start.15 = (bf16[4,64,1024]{2,1,0:T(8,128)(2,1)S(1)}, bf16[4,64,1024]{2,1,0:T(8,128)(2,1)S(1)}, u32[]{:S(2)}, u32[]{:S(2)}) collective-permute-start(bf16[4,64,1024]{2,1,0:T(8,128)(2,1)S(1)} %pad_maximum_fusion.9.refs_1_.refs_10_), channel_id=1, source_target_pairs={{0,1},{1,0},{2,3},{3,2},{4,5},{5,4},{6,7},{7,6},{8,9},{9,8},{10,11... | collective-permute-start | bytes 1572872 | tf_op jit(solution)/shard_map/ppermute | solution.py:54
  52.7 3.2 %collective-permute-start.14 = (bf16[4,64,1024]{2,1,0:T(8,128)(2,1)S(1)}, bf16[4,64,1024]{2,1,0:T(8,128)(2,1)S(1)}, u32[]{:S(2)}, u32[]{:S(2)}) collective-permute-start(bf16[4,64,1024]{2,1,0:T(8,128)(2,1)S(1)} %pad_maximum_fusion.8.refs_0_.refs_9_), channel_id=1, source_target_pairs={{0,1},{1,0},{2,3},{3,2},{4,5},{5,4},{6,7},{7,6},{8,9},{9,8},{10,11... | collective-permute-start | bytes 1572872 | tf_op jit(solution)/shard_map/ppermute | solution.py:54
  52.8 11.5 %collective-permute-start.10 = (bf16[64,2688]{1,0:T(8,128)(2,1)S(1)}, bf16[64,2688]{1,0:T(8,128)(2,1)S(1)}, u32[]{:S(2)}, u32[]{:S(2)}) collective-permute-start(bf16[64,2688]{1,0:T(8,128)(2,1)S(1)} %slice_add_fusion.2), channel_id=1, source_target_pairs={{0,48},{1,17},{2,50},{3,19},{4,52},{5,21},{6,54},{7,23},{8,56},{9,... | collective-permute-start | bytes 1032200 | tf_op jit(solution)/shard_map/ppermute | solution.py:54
  55.9 8.6 %collective-permute-start.8 = (bf16[64,2688]{1,0:T(8,128)(2,1)S(1)}, bf16[64,2688]{1,0:T(8,128)(2,1)S(1)}, u32[]{:S(2)}, u32[]{:S(2)}) collective-permute-start(bf16[64,2688]{1,0:T(8,128)(2,1)S(1)} %slice_add_fusion.3), channel_id=1, source_target_pairs={{0,16},{1,49},{2,18},{3,51},{4,20},{5,53},{6,22},{7,55},{8,24},{9,... | collective-permute-start | bytes 1032200 | tf_op jit(solution)/shard_map/ppermute | solution.py:54
  59.3 16.4 %collective-permute-start.17 = (bf16[128,2688]{1,0:T(8,128)(2,1)S(1)}, bf16[128,2688]{1,0:T(8,128)(2,1)S(1)}, u32[]{:S(2)}, u32[]{:S(2)}) collective-permute-start(bf16[128,2688]{1,0:T(8,128)(2,1)S(1)} %get-tuple-element.125), channel_id=1, source_target_pairs={{0,16},{1,49},{2,18},{3,51},{4,20},{5,53},{6,22},{7,55},{8,24},{9,... | collective-permute-start | bytes 2064392 | tf_op jit(solution)/shard_map/ppermute | solution.py:54
  64.4 15.4 %collective-permute-start.18 = (bf16[128,2688]{1,0:T(8,128)(2,1)S(1)}, bf16[128,2688]{1,0:T(8,128)(2,1)S(1)}, u32[]{:S(2)}, u32[]{:S(2)}) collective-permute-start(bf16[128,2688]{1,0:T(8,128)(2,1)S(1)} %get-tuple-element.131), channel_id=1, source_target_pairs={{0,48},{1,17},{2,50},{3,19},{4,52},{5,21},{6,54},{7,23},{8,56},{9,... | collective-permute-start | bytes 2064392 | tf_op jit(solution)/shard_map/ppermute | solution.py:54
  68.3 15.3 %collective-permute-start.16 = (bf16[128,2688]{1,0:T(8,128)(2,1)S(1)}, bf16[128,2688]{1,0:T(8,128)(2,1)S(1)}, u32[]{:S(2)}, u32[]{:S(2)}) collective-permute-start(bf16[128,2688]{1,0:T(8,128)(2,1)S(1)} %pad_maximum_fusion.2), channel_id=1, source_target_pairs={{0,64},{1,65},{2,66},{3,67},{4,68},{5,69},{6,70},{7,71},{8,72},{9,... | collective-permute-start | bytes 2064392 | tf_op jit(solution)/shard_map/ppermute | solution.py:54
  75.8 16.2 %collective-permute-start.21 = (bf16[64,2688]{1,0:T(8,128)(2,1)S(1)}, bf16[64,2688]{1,0:T(8,128)(2,1)S(1)}, u32[]{:S(2)}, u32[]{:S(2)}) collective-permute-start(bf16[64,2688]{1,0:T(8,128)(2,1)S(1)} %slice_add_fusion.1), channel_id=1, source_target_pairs={{0,16},{1,49},{2,18},{3,51},{4,20},{5,53},{6,22},{7,55},{8,24},{9,... | collective-permute-start | bytes 1032200 | tf_op jit(solution)/shard_map/ppermute | solution.py:54
  79.9 12.1 %collective-permute-start.22 = (bf16[64,2688]{1,0:T(8,128)(2,1)S(1)}, bf16[64,2688]{1,0:T(8,128)(2,1)S(1)}, u32[]{:S(2)}, u32[]{:S(2)}) collective-permute-start(bf16[64,2688]{1,0:T(8,128)(2,1)S(1)} %slice_add_fusion), channel_id=1, source_target_pairs={{0,48},{1,17},{2,50},{3,19},{4,52},{5,21},{6,54},{7,23},{8,56},{9,... | collective-permute-start | bytes 1032200 | tf_op jit(solution)/shard_map/ppermute | solution.py:54
  84.0 18.7 %collective-permute-start.20 = (bf16[128,2688]{1,0:T(8,128)(2,1)S(1)}, bf16[128,2688]{1,0:T(8,128)(2,1)S(1)}, u32[]{:S(2)}, u32[]{:S(2)}) collective-permute-start(bf16[128,2688]{1,0:T(8,128)(2,1)S(1)} %pad_maximum_fusion.3.refs_0_.refs_4_), channel_id=1, source_target_pairs={{0,16},{1,49},{2,18},{3,51},{4,20},{5,53},{6,22},{7,55},{8,24},{9,... | collective-permute-start | bytes 2064392 | tf_op jit(solution)/shard_map/ppermute | solution.py:54
  84.5 18.4 %collective-permute-start.19 = (bf16[128,2688]{1,0:T(8,128)(2,1)S(1)}, bf16[128,2688]{1,0:T(8,128)(2,1)S(1)}, u32[]{:S(2)}, u32[]{:S(2)}) collective-permute-start(bf16[128,2688]{1,0:T(8,128)(2,1)S(1)} %pad_maximum_fusion.3.refs_0_.refs_4_), channel_id=1, source_target_pairs={{0,48},{1,17},{2,50},{3,19},{4,52},{5,21},{6,54},{7,23},{8,56},{9,... | collective-permute-start | bytes 2064392 | tf_op jit(solution)/shard_map/ppermute | solution.py:54
  92.4 14.1 %collective-permute-start.25 = (bf16[128,2688]{1,0:T(8,128)(2,1)S(1)}, bf16[128,2688]{1,0:T(8,128)(2,1)S(1)}, u32[]{:S(2)}, u32[]{:S(2)}) collective-permute-start(bf16[128,2688]{1,0:T(8,128)(2,1)S(1)} %pad_maximum_fusion.4), channel_id=1, source_target_pairs={{0,64},{1,65},{2,66},{3,67},{4,68},{5,69},{6,70},{7,71},{8,72},{9,... | collective-permute-start | bytes 2064392 | tf_op jit(solution)/shard_map/ppermute | solution.py:54
  102.8 12.3 %collective-permute-start.23 = (bf16[64,2688]{1,0:T(8,128)(2,1)S(1)}, bf16[64,2688]{1,0:T(8,128)(2,1)S(1)}, u32[]{:S(2)}, u32[]{:S(2)}) collective-permute-start(bf16[64,2688]{1,0:T(8,128)(2,1)S(1)} %slice.203), channel_id=1, source_target_pairs={{0,16},{1,49},{2,18},{3,51},{4,20},{5,53},{6,22},{7,55},{8,24},{9,... | collective-permute-start | bytes 1032200 | tf_op jit(solution)/shard_map/ppermute | solution.py:54
  102.9 12.1 %collective-permute-start.24 = (bf16[64,2688]{1,0:T(8,128)(2,1)S(1)}, bf16[64,2688]{1,0:T(8,128)(2,1)S(1)}, u32[]{:S(2)}, u32[]{:S(2)}) collective-permute-start(bf16[64,2688]{1,0:T(8,128)(2,1)S(1)} %slice.204), channel_id=1, source_target_pairs={{0,48},{1,17},{2,50},{3,19},{4,52},{5,21},{6,54},{7,23},{8,56},{9,... | collective-permute-start | bytes 1032200 | tf_op jit(solution)/shard_map/ppermute | solution.py:54
  107.0 21.0 %collective-permute-start.28 = (bf16[128,2688]{1,0:T(8,128)(2,1)S(1)}, bf16[128,2688]{1,0:T(8,128)(2,1)S(1)}, u32[]{:S(2)}, u32[]{:S(2)}) collective-permute-start(bf16[128,2688]{1,0:T(8,128)(2,1)S(1)} %pad_maximum_fusion.5.refs_0_.refs_13_), channel_id=1, source_target_pairs={{0,16},{1,49},{2,18},{3,51},{4,20},{5,53},{6,22},{7,55},{8,24},{9,... | collective-permute-start | bytes 2064392 | tf_op jit(solution)/shard_map/ppermute | solution.py:54
  107.0 21.1 %collective-permute-start.29 = (bf16[128,2688]{1,0:T(8,128)(2,1)S(1)}, bf16[128,2688]{1,0:T(8,128)(2,1)S(1)}, u32[]{:S(2)}, u32[]{:S(2)}) collective-permute-start(bf16[128,2688]{1,0:T(8,128)(2,1)S(1)} %pad_maximum_fusion.5.refs_0_.refs_13_), channel_id=1, source_target_pairs={{0,48},{1,17},{2,50},{3,19},{4,52},{5,21},{6,54},{7,23},{8,56},{9,... | collective-permute-start | bytes 2064392 | tf_op jit(solution)/shard_map/ppermute | solution.py:54
  118.3 13.2 %collective-permute-start.26 = (bf16[256,1024]{1,0:T(8,128)(2,1)S(1)}, bf16[256,1024]{1,0:T(8,128)(2,1)S(1)}, u32[]{:S(2)}, u32[]{:S(2)}) collective-permute-start(bf16[256,1024]{1,0:T(8,128)(2,1)S(1)} %bitcast.27), channel_id=1, source_target_pairs={{0,1},{1,0},{2,3},{3,2},{4,5},{5,4},{6,7},{7,6},{8,9},{9,8},{10,11... | collective-permute-start | bytes 1572872 | tf_op jit(solution)/shard_map/ppermute | solution.py:54
  118.4 13.1 %collective-permute-start.27 = (bf16[256,1024]{1,0:T(8,128)(2,1)S(1)}, bf16[256,1024]{1,0:T(8,128)(2,1)S(1)}, u32[]{:S(2)}, u32[]{:S(2)}) collective-permute-start(bf16[256,1024]{1,0:T(8,128)(2,1)S(1)} %bitcast.26), channel_id=1, source_target_pairs={{0,1},{1,0},{2,3},{3,2},{4,5},{5,4},{6,7},{7,6},{8,9},{9,8},{10,11... | collective-permute-start | bytes 1572872 | tf_op jit(solution)/shard_map/ppermute | solution.py:54
  128.0 9.5 %collective-permute-start.33 = (bf16[64,2688]{1,0:T(8,128)(2,1)S(1)}, bf16[64,2688]{1,0:T(8,128)(2,1)S(1)}, u32[]{:S(2)}, u32[]{:S(2)}) collective-permute-start(bf16[64,2688]{1,0:T(8,128)(2,1)S(1)} %slice.208), channel_id=1, source_target_pairs={{0,16},{1,49},{2,18},{3,51},{4,20},{5,53},{6,22},{7,55},{8,24},{9,... | collective-permute-start | bytes 1032200 | tf_op jit(solution)/shard_map/ppermute | solution.py:54
  128.1 8.0 %collective-permute-start.34 = (bf16[64,2688]{1,0:T(8,128)(2,1)S(1)}, bf16[64,2688]{1,0:T(8,128)(2,1)S(1)}, u32[]{:S(2)}, u32[]{:S(2)}) collective-permute-start(bf16[64,2688]{1,0:T(8,128)(2,1)S(1)} %slice.209), channel_id=1, source_target_pairs={{0,48},{1,17},{2,50},{3,19},{4,52},{5,21},{6,54},{7,23},{8,56},{9,... | collective-permute-start | bytes 1032200 | tf_op jit(solution)/shard_map/ppermute | solution.py:54
  132.0 10.5 %collective-permute-start.30 = (bf16[64,2048]{1,0:T(8,128)(2,1)S(1)}, bf16[64,2048]{1,0:T(8,128)(2,1)S(1)}, u32[]{:S(2)}, u32[]{:S(2)}) collective-permute-start(bf16[64,2048]{1,0:T(8,128)(2,1)S(1)} %get-tuple-element.208), channel_id=1, source_target_pairs={{0,4},{1,5},{2,6},{3,7},{4,8},{5,9},{6,10},{7,11},{8,12},{9,13},{1... | collective-permute-start | bytes 786440 | tf_op jit(solution)/shard_map/ppermute | solution.py:54
  132.0 10.4 %collective-permute-start.31 = (bf16[64,2048]{1,0:T(8,128)(2,1)S(1)}, bf16[64,2048]{1,0:T(8,128)(2,1)S(1)}, u32[]{:S(2)}, u32[]{:S(2)}) collective-permute-start(bf16[64,2048]{1,0:T(8,128)(2,1)S(1)} %get-tuple-element.209), channel_id=1, source_target_pairs={{0,8},{1,9},{2,10},{3,11},{4,12},{5,13},{6,14},{7,15},{8,0},{9,1},... | collective-permute-start | bytes 786440 | tf_op jit(solution)/shard_map/ppermute | solution.py:54
  134.1 9.2 %collective-permute-start.32 = (bf16[64,2048]{1,0:T(8,128)(2,1)S(1)}, bf16[64,2048]{1,0:T(8,128)(2,1)S(1)}, u32[]{:S(2)}, u32[]{:S(2)}) collective-permute-start(bf16[64,2048]{1,0:T(8,128)(2,1)S(1)} %get-tuple-element.207), channel_id=1, source_target_pairs={{0,12},{1,13},{2,14},{3,15},{4,0},{5,1},{6,2},{7,3},{8,4},{9,5},{1... | collective-permute-start | bytes 786440 | tf_op jit(solution)/shard_map/ppermute | solution.py:54
  143.5 3.9 %collective-permute-start.36 = (bf16[256,1024]{1,0:T(8,128)(2,1)S(1)}, bf16[256,1024]{1,0:T(8,128)(2,1)S(1)}, u32[]{:S(2)}, u32[]{:S(2)}) collective-permute-start(bf16[256,1024]{1,0:T(8,128)(2,1)S(1)} %bitcast.25), channel_id=1, source_target_pairs={{0,1},{1,0},{2,3},{3,2},{4,5},{5,4},{6,7},{7,6},{8,9},{9,8},{10,11... | collective-permute-start | bytes 1572872 | tf_op jit(solution)/shard_map/ppermute | solution.py:54
  143.8 3.6 %collective-permute-start.37 = (bf16[256,1024]{1,0:T(8,128)(2,1)S(1)}, bf16[256,1024]{1,0:T(8,128)(2,1)S(1)}, u32[]{:S(2)}, u32[]{:S(2)}) collective-permute-start(bf16[256,1024]{1,0:T(8,128)(2,1)S(1)} %bitcast.24), channel_id=1, source_target_pairs={{0,1},{1,0},{2,3},{3,2},{4,5},{5,4},{6,7},{7,6},{8,9},{9,8},{10,11... | collective-permute-start | bytes 1572872 | tf_op jit(solution)/shard_map/ppermute | solution.py:54
  144.3 21.8 %collective-permute-start.35 = (bf16[32,2048]{1,0:T(8,128)(2,1)S(1)}, bf16[32,2048]{1,0:T(8,128)(2,1)S(1)}, u32[]{:S(2)}, u32[]{:S(2)}) collective-permute-start(bf16[32,2048]{1,0:T(8,128)(2,1)S(1)} %slice.239), channel_id=1, source_target_pairs={{0,2},{1,3},{2,0},{3,1},{4,6},{5,7},{6,4},{7,5},{8,10},{9,11},{10,... | collective-permute-start | bytes 393224 | tf_op jit(solution)/shard_map/ppermute | solution.py:54
  147.9 13.5 %collective-permute-start.38 = (bf16[64,2048]{1,0:T(8,128)(2,1)S(1)}, bf16[64,2048]{1,0:T(8,128)(2,1)S(1)}, u32[]{:S(2)}, u32[]{:S(2)}) collective-permute-start(bf16[64,2048]{1,0:T(8,128)(2,1)S(1)} %get-tuple-element.204), channel_id=1, source_target_pairs={{0,4},{1,5},{2,6},{3,7},{4,8},{5,9},{6,10},{7,11},{8,12},{9,13},{1... | collective-permute-start | bytes 786440 | tf_op jit(solution)/shard_map/ppermute | solution.py:54
  148.0 15.4 %collective-permute-start.39 = (bf16[64,2048]{1,0:T(8,128)(2,1)S(1)}, bf16[64,2048]{1,0:T(8,128)(2,1)S(1)}, u32[]{:S(2)}, u32[]{:S(2)}) collective-permute-start(bf16[64,2048]{1,0:T(8,128)(2,1)S(1)} %get-tuple-element.205), channel_id=1, source_target_pairs={{0,8},{1,9},{2,10},{3,11},{4,12},{5,13},{6,14},{7,15},{8,0},{9,1},... | collective-permute-start | bytes 786440 | tf_op jit(solution)/shard_map/ppermute | solution.py:54
  151.8 11.7 %collective-permute-start.40 = (bf16[64,2048]{1,0:T(8,128)(2,1)S(1)}, bf16[64,2048]{1,0:T(8,128)(2,1)S(1)}, u32[]{:S(2)}, u32[]{:S(2)}) collective-permute-start(bf16[64,2048]{1,0:T(8,128)(2,1)S(1)} %get-tuple-element.203), channel_id=1, source_target_pairs={{0,12},{1,13},{2,14},{3,15},{4,0},{5,1},{6,2},{7,3},{8,4},{9,5},{1... | collective-permute-start | bytes 786440 | tf_op jit(solution)/shard_map/ppermute | solution.py:54
  163.6 6.6 %collective-permute-start.41 = (bf16[32,2048]{1,0:T(8,128)(2,1)S(1)}, bf16[32,2048]{1,0:T(8,128)(2,1)S(1)}, u32[]{:S(2)}, u32[]{:S(2)}) collective-permute-start(bf16[32,2048]{1,0:T(8,128)(2,1)S(1)} %slice.249), channel_id=1, source_target_pairs={{0,2},{1,3},{2,0},{3,1},{4,6},{5,7},{6,4},{7,5},{8,10},{9,11},{10,... | collective-permute-start | bytes 393224 | tf_op jit(solution)/shard_map/ppermute | solution.py:54

commit v8 on v7

--- a/solution.py
+++ b/solution.py
@@ -12,11 +12,13 @@
 GATHERS = ((0,), (1,))
 ORDER = (
     "forward 0",
-    "relay 0",
+    "relay_up 0",
     "core 1",
     "forward 1",
+    "relay_down 0",
     "swap 0",
-    "relay 1",
+    "relay_up 1",
+    "relay_down 1",
     "spread 0",
     "swap 1",
     "far 0",
@@ -26,8 +28,8 @@
     "far 1",
     "chip 0",
     "backward 1",
+    "send 1",
     "last 0",
-    "send 1",
     "chip 1",
     "grads",
     "last 1",
@@ -313,16 +315,19 @@
         self.from_up = move(outs[1], dz=-1)
         return outs[0]
 
-    def relay(self, *others):
-        rows = self.rows
+    def relay_up(self, *others):
         down = after(self.from_down, *others)
-        send_up = self.late_up + down[:rows]
+        send_up = self.late_up + down[: self.rows]
         self.last_down = move(send_up, dz=1)
-        up = after(self.from_up, send_up)
-        send_down = self.late_down + up[:rows]
+        self.direct_down = down[self.rows :]
+        return send_up
+
+    def relay_down(self, *others):
+        up = after(self.from_up, *others)
+        send_down = self.late_down + up[: self.rows]
         self.last_up = move(send_down, dz=-1)
-        self.direct = (up[rows:], down[rows:])
-        return send_up, send_down
+        self.direct = (up[self.rows :], self.direct_down)
+        return send_down
 
     def swap(self, *others):
         last_down, last_up = after((self.last_down, self.last_up), *others)

time: 171 us -> 172 us (level)
  waiting for transfers between devices: 73.5 us -> 75.9 us
    ppermute x42, waiting for transfers between devices: 73.5 us -> 75.9 us  [move(): return lax.ppermute(array, ('row', 'col'), pairs)]
  transfers between devices with their start and end apart: 42 -> 42, of which waited for: 21 -> 24; matrix products, arithmetic and copies ran while one was open for 2% -> 2% of each run, Pallas kernels for 13% -> 13%
where the time goes in v8:
time: 172 us
  waiting for transfers between devices  75.9 us (44%)
  starting transfers between devices  59.3 us (34%)
  Pallas kernels  25.6 us (15%)
  local copies, waits for them, and re-layouts  5.75 us (3%)
  other arithmetic  4.22 us (2%)
    ppermute x42, waiting for transfers between devices, move(): return lax.ppermute(array, ('row', 'col'), pairs)  75.9 us
    ppermute x42, starting transfers between devices, move(): return lax.ppermute(array, ('row', 'col'), pairs)  59.3 us
    pallas_call x1, Pallas kernels, weight_grads(): pl.pallas_call(functools.partial(weight_grad_kernel, offsets), in_specs=[...  9.6 us
    pallas_call x2, Pallas kernels, forward(): pl.pallas_call(functools.partial(forward_kernel, offset, rows), in_specs=...  6.86 us
    pallas_call x2, Pallas kernels, backward(): pl.pallas_call(backward_kernel, in_specs=[VMEM] * 6, out_specs=[VMEM] * 4...  6.35 us
    unnamed x12, local copies, waits for them, and re-layouts  4.51 us
  transfers between devices with their start and end apart: 42, of which 24 were waited for; matrix products, arithmetic and copies ran while one was open for 2% of the time, Pallas kernels for 13%

profile of v8, /device:TPU:0, one launch (start us, length us, event | category | flops | bytes accessed | tf_op | source)
XLA Modules:
  0.0 172.0 jit_solution(17966235662329148200)
XLA Ops:
  0.7 1.0 slice_bitcast_fusion
  1.7 3.2 %collective-permute-start = (bf16[2,32,1024]{2,1,0:T(8,128)(2,1)S(1)}, bf16[2,32,1024]{2,1,0:T(8,128)(2,1)S(1)}, u32[]{:S(2)}, u32[]{:S(2)}) collective-permute-start(bf16[2,32,1024]{2,1,0:T(8,128)(2,1)S(1)} %pad_maximum_fusion.13), channel_id=1, source_target_pairs={{0,2},{1,3},{2,0},{3,1},{4,6},{5,7},{6,4},{7,5},{8,10},{9,11},{10,... | collective-permute-start | bytes 393224 | tf_op jit(solution)/shard_map/ppermute | solution.py:56
  4.8 3.5 %collective-permute-done = bf16[2,32,1024]{2,1,0:T(8,128)(2,1)S(1)} collective-permute-done((bf16[2,32,1024]{2,1,0:T(8,128)(2,1)S(1)}, bf16[2,32,1024]{2,1,0:T(8,128)(2,1)S(1)}, u32[]{:S(2)}, u32[]{:S(2)}) %collective-permute-start) | collective-permute-done | bytes 131104 | tf_op jit(solution)/shard_map/ppermute | solution.py:56
  8.4 3.3 %collective-permute-start.1 = (bf16[2,64,1024]{2,1,0:T(8,128)(2,1)S(1)}, bf16[2,64,1024]{2,1,0:T(8,128)(2,1)S(1)}, u32[]{:S(2)}, u32[]{:S(2)}) collective-permute-start(bf16[2,64,1024]{2,1,0:T(8,128)(2,1)S(1)} %pad_maximum_fusion.10), channel_id=1, source_target_pairs={{0,12},{1,13},{2,14},{3,15},{4,0},{5,1},{6,2},{7,3},{8,4},{9,5},{1... | collective-permute-start | bytes 786440 | tf_op jit(solution)/shard_map/ppermute | solution.py:56
  12.3 1.0 collective-permute-start.3
  13.3 3.1 %collective-permute-start.4 = (bf16[2,32,1024]{2,1,0:T(8,128)(2,1)S(1)}, bf16[2,32,1024]{2,1,0:T(8,128)(2,1)S(1)}, u32[]{:S(2)}, u32[]{:S(2)}) collective-permute-start(bf16[2,32,1024]{2,1,0:T(8,128)(2,1)S(1)} %pad_maximum_fusion.14), channel_id=1, source_target_pairs={{0,2},{1,3},{2,0},{3,1},{4,6},{5,7},{6,4},{7,5},{8,10},{9,11},{10,... | collective-permute-start | bytes 393224 | tf_op jit(solution)/shard_map/ppermute | solution.py:56
  16.4 1.5 copy-done
  17.9 1.5 copy-done.1
  19.4 1.5 copy-done.2
  20.9 2.8 %mask_weights.1.refs_4_.refs_5_ = bf16[1024,2688]{1,0:T(8,128)(2,1)S(1)} custom-call(bf16[1024,896]{1,0:T(8,128)(2,1)S(1)} %copy-done, bf16[1024,896]{1,0:T(8,128)(2,1)S(1)} %copy-done.1, bf16[896,1024]{1,0:T(8,128)(2,1)S(1)} %copy-done.2, s32[8,7]{1,0:T(8,128)S(1)} %copy-done.3, s32[8,7]{1,0:T(8,128)S(1)} %copy-done.4, s32[7,8]{1,0:T(8,128)S(1)} %copy-done.5), custom_call_target="tpu_custom_call" | custom-call | flops 2752512 | bytes 11010048 | tf_op jit(solution)/shard_map/mask_weights/pallas_call | solution.py:122
  23.7 1.9 %collective-permute-done.3 = bf16[2,64,1024]{2,1,0:T(8,128)(2,1)S(1)} collective-permute-done((bf16[2,64,1024]{2,1,0:T(8,128)(2,1)S(1)}, bf16[2,64,1024]{2,1,0:T(8,128)(2,1)S(1)}, u32[]{:S(2)}, u32[]{:S(2)}) %collective-permute-start.3) | collective-permute-done | bytes 262176 | tf_op jit(solution)/shard_map/ppermute | solution.py:56
  26.6 1.2 collective-permute-done.6.refs_3_
  28.6 3.4 %forward.2 = (bf16[128,2688]{1,0:T(8,128)(2,1)S(1)}, bf16[128,2688]{1,0:T(8,128)(2,1)S(1)}, bf16[64,2688]{1,0:T(8,128)(2,1)S(1)}, bf16[64,2688]{1,0:T(8,128)(2,1)S(1)}, bf16[128,2688]{1,0:T(8,128)(2,1)S(1)}) custom-call(bf16[4,64,1024]{2,1,0:T(8,128)(2,1)S(1)} %pad_maximum_fusion.6.refs_0_, bf16[4,64,1024]{2,1,0:T(8,128)(2,1)S(1)} %pad_maximum_fusion.7.refs_1_, ...), custom_call_target="tpu_custom_call" | custom-call | flops 1024 | bytes 1024 | tf_op jit(solution)/shard_map/forward/pallas_call | solution.py:160
  32.0 2.0 %collective-permute-start.7 = (bf16[128,2688]{1,0:T(8,128)(2,1)S(1)}, bf16[128,2688]{1,0:T(8,128)(2,1)S(1)}, u32[]{:S(2)}, u32[]{:S(2)}) collective-permute-start(bf16[128,2688]{1,0:T(8,128)(2,1)S(1)} %get-tuple-element.111), channel_id=1, source_target_pairs={{0,16},{1,49},{2,18},{3,51},{4,20},{5,53},{6,22},{7,55},{8,24},{9,... | collective-permute-start | bytes 2064392 | tf_op jit(solution)/shard_map/ppermute | solution.py:56
  34.6 1.4 collective-permute-start.11
  36.1 2.2 %collective-permute-start.9 = (bf16[128,2688]{1,0:T(8,128)(2,1)S(1)}, bf16[128,2688]{1,0:T(8,128)(2,1)S(1)}, u32[]{:S(2)}, u32[]{:S(2)}) collective-permute-start(bf16[128,2688]{1,0:T(8,128)(2,1)S(1)} %get-tuple-element.114), channel_id=1, source_target_pairs={{0,48},{1,17},{2,50},{3,19},{4,52},{5,21},{6,54},{7,23},{8,56},{9,... | collective-permute-start | bytes 2064392 | tf_op jit(solution)/shard_map/ppermute | solution.py:56
  38.3 10.5 %collective-permute-done.7 = bf16[128,2688]{1,0:T(8,128)(2,1)S(1)} collective-permute-done((bf16[128,2688]{1,0:T(8,128)(2,1)S(1)}, bf16[128,2688]{1,0:T(8,128)(2,1)S(1)}, u32[]{:S(2)}, u32[]{:S(2)}) %collective-permute-start.7) | collective-permute-done | bytes 688160 | tf_op jit(solution)/shard_map/ppermute | solution.py:56
  48.9 2.0 %collective-permute-done.12 = bf16[2,64,1024]{2,1,0:T(8,128)(2,1)S(1)} collective-permute-done((bf16[2,64,1024]{2,1,0:T(8,128)(2,1)S(1)}, bf16[2,64,1024]{2,1,0:T(8,128)(2,1)S(1)}, u32[]{:S(2)}, u32[]{:S(2)}) %collective-permute-start.12) | collective-permute-done | bytes 262176 | tf_op jit(solution)/shard_map/ppermute | solution.py:56
  52.1 1.0 collective-permute-done.14.refs_3_.refs_12_
  53.8 3.4 %forward.3 = (bf16[128,2688]{1,0:T(8,128)(2,1)S(1)}, bf16[128,2688]{1,0:T(8,128)(2,1)S(1)}, bf16[64,2688]{1,0:T(8,128)(2,1)S(1)}, bf16[64,2688]{1,0:T(8,128)(2,1)S(1)}, bf16[128,2688]{1,0:T(8,128)(2,1)S(1)}) custom-call(bf16[4,64,1024]{2,1,0:T(8,128)(2,1)S(1)} %pad_maximum_fusion.8.refs_0_.refs_9_, ...), custom_call_target="tpu_custom_call" | custom-call | flops 1024 | bytes 1024 | tf_op jit(solution)/shard_map/forward/pallas_call | solution.py:160
  57.3 3.0 %collective-permute-start.15 = (bf16[64,2688]{1,0:T(8,128)(2,1)S(1)}, bf16[64,2688]{1,0:T(8,128)(2,1)S(1)}, u32[]{:S(2)}, u32[]{:S(2)}) collective-permute-start(bf16[64,2688]{1,0:T(8,128)(2,1)S(1)} %slice_add_fusion.2), channel_id=1, source_target_pairs={{0,48},{1,17},{2,50},{3,19},{4,52},{5,21},{6,54},{7,23},{8,56},{9,... | collective-permute-start | bytes 1032200 | tf_op jit(solution)/shard_map/ppermute | solution.py:56
  60.3 3.2 %collective-permute-start.17 = (bf16[128,2688]{1,0:T(8,128)(2,1)S(1)}, bf16[128,2688]{1,0:T(8,128)(2,1)S(1)}, u32[]{:S(2)}, u32[]{:S(2)}) collective-permute-start(bf16[128,2688]{1,0:T(8,128)(2,1)S(1)} %get-tuple-element.129), channel_id=1, source_target_pairs={{0,48},{1,17},{2,50},{3,19},{4,52},{5,21},{6,54},{7,23},{8,56},{9,... | collective-permute-start | bytes 2064392 | tf_op jit(solution)/shard_map/ppermute | solution.py:56
  63.6 5.2 %collective-permute-done.15 = bf16[64,2688]{1,0:T(8,128)(2,1)S(1)} collective-permute-done((bf16[64,2688]{1,0:T(8,128)(2,1)S(1)}, bf16[64,2688]{1,0:T(8,128)(2,1)S(1)}, u32[]{:S(2)}, u32[]{:S(2)}) %collective-permute-start.15) | collective-permute-done | bytes 344096 | tf_op jit(solution)/shard_map/ppermute | solution.py:56
  69.1 1.8 %collective-permute-start.16 = (bf16[128,2688]{1,0:T(8,128)(2,1)S(1)}, bf16[128,2688]{1,0:T(8,128)(2,1)S(1)}, u32[]{:S(2)}, u32[]{:S(2)}) collective-permute-start(bf16[128,2688]{1,0:T(8,128)(2,1)S(1)} %pad_maximum_fusion.2), channel_id=1, source_target_pairs={{0,64},{1,65},{2,66},{3,67},{4,68},{5,69},{6,70},{7,71},{8,72},{9,... | collective-permute-start | bytes 2064392 | tf_op jit(solution)/shard_map/ppermute | solution.py:56
  70.9 9.0 %collective-permute-done.18 = bf16[128,2688]{1,0:T(8,128)(2,1)S(1)} collective-permute-done((bf16[128,2688]{1,0:T(8,128)(2,1)S(1)}, bf16[128,2688]{1,0:T(8,128)(2,1)S(1)}, u32[]{:S(2)}, u32[]{:S(2)}) %collective-permute-start.18) | collective-permute-done | bytes 688160 | tf_op jit(solution)/shard_map/ppermute | solution.py:56
  80.1 3.4 %collective-permute-start.22 = (bf16[64,2688]{1,0:T(8,128)(2,1)S(1)}, bf16[64,2688]{1,0:T(8,128)(2,1)S(1)}, u32[]{:S(2)}, u32[]{:S(2)}) collective-permute-start(bf16[64,2688]{1,0:T(8,128)(2,1)S(1)} %slice_add_fusion), channel_id=1, source_target_pairs={{0,48},{1,17},{2,50},{3,19},{4,52},{5,21},{6,54},{7,23},{8,56},{9,... | collective-permute-start | bytes 1032200 | tf_op jit(solution)/shard_map/ppermute | solution.py:56
  84.6 0.9 collective-permute-start.20
  85.5 2.4 %collective-permute-start.19 = (bf16[128,2688]{1,0:T(8,128)(2,1)S(1)}, bf16[128,2688]{1,0:T(8,128)(2,1)S(1)}, u32[]{:S(2)}, u32[]{:S(2)}) collective-permute-start(bf16[128,2688]{1,0:T(8,128)(2,1)S(1)} %pad_maximum_fusion.3.refs_0_.refs_4_), channel_id=1, source_target_pairs={{0,48},{1,17},{2,50},{3,19},{4,52},{5,21},{6,54},{7,23},{8,56},{9,... | collective-permute-start | bytes 2064392 | tf_op jit(solution)/shard_map/ppermute | solution.py:56
  87.9 4.0 %collective-permute-done.22 = bf16[64,2688]{1,0:T(8,128)(2,1)S(1)} collective-permute-done((bf16[64,2688]{1,0:T(8,128)(2,1)S(1)}, bf16[64,2688]{1,0:T(8,128)(2,1)S(1)}, u32[]{:S(2)}, u32[]{:S(2)}) %collective-permute-start.22) | collective-permute-done | bytes 344096 | tf_op jit(solution)/shard_map/ppermute | solution.py:56
  92.5 1.6 collective-permute-start.25
  94.0 12.2 %collective-permute-done.20.refs_2_.refs_6_ = bf16[128,2688]{1,0:T(8,128)(2,1)S(1)} collective-permute-done((bf16[128,2688]{1,0:T(8,128)(2,1)S(1)}, bf16[128,2688]{1,0:T(8,128)(2,1)S(1)}, u32[]{:S(2)}, u32[]{:S(2)}) %collective-permute-start.20) | collective-permute-done | bytes 688160 | tf_op jit(solution)/shard_map/ppermute | solution.py:56
  106.4 3.3 %collective-permute-start.24 = (bf16[64,2688]{1,0:T(8,128)(2,1)S(1)}, bf16[64,2688]{1,0:T(8,128)(2,1)S(1)}, u32[]{:S(2)}, u32[]{:S(2)}) collective-permute-start(bf16[64,2688]{1,0:T(8,128)(2,1)S(1)} %slice.204), channel_id=1, source_target_pairs={{0,48},{1,17},{2,50},{3,19},{4,52},{5,21},{6,54},{7,23},{8,56},{9,... | collective-permute-start | bytes 1032200 | tf_op jit(solution)/shard_map/ppermute | solution.py:56
  110.2 3.2 %collective-permute-start.29 = (bf16[128,2688]{1,0:T(8,128)(2,1)S(1)}, bf16[128,2688]{1,0:T(8,128)(2,1)S(1)}, u32[]{:S(2)}, u32[]{:S(2)}) collective-permute-start(bf16[128,2688]{1,0:T(8,128)(2,1)S(1)} %pad_maximum_fusion.5.refs_0_.refs_13_), channel_id=1, source_target_pairs={{0,48},{1,17},{2,50},{3,19},{4,52},{5,21},{6,54},{7,23},{8,56},{9,... | collective-permute-start | bytes 2064392 | tf_op jit(solution)/shard_map/ppermute | solution.py:56
  113.5 4.7 %collective-permute-done.24.refs_4_.refs_8_ = bf16[64,2688]{1,0:T(8,128)(2,1)S(1)} collective-permute-done((bf16[64,2688]{1,0:T(8,128)(2,1)S(1)}, bf16[64,2688]{1,0:T(8,128)(2,1)S(1)}, u32[]{:S(2)}, u32[]{:S(2)}) %collective-permute-start.24) | collective-permute-done | bytes 344096 | tf_op jit(solution)/shard_map/ppermute | solution.py:56
  118.5 3.2 %backward.2 = (bf16[4,64,1024]{2,1,0:T(8,128)(2,1)S(1)}, bf16[4,64,1024]{2,1,0:T(8,128)(2,1)S(1)}, bf16[4,64,1024]{2,1,0:T(8,128)(2,1)S(1)}, bf16[4,64,1024]{2,1,0:T(8,128)(2,1)S(1)}) custom-call(bf16[128,2688]{1,0:T(8,128)(2,1)S(1)} %pad_maximum_fusion.3.refs_0_.refs_4_, bf16[128,2688]{1,0:T(8,128)(2,1)S(1)} %collective-permute-done.19.refs_1_.refs_5_, ...), custom_call_target="tpu_custom_call" | custom-call | flops 2818572288 | bytes 22020096 | tf_op jit(solution)/shard_map/backward/pallas_call | solution.py:188
  122.3 9.4 %collective-permute-done.28.refs_2_.refs_15_ = bf16[128,2688]{1,0:T(8,128)(2,1)S(1)} collective-permute-done((bf16[128,2688]{1,0:T(8,128)(2,1)S(1)}, bf16[128,2688]{1,0:T(8,128)(2,1)S(1)}, u32[]{:S(2)}, u32[]{:S(2)}) %collective-permute-start.28) | collective-permute-done | bytes 688160 | tf_op jit(solution)/shard_map/ppermute | solution.py:56
  131.9 3.3 %collective-permute-start.34 = (bf16[64,2688]{1,0:T(8,128)(2,1)S(1)}, bf16[64,2688]{1,0:T(8,128)(2,1)S(1)}, u32[]{:S(2)}, u32[]{:S(2)}) collective-permute-start(bf16[64,2688]{1,0:T(8,128)(2,1)S(1)} %slice.209), channel_id=1, source_target_pairs={{0,48},{1,17},{2,50},{3,19},{4,52},{5,21},{6,54},{7,23},{8,56},{9,... | collective-permute-start | bytes 1032200 | tf_op jit(solution)/shard_map/ppermute | solution.py:56
  135.8 1.8 %collective-permute-start.31 = (bf16[64,2048]{1,0:T(8,128)(2,1)S(1)}, bf16[64,2048]{1,0:T(8,128)(2,1)S(1)}, u32[]{:S(2)}, u32[]{:S(2)}) collective-permute-start(bf16[64,2048]{1,0:T(8,128)(2,1)S(1)} %get-tuple-element.209), channel_id=1, source_target_pairs={{0,8},{1,9},{2,10},{3,11},{4,12},{5,13},{6,14},{7,15},{8,0},{9,1},... | collective-permute-start | bytes 786440 | tf_op jit(solution)/shard_map/ppermute | solution.py:56
  137.6 1.6 collective-permute-start.32
  139.9 1.6 collective-permute-done.33.refs_3_.refs_16_
  141.6 3.2 %backward.3 = (bf16[4,64,1024]{2,1,0:T(8,128)(2,1)S(1)}, bf16[4,64,1024]{2,1,0:T(8,128)(2,1)S(1)}, bf16[4,64,1024]{2,1,0:T(8,128)(2,1)S(1)}, bf16[4,64,1024]{2,1,0:T(8,128)(2,1)S(1)}) custom-call(bf16[128,2688]{1,0:T(8,128)(2,1)S(1)} %pad_maximum_fusion.5.refs_0_.refs_13_, bf16[128,2688]{1,0:T(8,128)(2,1)S(1)} %collective-permute-done.29.refs_1_.refs_14_, ...), custom_call_target="tpu_custom_call" | custom-call | flops 2818572288 | bytes 22020096 | tf_op jit(solution)/shard_map/backward/pallas_call | solution.py:188
  146.2 0.9 collective-permute-done.32
  148.4 3.4 %collective-permute-start.39 = (bf16[64,2048]{1,0:T(8,128)(2,1)S(1)}, bf16[64,2048]{1,0:T(8,128)(2,1)S(1)}, u32[]{:S(2)}, u32[]{:S(2)}) collective-permute-start(bf16[64,2048]{1,0:T(8,128)(2,1)S(1)} %get-tuple-element.205), channel_id=1, source_target_pairs={{0,8},{1,9},{2,10},{3,11},{4,12},{5,13},{6,14},{7,15},{8,0},{9,1},... | collective-permute-start | bytes 786440 | tf_op jit(solution)/shard_map/ppermute | solution.py:56
  152.2 9.6 %weight_grads.1 = (bf16[1024,896]{1,0:T(8,128)(2,1)}, bf16[1024,896]{1,0:T(8,128)(2,1)}, bf16[896,1024]{1,0:T(8,128)(2,1)}) custom-call(bf16[4,64,1024]{2,1,0:T(8,128)(2,1)S(1)} %pad_maximum_fusion.6.refs_0_, bf16[4,64,1024]{2,1,0:T(8,128)(2,1)S(1)} %pad_maximum_fusion.7.refs_1_, bf16[4,64,1024]{2,1,0:T(8,128)(2,1)S(1)} %collective-permute-done.5.refs_2_, ...), custom_call_target="tpu_custom_call" | custom-call | flops 5637144576 | bytes 44040192 | tf_op jit(solution)/shard_map/weight_grads/pallas_call | solution.py:247
  161.8 2.5 %collective-permute-start.35 = (bf16[32,2048]{1,0:T(8,128)(2,1)S(1)}, bf16[32,2048]{1,0:T(8,128)(2,1)S(1)}, u32[]{:S(2)}, u32[]{:S(2)}) collective-permute-start(bf16[32,2048]{1,0:T(8,128)(2,1)S(1)} %slice.239), channel_id=1, source_target_pairs={{0,2},{1,3},{2,0},{3,1},{4,6},{5,7},{6,4},{7,5},{8,10},{9,11},{10,... | collective-permute-start | bytes 393224 | tf_op jit(solution)/shard_map/ppermute | solution.py:56
  164.5 2.6 %collective-permute-start.41 = (bf16[32,2048]{1,0:T(8,128)(2,1)S(1)}, bf16[32,2048]{1,0:T(8,128)(2,1)S(1)}, u32[]{:S(2)}, u32[]{:S(2)}) collective-permute-start(bf16[32,2048]{1,0:T(8,128)(2,1)S(1)} %slice.249), channel_id=1, source_target_pairs={{0,2},{1,3},{2,0},{3,1},{4,6},{5,7},{6,4},{7,5},{8,10},{9,11},{10,... | collective-permute-start | bytes 393224 | tf_op jit(solution)/shard_map/ppermute | solution.py:56
  167.1 2.0 %collective-permute-done.35 = bf16[32,2048]{1,0:T(8,128)(2,1)S(1)} collective-permute-done((bf16[32,2048]{1,0:T(8,128)(2,1)S(1)}, bf16[32,2048]{1,0:T(8,128)(2,1)S(1)}, u32[]{:S(2)}, u32[]{:S(2)}) %collective-permute-start.35) | collective-permute-done | bytes 131104 | tf_op jit(solution)/shard_map/ppermute | solution.py:56
  169.2 2.0 %collective-permute-done.41 = bf16[32,2048]{1,0:T(8,128)(2,1)S(1)} collective-permute-done((bf16[32,2048]{1,0:T(8,128)(2,1)S(1)}, bf16[32,2048]{1,0:T(8,128)(2,1)S(1)}, u32[]{:S(2)}, u32[]{:S(2)}) %collective-permute-start.41) | collective-permute-done | bytes 131104 | tf_op jit(solution)/shard_map/ppermute | solution.py:56
  (102 shorter events, 14.4 us)
Async XLA Ops:
  0.6 15.8 %copy-start.3 = (s32[8,7]{1,0:T(8,128)S(1)}, s32[8,7]{1,0:T(8,128)}, u32[]{:S(2)}) copy-start(s32[8,7]{1,0:T(8,128)} %refs_18_.1) | copy-start | bytes 676
  0.6 15.8 %copy-start.4 = (s32[8,7]{1,0:T(8,128)S(1)}, s32[8,7]{1,0:T(8,128)}, u32[]{:S(2)}) copy-start(s32[8,7]{1,0:T(8,128)} %refs_19_.1) | copy-start | bytes 676
  0.7 15.7 %copy-start.5 = (s32[7,8]{1,0:T(8,128)S(1)}, s32[7,8]{1,0:T(8,128)}, u32[]{:S(2)}) copy-start(s32[7,8]{1,0:T(8,128)} %refs_20_.1) | copy-start | bytes 676
  1.7 6.7 %collective-permute-start = (bf16[2,32,1024]{2,1,0:T(8,128)(2,1)S(1)}, bf16[2,32,1024]{2,1,0:T(8,128)(2,1)S(1)}, u32[]{:S(2)}, u32[]{:S(2)}) collective-permute-start(bf16[2,32,1024]{2,1,0:T(8,128)(2,1)S(1)} %pad_maximum_fusion.13), channel_id=1, source_target_pairs={{0,2},{1,3},{2,0},{3,1},{4,6},{5,7},{6,4},{7,5},{8,10},{9,11},{10,... | collective-permute-start | bytes 393224 | tf_op jit(solution)/shard_map/ppermute | solution.py:56
  8.4 15.4 %collective-permute-start.1 = (bf16[2,64,1024]{2,1,0:T(8,128)(2,1)S(1)}, bf16[2,64,1024]{2,1,0:T(8,128)(2,1)S(1)}, u32[]{:S(2)}, u32[]{:S(2)}) collective-permute-start(bf16[2,64,1024]{2,1,0:T(8,128)(2,1)S(1)} %pad_maximum_fusion.10), channel_id=1, source_target_pairs={{0,12},{1,13},{2,14},{3,15},{4,0},{5,1},{6,2},{7,3},{8,4},{9,5},{1... | collective-permute-start | bytes 786440 | tf_op jit(solution)/shard_map/ppermute | solution.py:56
  11.7 12.1 %collective-permute-start.2 = (bf16[2,64,1024]{2,1,0:T(8,128)(2,1)S(1)}, bf16[2,64,1024]{2,1,0:T(8,128)(2,1)S(1)}, u32[]{:S(2)}, u32[]{:S(2)}) collective-permute-start(bf16[2,64,1024]{2,1,0:T(8,128)(2,1)S(1)} %pad_maximum_fusion.10), channel_id=1, source_target_pairs={{0,8},{1,9},{2,10},{3,11},{4,12},{5,13},{6,14},{7,15},{8,0},{9,1},... | collective-permute-start | bytes 786440 | tf_op jit(solution)/shard_map/ppermute | solution.py:56
  12.3 13.4 %collective-permute-start.3 = (bf16[2,64,1024]{2,1,0:T(8,128)(2,1)S(1)}, bf16[2,64,1024]{2,1,0:T(8,128)(2,1)S(1)}, u32[]{:S(2)}, u32[]{:S(2)}) collective-permute-start(bf16[2,64,1024]{2,1,0:T(8,128)(2,1)S(1)} %pad_maximum_fusion.10), channel_id=1, source_target_pairs={{0,4},{1,5},{2,6},{3,7},{4,8},{5,9},{6,10},{7,11},{8,12},{9,13},{1... | collective-permute-start | bytes 786440 | tf_op jit(solution)/shard_map/ppermute | solution.py:56
  13.3 10.4 %collective-permute-start.4 = (bf16[2,32,1024]{2,1,0:T(8,128)(2,1)S(1)}, bf16[2,32,1024]{2,1,0:T(8,128)(2,1)S(1)}, u32[]{:S(2)}, u32[]{:S(2)}) collective-permute-start(bf16[2,32,1024]{2,1,0:T(8,128)(2,1)S(1)} %pad_maximum_fusion.14), channel_id=1, source_target_pairs={{0,2},{1,3},{2,0},{3,1},{4,6},{5,7},{6,4},{7,5},{8,10},{9,11},{10,... | collective-permute-start | bytes 393224 | tf_op jit(solution)/shard_map/ppermute | solution.py:56
  16.4 1.5 copy-start
  17.9 1.5 copy-start.1
  19.4 1.5 copy-start.2
  25.9 2.0 %collective-permute-start.6 = (bf16[4,64,1024]{2,1,0:T(8,128)(2,1)S(1)}, bf16[4,64,1024]{2,1,0:T(8,128)(2,1)S(1)}, u32[]{:S(2)}, u32[]{:S(2)}) collective-permute-start(bf16[4,64,1024]{2,1,0:T(8,128)(2,1)S(1)} %pad_maximum_fusion.7.refs_1_), channel_id=1, source_target_pairs={{0,1},{1,0},{2,3},{3,2},{4,5},{5,4},{6,7},{7,6},{8,9},{9,8},{10,11... | collective-permute-start | bytes 1572872 | tf_op jit(solution)/shard_map/ppermute | solution.py:56
  26.0 2.6 %collective-permute-start.5 = (bf16[4,64,1024]{2,1,0:T(8,128)(2,1)S(1)}, bf16[4,64,1024]{2,1,0:T(8,128)(2,1)S(1)}, u32[]{:S(2)}, u32[]{:S(2)}) collective-permute-start(bf16[4,64,1024]{2,1,0:T(8,128)(2,1)S(1)} %pad_maximum_fusion.6.refs_0_), channel_id=1, source_target_pairs={{0,1},{1,0},{2,3},{3,2},{4,5},{5,4},{6,7},{7,6},{8,9},{9,8},{10,11... | collective-permute-start | bytes 1572872 | tf_op jit(solution)/shard_map/ppermute | solution.py:56
  32.0 16.7 %collective-permute-start.7 = (bf16[128,2688]{1,0:T(8,128)(2,1)S(1)}, bf16[128,2688]{1,0:T(8,128)(2,1)S(1)}, u32[]{:S(2)}, u32[]{:S(2)}) collective-permute-start(bf16[128,2688]{1,0:T(8,128)(2,1)S(1)} %get-tuple-element.111), channel_id=1, source_target_pairs={{0,16},{1,49},{2,18},{3,51},{4,20},{5,53},{6,22},{7,55},{8,24},{9,... | collective-permute-start | bytes 2064392 | tf_op jit(solution)/shard_map/ppermute | solution.py:56
  34.0 14.8 %collective-permute-start.10 = (bf16[2,64,1024]{2,1,0:T(8,128)(2,1)S(1)}, bf16[2,64,1024]{2,1,0:T(8,128)(2,1)S(1)}, u32[]{:S(2)}, u32[]{:S(2)}) collective-permute-start(bf16[2,64,1024]{2,1,0:T(8,128)(2,1)S(1)} %pad_maximum_fusion.11), channel_id=1, source_target_pairs={{0,12},{1,13},{2,14},{3,15},{4,0},{5,1},{6,2},{7,3},{8,4},{9,5},{1... | collective-permute-start | bytes 786440 | tf_op jit(solution)/shard_map/ppermute | solution.py:56
  34.6 14.2 %collective-permute-start.11 = (bf16[2,64,1024]{2,1,0:T(8,128)(2,1)S(1)}, bf16[2,64,1024]{2,1,0:T(8,128)(2,1)S(1)}, u32[]{:S(2)}, u32[]{:S(2)}) collective-permute-start(bf16[2,64,1024]{2,1,0:T(8,128)(2,1)S(1)} %pad_maximum_fusion.11), channel_id=1, source_target_pairs={{0,8},{1,9},{2,10},{3,11},{4,12},{5,13},{6,14},{7,15},{8,0},{9,1},... | collective-permute-start | bytes 786440 | tf_op jit(solution)/shard_map/ppermute | solution.py:56
  36.1 14.8 %collective-permute-start.12 = (bf16[2,64,1024]{2,1,0:T(8,128)(2,1)S(1)}, bf16[2,64,1024]{2,1,0:T(8,128)(2,1)S(1)}, u32[]{:S(2)}, u32[]{:S(2)}) collective-permute-start(bf16[2,64,1024]{2,1,0:T(8,128)(2,1)S(1)} %pad_maximum_fusion.11), channel_id=1, source_target_pairs={{0,4},{1,5},{2,6},{3,7},{4,8},{5,9},{6,10},{7,11},{8,12},{9,13},{1... | collective-permute-start | bytes 786440 | tf_op jit(solution)/shard_map/ppermute | solution.py:56
  36.1 21.2 %collective-permute-start.9 = (bf16[128,2688]{1,0:T(8,128)(2,1)S(1)}, bf16[128,2688]{1,0:T(8,128)(2,1)S(1)}, u32[]{:S(2)}, u32[]{:S(2)}) collective-permute-start(bf16[128,2688]{1,0:T(8,128)(2,1)S(1)} %get-tuple-element.114), channel_id=1, source_target_pairs={{0,48},{1,17},{2,50},{3,19},{4,52},{5,21},{6,54},{7,23},{8,56},{9,... | collective-permute-start | bytes 2064392 | tf_op jit(solution)/shard_map/ppermute | solution.py:56
  51.1 2.0 %collective-permute-start.14 = (bf16[4,64,1024]{2,1,0:T(8,128)(2,1)S(1)}, bf16[4,64,1024]{2,1,0:T(8,128)(2,1)S(1)}, u32[]{:S(2)}, u32[]{:S(2)}) collective-permute-start(bf16[4,64,1024]{2,1,0:T(8,128)(2,1)S(1)} %pad_maximum_fusion.9.refs_1_.refs_10_), channel_id=1, source_target_pairs={{0,1},{1,0},{2,3},{3,2},{4,5},{5,4},{6,7},{7,6},{8,9},{9,8},{10,11... | collective-permute-start | bytes 1572872 | tf_op jit(solution)/shard_map/ppermute | solution.py:56
  51.3 2.5 %collective-permute-start.13 = (bf16[4,64,1024]{2,1,0:T(8,128)(2,1)S(1)}, bf16[4,64,1024]{2,1,0:T(8,128)(2,1)S(1)}, u32[]{:S(2)}, u32[]{:S(2)}) collective-permute-start(bf16[4,64,1024]{2,1,0:T(8,128)(2,1)S(1)} %pad_maximum_fusion.8.refs_0_.refs_9_), channel_id=1, source_target_pairs={{0,1},{1,0},{2,3},{3,2},{4,5},{5,4},{6,7},{7,6},{8,9},{9,8},{10,11... | collective-permute-start | bytes 1572872 | tf_op jit(solution)/shard_map/ppermute | solution.py:56
  51.8 11.7 %collective-permute-start.8 = (bf16[64,2688]{1,0:T(8,128)(2,1)S(1)}, bf16[64,2688]{1,0:T(8,128)(2,1)S(1)}, u32[]{:S(2)}, u32[]{:S(2)}) collective-permute-start(bf16[64,2688]{1,0:T(8,128)(2,1)S(1)} %slice_add_fusion.3), channel_id=1, source_target_pairs={{0,16},{1,49},{2,18},{3,51},{4,20},{5,53},{6,22},{7,55},{8,24},{9,... | collective-permute-start | bytes 1032200 | tf_op jit(solution)/shard_map/ppermute | solution.py:56
  57.3 11.4 %collective-permute-start.15 = (bf16[64,2688]{1,0:T(8,128)(2,1)S(1)}, bf16[64,2688]{1,0:T(8,128)(2,1)S(1)}, u32[]{:S(2)}, u32[]{:S(2)}) collective-permute-start(bf16[64,2688]{1,0:T(8,128)(2,1)S(1)} %slice_add_fusion.2), channel_id=1, source_target_pairs={{0,48},{1,17},{2,50},{3,19},{4,52},{5,21},{6,54},{7,23},{8,56},{9,... | collective-permute-start | bytes 1032200 | tf_op jit(solution)/shard_map/ppermute | solution.py:56
  60.3 19.6 %collective-permute-start.18 = (bf16[128,2688]{1,0:T(8,128)(2,1)S(1)}, bf16[128,2688]{1,0:T(8,128)(2,1)S(1)}, u32[]{:S(2)}, u32[]{:S(2)}) collective-permute-start(bf16[128,2688]{1,0:T(8,128)(2,1)S(1)} %get-tuple-element.124), channel_id=1, source_target_pairs={{0,16},{1,49},{2,18},{3,51},{4,20},{5,53},{6,22},{7,55},{8,24},{9,... | collective-permute-start | bytes 2064392 | tf_op jit(solution)/shard_map/ppermute | solution.py:56
  60.3 19.7 %collective-permute-start.17 = (bf16[128,2688]{1,0:T(8,128)(2,1)S(1)}, bf16[128,2688]{1,0:T(8,128)(2,1)S(1)}, u32[]{:S(2)}, u32[]{:S(2)}) collective-permute-start(bf16[128,2688]{1,0:T(8,128)(2,1)S(1)} %get-tuple-element.129), channel_id=1, source_target_pairs={{0,48},{1,17},{2,50},{3,19},{4,52},{5,21},{6,54},{7,23},{8,56},{9,... | collective-permute-start | bytes 2064392 | tf_op jit(solution)/shard_map/ppermute | solution.py:56
  69.1 15.0 %collective-permute-start.16 = (bf16[128,2688]{1,0:T(8,128)(2,1)S(1)}, bf16[128,2688]{1,0:T(8,128)(2,1)S(1)}, u32[]{:S(2)}, u32[]{:S(2)}) collective-permute-start(bf16[128,2688]{1,0:T(8,128)(2,1)S(1)} %pad_maximum_fusion.2), channel_id=1, source_target_pairs={{0,64},{1,65},{2,66},{3,67},{4,68},{5,69},{6,70},{7,71},{8,72},{9,... | collective-permute-start | bytes 2064392 | tf_op jit(solution)/shard_map/ppermute | solution.py:56
  80.0 12.2 %collective-permute-start.21 = (bf16[64,2688]{1,0:T(8,128)(2,1)S(1)}, bf16[64,2688]{1,0:T(8,128)(2,1)S(1)}, u32[]{:S(2)}, u32[]{:S(2)}) collective-permute-start(bf16[64,2688]{1,0:T(8,128)(2,1)S(1)} %slice_add_fusion.1), channel_id=1, source_target_pairs={{0,16},{1,49},{2,18},{3,51},{4,20},{5,53},{6,22},{7,55},{8,24},{9,... | collective-permute-start | bytes 1032200 | tf_op jit(solution)/shard_map/ppermute | solution.py:56
  80.1 11.8 %collective-permute-start.22 = (bf16[64,2688]{1,0:T(8,128)(2,1)S(1)}, bf16[64,2688]{1,0:T(8,128)(2,1)S(1)}, u32[]{:S(2)}, u32[]{:S(2)}) collective-permute-start(bf16[64,2688]{1,0:T(8,128)(2,1)S(1)} %slice_add_fusion), channel_id=1, source_target_pairs={{0,48},{1,17},{2,50},{3,19},{4,52},{5,21},{6,54},{7,23},{8,56},{9,... | collective-permute-start | bytes 1032200 | tf_op jit(solution)/shard_map/ppermute | solution.py:56
  84.6 21.6 %collective-permute-start.20 = (bf16[128,2688]{1,0:T(8,128)(2,1)S(1)}, bf16[128,2688]{1,0:T(8,128)(2,1)S(1)}, u32[]{:S(2)}, u32[]{:S(2)}) collective-permute-start(bf16[128,2688]{1,0:T(8,128)(2,1)S(1)} %pad_maximum_fusion.3.refs_0_.refs_4_), channel_id=1, source_target_pairs={{0,16},{1,49},{2,18},{3,51},{4,20},{5,53},{6,22},{7,55},{8,24},{9,... | collective-permute-start | bytes 2064392 | tf_op jit(solution)/shard_map/ppermute | solution.py:56
  85.5 20.9 %collective-permute-start.19 = (bf16[128,2688]{1,0:T(8,128)(2,1)S(1)}, bf16[128,2688]{1,0:T(8,128)(2,1)S(1)}, u32[]{:S(2)}, u32[]{:S(2)}) collective-permute-start(bf16[128,2688]{1,0:T(8,128)(2,1)S(1)} %pad_maximum_fusion.3.refs_0_.refs_4_), channel_id=1, source_target_pairs={{0,48},{1,17},{2,50},{3,19},{4,52},{5,21},{6,54},{7,23},{8,56},{9,... | collective-permute-start | bytes 2064392 | tf_op jit(solution)/shard_map/ppermute | solution.py:56
  92.5 17.2 %collective-permute-start.25 = (bf16[128,2688]{1,0:T(8,128)(2,1)S(1)}, bf16[128,2688]{1,0:T(8,128)(2,1)S(1)}, u32[]{:S(2)}, u32[]{:S(2)}) collective-permute-start(bf16[128,2688]{1,0:T(8,128)(2,1)S(1)} %pad_maximum_fusion.4), channel_id=1, source_target_pairs={{0,64},{1,65},{2,66},{3,67},{4,68},{5,69},{6,70},{7,71},{8,72},{9,... | collective-permute-start | bytes 2064392 | tf_op jit(solution)/shard_map/ppermute | solution.py:56
  106.3 12.3 %collective-permute-start.23 = (bf16[64,2688]{1,0:T(8,128)(2,1)S(1)}, bf16[64,2688]{1,0:T(8,128)(2,1)S(1)}, u32[]{:S(2)}, u32[]{:S(2)}) collective-permute-start(bf16[64,2688]{1,0:T(8,128)(2,1)S(1)} %slice.203), channel_id=1, source_target_pairs={{0,16},{1,49},{2,18},{3,51},{4,20},{5,53},{6,22},{7,55},{8,24},{9,... | collective-permute-start | bytes 1032200 | tf_op jit(solution)/shard_map/ppermute | solution.py:56
  106.4 11.8 %collective-permute-start.24 = (bf16[64,2688]{1,0:T(8,128)(2,1)S(1)}, bf16[64,2688]{1,0:T(8,128)(2,1)S(1)}, u32[]{:S(2)}, u32[]{:S(2)}) collective-permute-start(bf16[64,2688]{1,0:T(8,128)(2,1)S(1)} %slice.204), channel_id=1, source_target_pairs={{0,48},{1,17},{2,50},{3,19},{4,52},{5,21},{6,54},{7,23},{8,56},{9,... | collective-permute-start | bytes 1032200 | tf_op jit(solution)/shard_map/ppermute | solution.py:56
  110.2 21.6 %collective-permute-start.28 = (bf16[128,2688]{1,0:T(8,128)(2,1)S(1)}, bf16[128,2688]{1,0:T(8,128)(2,1)S(1)}, u32[]{:S(2)}, u32[]{:S(2)}) collective-permute-start(bf16[128,2688]{1,0:T(8,128)(2,1)S(1)} %pad_maximum_fusion.5.refs_0_.refs_13_), channel_id=1, source_target_pairs={{0,16},{1,49},{2,18},{3,51},{4,20},{5,53},{6,22},{7,55},{8,24},{9,... | collective-permute-start | bytes 2064392 | tf_op jit(solution)/shard_map/ppermute | solution.py:56
  110.2 21.6 %collective-permute-start.29 = (bf16[128,2688]{1,0:T(8,128)(2,1)S(1)}, bf16[128,2688]{1,0:T(8,128)(2,1)S(1)}, u32[]{:S(2)}, u32[]{:S(2)}) collective-permute-start(bf16[128,2688]{1,0:T(8,128)(2,1)S(1)} %pad_maximum_fusion.5.refs_0_.refs_13_), channel_id=1, source_target_pairs={{0,48},{1,17},{2,50},{3,19},{4,52},{5,21},{6,54},{7,23},{8,56},{9,... | collective-permute-start | bytes 2064392 | tf_op jit(solution)/shard_map/ppermute | solution.py:56
  121.7 13.5 %collective-permute-start.26 = (bf16[256,1024]{1,0:T(8,128)(2,1)S(1)}, bf16[256,1024]{1,0:T(8,128)(2,1)S(1)}, u32[]{:S(2)}, u32[]{:S(2)}) collective-permute-start(bf16[256,1024]{1,0:T(8,128)(2,1)S(1)} %bitcast.27), channel_id=1, source_target_pairs={{0,1},{1,0},{2,3},{3,2},{4,5},{5,4},{6,7},{7,6},{8,9},{9,8},{10,11... | collective-permute-start | bytes 1572872 | tf_op jit(solution)/shard_map/ppermute | solution.py:56
  121.8 13.4 %collective-permute-start.27 = (bf16[256,1024]{1,0:T(8,128)(2,1)S(1)}, bf16[256,1024]{1,0:T(8,128)(2,1)S(1)}, u32[]{:S(2)}, u32[]{:S(2)}) collective-permute-start(bf16[256,1024]{1,0:T(8,128)(2,1)S(1)} %bitcast.25), channel_id=1, source_target_pairs={{0,1},{1,0},{2,3},{3,2},{4,5},{5,4},{6,7},{7,6},{8,9},{9,8},{10,11... | collective-permute-start | bytes 1572872 | tf_op jit(solution)/shard_map/ppermute | solution.py:56
  131.8 9.8 %collective-permute-start.33 = (bf16[64,2688]{1,0:T(8,128)(2,1)S(1)}, bf16[64,2688]{1,0:T(8,128)(2,1)S(1)}, u32[]{:S(2)}, u32[]{:S(2)}) collective-permute-start(bf16[64,2688]{1,0:T(8,128)(2,1)S(1)} %slice.208), channel_id=1, source_target_pairs={{0,16},{1,49},{2,18},{3,51},{4,20},{5,53},{6,22},{7,55},{8,24},{9,... | collective-permute-start | bytes 1032200 | tf_op jit(solution)/shard_map/ppermute | solution.py:56
  131.9 8.0 %collective-permute-start.34 = (bf16[64,2688]{1,0:T(8,128)(2,1)S(1)}, bf16[64,2688]{1,0:T(8,128)(2,1)S(1)}, u32[]{:S(2)}, u32[]{:S(2)}) collective-permute-start(bf16[64,2688]{1,0:T(8,128)(2,1)S(1)} %slice.209), channel_id=1, source_target_pairs={{0,48},{1,17},{2,50},{3,19},{4,52},{5,21},{6,54},{7,23},{8,56},{9,... | collective-permute-start | bytes 1032200 | tf_op jit(solution)/shard_map/ppermute | solution.py:56
  135.7 10.5 %collective-permute-start.30 = (bf16[64,2048]{1,0:T(8,128)(2,1)S(1)}, bf16[64,2048]{1,0:T(8,128)(2,1)S(1)}, u32[]{:S(2)}, u32[]{:S(2)}) collective-permute-start(bf16[64,2048]{1,0:T(8,128)(2,1)S(1)} %get-tuple-element.208), channel_id=1, source_target_pairs={{0,4},{1,5},{2,6},{3,7},{4,8},{5,9},{6,10},{7,11},{8,12},{9,13},{1... | collective-permute-start | bytes 786440 | tf_op jit(solution)/shard_map/ppermute | solution.py:56
  135.8 10.4 %collective-permute-start.31 = (bf16[64,2048]{1,0:T(8,128)(2,1)S(1)}, bf16[64,2048]{1,0:T(8,128)(2,1)S(1)}, u32[]{:S(2)}, u32[]{:S(2)}) collective-permute-start(bf16[64,2048]{1,0:T(8,128)(2,1)S(1)} %get-tuple-element.209), channel_id=1, source_target_pairs={{0,8},{1,9},{2,10},{3,11},{4,12},{5,13},{6,14},{7,15},{8,0},{9,1},... | collective-permute-start | bytes 786440 | tf_op jit(solution)/shard_map/ppermute | solution.py:56
  137.6 9.5 %collective-permute-start.32 = (bf16[64,2048]{1,0:T(8,128)(2,1)S(1)}, bf16[64,2048]{1,0:T(8,128)(2,1)S(1)}, u32[]{:S(2)}, u32[]{:S(2)}) collective-permute-start(bf16[64,2048]{1,0:T(8,128)(2,1)S(1)} %get-tuple-element.207), channel_id=1, source_target_pairs={{0,12},{1,13},{2,14},{3,15},{4,0},{5,1},{6,2},{7,3},{8,4},{9,5},{1... | collective-permute-start | bytes 786440 | tf_op jit(solution)/shard_map/ppermute | solution.py:56
  144.8 2.5 %collective-permute-start.36 = (bf16[256,1024]{1,0:T(8,128)(2,1)S(1)}, bf16[256,1024]{1,0:T(8,128)(2,1)S(1)}, u32[]{:S(2)}, u32[]{:S(2)}) collective-permute-start(bf16[256,1024]{1,0:T(8,128)(2,1)S(1)} %bitcast.26), channel_id=1, source_target_pairs={{0,1},{1,0},{2,3},{3,2},{4,5},{5,4},{6,7},{7,6},{8,9},{9,8},{10,11... | collective-permute-start | bytes 1572872 | tf_op jit(solution)/shard_map/ppermute | solution.py:56
  144.8 2.6 %collective-permute-start.37 = (bf16[256,1024]{1,0:T(8,128)(2,1)S(1)}, bf16[256,1024]{1,0:T(8,128)(2,1)S(1)}, u32[]{:S(2)}, u32[]{:S(2)}) collective-permute-start(bf16[256,1024]{1,0:T(8,128)(2,1)S(1)} %bitcast.24), channel_id=1, source_target_pairs={{0,1},{1,0},{2,3},{3,2},{4,5},{5,4},{6,7},{7,6},{8,9},{9,8},{10,11... | collective-permute-start | bytes 1572872 | tf_op jit(solution)/shard_map/ppermute | solution.py:56
  148.0 16.3 %collective-permute-start.38 = (bf16[64,2048]{1,0:T(8,128)(2,1)S(1)}, bf16[64,2048]{1,0:T(8,128)(2,1)S(1)}, u32[]{:S(2)}, u32[]{:S(2)}) collective-permute-start(bf16[64,2048]{1,0:T(8,128)(2,1)S(1)} %get-tuple-element.204), channel_id=1, source_target_pairs={{0,4},{1,5},{2,6},{3,7},{4,8},{5,9},{6,10},{7,11},{8,12},{9,13},{1... | collective-permute-start | bytes 786440 | tf_op jit(solution)/shard_map/ppermute | solution.py:56
  148.4 16.0 %collective-permute-start.39 = (bf16[64,2048]{1,0:T(8,128)(2,1)S(1)}, bf16[64,2048]{1,0:T(8,128)(2,1)S(1)}, u32[]{:S(2)}, u32[]{:S(2)}) collective-permute-start(bf16[64,2048]{1,0:T(8,128)(2,1)S(1)} %get-tuple-element.205), channel_id=1, source_target_pairs={{0,8},{1,9},{2,10},{3,11},{4,12},{5,13},{6,14},{7,15},{8,0},{9,1},... | collective-permute-start | bytes 786440 | tf_op jit(solution)/shard_map/ppermute | solution.py:56
  151.8 12.6 %collective-permute-start.40 = (bf16[64,2048]{1,0:T(8,128)(2,1)S(1)}, bf16[64,2048]{1,0:T(8,128)(2,1)S(1)}, u32[]{:S(2)}, u32[]{:S(2)}) collective-permute-start(bf16[64,2048]{1,0:T(8,128)(2,1)S(1)} %get-tuple-element.203), channel_id=1, source_target_pairs={{0,12},{1,13},{2,14},{3,15},{4,0},{5,1},{6,2},{7,3},{8,4},{9,5},{1... | collective-permute-start | bytes 786440 | tf_op jit(solution)/shard_map/ppermute | solution.py:56
  161.8 7.3 %collective-permute-start.35 = (bf16[32,2048]{1,0:T(8,128)(2,1)S(1)}, bf16[32,2048]{1,0:T(8,128)(2,1)S(1)}, u32[]{:S(2)}, u32[]{:S(2)}) collective-permute-start(bf16[32,2048]{1,0:T(8,128)(2,1)S(1)} %slice.239), channel_id=1, source_target_pairs={{0,2},{1,3},{2,0},{3,1},{4,6},{5,7},{6,4},{7,5},{8,10},{9,11},{10,... | collective-permute-start | bytes 393224 | tf_op jit(solution)/shard_map/ppermute | solution.py:56
  164.5 6.7 %collective-permute-start.41 = (bf16[32,2048]{1,0:T(8,128)(2,1)S(1)}, bf16[32,2048]{1,0:T(8,128)(2,1)S(1)}, u32[]{:S(2)}, u32[]{:S(2)}) collective-permute-start(bf16[32,2048]{1,0:T(8,128)(2,1)S(1)} %slice.249), channel_id=1, source_target_pairs={{0,2},{1,3},{2,0},{3,1},{4,6},{5,7},{6,4},{7,5},{8,10},{9,11},{10,... | collective-permute-start | bytes 393224 | tf_op jit(solution)/shard_map/ppermute | solution.py:56

commit v9 on v7

--- a/solution.py
+++ b/solution.py
@@ -26,8 +26,8 @@
     "far 1",
     "chip 0",
     "backward 1",
+    "send 1",
     "last 0",
-    "send 1",
     "chip 1",
     "grads",
     "last 1",

time: 171 us -> 169 us (0.988)
  waiting for transfers between devices: 73.5 us -> 71.5 us
    ppermute x42, waiting for transfers between devices: 73.5 us -> 71.5 us  [move(): return lax.ppermute(array, ('row', 'col'), pairs)]
where the time goes in v9:
time: 169 us; the launch traced here: 168 us
  waiting for transfers between devices  71.5 us (42%)
  starting transfers between devices  60.2 us (36%)
  Pallas kernels  25.6 us (15%)
  local copies, waits for them, and re-layouts  5.75 us (3%)
  other arithmetic  4.19 us (2%)
    ppermute x42, waiting for transfers between devices, move(): return lax.ppermute(array, ('row', 'col'), pairs)  71.5 us
    ppermute x42, starting transfers between devices, move(): return lax.ppermute(array, ('row', 'col'), pairs)  60.2 us
    pallas_call x1, Pallas kernels, weight_grads(): pl.pallas_call(functools.partial(weight_grad_kernel, offsets), in_specs=[...  9.6 us
    pallas_call x2, Pallas kernels, forward(): pl.pallas_call(functools.partial(forward_kernel, offset, rows), in_specs=...  6.86 us
    pallas_call x2, Pallas kernels, backward(): pl.pallas_call(backward_kernel, in_specs=[VMEM] * 6, out_specs=[VMEM] * 4...  6.35 us
    unnamed x12, local copies, waits for them, and re-layouts  4.51 us
  transfers between devices with their start and end apart: 42, of which 21 were waited for; matrix products, arithmetic and copies ran while one was open for 2% of the time, Pallas kernels for 13%

profile of v9, /device:TPU:0, one launch (start us, length us, event | category | flops | bytes accessed | tf_op | source)
XLA Modules:
  0.0 168.3 jit_solution(9556063698591658522)
XLA Ops:
  0.7 1.0 slice_bitcast_fusion
  1.7 3.2 %collective-permute-start = (bf16[2,32,1024]{2,1,0:T(8,128)(2,1)S(1)}, bf16[2,32,1024]{2,1,0:T(8,128)(2,1)S(1)}, u32[]{:S(2)}, u32[]{:S(2)}) collective-permute-start(bf16[2,32,1024]{2,1,0:T(8,128)(2,1)S(1)} %pad_maximum_fusion.13), channel_id=1, source_target_pairs={{0,2},{1,3},{2,0},{3,1},{4,6},{5,7},{6,4},{7,5},{8,10},{9,11},{10,... | collective-permute-start | bytes 393224 | tf_op jit(solution)/shard_map/ppermute | solution.py:54
  4.8 3.5 %collective-permute-done = bf16[2,32,1024]{2,1,0:T(8,128)(2,1)S(1)} collective-permute-done((bf16[2,32,1024]{2,1,0:T(8,128)(2,1)S(1)}, bf16[2,32,1024]{2,1,0:T(8,128)(2,1)S(1)}, u32[]{:S(2)}, u32[]{:S(2)}) %collective-permute-start) | collective-permute-done | bytes 131104 | tf_op jit(solution)/shard_map/ppermute | solution.py:54
  8.4 3.3 %collective-permute-start.1 = (bf16[2,64,1024]{2,1,0:T(8,128)(2,1)S(1)}, bf16[2,64,1024]{2,1,0:T(8,128)(2,1)S(1)}, u32[]{:S(2)}, u32[]{:S(2)}) collective-permute-start(bf16[2,64,1024]{2,1,0:T(8,128)(2,1)S(1)} %pad_maximum_fusion.10), channel_id=1, source_target_pairs={{0,12},{1,13},{2,14},{3,15},{4,0},{5,1},{6,2},{7,3},{8,4},{9,5},{1... | collective-permute-start | bytes 786440 | tf_op jit(solution)/shard_map/ppermute | solution.py:54
  12.3 1.0 collective-permute-start.3
  13.3 3.1 %collective-permute-start.4 = (bf16[2,32,1024]{2,1,0:T(8,128)(2,1)S(1)}, bf16[2,32,1024]{2,1,0:T(8,128)(2,1)S(1)}, u32[]{:S(2)}, u32[]{:S(2)}) collective-permute-start(bf16[2,32,1024]{2,1,0:T(8,128)(2,1)S(1)} %pad_maximum_fusion.14), channel_id=1, source_target_pairs={{0,2},{1,3},{2,0},{3,1},{4,6},{5,7},{6,4},{7,5},{8,10},{9,11},{10,... | collective-permute-start | bytes 393224 | tf_op jit(solution)/shard_map/ppermute | solution.py:54
  16.4 1.5 copy-done
  17.9 1.5 copy-done.1
  19.4 1.5 copy-done.2
  20.9 2.8 %mask_weights.1.refs_4_.refs_5_ = bf16[1024,2688]{1,0:T(8,128)(2,1)S(1)} custom-call(bf16[1024,896]{1,0:T(8,128)(2,1)S(1)} %copy-done, bf16[1024,896]{1,0:T(8,128)(2,1)S(1)} %copy-done.1, bf16[896,1024]{1,0:T(8,128)(2,1)S(1)} %copy-done.2, s32[8,7]{1,0:T(8,128)S(1)} %copy-done.3, s32[8,7]{1,0:T(8,128)S(1)} %copy-done.4, s32[7,8]{1,0:T(8,128)S(1)} %copy-done.5), custom_call_target="tpu_custom_call" | custom-call | flops 2752512 | bytes 11010048 | tf_op jit(solution)/shard_map/mask_weights/pallas_call | solution.py:120
  23.7 1.9 %collective-permute-done.3 = bf16[2,64,1024]{2,1,0:T(8,128)(2,1)S(1)} collective-permute-done((bf16[2,64,1024]{2,1,0:T(8,128)(2,1)S(1)}, bf16[2,64,1024]{2,1,0:T(8,128)(2,1)S(1)}, u32[]{:S(2)}, u32[]{:S(2)}) %collective-permute-start.3) | collective-permute-done | bytes 262176 | tf_op jit(solution)/shard_map/ppermute | solution.py:54
  26.6 1.2 collective-permute-done.6.refs_3_
  28.6 3.4 %forward.2 = (bf16[128,2688]{1,0:T(8,128)(2,1)S(1)}, bf16[128,2688]{1,0:T(8,128)(2,1)S(1)}, bf16[64,2688]{1,0:T(8,128)(2,1)S(1)}, bf16[64,2688]{1,0:T(8,128)(2,1)S(1)}, bf16[128,2688]{1,0:T(8,128)(2,1)S(1)}) custom-call(bf16[4,64,1024]{2,1,0:T(8,128)(2,1)S(1)} %pad_maximum_fusion.6.refs_0_, bf16[4,64,1024]{2,1,0:T(8,128)(2,1)S(1)} %pad_maximum_fusion.7.refs_1_, ...), custom_call_target="tpu_custom_call" | custom-call | flops 1024 | bytes 1024 | tf_op jit(solution)/shard_map/forward/pallas_call | solution.py:158
  32.0 2.0 %collective-permute-start.7 = (bf16[128,2688]{1,0:T(8,128)(2,1)S(1)}, bf16[128,2688]{1,0:T(8,128)(2,1)S(1)}, u32[]{:S(2)}, u32[]{:S(2)}) collective-permute-start(bf16[128,2688]{1,0:T(8,128)(2,1)S(1)} %get-tuple-element.111), channel_id=1, source_target_pairs={{0,16},{1,49},{2,18},{3,51},{4,20},{5,53},{6,22},{7,55},{8,24},{9,... | collective-permute-start | bytes 2064392 | tf_op jit(solution)/shard_map/ppermute | solution.py:54
  34.6 1.4 collective-permute-start.12
  36.1 2.2 %collective-permute-start.9 = (bf16[128,2688]{1,0:T(8,128)(2,1)S(1)}, bf16[128,2688]{1,0:T(8,128)(2,1)S(1)}, u32[]{:S(2)}, u32[]{:S(2)}) collective-permute-start(bf16[128,2688]{1,0:T(8,128)(2,1)S(1)} %get-tuple-element.114), channel_id=1, source_target_pairs={{0,48},{1,17},{2,50},{3,19},{4,52},{5,21},{6,54},{7,23},{8,56},{9,... | collective-permute-start | bytes 2064392 | tf_op jit(solution)/shard_map/ppermute | solution.py:54
  38.3 10.5 %collective-permute-done.7 = bf16[128,2688]{1,0:T(8,128)(2,1)S(1)} collective-permute-done((bf16[128,2688]{1,0:T(8,128)(2,1)S(1)}, bf16[128,2688]{1,0:T(8,128)(2,1)S(1)}, u32[]{:S(2)}, u32[]{:S(2)}) %collective-permute-start.7) | collective-permute-done | bytes 688160 | tf_op jit(solution)/shard_map/ppermute | solution.py:54
  48.8 2.3 %collective-permute-done.9 = bf16[128,2688]{1,0:T(8,128)(2,1)S(1)} collective-permute-done((bf16[128,2688]{1,0:T(8,128)(2,1)S(1)}, bf16[128,2688]{1,0:T(8,128)(2,1)S(1)}, u32[]{:S(2)}, u32[]{:S(2)}) %collective-permute-start.9) | collective-permute-done | bytes 688160 | tf_op jit(solution)/shard_map/ppermute | solution.py:54
  51.4 1.2 collective-permute-start.15
  52.8 3.1 %collective-permute-start.10 = (bf16[64,2688]{1,0:T(8,128)(2,1)S(1)}, bf16[64,2688]{1,0:T(8,128)(2,1)S(1)}, u32[]{:S(2)}, u32[]{:S(2)}) collective-permute-start(bf16[64,2688]{1,0:T(8,128)(2,1)S(1)} %slice_add_fusion.2), channel_id=1, source_target_pairs={{0,48},{1,17},{2,50},{3,19},{4,52},{5,21},{6,54},{7,23},{8,56},{9,... | collective-permute-start | bytes 1032200 | tf_op jit(solution)/shard_map/ppermute | solution.py:54
  55.9 3.4 %forward.3 = (bf16[128,2688]{1,0:T(8,128)(2,1)S(1)}, bf16[128,2688]{1,0:T(8,128)(2,1)S(1)}, bf16[64,2688]{1,0:T(8,128)(2,1)S(1)}, bf16[64,2688]{1,0:T(8,128)(2,1)S(1)}, bf16[128,2688]{1,0:T(8,128)(2,1)S(1)}) custom-call(bf16[4,64,1024]{2,1,0:T(8,128)(2,1)S(1)} %pad_maximum_fusion.8.refs_0_.refs_9_, ...), custom_call_target="tpu_custom_call" | custom-call | flops 1024 | bytes 1024 | tf_op jit(solution)/shard_map/forward/pallas_call | solution.py:158
  59.4 4.9 %collective-permute-done.10 = bf16[64,2688]{1,0:T(8,128)(2,1)S(1)} collective-permute-done((bf16[64,2688]{1,0:T(8,128)(2,1)S(1)}, bf16[64,2688]{1,0:T(8,128)(2,1)S(1)}, u32[]{:S(2)}, u32[]{:S(2)}) %collective-permute-start.10) | collective-permute-done | bytes 344096 | tf_op jit(solution)/shard_map/ppermute | solution.py:54
  64.4 3.5 %collective-permute-start.18 = (bf16[128,2688]{1,0:T(8,128)(2,1)S(1)}, bf16[128,2688]{1,0:T(8,128)(2,1)S(1)}, u32[]{:S(2)}, u32[]{:S(2)}) collective-permute-start(bf16[128,2688]{1,0:T(8,128)(2,1)S(1)} %get-tuple-element.131), channel_id=1, source_target_pairs={{0,48},{1,17},{2,50},{3,19},{4,52},{5,21},{6,54},{7,23},{8,56},{9,... | collective-permute-start | bytes 2064392 | tf_op jit(solution)/shard_map/ppermute | solution.py:54
  68.3 1.8 %collective-permute-start.16 = (bf16[128,2688]{1,0:T(8,128)(2,1)S(1)}, bf16[128,2688]{1,0:T(8,128)(2,1)S(1)}, u32[]{:S(2)}, u32[]{:S(2)}) collective-permute-start(bf16[128,2688]{1,0:T(8,128)(2,1)S(1)} %pad_maximum_fusion.2), channel_id=1, source_target_pairs={{0,64},{1,65},{2,66},{3,67},{4,68},{5,69},{6,70},{7,71},{8,72},{9,... | collective-permute-start | bytes 2064392 | tf_op jit(solution)/shard_map/ppermute | solution.py:54
  70.0 5.7 %collective-permute-done.17 = bf16[128,2688]{1,0:T(8,128)(2,1)S(1)} collective-permute-done((bf16[128,2688]{1,0:T(8,128)(2,1)S(1)}, bf16[128,2688]{1,0:T(8,128)(2,1)S(1)}, u32[]{:S(2)}, u32[]{:S(2)}) %collective-permute-start.17) | collective-permute-done | bytes 688160 | tf_op jit(solution)/shard_map/ppermute | solution.py:54
  75.9 4.0 %collective-permute-done.18 = bf16[128,2688]{1,0:T(8,128)(2,1)S(1)} collective-permute-done((bf16[128,2688]{1,0:T(8,128)(2,1)S(1)}, bf16[128,2688]{1,0:T(8,128)(2,1)S(1)}, u32[]{:S(2)}, u32[]{:S(2)}) %collective-permute-start.18) | collective-permute-done | bytes 688160 | tf_op jit(solution)/shard_map/ppermute | solution.py:54
  79.9 3.6 %collective-permute-start.22 = (bf16[64,2688]{1,0:T(8,128)(2,1)S(1)}, bf16[64,2688]{1,0:T(8,128)(2,1)S(1)}, u32[]{:S(2)}, u32[]{:S(2)}) collective-permute-start(bf16[64,2688]{1,0:T(8,128)(2,1)S(1)} %slice_add_fusion), channel_id=1, source_target_pairs={{0,48},{1,17},{2,50},{3,19},{4,52},{5,21},{6,54},{7,23},{8,56},{9,... | collective-permute-start | bytes 1032200 | tf_op jit(solution)/shard_map/ppermute | solution.py:54
  84.5 2.9 %collective-permute-start.19 = (bf16[128,2688]{1,0:T(8,128)(2,1)S(1)}, bf16[128,2688]{1,0:T(8,128)(2,1)S(1)}, u32[]{:S(2)}, u32[]{:S(2)}) collective-permute-start(bf16[128,2688]{1,0:T(8,128)(2,1)S(1)} %pad_maximum_fusion.3.refs_0_.refs_4_), channel_id=1, source_target_pairs={{0,48},{1,17},{2,50},{3,19},{4,52},{5,21},{6,54},{7,23},{8,56},{9,... | collective-permute-start | bytes 2064392 | tf_op jit(solution)/shard_map/ppermute | solution.py:54
  87.3 4.7 %collective-permute-done.22 = bf16[64,2688]{1,0:T(8,128)(2,1)S(1)} collective-permute-done((bf16[64,2688]{1,0:T(8,128)(2,1)S(1)}, bf16[64,2688]{1,0:T(8,128)(2,1)S(1)}, u32[]{:S(2)}, u32[]{:S(2)}) %collective-permute-start.22) | collective-permute-done | bytes 344096 | tf_op jit(solution)/shard_map/ppermute | solution.py:54
  92.4 1.6 collective-permute-start.25
  93.9 8.8 %collective-permute-done.20.refs_2_.refs_6_ = bf16[128,2688]{1,0:T(8,128)(2,1)S(1)} collective-permute-done((bf16[128,2688]{1,0:T(8,128)(2,1)S(1)}, bf16[128,2688]{1,0:T(8,128)(2,1)S(1)}, u32[]{:S(2)}, u32[]{:S(2)}) %collective-permute-start.20) | collective-permute-done | bytes 688160 | tf_op jit(solution)/shard_map/ppermute | solution.py:54
  102.9 3.5 %collective-permute-start.24 = (bf16[64,2688]{1,0:T(8,128)(2,1)S(1)}, bf16[64,2688]{1,0:T(8,128)(2,1)S(1)}, u32[]{:S(2)}, u32[]{:S(2)}) collective-permute-start(bf16[64,2688]{1,0:T(8,128)(2,1)S(1)} %slice.204), channel_id=1, source_target_pairs={{0,48},{1,17},{2,50},{3,19},{4,52},{5,21},{6,54},{7,23},{8,56},{9,... | collective-permute-start | bytes 1032200 | tf_op jit(solution)/shard_map/ppermute | solution.py:54
  107.0 3.2 %collective-permute-start.29 = (bf16[128,2688]{1,0:T(8,128)(2,1)S(1)}, bf16[128,2688]{1,0:T(8,128)(2,1)S(1)}, u32[]{:S(2)}, u32[]{:S(2)}) collective-permute-start(bf16[128,2688]{1,0:T(8,128)(2,1)S(1)} %pad_maximum_fusion.5.refs_0_.refs_13_), channel_id=1, source_target_pairs={{0,48},{1,17},{2,50},{3,19},{4,52},{5,21},{6,54},{7,23},{8,56},{9,... | collective-permute-start | bytes 2064392 | tf_op jit(solution)/shard_map/ppermute | solution.py:54
  110.3 4.7 %collective-permute-done.24.refs_4_.refs_8_ = bf16[64,2688]{1,0:T(8,128)(2,1)S(1)} collective-permute-done((bf16[64,2688]{1,0:T(8,128)(2,1)S(1)}, bf16[64,2688]{1,0:T(8,128)(2,1)S(1)}, u32[]{:S(2)}, u32[]{:S(2)}) %collective-permute-start.24) | collective-permute-done | bytes 344096 | tf_op jit(solution)/shard_map/ppermute | solution.py:54
  115.1 3.2 %backward.2 = (bf16[4,64,1024]{2,1,0:T(8,128)(2,1)S(1)}, bf16[4,64,1024]{2,1,0:T(8,128)(2,1)S(1)}, bf16[4,64,1024]{2,1,0:T(8,128)(2,1)S(1)}, bf16[4,64,1024]{2,1,0:T(8,128)(2,1)S(1)}) custom-call(bf16[128,2688]{1,0:T(8,128)(2,1)S(1)} %pad_maximum_fusion.3.refs_0_.refs_4_, bf16[128,2688]{1,0:T(8,128)(2,1)S(1)} %collective-permute-done.19.refs_1_.refs_5_, ...), custom_call_target="tpu_custom_call" | custom-call | flops 2818572288 | bytes 22020096 | tf_op jit(solution)/shard_map/backward/pallas_call | solution.py:186
  118.9 9.1 %collective-permute-done.28.refs_2_.refs_15_ = bf16[128,2688]{1,0:T(8,128)(2,1)S(1)} collective-permute-done((bf16[128,2688]{1,0:T(8,128)(2,1)S(1)}, bf16[128,2688]{1,0:T(8,128)(2,1)S(1)}, u32[]{:S(2)}, u32[]{:S(2)}) %collective-permute-start.28) | collective-permute-done | bytes 688160 | tf_op jit(solution)/shard_map/ppermute | solution.py:54
  128.1 3.3 %collective-permute-start.34 = (bf16[64,2688]{1,0:T(8,128)(2,1)S(1)}, bf16[64,2688]{1,0:T(8,128)(2,1)S(1)}, u32[]{:S(2)}, u32[]{:S(2)}) collective-permute-start(bf16[64,2688]{1,0:T(8,128)(2,1)S(1)} %slice.209), channel_id=1, source_target_pairs={{0,48},{1,17},{2,50},{3,19},{4,52},{5,21},{6,54},{7,23},{8,56},{9,... | collective-permute-start | bytes 1032200 | tf_op jit(solution)/shard_map/ppermute | solution.py:54
  132.0 2.1 %collective-permute-start.31 = (bf16[64,2048]{1,0:T(8,128)(2,1)S(1)}, bf16[64,2048]{1,0:T(8,128)(2,1)S(1)}, u32[]{:S(2)}, u32[]{:S(2)}) collective-permute-start(bf16[64,2048]{1,0:T(8,128)(2,1)S(1)} %get-tuple-element.209), channel_id=1, source_target_pairs={{0,8},{1,9},{2,10},{3,11},{4,12},{5,13},{6,14},{7,15},{8,0},{9,1},... | collective-permute-start | bytes 786440 | tf_op jit(solution)/shard_map/ppermute | solution.py:54
  134.1 1.2 collective-permute-start.32
  136.2 1.3 collective-permute-done.33.refs_3_.refs_16_
  137.5 3.2 %backward.3 = (bf16[4,64,1024]{2,1,0:T(8,128)(2,1)S(1)}, bf16[4,64,1024]{2,1,0:T(8,128)(2,1)S(1)}, bf16[4,64,1024]{2,1,0:T(8,128)(2,1)S(1)}, bf16[4,64,1024]{2,1,0:T(8,128)(2,1)S(1)}) custom-call(bf16[128,2688]{1,0:T(8,128)(2,1)S(1)} %pad_maximum_fusion.5.refs_0_.refs_13_, bf16[128,2688]{1,0:T(8,128)(2,1)S(1)} %collective-permute-done.29.refs_1_.refs_14_, ...), custom_call_target="tpu_custom_call" | custom-call | flops 2818572288 | bytes 22020096 | tf_op jit(solution)/shard_map/backward/pallas_call | solution.py:186
  141.3 1.1 collective-permute-done.30
  142.4 0.9 collective-permute-done.32
  143.5 3.1 %collective-permute-start.35 = (bf16[32,2048]{1,0:T(8,128)(2,1)S(1)}, bf16[32,2048]{1,0:T(8,128)(2,1)S(1)}, u32[]{:S(2)}, u32[]{:S(2)}) collective-permute-start(bf16[32,2048]{1,0:T(8,128)(2,1)S(1)} %slice.239), channel_id=1, source_target_pairs={{0,2},{1,3},{2,0},{3,1},{4,6},{5,7},{6,4},{7,5},{8,10},{9,11},{10,... | collective-permute-start | bytes 393224 | tf_op jit(solution)/shard_map/ppermute | solution.py:54
  147.2 3.8 %collective-permute-start.39 = (bf16[64,2048]{1,0:T(8,128)(2,1)S(1)}, bf16[64,2048]{1,0:T(8,128)(2,1)S(1)}, u32[]{:S(2)}, u32[]{:S(2)}) collective-permute-start(bf16[64,2048]{1,0:T(8,128)(2,1)S(1)} %get-tuple-element.205), channel_id=1, source_target_pairs={{0,8},{1,9},{2,10},{3,11},{4,12},{5,13},{6,14},{7,15},{8,0},{9,1},... | collective-permute-start | bytes 786440 | tf_op jit(solution)/shard_map/ppermute | solution.py:54
  151.0 9.6 %weight_grads.1 = (bf16[1024,896]{1,0:T(8,128)(2,1)}, bf16[1024,896]{1,0:T(8,128)(2,1)}, bf16[896,1024]{1,0:T(8,128)(2,1)}) custom-call(bf16[4,64,1024]{2,1,0:T(8,128)(2,1)S(1)} %pad_maximum_fusion.6.refs_0_, bf16[4,64,1024]{2,1,0:T(8,128)(2,1)S(1)} %pad_maximum_fusion.7.refs_1_, bf16[4,64,1024]{2,1,0:T(8,128)(2,1)S(1)} %collective-permute-done.5.refs_2_, ...), custom_call_target="tpu_custom_call" | custom-call | flops 5637144576 | bytes 44040192 | tf_op jit(solution)/shard_map/weight_grads/pallas_call | solution.py:245
  161.0 2.1 %collective-permute-start.41 = (bf16[32,2048]{1,0:T(8,128)(2,1)S(1)}, bf16[32,2048]{1,0:T(8,128)(2,1)S(1)}, u32[]{:S(2)}, u32[]{:S(2)}) collective-permute-start(bf16[32,2048]{1,0:T(8,128)(2,1)S(1)} %slice.249), channel_id=1, source_target_pairs={{0,2},{1,3},{2,0},{3,1},{4,6},{5,7},{6,4},{7,5},{8,10},{9,11},{10,... | collective-permute-start | bytes 393224 | tf_op jit(solution)/shard_map/ppermute | solution.py:54
  163.1 4.4 %collective-permute-done.41 = bf16[32,2048]{1,0:T(8,128)(2,1)S(1)} collective-permute-done((bf16[32,2048]{1,0:T(8,128)(2,1)S(1)}, bf16[32,2048]{1,0:T(8,128)(2,1)S(1)}, u32[]{:S(2)}, u32[]{:S(2)}) %collective-permute-start.41) | collective-permute-done | bytes 131104 | tf_op jit(solution)/shard_map/ppermute | solution.py:54
  (102 shorter events, 10.9 us)
Async XLA Ops:
  0.6 15.8 %copy-start.3 = (s32[8,7]{1,0:T(8,128)S(1)}, s32[8,7]{1,0:T(8,128)}, u32[]{:S(2)}) copy-start(s32[8,7]{1,0:T(8,128)} %refs_18_.1) | copy-start | bytes 676
  0.6 15.8 %copy-start.4 = (s32[8,7]{1,0:T(8,128)S(1)}, s32[8,7]{1,0:T(8,128)}, u32[]{:S(2)}) copy-start(s32[8,7]{1,0:T(8,128)} %refs_19_.1) | copy-start | bytes 676
  0.7 15.7 %copy-start.5 = (s32[7,8]{1,0:T(8,128)S(1)}, s32[7,8]{1,0:T(8,128)}, u32[]{:S(2)}) copy-start(s32[7,8]{1,0:T(8,128)} %refs_20_.1) | copy-start | bytes 676
  1.7 6.7 %collective-permute-start = (bf16[2,32,1024]{2,1,0:T(8,128)(2,1)S(1)}, bf16[2,32,1024]{2,1,0:T(8,128)(2,1)S(1)}, u32[]{:S(2)}, u32[]{:S(2)}) collective-permute-start(bf16[2,32,1024]{2,1,0:T(8,128)(2,1)S(1)} %pad_maximum_fusion.13), channel_id=1, source_target_pairs={{0,2},{1,3},{2,0},{3,1},{4,6},{5,7},{6,4},{7,5},{8,10},{9,11},{10,... | collective-permute-start | bytes 393224 | tf_op jit(solution)/shard_map/ppermute | solution.py:54
  8.4 15.4 %collective-permute-start.1 = (bf16[2,64,1024]{2,1,0:T(8,128)(2,1)S(1)}, bf16[2,64,1024]{2,1,0:T(8,128)(2,1)S(1)}, u32[]{:S(2)}, u32[]{:S(2)}) collective-permute-start(bf16[2,64,1024]{2,1,0:T(8,128)(2,1)S(1)} %pad_maximum_fusion.10), channel_id=1, source_target_pairs={{0,12},{1,13},{2,14},{3,15},{4,0},{5,1},{6,2},{7,3},{8,4},{9,5},{1... | collective-permute-start | bytes 786440 | tf_op jit(solution)/shard_map/ppermute | solution.py:54
  11.7 12.1 %collective-permute-start.2 = (bf16[2,64,1024]{2,1,0:T(8,128)(2,1)S(1)}, bf16[2,64,1024]{2,1,0:T(8,128)(2,1)S(1)}, u32[]{:S(2)}, u32[]{:S(2)}) collective-permute-start(bf16[2,64,1024]{2,1,0:T(8,128)(2,1)S(1)} %pad_maximum_fusion.10), channel_id=1, source_target_pairs={{0,8},{1,9},{2,10},{3,11},{4,12},{5,13},{6,14},{7,15},{8,0},{9,1},... | collective-permute-start | bytes 786440 | tf_op jit(solution)/shard_map/ppermute | solution.py:54
  12.3 13.4 %collective-permute-start.3 = (bf16[2,64,1024]{2,1,0:T(8,128)(2,1)S(1)}, bf16[2,64,1024]{2,1,0:T(8,128)(2,1)S(1)}, u32[]{:S(2)}, u32[]{:S(2)}) collective-permute-start(bf16[2,64,1024]{2,1,0:T(8,128)(2,1)S(1)} %pad_maximum_fusion.10), channel_id=1, source_target_pairs={{0,4},{1,5},{2,6},{3,7},{4,8},{5,9},{6,10},{7,11},{8,12},{9,13},{1... | collective-permute-start | bytes 786440 | tf_op jit(solution)/shard_map/ppermute | solution.py:54
  13.3 10.4 %collective-permute-start.4 = (bf16[2,32,1024]{2,1,0:T(8,128)(2,1)S(1)}, bf16[2,32,1024]{2,1,0:T(8,128)(2,1)S(1)}, u32[]{:S(2)}, u32[]{:S(2)}) collective-permute-start(bf16[2,32,1024]{2,1,0:T(8,128)(2,1)S(1)} %pad_maximum_fusion.14), channel_id=1, source_target_pairs={{0,2},{1,3},{2,0},{3,1},{4,6},{5,7},{6,4},{7,5},{8,10},{9,11},{10,... | collective-permute-start | bytes 393224 | tf_op jit(solution)/shard_map/ppermute | solution.py:54
  16.4 1.5 copy-start
  17.9 1.5 copy-start.1
  19.4 1.5 copy-start.2
  25.9 2.0 %collective-permute-start.6 = (bf16[4,64,1024]{2,1,0:T(8,128)(2,1)S(1)}, bf16[4,64,1024]{2,1,0:T(8,128)(2,1)S(1)}, u32[]{:S(2)}, u32[]{:S(2)}) collective-permute-start(bf16[4,64,1024]{2,1,0:T(8,128)(2,1)S(1)} %pad_maximum_fusion.7.refs_1_), channel_id=1, source_target_pairs={{0,1},{1,0},{2,3},{3,2},{4,5},{5,4},{6,7},{7,6},{8,9},{9,8},{10,11... | collective-permute-start | bytes 1572872 | tf_op jit(solution)/shard_map/ppermute | solution.py:54
  26.0 2.6 %collective-permute-start.5 = (bf16[4,64,1024]{2,1,0:T(8,128)(2,1)S(1)}, bf16[4,64,1024]{2,1,0:T(8,128)(2,1)S(1)}, u32[]{:S(2)}, u32[]{:S(2)}) collective-permute-start(bf16[4,64,1024]{2,1,0:T(8,128)(2,1)S(1)} %pad_maximum_fusion.6.refs_0_), channel_id=1, source_target_pairs={{0,1},{1,0},{2,3},{3,2},{4,5},{5,4},{6,7},{7,6},{8,9},{9,8},{10,11... | collective-permute-start | bytes 1572872 | tf_op jit(solution)/shard_map/ppermute | solution.py:54
  32.0 16.7 %collective-permute-start.7 = (bf16[128,2688]{1,0:T(8,128)(2,1)S(1)}, bf16[128,2688]{1,0:T(8,128)(2,1)S(1)}, u32[]{:S(2)}, u32[]{:S(2)}) collective-permute-start(bf16[128,2688]{1,0:T(8,128)(2,1)S(1)} %get-tuple-element.111), channel_id=1, source_target_pairs={{0,16},{1,49},{2,18},{3,51},{4,20},{5,53},{6,22},{7,55},{8,24},{9,... | collective-permute-start | bytes 2064392 | tf_op jit(solution)/shard_map/ppermute | solution.py:54
  34.0 17.2 %collective-permute-start.11 = (bf16[2,64,1024]{2,1,0:T(8,128)(2,1)S(1)}, bf16[2,64,1024]{2,1,0:T(8,128)(2,1)S(1)}, u32[]{:S(2)}, u32[]{:S(2)}) collective-permute-start(bf16[2,64,1024]{2,1,0:T(8,128)(2,1)S(1)} %pad_maximum_fusion.11), channel_id=1, source_target_pairs={{0,12},{1,13},{2,14},{3,15},{4,0},{5,1},{6,2},{7,3},{8,4},{9,5},{1... | collective-permute-start | bytes 786440 | tf_op jit(solution)/shard_map/ppermute | solution.py:54
  34.6 16.6 %collective-permute-start.12 = (bf16[2,64,1024]{2,1,0:T(8,128)(2,1)S(1)}, bf16[2,64,1024]{2,1,0:T(8,128)(2,1)S(1)}, u32[]{:S(2)}, u32[]{:S(2)}) collective-permute-start(bf16[2,64,1024]{2,1,0:T(8,128)(2,1)S(1)} %pad_maximum_fusion.11), channel_id=1, source_target_pairs={{0,8},{1,9},{2,10},{3,11},{4,12},{5,13},{6,14},{7,15},{8,0},{9,1},... | collective-permute-start | bytes 786440 | tf_op jit(solution)/shard_map/ppermute | solution.py:54
  36.1 15.2 %collective-permute-start.13 = (bf16[2,64,1024]{2,1,0:T(8,128)(2,1)S(1)}, bf16[2,64,1024]{2,1,0:T(8,128)(2,1)S(1)}, u32[]{:S(2)}, u32[]{:S(2)}) collective-permute-start(bf16[2,64,1024]{2,1,0:T(8,128)(2,1)S(1)} %pad_maximum_fusion.11), channel_id=1, source_target_pairs={{0,4},{1,5},{2,6},{3,7},{4,8},{5,9},{6,10},{7,11},{8,12},{9,13},{1... | collective-permute-start | bytes 786440 | tf_op jit(solution)/shard_map/ppermute | solution.py:54
  36.1 15.1 %collective-permute-start.9 = (bf16[128,2688]{1,0:T(8,128)(2,1)S(1)}, bf16[128,2688]{1,0:T(8,128)(2,1)S(1)}, u32[]{:S(2)}, u32[]{:S(2)}) collective-permute-start(bf16[128,2688]{1,0:T(8,128)(2,1)S(1)} %get-tuple-element.114), channel_id=1, source_target_pairs={{0,48},{1,17},{2,50},{3,19},{4,52},{5,21},{6,54},{7,23},{8,56},{9,... | collective-permute-start | bytes 2064392 | tf_op jit(solution)/shard_map/ppermute | solution.py:54
  51.4 4.5 %collective-permute-start.15 = (bf16[4,64,1024]{2,1,0:T(8,128)(2,1)S(1)}, bf16[4,64,1024]{2,1,0:T(8,128)(2,1)S(1)}, u32[]{:S(2)}, u32[]{:S(2)}) collective-permute-start(bf16[4,64,1024]{2,1,0:T(8,128)(2,1)S(1)} %pad_maximum_fusion.9.refs_1_.refs_10_), channel_id=1, source_target_pairs={{0,1},{1,0},{2,3},{3,2},{4,5},{5,4},{6,7},{7,6},{8,9},{9,8},{10,11... | collective-permute-start | bytes 1572872 | tf_op jit(solution)/shard_map/ppermute | solution.py:54
  52.7 3.2 %collective-permute-start.14 = (bf16[4,64,1024]{2,1,0:T(8,128)(2,1)S(1)}, bf16[4,64,1024]{2,1,0:T(8,128)(2,1)S(1)}, u32[]{:S(2)}, u32[]{:S(2)}) collective-permute-start(bf16[4,64,1024]{2,1,0:T(8,128)(2,1)S(1)} %pad_maximum_fusion.8.refs_0_.refs_9_), channel_id=1, source_target_pairs={{0,1},{1,0},{2,3},{3,2},{4,5},{5,4},{6,7},{7,6},{8,9},{9,8},{10,11... | collective-permute-start | bytes 1572872 | tf_op jit(solution)/shard_map/ppermute | solution.py:54
  52.8 11.5 %collective-permute-start.10 = (bf16[64,2688]{1,0:T(8,128)(2,1)S(1)}, bf16[64,2688]{1,0:T(8,128)(2,1)S(1)}, u32[]{:S(2)}, u32[]{:S(2)}) collective-permute-start(bf16[64,2688]{1,0:T(8,128)(2,1)S(1)} %slice_add_fusion.2), channel_id=1, source_target_pairs={{0,48},{1,17},{2,50},{3,19},{4,52},{5,21},{6,54},{7,23},{8,56},{9,... | collective-permute-start | bytes 1032200 | tf_op jit(solution)/shard_map/ppermute | solution.py:54
  55.9 8.6 %collective-permute-start.8 = (bf16[64,2688]{1,0:T(8,128)(2,1)S(1)}, bf16[64,2688]{1,0:T(8,128)(2,1)S(1)}, u32[]{:S(2)}, u32[]{:S(2)}) collective-permute-start(bf16[64,2688]{1,0:T(8,128)(2,1)S(1)} %slice_add_fusion.3), channel_id=1, source_target_pairs={{0,16},{1,49},{2,18},{3,51},{4,20},{5,53},{6,22},{7,55},{8,24},{9,... | collective-permute-start | bytes 1032200 | tf_op jit(solution)/shard_map/ppermute | solution.py:54
  59.3 16.4 %collective-permute-start.17 = (bf16[128,2688]{1,0:T(8,128)(2,1)S(1)}, bf16[128,2688]{1,0:T(8,128)(2,1)S(1)}, u32[]{:S(2)}, u32[]{:S(2)}) collective-permute-start(bf16[128,2688]{1,0:T(8,128)(2,1)S(1)} %get-tuple-element.125), channel_id=1, source_target_pairs={{0,16},{1,49},{2,18},{3,51},{4,20},{5,53},{6,22},{7,55},{8,24},{9,... | collective-permute-start | bytes 2064392 | tf_op jit(solution)/shard_map/ppermute | solution.py:54
  64.4 15.4 %collective-permute-start.18 = (bf16[128,2688]{1,0:T(8,128)(2,1)S(1)}, bf16[128,2688]{1,0:T(8,128)(2,1)S(1)}, u32[]{:S(2)}, u32[]{:S(2)}) collective-permute-start(bf16[128,2688]{1,0:T(8,128)(2,1)S(1)} %get-tuple-element.131), channel_id=1, source_target_pairs={{0,48},{1,17},{2,50},{3,19},{4,52},{5,21},{6,54},{7,23},{8,56},{9,... | collective-permute-start | bytes 2064392 | tf_op jit(solution)/shard_map/ppermute | solution.py:54
  68.3 15.3 %collective-permute-start.16 = (bf16[128,2688]{1,0:T(8,128)(2,1)S(1)}, bf16[128,2688]{1,0:T(8,128)(2,1)S(1)}, u32[]{:S(2)}, u32[]{:S(2)}) collective-permute-start(bf16[128,2688]{1,0:T(8,128)(2,1)S(1)} %pad_maximum_fusion.2), channel_id=1, source_target_pairs={{0,64},{1,65},{2,66},{3,67},{4,68},{5,69},{6,70},{7,71},{8,72},{9,... | collective-permute-start | bytes 2064392 | tf_op jit(solution)/shard_map/ppermute | solution.py:54
  75.8 16.2 %collective-permute-start.21 = (bf16[64,2688]{1,0:T(8,128)(2,1)S(1)}, bf16[64,2688]{1,0:T(8,128)(2,1)S(1)}, u32[]{:S(2)}, u32[]{:S(2)}) collective-permute-start(bf16[64,2688]{1,0:T(8,128)(2,1)S(1)} %slice_add_fusion.1), channel_id=1, source_target_pairs={{0,16},{1,49},{2,18},{3,51},{4,20},{5,53},{6,22},{7,55},{8,24},{9,... | collective-permute-start | bytes 1032200 | tf_op jit(solution)/shard_map/ppermute | solution.py:54
  79.9 12.1 %collective-permute-start.22 = (bf16[64,2688]{1,0:T(8,128)(2,1)S(1)}, bf16[64,2688]{1,0:T(8,128)(2,1)S(1)}, u32[]{:S(2)}, u32[]{:S(2)}) collective-permute-start(bf16[64,2688]{1,0:T(8,128)(2,1)S(1)} %slice_add_fusion), channel_id=1, source_target_pairs={{0,48},{1,17},{2,50},{3,19},{4,52},{5,21},{6,54},{7,23},{8,56},{9,... | collective-permute-start | bytes 1032200 | tf_op jit(solution)/shard_map/ppermute | solution.py:54
  84.0 18.7 %collective-permute-start.20 = (bf16[128,2688]{1,0:T(8,128)(2,1)S(1)}, bf16[128,2688]{1,0:T(8,128)(2,1)S(1)}, u32[]{:S(2)}, u32[]{:S(2)}) collective-permute-start(bf16[128,2688]{1,0:T(8,128)(2,1)S(1)} %pad_maximum_fusion.3.refs_0_.refs_4_), channel_id=1, source_target_pairs={{0,16},{1,49},{2,18},{3,51},{4,20},{5,53},{6,22},{7,55},{8,24},{9,... | collective-permute-start | bytes 2064392 | tf_op jit(solution)/shard_map/ppermute | solution.py:54
  84.5 18.4 %collective-permute-start.19 = (bf16[128,2688]{1,0:T(8,128)(2,1)S(1)}, bf16[128,2688]{1,0:T(8,128)(2,1)S(1)}, u32[]{:S(2)}, u32[]{:S(2)}) collective-permute-start(bf16[128,2688]{1,0:T(8,128)(2,1)S(1)} %pad_maximum_fusion.3.refs_0_.refs_4_), channel_id=1, source_target_pairs={{0,48},{1,17},{2,50},{3,19},{4,52},{5,21},{6,54},{7,23},{8,56},{9,... | collective-permute-start | bytes 2064392 | tf_op jit(solution)/shard_map/ppermute | solution.py:54
  92.4 14.1 %collective-permute-start.25 = (bf16[128,2688]{1,0:T(8,128)(2,1)S(1)}, bf16[128,2688]{1,0:T(8,128)(2,1)S(1)}, u32[]{:S(2)}, u32[]{:S(2)}) collective-permute-start(bf16[128,2688]{1,0:T(8,128)(2,1)S(1)} %pad_maximum_fusion.4), channel_id=1, source_target_pairs={{0,64},{1,65},{2,66},{3,67},{4,68},{5,69},{6,70},{7,71},{8,72},{9,... | collective-permute-start | bytes 2064392 | tf_op jit(solution)/shard_map/ppermute | solution.py:54
  102.8 12.3 %collective-permute-start.23 = (bf16[64,2688]{1,0:T(8,128)(2,1)S(1)}, bf16[64,2688]{1,0:T(8,128)(2,1)S(1)}, u32[]{:S(2)}, u32[]{:S(2)}) collective-permute-start(bf16[64,2688]{1,0:T(8,128)(2,1)S(1)} %slice.203), channel_id=1, source_target_pairs={{0,16},{1,49},{2,18},{3,51},{4,20},{5,53},{6,22},{7,55},{8,24},{9,... | collective-permute-start | bytes 1032200 | tf_op jit(solution)/shard_map/ppermute | solution.py:54
  102.9 12.1 %collective-permute-start.24 = (bf16[64,2688]{1,0:T(8,128)(2,1)S(1)}, bf16[64,2688]{1,0:T(8,128)(2,1)S(1)}, u32[]{:S(2)}, u32[]{:S(2)}) collective-permute-start(bf16[64,2688]{1,0:T(8,128)(2,1)S(1)} %slice.204), channel_id=1, source_target_pairs={{0,48},{1,17},{2,50},{3,19},{4,52},{5,21},{6,54},{7,23},{8,56},{9,... | collective-permute-start | bytes 1032200 | tf_op jit(solution)/shard_map/ppermute | solution.py:54
  107.0 21.0 %collective-permute-start.28 = (bf16[128,2688]{1,0:T(8,128)(2,1)S(1)}, bf16[128,2688]{1,0:T(8,128)(2,1)S(1)}, u32[]{:S(2)}, u32[]{:S(2)}) collective-permute-start(bf16[128,2688]{1,0:T(8,128)(2,1)S(1)} %pad_maximum_fusion.5.refs_0_.refs_13_), channel_id=1, source_target_pairs={{0,16},{1,49},{2,18},{3,51},{4,20},{5,53},{6,22},{7,55},{8,24},{9,... | collective-permute-start | bytes 2064392 | tf_op jit(solution)/shard_map/ppermute | solution.py:54
  107.0 21.1 %collective-permute-start.29 = (bf16[128,2688]{1,0:T(8,128)(2,1)S(1)}, bf16[128,2688]{1,0:T(8,128)(2,1)S(1)}, u32[]{:S(2)}, u32[]{:S(2)}) collective-permute-start(bf16[128,2688]{1,0:T(8,128)(2,1)S(1)} %pad_maximum_fusion.5.refs_0_.refs_13_), channel_id=1, source_target_pairs={{0,48},{1,17},{2,50},{3,19},{4,52},{5,21},{6,54},{7,23},{8,56},{9,... | collective-permute-start | bytes 2064392 | tf_op jit(solution)/shard_map/ppermute | solution.py:54
  118.3 13.2 %collective-permute-start.26 = (bf16[256,1024]{1,0:T(8,128)(2,1)S(1)}, bf16[256,1024]{1,0:T(8,128)(2,1)S(1)}, u32[]{:S(2)}, u32[]{:S(2)}) collective-permute-start(bf16[256,1024]{1,0:T(8,128)(2,1)S(1)} %bitcast.27), channel_id=1, source_target_pairs={{0,1},{1,0},{2,3},{3,2},{4,5},{5,4},{6,7},{7,6},{8,9},{9,8},{10,11... | collective-permute-start | bytes 1572872 | tf_op jit(solution)/shard_map/ppermute | solution.py:54
  118.4 13.1 %collective-permute-start.27 = (bf16[256,1024]{1,0:T(8,128)(2,1)S(1)}, bf16[256,1024]{1,0:T(8,128)(2,1)S(1)}, u32[]{:S(2)}, u32[]{:S(2)}) collective-permute-start(bf16[256,1024]{1,0:T(8,128)(2,1)S(1)} %bitcast.26), channel_id=1, source_target_pairs={{0,1},{1,0},{2,3},{3,2},{4,5},{5,4},{6,7},{7,6},{8,9},{9,8},{10,11... | collective-permute-start | bytes 1572872 | tf_op jit(solution)/shard_map/ppermute | solution.py:54
  128.0 9.5 %collective-permute-start.33 = (bf16[64,2688]{1,0:T(8,128)(2,1)S(1)}, bf16[64,2688]{1,0:T(8,128)(2,1)S(1)}, u32[]{:S(2)}, u32[]{:S(2)}) collective-permute-start(bf16[64,2688]{1,0:T(8,128)(2,1)S(1)} %slice.208), channel_id=1, source_target_pairs={{0,16},{1,49},{2,18},{3,51},{4,20},{5,53},{6,22},{7,55},{8,24},{9,... | collective-permute-start | bytes 1032200 | tf_op jit(solution)/shard_map/ppermute | solution.py:54
  128.1 8.0 %collective-permute-start.34 = (bf16[64,2688]{1,0:T(8,128)(2,1)S(1)}, bf16[64,2688]{1,0:T(8,128)(2,1)S(1)}, u32[]{:S(2)}, u32[]{:S(2)}) collective-permute-start(bf16[64,2688]{1,0:T(8,128)(2,1)S(1)} %slice.209), channel_id=1, source_target_pairs={{0,48},{1,17},{2,50},{3,19},{4,52},{5,21},{6,54},{7,23},{8,56},{9,... | collective-permute-start | bytes 1032200 | tf_op jit(solution)/shard_map/ppermute | solution.py:54
  132.0 10.5 %collective-permute-start.30 = (bf16[64,2048]{1,0:T(8,128)(2,1)S(1)}, bf16[64,2048]{1,0:T(8,128)(2,1)S(1)}, u32[]{:S(2)}, u32[]{:S(2)}) collective-permute-start(bf16[64,2048]{1,0:T(8,128)(2,1)S(1)} %get-tuple-element.208), channel_id=1, source_target_pairs={{0,4},{1,5},{2,6},{3,7},{4,8},{5,9},{6,10},{7,11},{8,12},{9,13},{1... | collective-permute-start | bytes 786440 | tf_op jit(solution)/shard_map/ppermute | solution.py:54
  132.0 10.4 %collective-permute-start.31 = (bf16[64,2048]{1,0:T(8,128)(2,1)S(1)}, bf16[64,2048]{1,0:T(8,128)(2,1)S(1)}, u32[]{:S(2)}, u32[]{:S(2)}) collective-permute-start(bf16[64,2048]{1,0:T(8,128)(2,1)S(1)} %get-tuple-element.209), channel_id=1, source_target_pairs={{0,8},{1,9},{2,10},{3,11},{4,12},{5,13},{6,14},{7,15},{8,0},{9,1},... | collective-permute-start | bytes 786440 | tf_op jit(solution)/shard_map/ppermute | solution.py:54
  134.1 9.2 %collective-permute-start.32 = (bf16[64,2048]{1,0:T(8,128)(2,1)S(1)}, bf16[64,2048]{1,0:T(8,128)(2,1)S(1)}, u32[]{:S(2)}, u32[]{:S(2)}) collective-permute-start(bf16[64,2048]{1,0:T(8,128)(2,1)S(1)} %get-tuple-element.207), channel_id=1, source_target_pairs={{0,12},{1,13},{2,14},{3,15},{4,0},{5,1},{6,2},{7,3},{8,4},{9,5},{1... | collective-permute-start | bytes 786440 | tf_op jit(solution)/shard_map/ppermute | solution.py:54
  140.7 5.9 %collective-permute-start.36 = (bf16[256,1024]{1,0:T(8,128)(2,1)S(1)}, bf16[256,1024]{1,0:T(8,128)(2,1)S(1)}, u32[]{:S(2)}, u32[]{:S(2)}) collective-permute-start(bf16[256,1024]{1,0:T(8,128)(2,1)S(1)} %bitcast.25), channel_id=1, source_target_pairs={{0,1},{1,0},{2,3},{3,2},{4,5},{5,4},{6,7},{7,6},{8,9},{9,8},{10,11... | collective-permute-start | bytes 1572872 | tf_op jit(solution)/shard_map/ppermute | solution.py:54
  140.8 5.8 %collective-permute-start.37 = (bf16[256,1024]{1,0:T(8,128)(2,1)S(1)}, bf16[256,1024]{1,0:T(8,128)(2,1)S(1)}, u32[]{:S(2)}, u32[]{:S(2)}) collective-permute-start(bf16[256,1024]{1,0:T(8,128)(2,1)S(1)} %bitcast.24), channel_id=1, source_target_pairs={{0,1},{1,0},{2,3},{3,2},{4,5},{5,4},{6,7},{7,6},{8,9},{9,8},{10,11... | collective-permute-start | bytes 1572872 | tf_op jit(solution)/shard_map/ppermute | solution.py:54
  143.5 19.6 %collective-permute-start.35 = (bf16[32,2048]{1,0:T(8,128)(2,1)S(1)}, bf16[32,2048]{1,0:T(8,128)(2,1)S(1)}, u32[]{:S(2)}, u32[]{:S(2)}) collective-permute-start(bf16[32,2048]{1,0:T(8,128)(2,1)S(1)} %slice.239), channel_id=1, source_target_pairs={{0,2},{1,3},{2,0},{3,1},{4,6},{5,7},{6,4},{7,5},{8,10},{9,11},{10,... | collective-permute-start | bytes 393224 | tf_op jit(solution)/shard_map/ppermute | solution.py:54
  147.1 13.5 %collective-permute-start.38 = (bf16[64,2048]{1,0:T(8,128)(2,1)S(1)}, bf16[64,2048]{1,0:T(8,128)(2,1)S(1)}, u32[]{:S(2)}, u32[]{:S(2)}) collective-permute-start(bf16[64,2048]{1,0:T(8,128)(2,1)S(1)} %get-tuple-element.204), channel_id=1, source_target_pairs={{0,4},{1,5},{2,6},{3,7},{4,8},{5,9},{6,10},{7,11},{8,12},{9,13},{1... | collective-permute-start | bytes 786440 | tf_op jit(solution)/shard_map/ppermute | solution.py:54
  147.2 13.4 %collective-permute-start.39 = (bf16[64,2048]{1,0:T(8,128)(2,1)S(1)}, bf16[64,2048]{1,0:T(8,128)(2,1)S(1)}, u32[]{:S(2)}, u32[]{:S(2)}) collective-permute-start(bf16[64,2048]{1,0:T(8,128)(2,1)S(1)} %get-tuple-element.205), channel_id=1, source_target_pairs={{0,8},{1,9},{2,10},{3,11},{4,12},{5,13},{6,14},{7,15},{8,0},{9,1},... | collective-permute-start | bytes 786440 | tf_op jit(solution)/shard_map/ppermute | solution.py:54
  151.0 9.9 %collective-permute-start.40 = (bf16[64,2048]{1,0:T(8,128)(2,1)S(1)}, bf16[64,2048]{1,0:T(8,128)(2,1)S(1)}, u32[]{:S(2)}, u32[]{:S(2)}) collective-permute-start(bf16[64,2048]{1,0:T(8,128)(2,1)S(1)} %get-tuple-element.203), channel_id=1, source_target_pairs={{0,12},{1,13},{2,14},{3,15},{4,0},{5,1},{6,2},{7,3},{8,4},{9,5},{1... | collective-permute-start | bytes 786440 | tf_op jit(solution)/shard_map/ppermute | solution.py:54
  161.0 6.6 %collective-permute-start.41 = (bf16[32,2048]{1,0:T(8,128)(2,1)S(1)}, bf16[32,2048]{1,0:T(8,128)(2,1)S(1)}, u32[]{:S(2)}, u32[]{:S(2)}) collective-permute-start(bf16[32,2048]{1,0:T(8,128)(2,1)S(1)} %slice.249), channel_id=1, source_target_pairs={{0,2},{1,3},{2,0},{3,1},{4,6},{5,7},{6,4},{7,5},{8,10},{9,11},{10,... | collective-permute-start | bytes 393224 | tf_op jit(solution)/shard_map/ppermute | solution.py:54

commit v10 on v9

--- a/solution.py
+++ b/solution.py
@@ -37,7 +37,8 @@
 NEXT_UP = ((1, 0),)
 NEXT_DOWN = ((3, 1),)
 OWN = ((0, 0), (0, 1))
-GROUPS = (SEND_UP, SEND_DOWN, NEXT_UP, NEXT_DOWN, OWN)
+TOGETHER = ((SEND_UP, SEND_DOWN, NEXT_UP, NEXT_DOWN, OWN),)
+APART = ((SEND_UP, SEND_DOWN), (NEXT_UP, NEXT_DOWN, OWN))
 GATHERED = tuple((dz, half) for dz in (0, 1, 3, 2) for half in range(2))
 VMEM_LIMIT = 24 * 1024 * 1024
 
@@ -90,10 +91,10 @@
     return lax.rem(z + dz + odd * ((4 - 2 * dz) % 4), 4)
 
 
-def tokens_of(kind, gathered, offset, rows, columns):
+def tokens_of(kind, gathered, offset, rows, columns, pieces):
     return [
         gathered[2 * half + kind][owner(dz), offset : offset + rows, columns]
-        for dz, half in GATHERED
+        for dz, half in pieces
     ]
 
 
@@ -138,29 +139,31 @@
     )(gate, up, down, gate_mask, up_mask, down_mask)
 
 
-def forward_kernel(offset, rows, *refs):
+def forward_kernel(groups, offset, rows, *refs):
     gathered, weights, outs = refs[:4], refs[4], refs[5:]
     width = weights.shape[1] // 3
-    every = slice(None)
+    pieces = [piece for group in groups for piece in group]
     for at in range(3):
         columns = slice(at * width, (at + 1) * width)
-        left = jnp.concatenate(tokens_of(at // 2, gathered, offset, rows, every))
+        left = jnp.concatenate(
+            tokens_of(at // 2, gathered, offset, rows, slice(None), pieces)
+        )
         part = nn(left, weights[:, columns]).astype(jnp.bfloat16)
-        for number, piece in enumerate(GATHERED):
-            for out, group in zip(outs, GROUPS):
-                if piece in group:
-                    first = group.index(piece) * rows
-                    out[first : first + rows, columns] = part[number * rows : (number + 1) * rows]
-
-
-def forward(gathered, offset, rows, weights):
+        first = 0
+        for out, group in zip(outs, groups):
+            size = len(group) * rows
+            out[:, columns] = part[first : first + size]
+            first += size
+
+
+def forward(groups, gathered, offset, rows, weights):
     total = weights.shape[1]
     return pl.pallas_call(
-        functools.partial(forward_kernel, offset, rows),
+        functools.partial(forward_kernel, groups, offset, rows),
         in_specs=[VMEM] * 5,
-        out_specs=[VMEM] * len(GROUPS),
+        out_specs=[VMEM] * len(groups),
         out_shape=[
-            jax.ShapeDtypeStruct((len(group) * rows, total), jnp.bfloat16) for group in GROUPS
+            jax.ShapeDtypeStruct((len(group) * rows, total), jnp.bfloat16) for group in groups
         ],
         compiler_params=params(),
         cost_estimate=cheap(),
@@ -168,34 +171,43 @@
     )(*gathered, weights)
 
 
-def backward_kernel(*refs):
+def backward_kernel(halves, *refs):
     arrays, weights, outs = refs[:5], refs[5], refs[6:]
+    own, up, down, far_first, far_second = arrays
     total = weights.shape[1]
     width = total // 3
-    rows = arrays[3].shape[0]
+    rows = far_first.shape[0]
     for which, columns in enumerate((slice(2 * width, total), slice(0, 2 * width))):
-        left = jnp.concatenate(values_of(arrays, columns))
-        part = nt(left, weights[:, columns]).astype(jnp.bfloat16)
-        for at, (dz, half) in enumerate(GATHERED):
-            outs[2 * half + which][owner(dz)] = part[at * rows : (at + 1) * rows]
-
-
-def backward(arrays, weights):
+        left = []
+        for half in halves:
+            at = slice(half * rows, (half + 1) * rows)
+            left += [array[at, columns] for array in (own, up, down)]
+            left.append((far_first, far_second)[half][:, columns])
+        part = nt(jnp.concatenate(left), weights[:, columns]).astype(jnp.bfloat16)
+        for at in range(len(halves)):
+            for number, dz in enumerate((0, 1, 3, 2)):
+                first = (4 * at + number) * rows
+                outs[2 * at + which][owner(dz)] = part[first : first + rows]
+
+
+def backward(halves, arrays, weights):
     rows = arrays[3].shape[0]
     depth, total = weights.shape
+    count = 2 * len(halves)
     outs = pl.pallas_call(
-        backward_kernel,
+        functools.partial(backward_kernel, halves),
         in_specs=[VMEM] * 6,
-        out_specs=[VMEM] * 4,
-        out_shape=[jax.ShapeDtypeStruct((4, rows, depth), jnp.bfloat16)] * 4,
+        out_specs=[VMEM] * count,
+        out_shape=[jax.ShapeDtypeStruct((4, rows, depth), jnp.bfloat16)] * count,
         compiler_params=params(),
         cost_estimate=pl.CostEstimate(
-            flops=16 * rows * depth * total, bytes_accessed=8 * depth * total, transcendentals=0
+            flops=4 * count * rows * depth * total,
+            bytes_accessed=8 * depth * total,
+            transcendentals=0,
         ),
         name="backward",
     )(*arrays, weights)
-    outs = [out.reshape(4 * rows, depth) for out in outs]
-    return outs[2:], outs[:2]
+    return [out.reshape(4 * rows, depth) for out in outs]
 
 
 def weight_grad_kernel(offsets, *refs):
@@ -208,7 +220,7 @@
         parts = []
         for which, offset in enumerate(offsets):
             chunk = refs[9 * which : 9 * which + 9]
-            parts += tokens_of(kind, chunk[:4], offset, chunk[7].shape[0], columns)
+            parts += tokens_of(kind, chunk[:4], offset, chunk[7].shape[0], columns, GATHERED)
         return jnp.concatenate(parts)
 
     def values(columns):
@@ -300,14 +312,18 @@
 
 
 class Chunk:
-    def __init__(self, gather, offset, rows, weights):
+    def __init__(self, gather, offset, rows, weights, last):
         self.source, self.offset, self.rows = gather, offset, 2 * rows
         self.weights = weights
+        self.groups = TOGETHER if last else APART
+        self.halves = ((1,), (0,)) if last else ((1, 0),)
 
     def forward(self, *others):
         self.gathered = self.source.arrays
         gathered = after(self.gathered, *others)
-        outs = forward(gathered, self.offset, self.rows, self.weights)
+        outs = []
+        for groups in self.groups:
+            outs += forward(groups, gathered, self.offset, self.rows, self.weights)
         self.late_up, self.late_down, self.kept = outs[2:]
         self.from_down = move(outs[0], dz=1)
         self.from_up = move(outs[1], dz=-1)
@@ -353,7 +369,10 @@
 
     def backward(self, *others):
         self.arrays = after(self.arrays, *others)
-        self.for_other, self.for_own = backward(self.arrays, self.weights)
+        outs = []
+        for halves in self.halves:
+            outs += backward(halves, self.arrays, self.weights)
+        self.for_other, self.for_own = outs[:2], outs[2:]
         return self.for_other
 
     def send(self, *others):
@@ -394,7 +413,7 @@
         )
         gathers.append(gather)
         for i in group:
-            chunks.append(Chunk(gather, 2 * (starts[i] - first), CHUNKS[i], weights))
+            chunks.append(Chunk(gather, 2 * (starts[i] - first), CHUNKS[i], weights, i == len(CHUNKS) - 1))
     gathers[0].far()
     before = gathers[0].core(weights, *[gather.pair for gather in gathers[1:]])
     gathers[1].far(before)

time: 169 us -> 173 us (1.024)
  waiting for transfers between devices: 71.5 us -> 76.1 us
    ppermute x42, waiting for transfers between devices: 71.5 us -> 76.1 us  [move(): return lax.ppermute(array, ('row', 'col'), pairs)]
    pallas_call x4 -> x6, Pallas kernels: 13.2 us -> 13.6 us  [the longest x3 7.05 us: forward(): pl.pallas_call(functools.partial(forward_kernel, groups, offset, rows), i...]
  transfers between devices with their start and end apart: 42 -> 42, of which waited for: 21 -> 21; matrix products, arithmetic and copies ran while one was open for 2% -> 2% of each run, Pallas kernels for 13% -> 14%
where the time goes in v10:
time: 173 us; the launch traced here: 172 us
  waiting for transfers between devices  76.1 us (44%)
  starting transfers between devices  59.2 us (34%)
  Pallas kernels  25.9 us (15%)
  local copies, waits for them, and re-layouts  5.75 us (3%)
  other arithmetic  4.15 us (2%)
    ppermute x42, waiting for transfers between devices, move(): return lax.ppermute(array, ('row', 'col'), pairs)  76.1 us
    ppermute x42, starting transfers between devices, move(): return lax.ppermute(array, ('row', 'col'), pairs)  59.2 us
    pallas_call x1, Pallas kernels, weight_grads(): pl.pallas_call(functools.partial(weight_grad_kernel, offsets), in_specs=[...  9.58 us
    pallas_call x3, Pallas kernels, forward(): pl.pallas_call(functools.partial(forward_kernel, groups, offset, rows), i...  7.05 us
    pallas_call x3, Pallas kernels, backward(): pl.pallas_call(functools.partial(backward_kernel, halves), in_specs=[VMEM...  6.53 us
    unnamed x12, local copies, waits for them, and re-layouts  4.51 us
  transfers between devices with their start and end apart: 42, of which 21 were waited for; matrix products, arithmetic and copies ran while one was open for 2% of the time, Pallas kernels for 14%

profile of v10, /device:TPU:0, one launch (start us, length us, event | category | flops | bytes accessed | tf_op | source)
XLA Modules:
  0.0 172.3 jit_solution(13187041787568093020)
XLA Ops:
  1.7 3.2 %collective-permute-start = (bf16[2,32,1024]{2,1,0:T(8,128)(2,1)S(1)}, bf16[2,32,1024]{2,1,0:T(8,128)(2,1)S(1)}, u32[]{:S(2)}, u32[]{:S(2)}) collective-permute-start(bf16[2,32,1024]{2,1,0:T(8,128)(2,1)S(1)} %pad_maximum_fusion.13), channel_id=1, source_target_pairs={{0,2},{1,3},{2,0},{3,1},{4,6},{5,7},{6,4},{7,5},{8,10},{9,11},{10,... | collective-permute-start | bytes 393224 | tf_op jit(solution)/shard_map/ppermute | solution.py:55
  4.8 3.5 %collective-permute-done = bf16[2,32,1024]{2,1,0:T(8,128)(2,1)S(1)} collective-permute-done((bf16[2,32,1024]{2,1,0:T(8,128)(2,1)S(1)}, bf16[2,32,1024]{2,1,0:T(8,128)(2,1)S(1)}, u32[]{:S(2)}, u32[]{:S(2)}) %collective-permute-start) | collective-permute-done | bytes 131104 | tf_op jit(solution)/shard_map/ppermute | solution.py:55
  8.4 3.3 %collective-permute-start.1 = (bf16[2,64,1024]{2,1,0:T(8,128)(2,1)S(1)}, bf16[2,64,1024]{2,1,0:T(8,128)(2,1)S(1)}, u32[]{:S(2)}, u32[]{:S(2)}) collective-permute-start(bf16[2,64,1024]{2,1,0:T(8,128)(2,1)S(1)} %pad_maximum_fusion.10), channel_id=1, source_target_pairs={{0,12},{1,13},{2,14},{3,15},{4,0},{5,1},{6,2},{7,3},{8,4},{9,5},{1... | collective-permute-start | bytes 786440 | tf_op jit(solution)/shard_map/ppermute | solution.py:55
  13.3 3.1 %collective-permute-start.4 = (bf16[2,32,1024]{2,1,0:T(8,128)(2,1)S(1)}, bf16[2,32,1024]{2,1,0:T(8,128)(2,1)S(1)}, u32[]{:S(2)}, u32[]{:S(2)}) collective-permute-start(bf16[2,32,1024]{2,1,0:T(8,128)(2,1)S(1)} %pad_maximum_fusion.14), channel_id=1, source_target_pairs={{0,2},{1,3},{2,0},{3,1},{4,6},{5,7},{6,4},{7,5},{8,10},{9,11},{10,... | collective-permute-start | bytes 393224 | tf_op jit(solution)/shard_map/ppermute | solution.py:55
  16.4 1.5 copy-done
  17.9 1.5 copy-done.1
  19.4 1.5 copy-done.2
  20.9 2.8 %mask_weights.1.refs_4_.refs_5_ = bf16[1024,2688]{1,0:T(8,128)(2,1)S(1)} custom-call(bf16[1024,896]{1,0:T(8,128)(2,1)S(1)} %copy-done, bf16[1024,896]{1,0:T(8,128)(2,1)S(1)} %copy-done.1, bf16[896,1024]{1,0:T(8,128)(2,1)S(1)} %copy-done.2, s32[8,7]{1,0:T(8,128)S(1)} %copy-done.3, s32[8,7]{1,0:T(8,128)S(1)} %copy-done.4, s32[7,8]{1,0:T(8,128)S(1)} %copy-done.5), custom_call_target="tpu_custom_call" | custom-call | flops 2752512 | bytes 11010048 | tf_op jit(solution)/shard_map/mask_weights/pallas_call | solution.py:121
  23.7 1.9 %collective-permute-done.3 = bf16[2,64,1024]{2,1,0:T(8,128)(2,1)S(1)} collective-permute-done((bf16[2,64,1024]{2,1,0:T(8,128)(2,1)S(1)}, bf16[2,64,1024]{2,1,0:T(8,128)(2,1)S(1)}, u32[]{:S(2)}, u32[]{:S(2)}) %collective-permute-start.3) | collective-permute-done | bytes 262176 | tf_op jit(solution)/shard_map/ppermute | solution.py:55
  26.6 1.2 collective-permute-done.5.refs_2_
  28.6 1.8 %forward.4 = (bf16[128,2688]{1,0:T(8,128)(2,1)S(1)}, bf16[128,2688]{1,0:T(8,128)(2,1)S(1)}) custom-call(bf16[4,64,1024]{2,1,0:T(8,128)(2,1)S(1)} %pad_maximum_fusion.6.refs_0_, bf16[4,64,1024]{2,1,0:T(8,128)(2,1)S(1)} %pad_maximum_fusion.7.refs_1_, bf16[4,64,1024]{2,1,0:T(8,128)(2,1)S(1)} %collective-permute-done.5.refs_2_, ...), custom_call_target="tpu_custom_call" | custom-call | flops 1024 | bytes 1024 | tf_op jit(solution)/shard_map/forward/pallas_call | solution.py:161
  30.4 2.0 %collective-permute-start.7 = (bf16[128,2688]{1,0:T(8,128)(2,1)S(1)}, bf16[128,2688]{1,0:T(8,128)(2,1)S(1)}, u32[]{:S(2)}, u32[]{:S(2)}) collective-permute-start(bf16[128,2688]{1,0:T(8,128)(2,1)S(1)} %get-tuple-element.111), channel_id=1, source_target_pairs={{0,16},{1,49},{2,18},{3,51},{4,20},{5,53},{6,22},{7,55},{8,24},{9,... | collective-permute-start | bytes 2064392 | tf_op jit(solution)/shard_map/ppermute | solution.py:55
  33.0 1.4 collective-permute-start.12
  34.5 1.8 %forward.3 = (bf16[64,2688]{1,0:T(8,128)(2,1)S(1)}, bf16[64,2688]{1,0:T(8,128)(2,1)S(1)}, bf16[128,2688]{1,0:T(8,128)(2,1)S(1)}) custom-call(bf16[4,64,1024]{2,1,0:T(8,128)(2,1)S(1)} %pad_maximum_fusion.6.refs_0_, bf16[4,64,1024]{2,1,0:T(8,128)(2,1)S(1)} %pad_maximum_fusion.7.refs_1_, bf16[4,64,1024]{2,1,0:T(8,128)(2,1)S(1)} %collective-permute-done.5.refs_2_, ...), custom_call_target="tpu_custom_call" | custom-call | flops 1024 | bytes 1024 | tf_op jit(solution)/shard_map/forward/pallas_call | solution.py:161
  36.3 2.3 %collective-permute-start.9 = (bf16[128,2688]{1,0:T(8,128)(2,1)S(1)}, bf16[128,2688]{1,0:T(8,128)(2,1)S(1)}, u32[]{:S(2)}, u32[]{:S(2)}) collective-permute-start(bf16[128,2688]{1,0:T(8,128)(2,1)S(1)} %get-tuple-element.114), channel_id=1, source_target_pairs={{0,48},{1,17},{2,50},{3,19},{4,52},{5,21},{6,54},{7,23},{8,56},{9,... | collective-permute-start | bytes 2064392 | tf_op jit(solution)/shard_map/ppermute | solution.py:55
  38.6 6.7 %collective-permute-done.7 = bf16[128,2688]{1,0:T(8,128)(2,1)S(1)} collective-permute-done((bf16[128,2688]{1,0:T(8,128)(2,1)S(1)}, bf16[128,2688]{1,0:T(8,128)(2,1)S(1)}, u32[]{:S(2)}, u32[]{:S(2)}) %collective-permute-start.7) | collective-permute-done | bytes 688160 | tf_op jit(solution)/shard_map/ppermute | solution.py:55
  45.3 4.2 %collective-permute-done.9 = bf16[128,2688]{1,0:T(8,128)(2,1)S(1)} collective-permute-done((bf16[128,2688]{1,0:T(8,128)(2,1)S(1)}, bf16[128,2688]{1,0:T(8,128)(2,1)S(1)}, u32[]{:S(2)}, u32[]{:S(2)}) %collective-permute-start.9) | collective-permute-done | bytes 688160 | tf_op jit(solution)/shard_map/ppermute | solution.py:55
  49.8 1.2 collective-permute-start.14
  51.2 3.2 %collective-permute-start.10 = (bf16[64,2688]{1,0:T(8,128)(2,1)S(1)}, bf16[64,2688]{1,0:T(8,128)(2,1)S(1)}, u32[]{:S(2)}, u32[]{:S(2)}) collective-permute-start(bf16[64,2688]{1,0:T(8,128)(2,1)S(1)} %slice_add_fusion.2), channel_id=1, source_target_pairs={{0,48},{1,17},{2,50},{3,19},{4,52},{5,21},{6,54},{7,23},{8,56},{9,... | collective-permute-start | bytes 1032200 | tf_op jit(solution)/shard_map/ppermute | solution.py:55
  54.5 3.4 %forward.5 = (bf16[128,2688]{1,0:T(8,128)(2,1)S(1)}, bf16[128,2688]{1,0:T(8,128)(2,1)S(1)}, bf16[64,2688]{1,0:T(8,128)(2,1)S(1)}, bf16[64,2688]{1,0:T(8,128)(2,1)S(1)}, bf16[128,2688]{1,0:T(8,128)(2,1)S(1)}) custom-call(bf16[4,64,1024]{2,1,0:T(8,128)(2,1)S(1)} %pad_maximum_fusion.8.refs_0_.refs_9_, ...), custom_call_target="tpu_custom_call" | custom-call | flops 1024 | bytes 1024 | tf_op jit(solution)/shard_map/forward/pallas_call | solution.py:161
  58.0 3.5 %collective-permute-done.8 = bf16[64,2688]{1,0:T(8,128)(2,1)S(1)} collective-permute-done((bf16[64,2688]{1,0:T(8,128)(2,1)S(1)}, bf16[64,2688]{1,0:T(8,128)(2,1)S(1)}, u32[]{:S(2)}, u32[]{:S(2)}) %collective-permute-start.8) | collective-permute-done | bytes 344096 | tf_op jit(solution)/shard_map/ppermute | solution.py:55
  61.5 1.5 collective-permute-done.10
  62.9 3.7 %collective-permute-start.18 = (bf16[128,2688]{1,0:T(8,128)(2,1)S(1)}, bf16[128,2688]{1,0:T(8,128)(2,1)S(1)}, u32[]{:S(2)}, u32[]{:S(2)}) collective-permute-start(bf16[128,2688]{1,0:T(8,128)(2,1)S(1)} %get-tuple-element.131), channel_id=1, source_target_pairs={{0,48},{1,17},{2,50},{3,19},{4,52},{5,21},{6,54},{7,23},{8,56},{9,... | collective-permute-start | bytes 2064392 | tf_op jit(solution)/shard_map/ppermute | solution.py:55
  67.0 1.6 collective-permute-start.16
  68.5 5.0 %collective-permute-done.17 = bf16[128,2688]{1,0:T(8,128)(2,1)S(1)} collective-permute-done((bf16[128,2688]{1,0:T(8,128)(2,1)S(1)}, bf16[128,2688]{1,0:T(8,128)(2,1)S(1)}, u32[]{:S(2)}, u32[]{:S(2)}) %collective-permute-start.17) | collective-permute-done | bytes 688160 | tf_op jit(solution)/shard_map/ppermute | solution.py:55
  73.7 4.7 %collective-permute-done.18 = bf16[128,2688]{1,0:T(8,128)(2,1)S(1)} collective-permute-done((bf16[128,2688]{1,0:T(8,128)(2,1)S(1)}, bf16[128,2688]{1,0:T(8,128)(2,1)S(1)}, u32[]{:S(2)}, u32[]{:S(2)}) %collective-permute-start.18) | collective-permute-done | bytes 688160 | tf_op jit(solution)/shard_map/ppermute | solution.py:55
  78.5 3.8 %collective-permute-start.22 = (bf16[64,2688]{1,0:T(8,128)(2,1)S(1)}, bf16[64,2688]{1,0:T(8,128)(2,1)S(1)}, u32[]{:S(2)}, u32[]{:S(2)}) collective-permute-start(bf16[64,2688]{1,0:T(8,128)(2,1)S(1)} %slice_add_fusion), channel_id=1, source_target_pairs={{0,48},{1,17},{2,50},{3,19},{4,52},{5,21},{6,54},{7,23},{8,56},{9,... | collective-permute-start | bytes 1032200 | tf_op jit(solution)/shard_map/ppermute | solution.py:55
  82.8 3.2 %collective-permute-start.19 = (bf16[128,2688]{1,0:T(8,128)(2,1)S(1)}, bf16[128,2688]{1,0:T(8,128)(2,1)S(1)}, u32[]{:S(2)}, u32[]{:S(2)}) collective-permute-start(bf16[128,2688]{1,0:T(8,128)(2,1)S(1)} %pad_maximum_fusion.3.refs_0_.refs_4_), channel_id=1, source_target_pairs={{0,48},{1,17},{2,50},{3,19},{4,52},{5,21},{6,54},{7,23},{8,56},{9,... | collective-permute-start | bytes 2064392 | tf_op jit(solution)/shard_map/ppermute | solution.py:55
  86.0 3.4 %collective-permute-done.22 = bf16[64,2688]{1,0:T(8,128)(2,1)S(1)} collective-permute-done((bf16[64,2688]{1,0:T(8,128)(2,1)S(1)}, bf16[64,2688]{1,0:T(8,128)(2,1)S(1)}, u32[]{:S(2)}, u32[]{:S(2)}) %collective-permute-start.22) | collective-permute-done | bytes 344096 | tf_op jit(solution)/shard_map/ppermute | solution.py:55
  89.8 1.6 collective-permute-start.25
  91.3 10.1 %collective-permute-done.20.refs_2_.refs_6_ = bf16[128,2688]{1,0:T(8,128)(2,1)S(1)} collective-permute-done((bf16[128,2688]{1,0:T(8,128)(2,1)S(1)}, bf16[128,2688]{1,0:T(8,128)(2,1)S(1)}, u32[]{:S(2)}, u32[]{:S(2)}) %collective-permute-start.20) | collective-permute-done | bytes 688160 | tf_op jit(solution)/shard_map/ppermute | solution.py:55
  101.8 3.8 %collective-permute-start.24 = (bf16[64,2688]{1,0:T(8,128)(2,1)S(1)}, bf16[64,2688]{1,0:T(8,128)(2,1)S(1)}, u32[]{:S(2)}, u32[]{:S(2)}) collective-permute-start(bf16[64,2688]{1,0:T(8,128)(2,1)S(1)} %slice.204), channel_id=1, source_target_pairs={{0,48},{1,17},{2,50},{3,19},{4,52},{5,21},{6,54},{7,23},{8,56},{9,... | collective-permute-start | bytes 1032200 | tf_op jit(solution)/shard_map/ppermute | solution.py:55
  106.1 2.0 %collective-permute-start.28 = (bf16[128,2688]{1,0:T(8,128)(2,1)S(1)}, bf16[128,2688]{1,0:T(8,128)(2,1)S(1)}, u32[]{:S(2)}, u32[]{:S(2)}) collective-permute-start(bf16[128,2688]{1,0:T(8,128)(2,1)S(1)} %pad_maximum_fusion.5.refs_0_.refs_13_), channel_id=1, source_target_pairs={{0,16},{1,49},{2,18},{3,51},{4,20},{5,53},{6,22},{7,55},{8,24},{9,... | collective-permute-start | bytes 2064392 | tf_op jit(solution)/shard_map/ppermute | solution.py:55
  108.1 4.7 %collective-permute-done.23.refs_3_.refs_7_ = bf16[64,2688]{1,0:T(8,128)(2,1)S(1)} collective-permute-done((bf16[64,2688]{1,0:T(8,128)(2,1)S(1)}, bf16[64,2688]{1,0:T(8,128)(2,1)S(1)}, u32[]{:S(2)}, u32[]{:S(2)}) %collective-permute-start.23) | collective-permute-done | bytes 344096 | tf_op jit(solution)/shard_map/ppermute | solution.py:55
  112.8 1.3 collective-permute-done.24.refs_4_.refs_8_
  114.1 3.2 %backward.3 = (bf16[4,64,1024]{2,1,0:T(8,128)(2,1)S(1)}, bf16[4,64,1024]{2,1,0:T(8,128)(2,1)S(1)}, bf16[4,64,1024]{2,1,0:T(8,128)(2,1)S(1)}, bf16[4,64,1024]{2,1,0:T(8,128)(2,1)S(1)}) custom-call(bf16[128,2688]{1,0:T(8,128)(2,1)S(1)} %pad_maximum_fusion.3.refs_0_.refs_4_, bf16[128,2688]{1,0:T(8,128)(2,1)S(1)} %collective-permute-done.19.refs_1_.refs_5_, ...), custom_call_target="tpu_custom_call" | custom-call | flops 2818572288 | bytes 22020096 | tf_op jit(solution)/shard_map/backward/pallas_call | solution.py:197
  118.1 9.4 %collective-permute-done.28.refs_2_.refs_15_ = bf16[128,2688]{1,0:T(8,128)(2,1)S(1)} collective-permute-done((bf16[128,2688]{1,0:T(8,128)(2,1)S(1)}, bf16[128,2688]{1,0:T(8,128)(2,1)S(1)}, u32[]{:S(2)}, u32[]{:S(2)}) %collective-permute-start.28) | collective-permute-done | bytes 688160 | tf_op jit(solution)/shard_map/ppermute | solution.py:55
  127.7 3.3 %collective-permute-start.34 = (bf16[64,2688]{1,0:T(8,128)(2,1)S(1)}, bf16[64,2688]{1,0:T(8,128)(2,1)S(1)}, u32[]{:S(2)}, u32[]{:S(2)}) collective-permute-start(bf16[64,2688]{1,0:T(8,128)(2,1)S(1)} %slice.209), channel_id=1, source_target_pairs={{0,48},{1,17},{2,50},{3,19},{4,52},{5,21},{6,54},{7,23},{8,56},{9,... | collective-permute-start | bytes 1032200 | tf_op jit(solution)/shard_map/ppermute | solution.py:55
  131.6 1.6 collective-permute-start.31
  133.2 2.1 %collective-permute-start.32 = (bf16[64,2048]{1,0:T(8,128)(2,1)S(1)}, bf16[64,2048]{1,0:T(8,128)(2,1)S(1)}, u32[]{:S(2)}, u32[]{:S(2)}) collective-permute-start(bf16[64,2048]{1,0:T(8,128)(2,1)S(1)} %get-tuple-element.207), channel_id=1, source_target_pairs={{0,12},{1,13},{2,14},{3,15},{4,0},{5,1},{6,2},{7,3},{8,4},{9,5},{1... | collective-permute-start | bytes 786440 | tf_op jit(solution)/shard_map/ppermute | solution.py:55
  135.2 4.3 %collective-permute-done.33.refs_3_.refs_16_ = bf16[64,2688]{1,0:T(8,128)(2,1)S(1)} collective-permute-done((bf16[64,2688]{1,0:T(8,128)(2,1)S(1)}, bf16[64,2688]{1,0:T(8,128)(2,1)S(1)}, u32[]{:S(2)}, u32[]{:S(2)}) %collective-permute-start.33) | collective-permute-done | bytes 344096 | tf_op jit(solution)/shard_map/ppermute | solution.py:55
  139.6 1.7 backward.4
  141.9 2.2 %collective-permute-done.30 = bf16[64,2048]{1,0:T(8,128)(2,1)S(1)} collective-permute-done((bf16[64,2048]{1,0:T(8,128)(2,1)S(1)}, bf16[64,2048]{1,0:T(8,128)(2,1)S(1)}, u32[]{:S(2)}, u32[]{:S(2)}) %collective-permute-start.30) | collective-permute-done | bytes 262176 | tf_op jit(solution)/shard_map/ppermute | solution.py:55
  144.8 3.1 %collective-permute-start.35 = (bf16[32,2048]{1,0:T(8,128)(2,1)S(1)}, bf16[32,2048]{1,0:T(8,128)(2,1)S(1)}, u32[]{:S(2)}, u32[]{:S(2)}) collective-permute-start(bf16[32,2048]{1,0:T(8,128)(2,1)S(1)} %slice.239), channel_id=1, source_target_pairs={{0,2},{1,3},{2,0},{3,1},{4,6},{5,7},{6,4},{7,5},{8,10},{9,11},{10,... | collective-permute-start | bytes 393224 | tf_op jit(solution)/shard_map/ppermute | solution.py:55
  147.9 1.7 backward.5
  151.0 3.4 %collective-permute-start.39 = (bf16[64,2048]{1,0:T(8,128)(2,1)S(1)}, bf16[64,2048]{1,0:T(8,128)(2,1)S(1)}, u32[]{:S(2)}, u32[]{:S(2)}) collective-permute-start(bf16[64,2048]{1,0:T(8,128)(2,1)S(1)} %get-tuple-element.205), channel_id=1, source_target_pairs={{0,8},{1,9},{2,10},{3,11},{4,12},{5,13},{6,14},{7,15},{8,0},{9,1},... | collective-permute-start | bytes 786440 | tf_op jit(solution)/shard_map/ppermute | solution.py:55
  154.4 9.6 %weight_grads.1 = (bf16[1024,896]{1,0:T(8,128)(2,1)}, bf16[1024,896]{1,0:T(8,128)(2,1)}, bf16[896,1024]{1,0:T(8,128)(2,1)}) custom-call(bf16[4,64,1024]{2,1,0:T(8,128)(2,1)S(1)} %pad_maximum_fusion.6.refs_0_, bf16[4,64,1024]{2,1,0:T(8,128)(2,1)S(1)} %pad_maximum_fusion.7.refs_1_, bf16[4,64,1024]{2,1,0:T(8,128)(2,1)S(1)} %collective-permute-done.5.refs_2_, ...), custom_call_target="tpu_custom_call" | custom-call | flops 5637144576 | bytes 44040192 | tf_op jit(solution)/shard_map/weight_grads/pallas_call | solution.py:257
  165.6 5.9 %collective-permute-done.41 = bf16[32,2048]{1,0:T(8,128)(2,1)S(1)} collective-permute-done((bf16[32,2048]{1,0:T(8,128)(2,1)S(1)}, bf16[32,2048]{1,0:T(8,128)(2,1)S(1)}, u32[]{:S(2)}, u32[]{:S(2)}) %collective-permute-start.41) | collective-permute-done | bytes 131104 | tf_op jit(solution)/shard_map/ppermute | solution.py:55
  (104 shorter events, 14.4 us)
Async XLA Ops:
  0.6 15.8 %copy-start.3 = (s32[8,7]{1,0:T(8,128)S(1)}, s32[8,7]{1,0:T(8,128)}, u32[]{:S(2)}) copy-start(s32[8,7]{1,0:T(8,128)} %refs_18_.1) | copy-start | bytes 676
  0.6 15.8 %copy-start.4 = (s32[8,7]{1,0:T(8,128)S(1)}, s32[8,7]{1,0:T(8,128)}, u32[]{:S(2)}) copy-start(s32[8,7]{1,0:T(8,128)} %refs_19_.1) | copy-start | bytes 676
  0.7 15.7 %copy-start.5 = (s32[7,8]{1,0:T(8,128)S(1)}, s32[7,8]{1,0:T(8,128)}, u32[]{:S(2)}) copy-start(s32[7,8]{1,0:T(8,128)} %refs_20_.1) | copy-start | bytes 676
  1.7 6.7 %collective-permute-start = (bf16[2,32,1024]{2,1,0:T(8,128)(2,1)S(1)}, bf16[2,32,1024]{2,1,0:T(8,128)(2,1)S(1)}, u32[]{:S(2)}, u32[]{:S(2)}) collective-permute-start(bf16[2,32,1024]{2,1,0:T(8,128)(2,1)S(1)} %pad_maximum_fusion.13), channel_id=1, source_target_pairs={{0,2},{1,3},{2,0},{3,1},{4,6},{5,7},{6,4},{7,5},{8,10},{9,11},{10,... | collective-permute-start | bytes 393224 | tf_op jit(solution)/shard_map/ppermute | solution.py:55
  8.4 15.4 %collective-permute-start.1 = (bf16[2,64,1024]{2,1,0:T(8,128)(2,1)S(1)}, bf16[2,64,1024]{2,1,0:T(8,128)(2,1)S(1)}, u32[]{:S(2)}, u32[]{:S(2)}) collective-permute-start(bf16[2,64,1024]{2,1,0:T(8,128)(2,1)S(1)} %pad_maximum_fusion.10), channel_id=1, source_target_pairs={{0,12},{1,13},{2,14},{3,15},{4,0},{5,1},{6,2},{7,3},{8,4},{9,5},{1... | collective-permute-start | bytes 786440 | tf_op jit(solution)/shard_map/ppermute | solution.py:55
  11.7 12.1 %collective-permute-start.2 = (bf16[2,64,1024]{2,1,0:T(8,128)(2,1)S(1)}, bf16[2,64,1024]{2,1,0:T(8,128)(2,1)S(1)}, u32[]{:S(2)}, u32[]{:S(2)}) collective-permute-start(bf16[2,64,1024]{2,1,0:T(8,128)(2,1)S(1)} %pad_maximum_fusion.10), channel_id=1, source_target_pairs={{0,8},{1,9},{2,10},{3,11},{4,12},{5,13},{6,14},{7,15},{8,0},{9,1},... | collective-permute-start | bytes 786440 | tf_op jit(solution)/shard_map/ppermute | solution.py:55
  12.3 13.4 %collective-permute-start.3 = (bf16[2,64,1024]{2,1,0:T(8,128)(2,1)S(1)}, bf16[2,64,1024]{2,1,0:T(8,128)(2,1)S(1)}, u32[]{:S(2)}, u32[]{:S(2)}) collective-permute-start(bf16[2,64,1024]{2,1,0:T(8,128)(2,1)S(1)} %pad_maximum_fusion.10), channel_id=1, source_target_pairs={{0,4},{1,5},{2,6},{3,7},{4,8},{5,9},{6,10},{7,11},{8,12},{9,13},{1... | collective-permute-start | bytes 786440 | tf_op jit(solution)/shard_map/ppermute | solution.py:55
  13.3 10.4 %collective-permute-start.4 = (bf16[2,32,1024]{2,1,0:T(8,128)(2,1)S(1)}, bf16[2,32,1024]{2,1,0:T(8,128)(2,1)S(1)}, u32[]{:S(2)}, u32[]{:S(2)}) collective-permute-start(bf16[2,32,1024]{2,1,0:T(8,128)(2,1)S(1)} %pad_maximum_fusion.14), channel_id=1, source_target_pairs={{0,2},{1,3},{2,0},{3,1},{4,6},{5,7},{6,4},{7,5},{8,10},{9,11},{10,... | collective-permute-start | bytes 393224 | tf_op jit(solution)/shard_map/ppermute | solution.py:55
  16.4 1.5 copy-start
  17.9 1.5 copy-start.1
  19.4 1.5 copy-start.2
  25.9 2.0 %collective-permute-start.5 = (bf16[4,64,1024]{2,1,0:T(8,128)(2,1)S(1)}, bf16[4,64,1024]{2,1,0:T(8,128)(2,1)S(1)}, u32[]{:S(2)}, u32[]{:S(2)}) collective-permute-start(bf16[4,64,1024]{2,1,0:T(8,128)(2,1)S(1)} %pad_maximum_fusion.6.refs_0_), channel_id=1, source_target_pairs={{0,1},{1,0},{2,3},{3,2},{4,5},{5,4},{6,7},{7,6},{8,9},{9,8},{10,11... | collective-permute-start | bytes 1572872 | tf_op jit(solution)/shard_map/ppermute | solution.py:55
  26.0 2.6 %collective-permute-start.6 = (bf16[4,64,1024]{2,1,0:T(8,128)(2,1)S(1)}, bf16[4,64,1024]{2,1,0:T(8,128)(2,1)S(1)}, u32[]{:S(2)}, u32[]{:S(2)}) collective-permute-start(bf16[4,64,1024]{2,1,0:T(8,128)(2,1)S(1)} %pad_maximum_fusion.7.refs_1_), channel_id=1, source_target_pairs={{0,1},{1,0},{2,3},{3,2},{4,5},{5,4},{6,7},{7,6},{8,9},{9,8},{10,11... | collective-permute-start | bytes 1572872 | tf_op jit(solution)/shard_map/ppermute | solution.py:55
  30.4 14.8 %collective-permute-start.7 = (bf16[128,2688]{1,0:T(8,128)(2,1)S(1)}, bf16[128,2688]{1,0:T(8,128)(2,1)S(1)}, u32[]{:S(2)}, u32[]{:S(2)}) collective-permute-start(bf16[128,2688]{1,0:T(8,128)(2,1)S(1)} %get-tuple-element.111), channel_id=1, source_target_pairs={{0,16},{1,49},{2,18},{3,51},{4,20},{5,53},{6,22},{7,55},{8,24},{9,... | collective-permute-start | bytes 2064392 | tf_op jit(solution)/shard_map/ppermute | solution.py:55
  32.4 17.2 %collective-permute-start.11 = (bf16[2,64,1024]{2,1,0:T(8,128)(2,1)S(1)}, bf16[2,64,1024]{2,1,0:T(8,128)(2,1)S(1)}, u32[]{:S(2)}, u32[]{:S(2)}) collective-permute-start(bf16[2,64,1024]{2,1,0:T(8,128)(2,1)S(1)} %pad_maximum_fusion.11), channel_id=1, source_target_pairs={{0,12},{1,13},{2,14},{3,15},{4,0},{5,1},{6,2},{7,3},{8,4},{9,5},{1... | collective-permute-start | bytes 786440 | tf_op jit(solution)/shard_map/ppermute | solution.py:55
  33.0 16.6 %collective-permute-start.12 = (bf16[2,64,1024]{2,1,0:T(8,128)(2,1)S(1)}, bf16[2,64,1024]{2,1,0:T(8,128)(2,1)S(1)}, u32[]{:S(2)}, u32[]{:S(2)}) collective-permute-start(bf16[2,64,1024]{2,1,0:T(8,128)(2,1)S(1)} %pad_maximum_fusion.11), channel_id=1, source_target_pairs={{0,8},{1,9},{2,10},{3,11},{4,12},{5,13},{6,14},{7,15},{8,0},{9,1},... | collective-permute-start | bytes 786440 | tf_op jit(solution)/shard_map/ppermute | solution.py:55
  34.4 15.2 %collective-permute-start.13 = (bf16[2,64,1024]{2,1,0:T(8,128)(2,1)S(1)}, bf16[2,64,1024]{2,1,0:T(8,128)(2,1)S(1)}, u32[]{:S(2)}, u32[]{:S(2)}) collective-permute-start(bf16[2,64,1024]{2,1,0:T(8,128)(2,1)S(1)} %pad_maximum_fusion.11), channel_id=1, source_target_pairs={{0,4},{1,5},{2,6},{3,7},{4,8},{5,9},{6,10},{7,11},{8,12},{9,13},{1... | collective-permute-start | bytes 786440 | tf_op jit(solution)/shard_map/ppermute | solution.py:55
  36.3 13.2 %collective-permute-start.9 = (bf16[128,2688]{1,0:T(8,128)(2,1)S(1)}, bf16[128,2688]{1,0:T(8,128)(2,1)S(1)}, u32[]{:S(2)}, u32[]{:S(2)}) collective-permute-start(bf16[128,2688]{1,0:T(8,128)(2,1)S(1)} %get-tuple-element.114), channel_id=1, source_target_pairs={{0,48},{1,17},{2,50},{3,19},{4,52},{5,21},{6,54},{7,23},{8,56},{9,... | collective-permute-start | bytes 2064392 | tf_op jit(solution)/shard_map/ppermute | solution.py:55
  49.8 4.7 %collective-permute-start.14 = (bf16[4,64,1024]{2,1,0:T(8,128)(2,1)S(1)}, bf16[4,64,1024]{2,1,0:T(8,128)(2,1)S(1)}, u32[]{:S(2)}, u32[]{:S(2)}) collective-permute-start(bf16[4,64,1024]{2,1,0:T(8,128)(2,1)S(1)} %pad_maximum_fusion.8.refs_0_.refs_9_), channel_id=1, source_target_pairs={{0,1},{1,0},{2,3},{3,2},{4,5},{5,4},{6,7},{7,6},{8,9},{9,8},{10,11... | collective-permute-start | bytes 1572872 | tf_op jit(solution)/shard_map/ppermute | solution.py:55
  51.1 3.4 %collective-permute-start.15 = (bf16[4,64,1024]{2,1,0:T(8,128)(2,1)S(1)}, bf16[4,64,1024]{2,1,0:T(8,128)(2,1)S(1)}, u32[]{:S(2)}, u32[]{:S(2)}) collective-permute-start(bf16[4,64,1024]{2,1,0:T(8,128)(2,1)S(1)} %pad_maximum_fusion.9.refs_1_.refs_10_), channel_id=1, source_target_pairs={{0,1},{1,0},{2,3},{3,2},{4,5},{5,4},{6,7},{7,6},{8,9},{9,8},{10,11... | collective-permute-start | bytes 1572872 | tf_op jit(solution)/shard_map/ppermute | solution.py:55
  51.2 10.3 %collective-permute-start.8 = (bf16[64,2688]{1,0:T(8,128)(2,1)S(1)}, bf16[64,2688]{1,0:T(8,128)(2,1)S(1)}, u32[]{:S(2)}, u32[]{:S(2)}) collective-permute-start(bf16[64,2688]{1,0:T(8,128)(2,1)S(1)} %slice_add_fusion.3), channel_id=1, source_target_pairs={{0,16},{1,49},{2,18},{3,51},{4,20},{5,53},{6,22},{7,55},{8,24},{9,... | collective-permute-start | bytes 1032200 | tf_op jit(solution)/shard_map/ppermute | solution.py:55
  51.2 11.7 %collective-permute-start.10 = (bf16[64,2688]{1,0:T(8,128)(2,1)S(1)}, bf16[64,2688]{1,0:T(8,128)(2,1)S(1)}, u32[]{:S(2)}, u32[]{:S(2)}) collective-permute-start(bf16[64,2688]{1,0:T(8,128)(2,1)S(1)} %slice_add_fusion.2), channel_id=1, source_target_pairs={{0,48},{1,17},{2,50},{3,19},{4,52},{5,21},{6,54},{7,23},{8,56},{9,... | collective-permute-start | bytes 1032200 | tf_op jit(solution)/shard_map/ppermute | solution.py:55
  57.9 15.7 %collective-permute-start.17 = (bf16[128,2688]{1,0:T(8,128)(2,1)S(1)}, bf16[128,2688]{1,0:T(8,128)(2,1)S(1)}, u32[]{:S(2)}, u32[]{:S(2)}) collective-permute-start(bf16[128,2688]{1,0:T(8,128)(2,1)S(1)} %get-tuple-element.125), channel_id=1, source_target_pairs={{0,16},{1,49},{2,18},{3,51},{4,20},{5,53},{6,22},{7,55},{8,24},{9,... | collective-permute-start | bytes 2064392 | tf_op jit(solution)/shard_map/ppermute | solution.py:55
  62.9 15.5 %collective-permute-start.18 = (bf16[128,2688]{1,0:T(8,128)(2,1)S(1)}, bf16[128,2688]{1,0:T(8,128)(2,1)S(1)}, u32[]{:S(2)}, u32[]{:S(2)}) collective-permute-start(bf16[128,2688]{1,0:T(8,128)(2,1)S(1)} %get-tuple-element.131), channel_id=1, source_target_pairs={{0,48},{1,17},{2,50},{3,19},{4,52},{5,21},{6,54},{7,23},{8,56},{9,... | collective-permute-start | bytes 2064392 | tf_op jit(solution)/shard_map/ppermute | solution.py:55
  67.0 15.3 %collective-permute-start.16 = (bf16[128,2688]{1,0:T(8,128)(2,1)S(1)}, bf16[128,2688]{1,0:T(8,128)(2,1)S(1)}, u32[]{:S(2)}, u32[]{:S(2)}) collective-permute-start(bf16[128,2688]{1,0:T(8,128)(2,1)S(1)} %pad_maximum_fusion.2), channel_id=1, source_target_pairs={{0,64},{1,65},{2,66},{3,67},{4,68},{5,69},{6,70},{7,71},{8,72},{9,... | collective-permute-start | bytes 2064392 | tf_op jit(solution)/shard_map/ppermute | solution.py:55
  73.6 12.4 %collective-permute-start.21 = (bf16[64,2688]{1,0:T(8,128)(2,1)S(1)}, bf16[64,2688]{1,0:T(8,128)(2,1)S(1)}, u32[]{:S(2)}, u32[]{:S(2)}) collective-permute-start(bf16[64,2688]{1,0:T(8,128)(2,1)S(1)} %slice_add_fusion.1), channel_id=1, source_target_pairs={{0,16},{1,49},{2,18},{3,51},{4,20},{5,53},{6,22},{7,55},{8,24},{9,... | collective-permute-start | bytes 1032200 | tf_op jit(solution)/shard_map/ppermute | solution.py:55
  78.5 11.0 %collective-permute-start.22 = (bf16[64,2688]{1,0:T(8,128)(2,1)S(1)}, bf16[64,2688]{1,0:T(8,128)(2,1)S(1)}, u32[]{:S(2)}, u32[]{:S(2)}) collective-permute-start(bf16[64,2688]{1,0:T(8,128)(2,1)S(1)} %slice_add_fusion), channel_id=1, source_target_pairs={{0,48},{1,17},{2,50},{3,19},{4,52},{5,21},{6,54},{7,23},{8,56},{9,... | collective-permute-start | bytes 1032200 | tf_op jit(solution)/shard_map/ppermute | solution.py:55
  82.7 18.8 %collective-permute-start.20 = (bf16[128,2688]{1,0:T(8,128)(2,1)S(1)}, bf16[128,2688]{1,0:T(8,128)(2,1)S(1)}, u32[]{:S(2)}, u32[]{:S(2)}) collective-permute-start(bf16[128,2688]{1,0:T(8,128)(2,1)S(1)} %pad_maximum_fusion.3.refs_0_.refs_4_), channel_id=1, source_target_pairs={{0,16},{1,49},{2,18},{3,51},{4,20},{5,53},{6,22},{7,55},{8,24},{9,... | collective-permute-start | bytes 2064392 | tf_op jit(solution)/shard_map/ppermute | solution.py:55
  82.8 19.0 %collective-permute-start.19 = (bf16[128,2688]{1,0:T(8,128)(2,1)S(1)}, bf16[128,2688]{1,0:T(8,128)(2,1)S(1)}, u32[]{:S(2)}, u32[]{:S(2)}) collective-permute-start(bf16[128,2688]{1,0:T(8,128)(2,1)S(1)} %pad_maximum_fusion.3.refs_0_.refs_4_), channel_id=1, source_target_pairs={{0,48},{1,17},{2,50},{3,19},{4,52},{5,21},{6,54},{7,23},{8,56},{9,... | collective-permute-start | bytes 2064392 | tf_op jit(solution)/shard_map/ppermute | solution.py:55
  89.8 15.8 %collective-permute-start.25 = (bf16[128,2688]{1,0:T(8,128)(2,1)S(1)}, bf16[128,2688]{1,0:T(8,128)(2,1)S(1)}, u32[]{:S(2)}, u32[]{:S(2)}) collective-permute-start(bf16[128,2688]{1,0:T(8,128)(2,1)S(1)} %pad_maximum_fusion.4), channel_id=1, source_target_pairs={{0,64},{1,65},{2,66},{3,67},{4,68},{5,69},{6,70},{7,71},{8,72},{9,... | collective-permute-start | bytes 2064392 | tf_op jit(solution)/shard_map/ppermute | solution.py:55
  101.5 11.3 %collective-permute-start.23 = (bf16[64,2688]{1,0:T(8,128)(2,1)S(1)}, bf16[64,2688]{1,0:T(8,128)(2,1)S(1)}, u32[]{:S(2)}, u32[]{:S(2)}) collective-permute-start(bf16[64,2688]{1,0:T(8,128)(2,1)S(1)} %slice.203), channel_id=1, source_target_pairs={{0,16},{1,49},{2,18},{3,51},{4,20},{5,53},{6,22},{7,55},{8,24},{9,... | collective-permute-start | bytes 1032200 | tf_op jit(solution)/shard_map/ppermute | solution.py:55
  101.8 12.3 %collective-permute-start.24 = (bf16[64,2688]{1,0:T(8,128)(2,1)S(1)}, bf16[64,2688]{1,0:T(8,128)(2,1)S(1)}, u32[]{:S(2)}, u32[]{:S(2)}) collective-permute-start(bf16[64,2688]{1,0:T(8,128)(2,1)S(1)} %slice.204), channel_id=1, source_target_pairs={{0,48},{1,17},{2,50},{3,19},{4,52},{5,21},{6,54},{7,23},{8,56},{9,... | collective-permute-start | bytes 1032200 | tf_op jit(solution)/shard_map/ppermute | solution.py:55
  106.0 21.6 %collective-permute-start.29 = (bf16[128,2688]{1,0:T(8,128)(2,1)S(1)}, bf16[128,2688]{1,0:T(8,128)(2,1)S(1)}, u32[]{:S(2)}, u32[]{:S(2)}) collective-permute-start(bf16[128,2688]{1,0:T(8,128)(2,1)S(1)} %pad_maximum_fusion.5.refs_0_.refs_13_), channel_id=1, source_target_pairs={{0,48},{1,17},{2,50},{3,19},{4,52},{5,21},{6,54},{7,23},{8,56},{9,... | collective-permute-start | bytes 2064392 | tf_op jit(solution)/shard_map/ppermute | solution.py:55
  106.1 21.4 %collective-permute-start.28 = (bf16[128,2688]{1,0:T(8,128)(2,1)S(1)}, bf16[128,2688]{1,0:T(8,128)(2,1)S(1)}, u32[]{:S(2)}, u32[]{:S(2)}) collective-permute-start(bf16[128,2688]{1,0:T(8,128)(2,1)S(1)} %pad_maximum_fusion.5.refs_0_.refs_13_), channel_id=1, source_target_pairs={{0,16},{1,49},{2,18},{3,51},{4,20},{5,53},{6,22},{7,55},{8,24},{9,... | collective-permute-start | bytes 2064392 | tf_op jit(solution)/shard_map/ppermute | solution.py:55
  117.2 13.7 %collective-permute-start.26 = (bf16[256,1024]{1,0:T(8,128)(2,1)S(1)}, bf16[256,1024]{1,0:T(8,128)(2,1)S(1)}, u32[]{:S(2)}, u32[]{:S(2)}) collective-permute-start(bf16[256,1024]{1,0:T(8,128)(2,1)S(1)} %bitcast.27), channel_id=1, source_target_pairs={{0,1},{1,0},{2,3},{3,2},{4,5},{5,4},{6,7},{7,6},{8,9},{9,8},{10,11... | collective-permute-start | bytes 1572872 | tf_op jit(solution)/shard_map/ppermute | solution.py:55
  118.1 12.9 %collective-permute-start.27 = (bf16[256,1024]{1,0:T(8,128)(2,1)S(1)}, bf16[256,1024]{1,0:T(8,128)(2,1)S(1)}, u32[]{:S(2)}, u32[]{:S(2)}) collective-permute-start(bf16[256,1024]{1,0:T(8,128)(2,1)S(1)} %bitcast.26), channel_id=1, source_target_pairs={{0,1},{1,0},{2,3},{3,2},{4,5},{5,4},{6,7},{7,6},{8,9},{9,8},{10,11... | collective-permute-start | bytes 1572872 | tf_op jit(solution)/shard_map/ppermute | solution.py:55
  127.5 12.0 %collective-permute-start.33 = (bf16[64,2688]{1,0:T(8,128)(2,1)S(1)}, bf16[64,2688]{1,0:T(8,128)(2,1)S(1)}, u32[]{:S(2)}, u32[]{:S(2)}) collective-permute-start(bf16[64,2688]{1,0:T(8,128)(2,1)S(1)} %slice.208), channel_id=1, source_target_pairs={{0,16},{1,49},{2,18},{3,51},{4,20},{5,53},{6,22},{7,55},{8,24},{9,... | collective-permute-start | bytes 1032200 | tf_op jit(solution)/shard_map/ppermute | solution.py:55
  127.7 11.9 %collective-permute-start.34 = (bf16[64,2688]{1,0:T(8,128)(2,1)S(1)}, bf16[64,2688]{1,0:T(8,128)(2,1)S(1)}, u32[]{:S(2)}, u32[]{:S(2)}) collective-permute-start(bf16[64,2688]{1,0:T(8,128)(2,1)S(1)} %slice.209), channel_id=1, source_target_pairs={{0,48},{1,17},{2,50},{3,19},{4,52},{5,21},{6,54},{7,23},{8,56},{9,... | collective-permute-start | bytes 1032200 | tf_op jit(solution)/shard_map/ppermute | solution.py:55
  131.5 12.6 %collective-permute-start.30 = (bf16[64,2048]{1,0:T(8,128)(2,1)S(1)}, bf16[64,2048]{1,0:T(8,128)(2,1)S(1)}, u32[]{:S(2)}, u32[]{:S(2)}) collective-permute-start(bf16[64,2048]{1,0:T(8,128)(2,1)S(1)} %get-tuple-element.208), channel_id=1, source_target_pairs={{0,4},{1,5},{2,6},{3,7},{4,8},{5,9},{6,10},{7,11},{8,12},{9,13},{1... | collective-permute-start | bytes 786440 | tf_op jit(solution)/shard_map/ppermute | solution.py:55
  131.6 12.5 %collective-permute-start.31 = (bf16[64,2048]{1,0:T(8,128)(2,1)S(1)}, bf16[64,2048]{1,0:T(8,128)(2,1)S(1)}, u32[]{:S(2)}, u32[]{:S(2)}) collective-permute-start(bf16[64,2048]{1,0:T(8,128)(2,1)S(1)} %get-tuple-element.209), channel_id=1, source_target_pairs={{0,8},{1,9},{2,10},{3,11},{4,12},{5,13},{6,14},{7,15},{8,0},{9,1},... | collective-permute-start | bytes 786440 | tf_op jit(solution)/shard_map/ppermute | solution.py:55
  133.2 11.5 %collective-permute-start.32 = (bf16[64,2048]{1,0:T(8,128)(2,1)S(1)}, bf16[64,2048]{1,0:T(8,128)(2,1)S(1)}, u32[]{:S(2)}, u32[]{:S(2)}) collective-permute-start(bf16[64,2048]{1,0:T(8,128)(2,1)S(1)} %get-tuple-element.207), channel_id=1, source_target_pairs={{0,12},{1,13},{2,14},{3,15},{4,0},{5,1},{6,2},{7,3},{8,4},{9,5},{1... | collective-permute-start | bytes 786440 | tf_op jit(solution)/shard_map/ppermute | solution.py:55
  141.3 8.4 %collective-permute-start.36 = (bf16[256,1024]{1,0:T(8,128)(2,1)S(1)}, bf16[256,1024]{1,0:T(8,128)(2,1)S(1)}, u32[]{:S(2)}, u32[]{:S(2)}) collective-permute-start(bf16[256,1024]{1,0:T(8,128)(2,1)S(1)} %bitcast.25), channel_id=1, source_target_pairs={{0,1},{1,0},{2,3},{3,2},{4,5},{5,4},{6,7},{7,6},{8,9},{9,8},{10,11... | collective-permute-start | bytes 1572872 | tf_op jit(solution)/shard_map/ppermute | solution.py:55
  141.4 8.3 %collective-permute-start.37 = (bf16[256,1024]{1,0:T(8,128)(2,1)S(1)}, bf16[256,1024]{1,0:T(8,128)(2,1)S(1)}, u32[]{:S(2)}, u32[]{:S(2)}) collective-permute-start(bf16[256,1024]{1,0:T(8,128)(2,1)S(1)} %bitcast.24), channel_id=1, source_target_pairs={{0,1},{1,0},{2,3},{3,2},{4,5},{5,4},{6,7},{7,6},{8,9},{9,8},{10,11... | collective-permute-start | bytes 1572872 | tf_op jit(solution)/shard_map/ppermute | solution.py:55
  144.8 20.8 %collective-permute-start.35 = (bf16[32,2048]{1,0:T(8,128)(2,1)S(1)}, bf16[32,2048]{1,0:T(8,128)(2,1)S(1)}, u32[]{:S(2)}, u32[]{:S(2)}) collective-permute-start(bf16[32,2048]{1,0:T(8,128)(2,1)S(1)} %slice.239), channel_id=1, source_target_pairs={{0,2},{1,3},{2,0},{3,1},{4,6},{5,7},{6,4},{7,5},{8,10},{9,11},{10,... | collective-permute-start | bytes 393224 | tf_op jit(solution)/shard_map/ppermute | solution.py:55
  150.2 13.7 %collective-permute-start.38 = (bf16[64,2048]{1,0:T(8,128)(2,1)S(1)}, bf16[64,2048]{1,0:T(8,128)(2,1)S(1)}, u32[]{:S(2)}, u32[]{:S(2)}) collective-permute-start(bf16[64,2048]{1,0:T(8,128)(2,1)S(1)} %get-tuple-element.204), channel_id=1, source_target_pairs={{0,4},{1,5},{2,6},{3,7},{4,8},{5,9},{6,10},{7,11},{8,12},{9,13},{1... | collective-permute-start | bytes 786440 | tf_op jit(solution)/shard_map/ppermute | solution.py:55
  151.0 13.9 %collective-permute-start.39 = (bf16[64,2048]{1,0:T(8,128)(2,1)S(1)}, bf16[64,2048]{1,0:T(8,128)(2,1)S(1)}, u32[]{:S(2)}, u32[]{:S(2)}) collective-permute-start(bf16[64,2048]{1,0:T(8,128)(2,1)S(1)} %get-tuple-element.205), channel_id=1, source_target_pairs={{0,8},{1,9},{2,10},{3,11},{4,12},{5,13},{6,14},{7,15},{8,0},{9,1},... | collective-permute-start | bytes 786440 | tf_op jit(solution)/shard_map/ppermute | solution.py:55
  154.4 10.5 %collective-permute-start.40 = (bf16[64,2048]{1,0:T(8,128)(2,1)S(1)}, bf16[64,2048]{1,0:T(8,128)(2,1)S(1)}, u32[]{:S(2)}, u32[]{:S(2)}) collective-permute-start(bf16[64,2048]{1,0:T(8,128)(2,1)S(1)} %get-tuple-element.203), channel_id=1, source_target_pairs={{0,12},{1,13},{2,14},{3,15},{4,0},{5,1},{6,2},{7,3},{8,4},{9,5},{1... | collective-permute-start | bytes 786440 | tf_op jit(solution)/shard_map/ppermute | solution.py:55
  165.0 6.6 %collective-permute-start.41 = (bf16[32,2048]{1,0:T(8,128)(2,1)S(1)}, bf16[32,2048]{1,0:T(8,128)(2,1)S(1)}, u32[]{:S(2)}, u32[]{:S(2)}) collective-permute-start(bf16[32,2048]{1,0:T(8,128)(2,1)S(1)} %slice.249), channel_id=1, source_target_pairs={{0,2},{1,3},{2,0},{3,1},{4,6},{5,7},{6,4},{7,5},{8,10},{9,11},{10,... | collective-permute-start | bytes 393224 | tf_op jit(solution)/shard_map/ppermute | solution.py:55

commit v11 on v10

--- a/solution.py
+++ b/solution.py
@@ -171,43 +171,34 @@
     )(*gathered, weights)
 
 
-def backward_kernel(halves, *refs):
+def backward_kernel(*refs):
     arrays, weights, outs = refs[:5], refs[5], refs[6:]
-    own, up, down, far_first, far_second = arrays
     total = weights.shape[1]
     width = total // 3
-    rows = far_first.shape[0]
+    rows = arrays[3].shape[0]
     for which, columns in enumerate((slice(2 * width, total), slice(0, 2 * width))):
-        left = []
-        for half in halves:
-            at = slice(half * rows, (half + 1) * rows)
-            left += [array[at, columns] for array in (own, up, down)]
-            left.append((far_first, far_second)[half][:, columns])
-        part = nt(jnp.concatenate(left), weights[:, columns]).astype(jnp.bfloat16)
-        for at in range(len(halves)):
-            for number, dz in enumerate((0, 1, 3, 2)):
-                first = (4 * at + number) * rows
-                outs[2 * at + which][owner(dz)] = part[first : first + rows]
-
-
-def backward(halves, arrays, weights):
+        left = jnp.concatenate(values_of(arrays, columns))
+        part = nt(left, weights[:, columns]).astype(jnp.bfloat16)
+        for at, (dz, half) in enumerate(GATHERED):
+            outs[2 * half + which][owner(dz)] = part[at * rows : (at + 1) * rows]
+
+
+def backward(arrays, weights):
     rows = arrays[3].shape[0]
     depth, total = weights.shape
-    count = 2 * len(halves)
     outs = pl.pallas_call(
-        functools.partial(backward_kernel, halves),
+        backward_kernel,
         in_specs=[VMEM] * 6,
-        out_specs=[VMEM] * count,
-        out_shape=[jax.ShapeDtypeStruct((4, rows, depth), jnp.bfloat16)] * count,
+        out_specs=[VMEM] * 4,
+        out_shape=[jax.ShapeDtypeStruct((4, rows, depth), jnp.bfloat16)] * 4,
         compiler_params=params(),
         cost_estimate=pl.CostEstimate(
-            flops=4 * count * rows * depth * total,
-            bytes_accessed=8 * depth * total,
-            transcendentals=0,
+            flops=16 * rows * depth * total, bytes_accessed=8 * depth * total, transcendentals=0
         ),
         name="backward",
     )(*arrays, weights)
-    return [out.reshape(4 * rows, depth) for out in outs]
+    outs = [out.reshape(4 * rows, depth) for out in outs]
+    return outs[2:], outs[:2]
 
 
 def weight_grad_kernel(offsets, *refs):
@@ -316,7 +307,6 @@
         self.source, self.offset, self.rows = gather, offset, 2 * rows
         self.weights = weights
         self.groups = TOGETHER if last else APART
-        self.halves = ((1,), (0,)) if last else ((1, 0),)
 
     def forward(self, *others):
         self.gathered = self.source.arrays
@@ -369,10 +359,7 @@
 
     def backward(self, *others):
         self.arrays = after(self.arrays, *others)
-        outs = []
-        for halves in self.halves:
-            outs += backward(halves, self.arrays, self.weights)
-        self.for_other, self.for_own = outs[:2], outs[2:]
+        self.for_other, self.for_own = backward(self.arrays, self.weights)
         return self.for_other
 
     def send(self, *others):

time: 173 us -> 169 us (0.977)
  waiting for transfers between devices: 76.1 us -> 68.7 us
  starting transfers between devices: 59.2 us -> 63.1 us
    ppermute x42, waiting for transfers between devices: 76.1 us -> 68.7 us  [move(): return lax.ppermute(array, ('row', 'col'), pairs)]
    ppermute x42, starting transfers between devices: 59.2 us -> 63.1 us  [move(): return lax.ppermute(array, ('row', 'col'), pairs)]
    pallas_call x3 -> x2, Pallas kernels: 6.53 us -> 6.35 us  [backward(): pl.pallas_call(backward_kernel, in_specs=[VMEM] * 6, out_specs=[VMEM] * 4...]
  transfers between devices with their start and end apart: 42 -> 42, of which waited for: 21 -> 16; matrix products, arithmetic and copies ran while one was open for 2% -> 2% of each run, Pallas kernels for 14% -> 14%
where the time goes in v11:
time: 169 us
  waiting for transfers between devices  68.7 us (41%)
  starting transfers between devices  63.1 us (37%)
  Pallas kernels  25.8 us (15%)
  local copies, waits for them, and re-layouts  5.75 us (3%)
  other arithmetic  4.22 us (2%)
    ppermute x42, waiting for transfers between devices, move(): return lax.ppermute(array, ('row', 'col'), pairs)  68.7 us
    ppermute x42, starting transfers between devices, move(): return lax.ppermute(array, ('row', 'col'), pairs)  63.1 us
    pallas_call x1, Pallas kernels, weight_grads(): pl.pallas_call(functools.partial(weight_grad_kernel, offsets), in_specs=[...  9.61 us
    pallas_call x3, Pallas kernels, forward(): pl.pallas_call(functools.partial(forward_kernel, groups, offset, rows), i...  7.05 us
    pallas_call x2, Pallas kernels, backward(): pl.pallas_call(backward_kernel, in_specs=[VMEM] * 6, out_specs=[VMEM] * 4...  6.35 us
    unnamed x12, local copies, waits for them, and re-layouts  4.51 us
  transfers between devices with their start and end apart: 42, of which 16 were waited for; matrix products, arithmetic and copies ran while one was open for 2% of the time, Pallas kernels for 14%

profile of v11, /device:TPU:0, one launch (start us, length us, event | category | flops | bytes accessed | tf_op | source)
XLA Modules:
  0.0 168.6 jit_solution(6917569623499984447)
XLA Ops:
  0.7 1.0 slice_bitcast_fusion
  1.7 3.2 %collective-permute-start = (bf16[2,32,1024]{2,1,0:T(8,128)(2,1)S(1)}, bf16[2,32,1024]{2,1,0:T(8,128)(2,1)S(1)}, u32[]{:S(2)}, u32[]{:S(2)}) collective-permute-start(bf16[2,32,1024]{2,1,0:T(8,128)(2,1)S(1)} %pad_maximum_fusion.13), channel_id=1, source_target_pairs={{0,2},{1,3},{2,0},{3,1},{4,6},{5,7},{6,4},{7,5},{8,10},{9,11},{10,... | collective-permute-start | bytes 393224 | tf_op jit(solution)/shard_map/ppermute | solution.py:55
  4.8 3.5 %collective-permute-done = bf16[2,32,1024]{2,1,0:T(8,128)(2,1)S(1)} collective-permute-done((bf16[2,32,1024]{2,1,0:T(8,128)(2,1)S(1)}, bf16[2,32,1024]{2,1,0:T(8,128)(2,1)S(1)}, u32[]{:S(2)}, u32[]{:S(2)}) %collective-permute-start) | collective-permute-done | bytes 131104 | tf_op jit(solution)/shard_map/ppermute | solution.py:55
  8.4 3.3 %collective-permute-start.1 = (bf16[2,64,1024]{2,1,0:T(8,128)(2,1)S(1)}, bf16[2,64,1024]{2,1,0:T(8,128)(2,1)S(1)}, u32[]{:S(2)}, u32[]{:S(2)}) collective-permute-start(bf16[2,64,1024]{2,1,0:T(8,128)(2,1)S(1)} %pad_maximum_fusion.10), channel_id=1, source_target_pairs={{0,12},{1,13},{2,14},{3,15},{4,0},{5,1},{6,2},{7,3},{8,4},{9,5},{1... | collective-permute-start | bytes 786440 | tf_op jit(solution)/shard_map/ppermute | solution.py:55
  12.3 1.0 collective-permute-start.3
  13.3 3.1 %collective-permute-start.4 = (bf16[2,32,1024]{2,1,0:T(8,128)(2,1)S(1)}, bf16[2,32,1024]{2,1,0:T(8,128)(2,1)S(1)}, u32[]{:S(2)}, u32[]{:S(2)}) collective-permute-start(bf16[2,32,1024]{2,1,0:T(8,128)(2,1)S(1)} %pad_maximum_fusion.14), channel_id=1, source_target_pairs={{0,2},{1,3},{2,0},{3,1},{4,6},{5,7},{6,4},{7,5},{8,10},{9,11},{10,... | collective-permute-start | bytes 393224 | tf_op jit(solution)/shard_map/ppermute | solution.py:55
  16.4 1.5 copy-done
  17.9 1.5 copy-done.1
  19.4 1.5 copy-done.2
  20.9 2.8 %mask_weights.1.refs_4_.refs_5_ = bf16[1024,2688]{1,0:T(8,128)(2,1)S(1)} custom-call(bf16[1024,896]{1,0:T(8,128)(2,1)S(1)} %copy-done, bf16[1024,896]{1,0:T(8,128)(2,1)S(1)} %copy-done.1, bf16[896,1024]{1,0:T(8,128)(2,1)S(1)} %copy-done.2, s32[8,7]{1,0:T(8,128)S(1)} %copy-done.3, s32[8,7]{1,0:T(8,128)S(1)} %copy-done.4, s32[7,8]{1,0:T(8,128)S(1)} %copy-done.5), custom_call_target="tpu_custom_call" | custom-call | flops 2752512 | bytes 11010048 | tf_op jit(solution)/shard_map/mask_weights/pallas_call | solution.py:121
  23.7 1.9 %collective-permute-done.3 = bf16[2,64,1024]{2,1,0:T(8,128)(2,1)S(1)} collective-permute-done((bf16[2,64,1024]{2,1,0:T(8,128)(2,1)S(1)}, bf16[2,64,1024]{2,1,0:T(8,128)(2,1)S(1)}, u32[]{:S(2)}, u32[]{:S(2)}) %collective-permute-start.3) | collective-permute-done | bytes 262176 | tf_op jit(solution)/shard_map/ppermute | solution.py:55
  26.6 1.2 collective-permute-done.6.refs_3_
  28.6 1.8 %forward.4 = (bf16[128,2688]{1,0:T(8,128)(2,1)S(1)}, bf16[128,2688]{1,0:T(8,128)(2,1)S(1)}) custom-call(bf16[4,64,1024]{2,1,0:T(8,128)(2,1)S(1)} %pad_maximum_fusion.6.refs_0_, bf16[4,64,1024]{2,1,0:T(8,128)(2,1)S(1)} %pad_maximum_fusion.7.refs_1_, bf16[4,64,1024]{2,1,0:T(8,128)(2,1)S(1)} %collective-permute-done.5.refs_2_, ...), custom_call_target="tpu_custom_call" | custom-call | flops 1024 | bytes 1024 | tf_op jit(solution)/shard_map/forward/pallas_call | solution.py:161
  30.4 2.0 %collective-permute-start.7 = (bf16[128,2688]{1,0:T(8,128)(2,1)S(1)}, bf16[128,2688]{1,0:T(8,128)(2,1)S(1)}, u32[]{:S(2)}, u32[]{:S(2)}) collective-permute-start(bf16[128,2688]{1,0:T(8,128)(2,1)S(1)} %get-tuple-element.111), channel_id=1, source_target_pairs={{0,16},{1,49},{2,18},{3,51},{4,20},{5,53},{6,22},{7,55},{8,24},{9,... | collective-permute-start | bytes 2064392 | tf_op jit(solution)/shard_map/ppermute | solution.py:55
  33.0 1.4 collective-permute-start.12
  34.5 1.8 %forward.3 = (bf16[64,2688]{1,0:T(8,128)(2,1)S(1)}, bf16[64,2688]{1,0:T(8,128)(2,1)S(1)}, bf16[128,2688]{1,0:T(8,128)(2,1)S(1)}) custom-call(bf16[4,64,1024]{2,1,0:T(8,128)(2,1)S(1)} %pad_maximum_fusion.6.refs_0_, bf16[4,64,1024]{2,1,0:T(8,128)(2,1)S(1)} %pad_maximum_fusion.7.refs_1_, bf16[4,64,1024]{2,1,0:T(8,128)(2,1)S(1)} %collective-permute-done.5.refs_2_, ...), custom_call_target="tpu_custom_call" | custom-call | flops 1024 | bytes 1024 | tf_op jit(solution)/shard_map/forward/pallas_call | solution.py:161
  36.3 2.3 %collective-permute-start.9 = (bf16[128,2688]{1,0:T(8,128)(2,1)S(1)}, bf16[128,2688]{1,0:T(8,128)(2,1)S(1)}, u32[]{:S(2)}, u32[]{:S(2)}) collective-permute-start(bf16[128,2688]{1,0:T(8,128)(2,1)S(1)} %get-tuple-element.114), channel_id=1, source_target_pairs={{0,48},{1,17},{2,50},{3,19},{4,52},{5,21},{6,54},{7,23},{8,56},{9,... | collective-permute-start | bytes 2064392 | tf_op jit(solution)/shard_map/ppermute | solution.py:55
  38.5 6.7 %collective-permute-done.7 = bf16[128,2688]{1,0:T(8,128)(2,1)S(1)} collective-permute-done((bf16[128,2688]{1,0:T(8,128)(2,1)S(1)}, bf16[128,2688]{1,0:T(8,128)(2,1)S(1)}, u32[]{:S(2)}, u32[]{:S(2)}) %collective-permute-start.7) | collective-permute-done | bytes 688160 | tf_op jit(solution)/shard_map/ppermute | solution.py:55
  45.3 4.2 %collective-permute-done.9 = bf16[128,2688]{1,0:T(8,128)(2,1)S(1)} collective-permute-done((bf16[128,2688]{1,0:T(8,128)(2,1)S(1)}, bf16[128,2688]{1,0:T(8,128)(2,1)S(1)}, u32[]{:S(2)}, u32[]{:S(2)}) %collective-permute-start.9) | collective-permute-done | bytes 688160 | tf_op jit(solution)/shard_map/ppermute | solution.py:55
  49.8 1.2 collective-permute-start.15
  51.1 3.1 %collective-permute-start.10 = (bf16[64,2688]{1,0:T(8,128)(2,1)S(1)}, bf16[64,2688]{1,0:T(8,128)(2,1)S(1)}, u32[]{:S(2)}, u32[]{:S(2)}) collective-permute-start(bf16[64,2688]{1,0:T(8,128)(2,1)S(1)} %slice_add_fusion.2), channel_id=1, source_target_pairs={{0,48},{1,17},{2,50},{3,19},{4,52},{5,21},{6,54},{7,23},{8,56},{9,... | collective-permute-start | bytes 1032200 | tf_op jit(solution)/shard_map/ppermute | solution.py:55
  54.2 3.4 %forward.5 = (bf16[128,2688]{1,0:T(8,128)(2,1)S(1)}, bf16[128,2688]{1,0:T(8,128)(2,1)S(1)}, bf16[64,2688]{1,0:T(8,128)(2,1)S(1)}, bf16[64,2688]{1,0:T(8,128)(2,1)S(1)}, bf16[128,2688]{1,0:T(8,128)(2,1)S(1)}) custom-call(bf16[4,64,1024]{2,1,0:T(8,128)(2,1)S(1)} %pad_maximum_fusion.8.refs_0_.refs_9_, ...), custom_call_target="tpu_custom_call" | custom-call | flops 1024 | bytes 1024 | tf_op jit(solution)/shard_map/forward/pallas_call | solution.py:161
  57.8 4.9 %collective-permute-done.10 = bf16[64,2688]{1,0:T(8,128)(2,1)S(1)} collective-permute-done((bf16[64,2688]{1,0:T(8,128)(2,1)S(1)}, bf16[64,2688]{1,0:T(8,128)(2,1)S(1)}, u32[]{:S(2)}, u32[]{:S(2)}) %collective-permute-start.10) | collective-permute-done | bytes 344096 | tf_op jit(solution)/shard_map/ppermute | solution.py:55
  62.8 3.5 %collective-permute-start.18 = (bf16[128,2688]{1,0:T(8,128)(2,1)S(1)}, bf16[128,2688]{1,0:T(8,128)(2,1)S(1)}, u32[]{:S(2)}, u32[]{:S(2)}) collective-permute-start(bf16[128,2688]{1,0:T(8,128)(2,1)S(1)} %get-tuple-element.131), channel_id=1, source_target_pairs={{0,48},{1,17},{2,50},{3,19},{4,52},{5,21},{6,54},{7,23},{8,56},{9,... | collective-permute-start | bytes 2064392 | tf_op jit(solution)/shard_map/ppermute | solution.py:55
  66.7 1.6 collective-permute-start.16
  68.2 5.9 %collective-permute-done.17 = bf16[128,2688]{1,0:T(8,128)(2,1)S(1)} collective-permute-done((bf16[128,2688]{1,0:T(8,128)(2,1)S(1)}, bf16[128,2688]{1,0:T(8,128)(2,1)S(1)}, u32[]{:S(2)}, u32[]{:S(2)}) %collective-permute-start.17) | collective-permute-done | bytes 688160 | tf_op jit(solution)/shard_map/ppermute | solution.py:55
  74.2 4.0 %collective-permute-done.18 = bf16[128,2688]{1,0:T(8,128)(2,1)S(1)} collective-permute-done((bf16[128,2688]{1,0:T(8,128)(2,1)S(1)}, bf16[128,2688]{1,0:T(8,128)(2,1)S(1)}, u32[]{:S(2)}, u32[]{:S(2)}) %collective-permute-start.18) | collective-permute-done | bytes 688160 | tf_op jit(solution)/shard_map/ppermute | solution.py:55
  78.3 3.6 %collective-permute-start.22 = (bf16[64,2688]{1,0:T(8,128)(2,1)S(1)}, bf16[64,2688]{1,0:T(8,128)(2,1)S(1)}, u32[]{:S(2)}, u32[]{:S(2)}) collective-permute-start(bf16[64,2688]{1,0:T(8,128)(2,1)S(1)} %slice_add_fusion), channel_id=1, source_target_pairs={{0,48},{1,17},{2,50},{3,19},{4,52},{5,21},{6,54},{7,23},{8,56},{9,... | collective-permute-start | bytes 1032200 | tf_op jit(solution)/shard_map/ppermute | solution.py:55
  82.7 3.0 %collective-permute-start.19 = (bf16[128,2688]{1,0:T(8,128)(2,1)S(1)}, bf16[128,2688]{1,0:T(8,128)(2,1)S(1)}, u32[]{:S(2)}, u32[]{:S(2)}) collective-permute-start(bf16[128,2688]{1,0:T(8,128)(2,1)S(1)} %pad_maximum_fusion.3.refs_0_.refs_4_), channel_id=1, source_target_pairs={{0,48},{1,17},{2,50},{3,19},{4,52},{5,21},{6,54},{7,23},{8,56},{9,... | collective-permute-start | bytes 2064392 | tf_op jit(solution)/shard_map/ppermute | solution.py:55
  85.8 4.7 %collective-permute-done.22 = bf16[64,2688]{1,0:T(8,128)(2,1)S(1)} collective-permute-done((bf16[64,2688]{1,0:T(8,128)(2,1)S(1)}, bf16[64,2688]{1,0:T(8,128)(2,1)S(1)}, u32[]{:S(2)}, u32[]{:S(2)}) %collective-permute-start.22) | collective-permute-done | bytes 344096 | tf_op jit(solution)/shard_map/ppermute | solution.py:55
  90.8 1.6 collective-permute-start.25
  92.3 8.8 %collective-permute-done.20.refs_2_.refs_6_ = bf16[128,2688]{1,0:T(8,128)(2,1)S(1)} collective-permute-done((bf16[128,2688]{1,0:T(8,128)(2,1)S(1)}, bf16[128,2688]{1,0:T(8,128)(2,1)S(1)}, u32[]{:S(2)}, u32[]{:S(2)}) %collective-permute-start.20) | collective-permute-done | bytes 688160 | tf_op jit(solution)/shard_map/ppermute | solution.py:55
  101.3 3.6 %collective-permute-start.24 = (bf16[64,2688]{1,0:T(8,128)(2,1)S(1)}, bf16[64,2688]{1,0:T(8,128)(2,1)S(1)}, u32[]{:S(2)}, u32[]{:S(2)}) collective-permute-start(bf16[64,2688]{1,0:T(8,128)(2,1)S(1)} %slice.204), channel_id=1, source_target_pairs={{0,48},{1,17},{2,50},{3,19},{4,52},{5,21},{6,54},{7,23},{8,56},{9,... | collective-permute-start | bytes 1032200 | tf_op jit(solution)/shard_map/ppermute | solution.py:55
  105.4 3.2 %collective-permute-start.29 = (bf16[128,2688]{1,0:T(8,128)(2,1)S(1)}, bf16[128,2688]{1,0:T(8,128)(2,1)S(1)}, u32[]{:S(2)}, u32[]{:S(2)}) collective-permute-start(bf16[128,2688]{1,0:T(8,128)(2,1)S(1)} %pad_maximum_fusion.5.refs_0_.refs_13_), channel_id=1, source_target_pairs={{0,48},{1,17},{2,50},{3,19},{4,52},{5,21},{6,54},{7,23},{8,56},{9,... | collective-permute-start | bytes 2064392 | tf_op jit(solution)/shard_map/ppermute | solution.py:55
  108.7 4.7 %collective-permute-done.24.refs_4_.refs_8_ = bf16[64,2688]{1,0:T(8,128)(2,1)S(1)} collective-permute-done((bf16[64,2688]{1,0:T(8,128)(2,1)S(1)}, bf16[64,2688]{1,0:T(8,128)(2,1)S(1)}, u32[]{:S(2)}, u32[]{:S(2)}) %collective-permute-start.24) | collective-permute-done | bytes 344096 | tf_op jit(solution)/shard_map/ppermute | solution.py:55
  113.4 3.2 %backward.2 = (bf16[4,64,1024]{2,1,0:T(8,128)(2,1)S(1)}, bf16[4,64,1024]{2,1,0:T(8,128)(2,1)S(1)}, bf16[4,64,1024]{2,1,0:T(8,128)(2,1)S(1)}, bf16[4,64,1024]{2,1,0:T(8,128)(2,1)S(1)}) custom-call(bf16[128,2688]{1,0:T(8,128)(2,1)S(1)} %pad_maximum_fusion.3.refs_0_.refs_4_, bf16[128,2688]{1,0:T(8,128)(2,1)S(1)} %collective-permute-done.19.refs_1_.refs_5_, ...), custom_call_target="tpu_custom_call" | custom-call | flops 2818572288 | bytes 22020096 | tf_op jit(solution)/shard_map/backward/pallas_call | solution.py:189
  117.2 9.1 %collective-permute-done.28.refs_2_.refs_15_ = bf16[128,2688]{1,0:T(8,128)(2,1)S(1)} collective-permute-done((bf16[128,2688]{1,0:T(8,128)(2,1)S(1)}, bf16[128,2688]{1,0:T(8,128)(2,1)S(1)}, u32[]{:S(2)}, u32[]{:S(2)}) %collective-permute-start.28) | collective-permute-done | bytes 688160 | tf_op jit(solution)/shard_map/ppermute | solution.py:55
  126.4 3.3 %collective-permute-start.34 = (bf16[64,2688]{1,0:T(8,128)(2,1)S(1)}, bf16[64,2688]{1,0:T(8,128)(2,1)S(1)}, u32[]{:S(2)}, u32[]{:S(2)}) collective-permute-start(bf16[64,2688]{1,0:T(8,128)(2,1)S(1)} %slice.209), channel_id=1, source_target_pairs={{0,48},{1,17},{2,50},{3,19},{4,52},{5,21},{6,54},{7,23},{8,56},{9,... | collective-permute-start | bytes 1032200 | tf_op jit(solution)/shard_map/ppermute | solution.py:55
  130.4 3.5 %collective-permute-start.31 = (bf16[64,2048]{1,0:T(8,128)(2,1)S(1)}, bf16[64,2048]{1,0:T(8,128)(2,1)S(1)}, u32[]{:S(2)}, u32[]{:S(2)}) collective-permute-start(bf16[64,2048]{1,0:T(8,128)(2,1)S(1)} %get-tuple-element.209), channel_id=1, source_target_pairs={{0,8},{1,9},{2,10},{3,11},{4,12},{5,13},{6,14},{7,15},{8,0},{9,1},... | collective-permute-start | bytes 786440 | tf_op jit(solution)/shard_map/ppermute | solution.py:55
  133.8 2.1 %collective-permute-start.32 = (bf16[64,2048]{1,0:T(8,128)(2,1)S(1)}, bf16[64,2048]{1,0:T(8,128)(2,1)S(1)}, u32[]{:S(2)}, u32[]{:S(2)}) collective-permute-start(bf16[64,2048]{1,0:T(8,128)(2,1)S(1)} %get-tuple-element.207), channel_id=1, source_target_pairs={{0,12},{1,13},{2,14},{3,15},{4,0},{5,1},{6,2},{7,3},{8,4},{9,5},{1... | collective-permute-start | bytes 786440 | tf_op jit(solution)/shard_map/ppermute | solution.py:55
  135.9 3.2 %backward.3 = (bf16[4,64,1024]{2,1,0:T(8,128)(2,1)S(1)}, bf16[4,64,1024]{2,1,0:T(8,128)(2,1)S(1)}, bf16[4,64,1024]{2,1,0:T(8,128)(2,1)S(1)}, bf16[4,64,1024]{2,1,0:T(8,128)(2,1)S(1)}) custom-call(bf16[128,2688]{1,0:T(8,128)(2,1)S(1)} %pad_maximum_fusion.5.refs_0_.refs_13_, bf16[128,2688]{1,0:T(8,128)(2,1)S(1)} %collective-permute-done.29.refs_1_.refs_14_, ...), custom_call_target="tpu_custom_call" | custom-call | flops 2818572288 | bytes 22020096 | tf_op jit(solution)/shard_map/backward/pallas_call | solution.py:189
  139.6 2.0 %collective-permute-done.31 = bf16[64,2048]{1,0:T(8,128)(2,1)S(1)} collective-permute-done((bf16[64,2048]{1,0:T(8,128)(2,1)S(1)}, bf16[64,2048]{1,0:T(8,128)(2,1)S(1)}, u32[]{:S(2)}, u32[]{:S(2)}) %collective-permute-start.31) | collective-permute-done | bytes 262176 | tf_op jit(solution)/shard_map/ppermute | solution.py:55
  141.9 3.0 %collective-permute-start.35 = (bf16[32,2048]{1,0:T(8,128)(2,1)S(1)}, bf16[32,2048]{1,0:T(8,128)(2,1)S(1)}, u32[]{:S(2)}, u32[]{:S(2)}) collective-permute-start(bf16[32,2048]{1,0:T(8,128)(2,1)S(1)} %slice.239), channel_id=1, source_target_pairs={{0,2},{1,3},{2,0},{3,1},{4,6},{5,7},{6,4},{7,5},{8,10},{9,11},{10,... | collective-permute-start | bytes 393224 | tf_op jit(solution)/shard_map/ppermute | solution.py:55
  145.4 2.1 %collective-permute-start.38 = (bf16[64,2048]{1,0:T(8,128)(2,1)S(1)}, bf16[64,2048]{1,0:T(8,128)(2,1)S(1)}, u32[]{:S(2)}, u32[]{:S(2)}) collective-permute-start(bf16[64,2048]{1,0:T(8,128)(2,1)S(1)} %get-tuple-element.204), channel_id=1, source_target_pairs={{0,4},{1,5},{2,6},{3,7},{4,8},{5,9},{6,10},{7,11},{8,12},{9,13},{1... | collective-permute-start | bytes 786440 | tf_op jit(solution)/shard_map/ppermute | solution.py:55
  147.5 2.1 %collective-permute-start.39 = (bf16[64,2048]{1,0:T(8,128)(2,1)S(1)}, bf16[64,2048]{1,0:T(8,128)(2,1)S(1)}, u32[]{:S(2)}, u32[]{:S(2)}) collective-permute-start(bf16[64,2048]{1,0:T(8,128)(2,1)S(1)} %get-tuple-element.205), channel_id=1, source_target_pairs={{0,8},{1,9},{2,10},{3,11},{4,12},{5,13},{6,14},{7,15},{8,0},{9,1},... | collective-permute-start | bytes 786440 | tf_op jit(solution)/shard_map/ppermute | solution.py:55
  149.6 1.9 %collective-permute-start.40 = (bf16[64,2048]{1,0:T(8,128)(2,1)S(1)}, bf16[64,2048]{1,0:T(8,128)(2,1)S(1)}, u32[]{:S(2)}, u32[]{:S(2)}) collective-permute-start(bf16[64,2048]{1,0:T(8,128)(2,1)S(1)} %get-tuple-element.203), channel_id=1, source_target_pairs={{0,12},{1,13},{2,14},{3,15},{4,0},{5,1},{6,2},{7,3},{8,4},{9,5},{1... | collective-permute-start | bytes 786440 | tf_op jit(solution)/shard_map/ppermute | solution.py:55
  151.5 9.6 %weight_grads.1 = (bf16[1024,896]{1,0:T(8,128)(2,1)}, bf16[1024,896]{1,0:T(8,128)(2,1)}, bf16[896,1024]{1,0:T(8,128)(2,1)}) custom-call(bf16[4,64,1024]{2,1,0:T(8,128)(2,1)S(1)} %pad_maximum_fusion.6.refs_0_, bf16[4,64,1024]{2,1,0:T(8,128)(2,1)S(1)} %pad_maximum_fusion.7.refs_1_, bf16[4,64,1024]{2,1,0:T(8,128)(2,1)S(1)} %collective-permute-done.5.refs_2_, ...), custom_call_target="tpu_custom_call" | custom-call | flops 5637144576 | bytes 44040192 | tf_op jit(solution)/shard_map/weight_grads/pallas_call | solution.py:248
  161.9 5.9 %collective-permute-done.41 = bf16[32,2048]{1,0:T(8,128)(2,1)S(1)} collective-permute-done((bf16[32,2048]{1,0:T(8,128)(2,1)S(1)}, bf16[32,2048]{1,0:T(8,128)(2,1)S(1)}, u32[]{:S(2)}, u32[]{:S(2)}) %collective-permute-start.41) | collective-permute-done | bytes 131104 | tf_op jit(solution)/shard_map/ppermute | solution.py:55
  (103 shorter events, 10.0 us)
Async XLA Ops:
  0.6 15.8 %copy-start.3 = (s32[8,7]{1,0:T(8,128)S(1)}, s32[8,7]{1,0:T(8,128)}, u32[]{:S(2)}) copy-start(s32[8,7]{1,0:T(8,128)} %refs_18_.1) | copy-start | bytes 676
  0.6 15.8 %copy-start.4 = (s32[8,7]{1,0:T(8,128)S(1)}, s32[8,7]{1,0:T(8,128)}, u32[]{:S(2)}) copy-start(s32[8,7]{1,0:T(8,128)} %refs_19_.1) | copy-start | bytes 676
  0.7 15.7 %copy-start.5 = (s32[7,8]{1,0:T(8,128)S(1)}, s32[7,8]{1,0:T(8,128)}, u32[]{:S(2)}) copy-start(s32[7,8]{1,0:T(8,128)} %refs_20_.1) | copy-start | bytes 676
  1.7 6.7 %collective-permute-start = (bf16[2,32,1024]{2,1,0:T(8,128)(2,1)S(1)}, bf16[2,32,1024]{2,1,0:T(8,128)(2,1)S(1)}, u32[]{:S(2)}, u32[]{:S(2)}) collective-permute-start(bf16[2,32,1024]{2,1,0:T(8,128)(2,1)S(1)} %pad_maximum_fusion.13), channel_id=1, source_target_pairs={{0,2},{1,3},{2,0},{3,1},{4,6},{5,7},{6,4},{7,5},{8,10},{9,11},{10,... | collective-permute-start | bytes 393224 | tf_op jit(solution)/shard_map/ppermute | solution.py:55
  8.4 15.4 %collective-permute-start.1 = (bf16[2,64,1024]{2,1,0:T(8,128)(2,1)S(1)}, bf16[2,64,1024]{2,1,0:T(8,128)(2,1)S(1)}, u32[]{:S(2)}, u32[]{:S(2)}) collective-permute-start(bf16[2,64,1024]{2,1,0:T(8,128)(2,1)S(1)} %pad_maximum_fusion.10), channel_id=1, source_target_pairs={{0,12},{1,13},{2,14},{3,15},{4,0},{5,1},{6,2},{7,3},{8,4},{9,5},{1... | collective-permute-start | bytes 786440 | tf_op jit(solution)/shard_map/ppermute | solution.py:55
  11.7 12.1 %collective-permute-start.2 = (bf16[2,64,1024]{2,1,0:T(8,128)(2,1)S(1)}, bf16[2,64,1024]{2,1,0:T(8,128)(2,1)S(1)}, u32[]{:S(2)}, u32[]{:S(2)}) collective-permute-start(bf16[2,64,1024]{2,1,0:T(8,128)(2,1)S(1)} %pad_maximum_fusion.10), channel_id=1, source_target_pairs={{0,8},{1,9},{2,10},{3,11},{4,12},{5,13},{6,14},{7,15},{8,0},{9,1},... | collective-permute-start | bytes 786440 | tf_op jit(solution)/shard_map/ppermute | solution.py:55
  12.3 13.4 %collective-permute-start.3 = (bf16[2,64,1024]{2,1,0:T(8,128)(2,1)S(1)}, bf16[2,64,1024]{2,1,0:T(8,128)(2,1)S(1)}, u32[]{:S(2)}, u32[]{:S(2)}) collective-permute-start(bf16[2,64,1024]{2,1,0:T(8,128)(2,1)S(1)} %pad_maximum_fusion.10), channel_id=1, source_target_pairs={{0,4},{1,5},{2,6},{3,7},{4,8},{5,9},{6,10},{7,11},{8,12},{9,13},{1... | collective-permute-start | bytes 786440 | tf_op jit(solution)/shard_map/ppermute | solution.py:55
  13.3 10.4 %collective-permute-start.4 = (bf16[2,32,1024]{2,1,0:T(8,128)(2,1)S(1)}, bf16[2,32,1024]{2,1,0:T(8,128)(2,1)S(1)}, u32[]{:S(2)}, u32[]{:S(2)}) collective-permute-start(bf16[2,32,1024]{2,1,0:T(8,128)(2,1)S(1)} %pad_maximum_fusion.14), channel_id=1, source_target_pairs={{0,2},{1,3},{2,0},{3,1},{4,6},{5,7},{6,4},{7,5},{8,10},{9,11},{10,... | collective-permute-start | bytes 393224 | tf_op jit(solution)/shard_map/ppermute | solution.py:55
  16.4 1.5 copy-start
  17.9 1.5 copy-start.1
  19.4 1.5 copy-start.2
  25.9 2.0 %collective-permute-start.6 = (bf16[4,64,1024]{2,1,0:T(8,128)(2,1)S(1)}, bf16[4,64,1024]{2,1,0:T(8,128)(2,1)S(1)}, u32[]{:S(2)}, u32[]{:S(2)}) collective-permute-start(bf16[4,64,1024]{2,1,0:T(8,128)(2,1)S(1)} %pad_maximum_fusion.7.refs_1_), channel_id=1, source_target_pairs={{0,1},{1,0},{2,3},{3,2},{4,5},{5,4},{6,7},{7,6},{8,9},{9,8},{10,11... | collective-permute-start | bytes 1572872 | tf_op jit(solution)/shard_map/ppermute | solution.py:55
  26.0 2.6 %collective-permute-start.5 = (bf16[4,64,1024]{2,1,0:T(8,128)(2,1)S(1)}, bf16[4,64,1024]{2,1,0:T(8,128)(2,1)S(1)}, u32[]{:S(2)}, u32[]{:S(2)}) collective-permute-start(bf16[4,64,1024]{2,1,0:T(8,128)(2,1)S(1)} %pad_maximum_fusion.6.refs_0_), channel_id=1, source_target_pairs={{0,1},{1,0},{2,3},{3,2},{4,5},{5,4},{6,7},{7,6},{8,9},{9,8},{10,11... | collective-permute-start | bytes 1572872 | tf_op jit(solution)/shard_map/ppermute | solution.py:55
  30.4 14.9 %collective-permute-start.7 = (bf16[128,2688]{1,0:T(8,128)(2,1)S(1)}, bf16[128,2688]{1,0:T(8,128)(2,1)S(1)}, u32[]{:S(2)}, u32[]{:S(2)}) collective-permute-start(bf16[128,2688]{1,0:T(8,128)(2,1)S(1)} %get-tuple-element.111), channel_id=1, source_target_pairs={{0,16},{1,49},{2,18},{3,51},{4,20},{5,53},{6,22},{7,55},{8,24},{9,... | collective-permute-start | bytes 2064392 | tf_op jit(solution)/shard_map/ppermute | solution.py:55
  32.4 17.2 %collective-permute-start.11 = (bf16[2,64,1024]{2,1,0:T(8,128)(2,1)S(1)}, bf16[2,64,1024]{2,1,0:T(8,128)(2,1)S(1)}, u32[]{:S(2)}, u32[]{:S(2)}) collective-permute-start(bf16[2,64,1024]{2,1,0:T(8,128)(2,1)S(1)} %pad_maximum_fusion.11), channel_id=1, source_target_pairs={{0,12},{1,13},{2,14},{3,15},{4,0},{5,1},{6,2},{7,3},{8,4},{9,5},{1... | collective-permute-start | bytes 786440 | tf_op jit(solution)/shard_map/ppermute | solution.py:55
  33.0 16.6 %collective-permute-start.12 = (bf16[2,64,1024]{2,1,0:T(8,128)(2,1)S(1)}, bf16[2,64,1024]{2,1,0:T(8,128)(2,1)S(1)}, u32[]{:S(2)}, u32[]{:S(2)}) collective-permute-start(bf16[2,64,1024]{2,1,0:T(8,128)(2,1)S(1)} %pad_maximum_fusion.11), channel_id=1, source_target_pairs={{0,8},{1,9},{2,10},{3,11},{4,12},{5,13},{6,14},{7,15},{8,0},{9,1},... | collective-permute-start | bytes 786440 | tf_op jit(solution)/shard_map/ppermute | solution.py:55
  34.4 15.2 %collective-permute-start.13 = (bf16[2,64,1024]{2,1,0:T(8,128)(2,1)S(1)}, bf16[2,64,1024]{2,1,0:T(8,128)(2,1)S(1)}, u32[]{:S(2)}, u32[]{:S(2)}) collective-permute-start(bf16[2,64,1024]{2,1,0:T(8,128)(2,1)S(1)} %pad_maximum_fusion.11), channel_id=1, source_target_pairs={{0,4},{1,5},{2,6},{3,7},{4,8},{5,9},{6,10},{7,11},{8,12},{9,13},{1... | collective-permute-start | bytes 786440 | tf_op jit(solution)/shard_map/ppermute | solution.py:55
  36.3 13.3 %collective-permute-start.9 = (bf16[128,2688]{1,0:T(8,128)(2,1)S(1)}, bf16[128,2688]{1,0:T(8,128)(2,1)S(1)}, u32[]{:S(2)}, u32[]{:S(2)}) collective-permute-start(bf16[128,2688]{1,0:T(8,128)(2,1)S(1)} %get-tuple-element.114), channel_id=1, source_target_pairs={{0,48},{1,17},{2,50},{3,19},{4,52},{5,21},{6,54},{7,23},{8,56},{9,... | collective-permute-start | bytes 2064392 | tf_op jit(solution)/shard_map/ppermute | solution.py:55
  49.8 4.5 %collective-permute-start.15 = (bf16[4,64,1024]{2,1,0:T(8,128)(2,1)S(1)}, bf16[4,64,1024]{2,1,0:T(8,128)(2,1)S(1)}, u32[]{:S(2)}, u32[]{:S(2)}) collective-permute-start(bf16[4,64,1024]{2,1,0:T(8,128)(2,1)S(1)} %pad_maximum_fusion.9.refs_1_.refs_10_), channel_id=1, source_target_pairs={{0,1},{1,0},{2,3},{3,2},{4,5},{5,4},{6,7},{7,6},{8,9},{9,8},{10,11... | collective-permute-start | bytes 1572872 | tf_op jit(solution)/shard_map/ppermute | solution.py:55
  51.0 3.2 %collective-permute-start.14 = (bf16[4,64,1024]{2,1,0:T(8,128)(2,1)S(1)}, bf16[4,64,1024]{2,1,0:T(8,128)(2,1)S(1)}, u32[]{:S(2)}, u32[]{:S(2)}) collective-permute-start(bf16[4,64,1024]{2,1,0:T(8,128)(2,1)S(1)} %pad_maximum_fusion.8.refs_0_.refs_9_), channel_id=1, source_target_pairs={{0,1},{1,0},{2,3},{3,2},{4,5},{5,4},{6,7},{7,6},{8,9},{9,8},{10,11... | collective-permute-start | bytes 1572872 | tf_op jit(solution)/shard_map/ppermute | solution.py:55
  51.1 11.5 %collective-permute-start.10 = (bf16[64,2688]{1,0:T(8,128)(2,1)S(1)}, bf16[64,2688]{1,0:T(8,128)(2,1)S(1)}, u32[]{:S(2)}, u32[]{:S(2)}) collective-permute-start(bf16[64,2688]{1,0:T(8,128)(2,1)S(1)} %slice_add_fusion.2), channel_id=1, source_target_pairs={{0,48},{1,17},{2,50},{3,19},{4,52},{5,21},{6,54},{7,23},{8,56},{9,... | collective-permute-start | bytes 1032200 | tf_op jit(solution)/shard_map/ppermute | solution.py:55
  54.2 8.6 %collective-permute-start.8 = (bf16[64,2688]{1,0:T(8,128)(2,1)S(1)}, bf16[64,2688]{1,0:T(8,128)(2,1)S(1)}, u32[]{:S(2)}, u32[]{:S(2)}) collective-permute-start(bf16[64,2688]{1,0:T(8,128)(2,1)S(1)} %slice_add_fusion.3), channel_id=1, source_target_pairs={{0,16},{1,49},{2,18},{3,51},{4,20},{5,53},{6,22},{7,55},{8,24},{9,... | collective-permute-start | bytes 1032200 | tf_op jit(solution)/shard_map/ppermute | solution.py:55
  57.7 16.4 %collective-permute-start.17 = (bf16[128,2688]{1,0:T(8,128)(2,1)S(1)}, bf16[128,2688]{1,0:T(8,128)(2,1)S(1)}, u32[]{:S(2)}, u32[]{:S(2)}) collective-permute-start(bf16[128,2688]{1,0:T(8,128)(2,1)S(1)} %get-tuple-element.125), channel_id=1, source_target_pairs={{0,16},{1,49},{2,18},{3,51},{4,20},{5,53},{6,22},{7,55},{8,24},{9,... | collective-permute-start | bytes 2064392 | tf_op jit(solution)/shard_map/ppermute | solution.py:55
  62.8 15.5 %collective-permute-start.18 = (bf16[128,2688]{1,0:T(8,128)(2,1)S(1)}, bf16[128,2688]{1,0:T(8,128)(2,1)S(1)}, u32[]{:S(2)}, u32[]{:S(2)}) collective-permute-start(bf16[128,2688]{1,0:T(8,128)(2,1)S(1)} %get-tuple-element.131), channel_id=1, source_target_pairs={{0,48},{1,17},{2,50},{3,19},{4,52},{5,21},{6,54},{7,23},{8,56},{9,... | collective-permute-start | bytes 2064392 | tf_op jit(solution)/shard_map/ppermute | solution.py:55
  66.7 15.3 %collective-permute-start.16 = (bf16[128,2688]{1,0:T(8,128)(2,1)S(1)}, bf16[128,2688]{1,0:T(8,128)(2,1)S(1)}, u32[]{:S(2)}, u32[]{:S(2)}) collective-permute-start(bf16[128,2688]{1,0:T(8,128)(2,1)S(1)} %pad_maximum_fusion.2), channel_id=1, source_target_pairs={{0,64},{1,65},{2,66},{3,67},{4,68},{5,69},{6,70},{7,71},{8,72},{9,... | collective-permute-start | bytes 2064392 | tf_op jit(solution)/shard_map/ppermute | solution.py:55
  74.2 16.3 %collective-permute-start.21 = (bf16[64,2688]{1,0:T(8,128)(2,1)S(1)}, bf16[64,2688]{1,0:T(8,128)(2,1)S(1)}, u32[]{:S(2)}, u32[]{:S(2)}) collective-permute-start(bf16[64,2688]{1,0:T(8,128)(2,1)S(1)} %slice_add_fusion.1), channel_id=1, source_target_pairs={{0,16},{1,49},{2,18},{3,51},{4,20},{5,53},{6,22},{7,55},{8,24},{9,... | collective-permute-start | bytes 1032200 | tf_op jit(solution)/shard_map/ppermute | solution.py:55
  78.3 12.1 %collective-permute-start.22 = (bf16[64,2688]{1,0:T(8,128)(2,1)S(1)}, bf16[64,2688]{1,0:T(8,128)(2,1)S(1)}, u32[]{:S(2)}, u32[]{:S(2)}) collective-permute-start(bf16[64,2688]{1,0:T(8,128)(2,1)S(1)} %slice_add_fusion), channel_id=1, source_target_pairs={{0,48},{1,17},{2,50},{3,19},{4,52},{5,21},{6,54},{7,23},{8,56},{9,... | collective-permute-start | bytes 1032200 | tf_op jit(solution)/shard_map/ppermute | solution.py:55
  82.4 18.7 %collective-permute-start.20 = (bf16[128,2688]{1,0:T(8,128)(2,1)S(1)}, bf16[128,2688]{1,0:T(8,128)(2,1)S(1)}, u32[]{:S(2)}, u32[]{:S(2)}) collective-permute-start(bf16[128,2688]{1,0:T(8,128)(2,1)S(1)} %pad_maximum_fusion.3.refs_0_.refs_4_), channel_id=1, source_target_pairs={{0,16},{1,49},{2,18},{3,51},{4,20},{5,53},{6,22},{7,55},{8,24},{9,... | collective-permute-start | bytes 2064392 | tf_op jit(solution)/shard_map/ppermute | solution.py:55
  82.7 18.5 %collective-permute-start.19 = (bf16[128,2688]{1,0:T(8,128)(2,1)S(1)}, bf16[128,2688]{1,0:T(8,128)(2,1)S(1)}, u32[]{:S(2)}, u32[]{:S(2)}) collective-permute-start(bf16[128,2688]{1,0:T(8,128)(2,1)S(1)} %pad_maximum_fusion.3.refs_0_.refs_4_), channel_id=1, source_target_pairs={{0,48},{1,17},{2,50},{3,19},{4,52},{5,21},{6,54},{7,23},{8,56},{9,... | collective-permute-start | bytes 2064392 | tf_op jit(solution)/shard_map/ppermute | solution.py:55
  90.8 14.1 %collective-permute-start.25 = (bf16[128,2688]{1,0:T(8,128)(2,1)S(1)}, bf16[128,2688]{1,0:T(8,128)(2,1)S(1)}, u32[]{:S(2)}, u32[]{:S(2)}) collective-permute-start(bf16[128,2688]{1,0:T(8,128)(2,1)S(1)} %pad_maximum_fusion.4), channel_id=1, source_target_pairs={{0,64},{1,65},{2,66},{3,67},{4,68},{5,69},{6,70},{7,71},{8,72},{9,... | collective-permute-start | bytes 2064392 | tf_op jit(solution)/shard_map/ppermute | solution.py:55
  101.2 12.3 %collective-permute-start.23 = (bf16[64,2688]{1,0:T(8,128)(2,1)S(1)}, bf16[64,2688]{1,0:T(8,128)(2,1)S(1)}, u32[]{:S(2)}, u32[]{:S(2)}) collective-permute-start(bf16[64,2688]{1,0:T(8,128)(2,1)S(1)} %slice.203), channel_id=1, source_target_pairs={{0,16},{1,49},{2,18},{3,51},{4,20},{5,53},{6,22},{7,55},{8,24},{9,... | collective-permute-start | bytes 1032200 | tf_op jit(solution)/shard_map/ppermute | solution.py:55
  101.3 12.1 %collective-permute-start.24 = (bf16[64,2688]{1,0:T(8,128)(2,1)S(1)}, bf16[64,2688]{1,0:T(8,128)(2,1)S(1)}, u32[]{:S(2)}, u32[]{:S(2)}) collective-permute-start(bf16[64,2688]{1,0:T(8,128)(2,1)S(1)} %slice.204), channel_id=1, source_target_pairs={{0,48},{1,17},{2,50},{3,19},{4,52},{5,21},{6,54},{7,23},{8,56},{9,... | collective-permute-start | bytes 1032200 | tf_op jit(solution)/shard_map/ppermute | solution.py:55
  105.4 20.9 %collective-permute-start.28 = (bf16[128,2688]{1,0:T(8,128)(2,1)S(1)}, bf16[128,2688]{1,0:T(8,128)(2,1)S(1)}, u32[]{:S(2)}, u32[]{:S(2)}) collective-permute-start(bf16[128,2688]{1,0:T(8,128)(2,1)S(1)} %pad_maximum_fusion.5.refs_0_.refs_13_), channel_id=1, source_target_pairs={{0,16},{1,49},{2,18},{3,51},{4,20},{5,53},{6,22},{7,55},{8,24},{9,... | collective-permute-start | bytes 2064392 | tf_op jit(solution)/shard_map/ppermute | solution.py:55
  105.4 21.0 %collective-permute-start.29 = (bf16[128,2688]{1,0:T(8,128)(2,1)S(1)}, bf16[128,2688]{1,0:T(8,128)(2,1)S(1)}, u32[]{:S(2)}, u32[]{:S(2)}) collective-permute-start(bf16[128,2688]{1,0:T(8,128)(2,1)S(1)} %pad_maximum_fusion.5.refs_0_.refs_13_), channel_id=1, source_target_pairs={{0,48},{1,17},{2,50},{3,19},{4,52},{5,21},{6,54},{7,23},{8,56},{9,... | collective-permute-start | bytes 2064392 | tf_op jit(solution)/shard_map/ppermute | solution.py:55
  116.6 13.1 %collective-permute-start.26 = (bf16[256,1024]{1,0:T(8,128)(2,1)S(1)}, bf16[256,1024]{1,0:T(8,128)(2,1)S(1)}, u32[]{:S(2)}, u32[]{:S(2)}) collective-permute-start(bf16[256,1024]{1,0:T(8,128)(2,1)S(1)} %bitcast.27), channel_id=1, source_target_pairs={{0,1},{1,0},{2,3},{3,2},{4,5},{5,4},{6,7},{7,6},{8,9},{9,8},{10,11... | collective-permute-start | bytes 1572872 | tf_op jit(solution)/shard_map/ppermute | solution.py:55
  116.7 13.0 %collective-permute-start.27 = (bf16[256,1024]{1,0:T(8,128)(2,1)S(1)}, bf16[256,1024]{1,0:T(8,128)(2,1)S(1)}, u32[]{:S(2)}, u32[]{:S(2)}) collective-permute-start(bf16[256,1024]{1,0:T(8,128)(2,1)S(1)} %bitcast.26), channel_id=1, source_target_pairs={{0,1},{1,0},{2,3},{3,2},{4,5},{5,4},{6,7},{7,6},{8,9},{9,8},{10,11... | collective-permute-start | bytes 1572872 | tf_op jit(solution)/shard_map/ppermute | solution.py:55
  126.3 9.6 %collective-permute-start.33 = (bf16[64,2688]{1,0:T(8,128)(2,1)S(1)}, bf16[64,2688]{1,0:T(8,128)(2,1)S(1)}, u32[]{:S(2)}, u32[]{:S(2)}) collective-permute-start(bf16[64,2688]{1,0:T(8,128)(2,1)S(1)} %slice.208), channel_id=1, source_target_pairs={{0,16},{1,49},{2,18},{3,51},{4,20},{5,53},{6,22},{7,55},{8,24},{9,... | collective-permute-start | bytes 1032200 | tf_op jit(solution)/shard_map/ppermute | solution.py:55
  126.4 9.4 %collective-permute-start.34 = (bf16[64,2688]{1,0:T(8,128)(2,1)S(1)}, bf16[64,2688]{1,0:T(8,128)(2,1)S(1)}, u32[]{:S(2)}, u32[]{:S(2)}) collective-permute-start(bf16[64,2688]{1,0:T(8,128)(2,1)S(1)} %slice.209), channel_id=1, source_target_pairs={{0,48},{1,17},{2,50},{3,19},{4,52},{5,21},{6,54},{7,23},{8,56},{9,... | collective-permute-start | bytes 1032200 | tf_op jit(solution)/shard_map/ppermute | solution.py:55
  130.3 9.4 %collective-permute-start.30 = (bf16[64,2048]{1,0:T(8,128)(2,1)S(1)}, bf16[64,2048]{1,0:T(8,128)(2,1)S(1)}, u32[]{:S(2)}, u32[]{:S(2)}) collective-permute-start(bf16[64,2048]{1,0:T(8,128)(2,1)S(1)} %get-tuple-element.208), channel_id=1, source_target_pairs={{0,4},{1,5},{2,6},{3,7},{4,8},{5,9},{6,10},{7,11},{8,12},{9,13},{1... | collective-permute-start | bytes 786440 | tf_op jit(solution)/shard_map/ppermute | solution.py:55
  130.4 11.3 %collective-permute-start.31 = (bf16[64,2048]{1,0:T(8,128)(2,1)S(1)}, bf16[64,2048]{1,0:T(8,128)(2,1)S(1)}, u32[]{:S(2)}, u32[]{:S(2)}) collective-permute-start(bf16[64,2048]{1,0:T(8,128)(2,1)S(1)} %get-tuple-element.209), channel_id=1, source_target_pairs={{0,8},{1,9},{2,10},{3,11},{4,12},{5,13},{6,14},{7,15},{8,0},{9,1},... | collective-permute-start | bytes 786440 | tf_op jit(solution)/shard_map/ppermute | solution.py:55
  133.8 7.9 %collective-permute-start.32 = (bf16[64,2048]{1,0:T(8,128)(2,1)S(1)}, bf16[64,2048]{1,0:T(8,128)(2,1)S(1)}, u32[]{:S(2)}, u32[]{:S(2)}) collective-permute-start(bf16[64,2048]{1,0:T(8,128)(2,1)S(1)} %get-tuple-element.207), channel_id=1, source_target_pairs={{0,12},{1,13},{2,14},{3,15},{4,0},{5,1},{6,2},{7,3},{8,4},{9,5},{1... | collective-permute-start | bytes 786440 | tf_op jit(solution)/shard_map/ppermute | solution.py:55
  139.1 5.8 %collective-permute-start.36 = (bf16[256,1024]{1,0:T(8,128)(2,1)S(1)}, bf16[256,1024]{1,0:T(8,128)(2,1)S(1)}, u32[]{:S(2)}, u32[]{:S(2)}) collective-permute-start(bf16[256,1024]{1,0:T(8,128)(2,1)S(1)} %bitcast.25), channel_id=1, source_target_pairs={{0,1},{1,0},{2,3},{3,2},{4,5},{5,4},{6,7},{7,6},{8,9},{9,8},{10,11... | collective-permute-start | bytes 1572872 | tf_op jit(solution)/shard_map/ppermute | solution.py:55
  139.1 5.7 %collective-permute-start.37 = (bf16[256,1024]{1,0:T(8,128)(2,1)S(1)}, bf16[256,1024]{1,0:T(8,128)(2,1)S(1)}, u32[]{:S(2)}, u32[]{:S(2)}) collective-permute-start(bf16[256,1024]{1,0:T(8,128)(2,1)S(1)} %bitcast.24), channel_id=1, source_target_pairs={{0,1},{1,0},{2,3},{3,2},{4,5},{5,4},{6,7},{7,6},{8,9},{9,8},{10,11... | collective-permute-start | bytes 1572872 | tf_op jit(solution)/shard_map/ppermute | solution.py:55
  141.9 20.1 %collective-permute-start.35 = (bf16[32,2048]{1,0:T(8,128)(2,1)S(1)}, bf16[32,2048]{1,0:T(8,128)(2,1)S(1)}, u32[]{:S(2)}, u32[]{:S(2)}) collective-permute-start(bf16[32,2048]{1,0:T(8,128)(2,1)S(1)} %slice.239), channel_id=1, source_target_pairs={{0,2},{1,3},{2,0},{3,1},{4,6},{5,7},{6,4},{7,5},{8,10},{9,11},{10,... | collective-permute-start | bytes 393224 | tf_op jit(solution)/shard_map/ppermute | solution.py:55
  145.4 15.8 %collective-permute-start.38 = (bf16[64,2048]{1,0:T(8,128)(2,1)S(1)}, bf16[64,2048]{1,0:T(8,128)(2,1)S(1)}, u32[]{:S(2)}, u32[]{:S(2)}) collective-permute-start(bf16[64,2048]{1,0:T(8,128)(2,1)S(1)} %get-tuple-element.204), channel_id=1, source_target_pairs={{0,4},{1,5},{2,6},{3,7},{4,8},{5,9},{6,10},{7,11},{8,12},{9,13},{1... | collective-permute-start | bytes 786440 | tf_op jit(solution)/shard_map/ppermute | solution.py:55
  147.5 13.7 %collective-permute-start.39 = (bf16[64,2048]{1,0:T(8,128)(2,1)S(1)}, bf16[64,2048]{1,0:T(8,128)(2,1)S(1)}, u32[]{:S(2)}, u32[]{:S(2)}) collective-permute-start(bf16[64,2048]{1,0:T(8,128)(2,1)S(1)} %get-tuple-element.205), channel_id=1, source_target_pairs={{0,8},{1,9},{2,10},{3,11},{4,12},{5,13},{6,14},{7,15},{8,0},{9,1},... | collective-permute-start | bytes 786440 | tf_op jit(solution)/shard_map/ppermute | solution.py:55
  149.6 11.6 %collective-permute-start.40 = (bf16[64,2048]{1,0:T(8,128)(2,1)S(1)}, bf16[64,2048]{1,0:T(8,128)(2,1)S(1)}, u32[]{:S(2)}, u32[]{:S(2)}) collective-permute-start(bf16[64,2048]{1,0:T(8,128)(2,1)S(1)} %get-tuple-element.203), channel_id=1, source_target_pairs={{0,12},{1,13},{2,14},{3,15},{4,0},{5,1},{6,2},{7,3},{8,4},{9,5},{1... | collective-permute-start | bytes 786440 | tf_op jit(solution)/shard_map/ppermute | solution.py:55
  161.3 6.6 %collective-permute-start.41 = (bf16[32,2048]{1,0:T(8,128)(2,1)S(1)}, bf16[32,2048]{1,0:T(8,128)(2,1)S(1)}, u32[]{:S(2)}, u32[]{:S(2)}) collective-permute-start(bf16[32,2048]{1,0:T(8,128)(2,1)S(1)} %slice.249), channel_id=1, source_target_pairs={{0,2},{1,3},{2,0},{3,1},{4,6},{5,7},{6,4},{7,5},{8,10},{9,11},{10,... | collective-permute-start | bytes 393224 | tf_op jit(solution)/shard_map/ppermute | solution.py:55

commit v12 on v9

--- a/solution.py
+++ b/solution.py
@@ -285,15 +285,28 @@
 
 
 class Gather:
-    def __init__(self, pair):
-        self.pair = pair
+    def __init__(self, part, slices, direct):
+        self.part, self.slices, self.direct = part, slices, direct
+        if not direct:
+            self.near = self.join(part, move(part, dxh=1))
+
+    def join(self, *halves):
+        return jnp.concatenate([half[:, at] for at in self.slices for half in halves], axis=1)
 
     def far(self, *others):
-        self.pair = after(self.pair, *others)
-        self.pairs = [self.pair] + [move(self.pair, dy=-dy) for dy in range(1, 4)]
+        if self.direct:
+            part = after(self.part, *others)
+            self.parts = [
+                [move(part, dy=-dy, dxh=dx) if dy or dx else part for dx in range(2)]
+                for dy in range(4)
+            ]
+        else:
+            near = after(self.near, *others)
+            self.parts = [[near]] + [[move(near, dy=-dy)] for dy in range(1, 4)]
 
     def core(self, *others):
-        pairs = after(self.pairs, *others)
+        parts = after(self.parts, *others)
+        pairs = [self.join(*part) if self.direct else part[0] for part in parts]
         own = [jnp.stack([pair[kind] for pair in pairs]) for kind in range(2)]
         self.arrays = (*own, *[move(array, dcore=1) for array in own])
         return own
@@ -387,16 +400,13 @@
     for group in GATHERS:
         first, last = starts[group[0]], starts[group[-1]] + CHUNKS[group[-1]]
         part = jnp.stack([tokens[first:last], out_grad[first:last]])
-        received = move(part, dxh=1)
         slices = [slice(starts[i] - first, starts[i] - first + CHUNKS[i]) for i in group]
-        gather = Gather(
-            jnp.concatenate([half[:, at] for at in slices for half in (part, received)], axis=1)
-        )
+        gather = Gather(part, slices, not gathers)
         gathers.append(gather)
         for i in group:
             chunks.append(Chunk(gather, 2 * (starts[i] - first), CHUNKS[i], weights))
     gathers[0].far()
-    before = gathers[0].core(weights, *[gather.pair for gather in gathers[1:]])
+    before = gathers[0].core(weights, *[gather.near for gather in gathers[1:]])
     gathers[1].far(before)
     for step in ORDER:
         name, _, which = step.partition(" ")

time: 169 us -> 176 us (1.041)
  starting transfers between devices: 60.2 us -> 67.9 us
  waiting for transfers between devices: 71.5 us -> 69.1 us
  local copies, waits for them, and re-layouts: 5.75 us -> 7.89 us
    ppermute x42 -> x45, starting transfers between devices: 60.2 us -> 67.9 us  [move(): return lax.ppermute(array, ('row', 'col'), pairs)]
    ppermute x42 -> x45, waiting for transfers between devices: 71.5 us -> 69.1 us  [move(): return lax.ppermute(array, ('row', 'col'), pairs)]
    unnamed x12 -> x22, local copies, waits for them, and re-layouts: 4.51 us -> 6.62 us
  transfers between devices with their start and end apart: 42 -> 45, of which waited for: 21 -> 21; matrix products, arithmetic and copies ran while one was open for 2% -> 2% of each run, Pallas kernels for 13% -> 13%
where the time goes in v12:
time: 176 us
  waiting for transfers between devices  69.1 us (39%)
  starting transfers between devices  67.9 us (39%)
  Pallas kernels  25.6 us (15%)
  local copies, waits for them, and re-layouts  7.89 us (4%)
  other arithmetic  4.16 us (2%)
    ppermute x45, waiting for transfers between devices, move(): return lax.ppermute(array, ('row', 'col'), pairs)  69.1 us
    ppermute x45, starting transfers between devices, move(): return lax.ppermute(array, ('row', 'col'), pairs)  67.9 us
    pallas_call x1, Pallas kernels, weight_grads(): pl.pallas_call(functools.partial(weight_grad_kernel, offsets), in_specs=[...  9.61 us
    pallas_call x2, Pallas kernels, forward(): pl.pallas_call(functools.partial(forward_kernel, offset, rows), in_specs=...  6.86 us
    unnamed x22, local copies, waits for them, and re-layouts  6.62 us
    pallas_call x2, Pallas kernels, backward(): pl.pallas_call(backward_kernel, in_specs=[VMEM] * 6, out_specs=[VMEM] * 4...  6.34 us
  transfers between devices with their start and end apart: 45, of which 21 were waited for; matrix products, arithmetic and copies ran while one was open for 2% of the time, Pallas kernels for 13%

profile of v12, /device:TPU:0, one launch (start us, length us, event | category | flops | bytes accessed | tf_op | source)
XLA Modules:
  0.0 175.9 jit_solution(12235214095418397379)
XLA Ops:
  0.6 1.0 slice_bitcast_fusion
  1.6 3.2 %collective-permute-start.7 = (bf16[2,32,1024]{2,1,0:T(8,128)(2,1)S(1)}, bf16[2,32,1024]{2,1,0:T(8,128)(2,1)S(1)}, u32[]{:S(2)}, u32[]{:S(2)}) collective-permute-start(bf16[2,32,1024]{2,1,0:T(8,128)(2,1)S(1)} %pad_maximum_fusion.13), channel_id=1, source_target_pairs={{0,2},{1,3},{2,0},{3,1},{4,6},{5,7},{6,4},{7,5},{8,10},{9,11},{10,... | collective-permute-start | bytes 393224 | tf_op jit(solution)/shard_map/ppermute | solution.py:54
  5.3 3.1 %collective-permute-start.1 = (bf16[2,32,1024]{2,1,0:T(8,128)(2,1)S(1)}, bf16[2,32,1024]{2,1,0:T(8,128)(2,1)S(1)}, u32[]{:S(2)}, u32[]{:S(2)}) collective-permute-start(bf16[2,32,1024]{2,1,0:T(8,128)(2,1)S(1)} %pad_maximum_fusion.12), channel_id=1, source_target_pairs={{0,12},{1,13},{2,14},{3,15},{4,0},{5,1},{6,2},{7,3},{8,4},{9,5},{1... | collective-permute-start | bytes 393224 | tf_op jit(solution)/shard_map/ppermute | solution.py:54
  8.4 3.2 %collective-permute-start.2 = (bf16[2,32,1024]{2,1,0:T(8,128)(2,1)S(1)}, bf16[2,32,1024]{2,1,0:T(8,128)(2,1)S(1)}, u32[]{:S(2)}, u32[]{:S(2)}) collective-permute-start(bf16[2,32,1024]{2,1,0:T(8,128)(2,1)S(1)} %pad_maximum_fusion.12), channel_id=1, source_target_pairs={{0,14},{1,15},{2,12},{3,13},{4,2},{5,3},{6,0},{7,1},{8,6},{9,7},{1... | collective-permute-start | bytes 393224 | tf_op jit(solution)/shard_map/ppermute | solution.py:54
  12.0 3.4 %collective-permute-start.4 = (bf16[2,32,1024]{2,1,0:T(8,128)(2,1)S(1)}, bf16[2,32,1024]{2,1,0:T(8,128)(2,1)S(1)}, u32[]{:S(2)}, u32[]{:S(2)}) collective-permute-start(bf16[2,32,1024]{2,1,0:T(8,128)(2,1)S(1)} %pad_maximum_fusion.12), channel_id=1, source_target_pairs={{0,10},{1,11},{2,8},{3,9},{4,14},{5,15},{6,12},{7,13},{8,2},{9,3},... | collective-permute-start | bytes 393224 | tf_op jit(solution)/shard_map/ppermute | solution.py:54
  15.3 1.1 collective-permute-start.5
  16.4 2.5 %collective-permute-start.6 = (bf16[2,32,1024]{2,1,0:T(8,128)(2,1)S(1)}, bf16[2,32,1024]{2,1,0:T(8,128)(2,1)S(1)}, u32[]{:S(2)}, u32[]{:S(2)}) collective-permute-start(bf16[2,32,1024]{2,1,0:T(8,128)(2,1)S(1)} %pad_maximum_fusion.12), channel_id=1, source_target_pairs={{0,6},{1,7},{2,4},{3,5},{4,10},{5,11},{6,8},{7,9},{8,14},{9,15},{1... | collective-permute-start | bytes 393224 | tf_op jit(solution)/shard_map/ppermute | solution.py:54
  18.9 1.5 copy-done
  20.4 1.5 copy-done.1
  21.9 1.5 copy-done.2
  25.5 2.8 %mask_weights.1.refs_4_.refs_5_ = bf16[1024,2688]{1,0:T(8,128)(2,1)S(1)} custom-call(bf16[1024,896]{1,0:T(8,128)(2,1)S(1)} %copy-done, bf16[1024,896]{1,0:T(8,128)(2,1)S(1)} %copy-done.1, bf16[896,1024]{1,0:T(8,128)(2,1)S(1)} %copy-done.2, s32[8,7]{1,0:T(8,128)S(1)} %copy-done.3, s32[8,7]{1,0:T(8,128)S(1)} %copy-done.5, s32[7,8]{1,0:T(8,128)S(1)} %copy-done.7), custom_call_target="tpu_custom_call" | custom-call | flops 2752512 | bytes 11010048 | tf_op jit(solution)/shard_map/mask_weights/pallas_call | solution.py:120
  29.4 1.2 collective-permute-done.9.refs_3_
  31.4 3.4 %forward.2 = (bf16[128,2688]{1,0:T(8,128)(2,1)S(1)}, bf16[128,2688]{1,0:T(8,128)(2,1)S(1)}, bf16[64,2688]{1,0:T(8,128)(2,1)S(1)}, bf16[64,2688]{1,0:T(8,128)(2,1)S(1)}, bf16[128,2688]{1,0:T(8,128)(2,1)S(1)}) custom-call(bf16[4,64,1024]{2,1,0:T(8,128)(2,1)S(1)} %pad_maximum_fusion.6.refs_0_, bf16[4,64,1024]{2,1,0:T(8,128)(2,1)S(1)} %pad_maximum_fusion.7.refs_1_, ...), custom_call_target="tpu_custom_call" | custom-call | flops 1024 | bytes 1024 | tf_op jit(solution)/shard_map/forward/pallas_call | solution.py:158
  34.9 2.0 %collective-permute-start.10 = (bf16[128,2688]{1,0:T(8,128)(2,1)S(1)}, bf16[128,2688]{1,0:T(8,128)(2,1)S(1)}, u32[]{:S(2)}, u32[]{:S(2)}) collective-permute-start(bf16[128,2688]{1,0:T(8,128)(2,1)S(1)} %get-tuple-element.119), channel_id=1, source_target_pairs={{0,16},{1,49},{2,18},{3,51},{4,20},{5,53},{6,22},{7,55},{8,24},{9,... | collective-permute-start | bytes 2064392 | tf_op jit(solution)/shard_map/ppermute | solution.py:54
  36.8 5.3 %collective-permute-start.14 = (bf16[2,64,1024]{2,1,0:T(8,128)(2,1)S(1)}, bf16[2,64,1024]{2,1,0:T(8,128)(2,1)S(1)}, u32[]{:S(2)}, u32[]{:S(2)}) collective-permute-start(bf16[2,64,1024]{2,1,0:T(8,128)(2,1)S(1)} %pad_maximum_fusion.10), channel_id=1, source_target_pairs={{0,12},{1,13},{2,14},{3,15},{4,0},{5,1},{6,2},{7,3},{8,4},{9,5},{1... | collective-permute-start | bytes 786440 | tf_op jit(solution)/shard_map/ppermute | solution.py:54
  42.1 2.1 %collective-permute-start.15 = (bf16[2,64,1024]{2,1,0:T(8,128)(2,1)S(1)}, bf16[2,64,1024]{2,1,0:T(8,128)(2,1)S(1)}, u32[]{:S(2)}, u32[]{:S(2)}) collective-permute-start(bf16[2,64,1024]{2,1,0:T(8,128)(2,1)S(1)} %pad_maximum_fusion.10), channel_id=1, source_target_pairs={{0,8},{1,9},{2,10},{3,11},{4,12},{5,13},{6,14},{7,15},{8,0},{9,1},... | collective-permute-start | bytes 786440 | tf_op jit(solution)/shard_map/ppermute | solution.py:54
  44.2 1.4 collective-permute-start.16
  45.6 2.2 %collective-permute-start.12 = (bf16[128,2688]{1,0:T(8,128)(2,1)S(1)}, bf16[128,2688]{1,0:T(8,128)(2,1)S(1)}, u32[]{:S(2)}, u32[]{:S(2)}) collective-permute-start(bf16[128,2688]{1,0:T(8,128)(2,1)S(1)} %get-tuple-element.122), channel_id=1, source_target_pairs={{0,48},{1,17},{2,50},{3,19},{4,52},{5,21},{6,54},{7,23},{8,56},{9,... | collective-permute-start | bytes 2064392 | tf_op jit(solution)/shard_map/ppermute | solution.py:54
  47.9 8.6 %collective-permute-done.12 = bf16[128,2688]{1,0:T(8,128)(2,1)S(1)} collective-permute-done((bf16[128,2688]{1,0:T(8,128)(2,1)S(1)}, bf16[128,2688]{1,0:T(8,128)(2,1)S(1)}, u32[]{:S(2)}, u32[]{:S(2)}) %collective-permute-start.12) | collective-permute-done | bytes 688160 | tf_op jit(solution)/shard_map/ppermute | solution.py:54
  56.6 1.7 collective-permute-done.16
  59.3 1.7 collective-permute-start.13
  61.3 3.4 %forward.3 = (bf16[128,2688]{1,0:T(8,128)(2,1)S(1)}, bf16[128,2688]{1,0:T(8,128)(2,1)S(1)}, bf16[64,2688]{1,0:T(8,128)(2,1)S(1)}, bf16[64,2688]{1,0:T(8,128)(2,1)S(1)}, bf16[128,2688]{1,0:T(8,128)(2,1)S(1)}) custom-call(bf16[4,64,1024]{2,1,0:T(8,128)(2,1)S(1)} %pad_maximum_fusion.8.refs_0_.refs_9_, ...), custom_call_target="tpu_custom_call" | custom-call | flops 1024 | bytes 1024 | tf_op jit(solution)/shard_map/forward/pallas_call | solution.py:158
  65.2 5.0 %collective-permute-done.13 = bf16[64,2688]{1,0:T(8,128)(2,1)S(1)} collective-permute-done((bf16[64,2688]{1,0:T(8,128)(2,1)S(1)}, bf16[64,2688]{1,0:T(8,128)(2,1)S(1)}, u32[]{:S(2)}, u32[]{:S(2)}) %collective-permute-start.13) | collective-permute-done | bytes 344096 | tf_op jit(solution)/shard_map/ppermute | solution.py:54
  70.6 2.2 %collective-permute-start.21 = (bf16[128,2688]{1,0:T(8,128)(2,1)S(1)}, bf16[128,2688]{1,0:T(8,128)(2,1)S(1)}, u32[]{:S(2)}, u32[]{:S(2)}) collective-permute-start(bf16[128,2688]{1,0:T(8,128)(2,1)S(1)} %get-tuple-element.139), channel_id=1, source_target_pairs={{0,48},{1,17},{2,50},{3,19},{4,52},{5,21},{6,54},{7,23},{8,56},{9,... | collective-permute-start | bytes 2064392 | tf_op jit(solution)/shard_map/ppermute | solution.py:54
  73.3 8.7 %collective-permute-done.20 = bf16[128,2688]{1,0:T(8,128)(2,1)S(1)} collective-permute-done((bf16[128,2688]{1,0:T(8,128)(2,1)S(1)}, bf16[128,2688]{1,0:T(8,128)(2,1)S(1)}, u32[]{:S(2)}, u32[]{:S(2)}) %collective-permute-start.20) | collective-permute-done | bytes 688160 | tf_op jit(solution)/shard_map/ppermute | solution.py:54
  82.2 3.1 %collective-permute-done.21 = bf16[128,2688]{1,0:T(8,128)(2,1)S(1)} collective-permute-done((bf16[128,2688]{1,0:T(8,128)(2,1)S(1)}, bf16[128,2688]{1,0:T(8,128)(2,1)S(1)}, u32[]{:S(2)}, u32[]{:S(2)}) %collective-permute-start.21) | collective-permute-done | bytes 688160 | tf_op jit(solution)/shard_map/ppermute | solution.py:54
  85.3 3.1 %collective-permute-start.25 = (bf16[64,2688]{1,0:T(8,128)(2,1)S(1)}, bf16[64,2688]{1,0:T(8,128)(2,1)S(1)}, u32[]{:S(2)}, u32[]{:S(2)}) collective-permute-start(bf16[64,2688]{1,0:T(8,128)(2,1)S(1)} %slice_add_fusion), channel_id=1, source_target_pairs={{0,48},{1,17},{2,50},{3,19},{4,52},{5,21},{6,54},{7,23},{8,56},{9,... | collective-permute-start | bytes 1032200 | tf_op jit(solution)/shard_map/ppermute | solution.py:54
  88.9 1.3 collective-permute-start.23
  90.2 2.0 %collective-permute-start.22 = (bf16[128,2688]{1,0:T(8,128)(2,1)S(1)}, bf16[128,2688]{1,0:T(8,128)(2,1)S(1)}, u32[]{:S(2)}, u32[]{:S(2)}) collective-permute-start(bf16[128,2688]{1,0:T(8,128)(2,1)S(1)} %pad_maximum_fusion.3.refs_0_.refs_4_), channel_id=1, source_target_pairs={{0,48},{1,17},{2,50},{3,19},{4,52},{5,21},{6,54},{7,23},{8,56},{9,... | collective-permute-start | bytes 2064392 | tf_op jit(solution)/shard_map/ppermute | solution.py:54
  92.2 3.8 %collective-permute-done.25 = bf16[64,2688]{1,0:T(8,128)(2,1)S(1)} collective-permute-done((bf16[64,2688]{1,0:T(8,128)(2,1)S(1)}, bf16[64,2688]{1,0:T(8,128)(2,1)S(1)}, u32[]{:S(2)}, u32[]{:S(2)}) %collective-permute-start.25) | collective-permute-done | bytes 344096 | tf_op jit(solution)/shard_map/ppermute | solution.py:54
  96.4 12.1 %collective-permute-done.23.refs_2_.refs_6_ = bf16[128,2688]{1,0:T(8,128)(2,1)S(1)} collective-permute-done((bf16[128,2688]{1,0:T(8,128)(2,1)S(1)}, bf16[128,2688]{1,0:T(8,128)(2,1)S(1)}, u32[]{:S(2)}, u32[]{:S(2)}) %collective-permute-start.23) | collective-permute-done | bytes 688160 | tf_op jit(solution)/shard_map/ppermute | solution.py:54
  108.7 3.3 %collective-permute-start.27 = (bf16[64,2688]{1,0:T(8,128)(2,1)S(1)}, bf16[64,2688]{1,0:T(8,128)(2,1)S(1)}, u32[]{:S(2)}, u32[]{:S(2)}) collective-permute-start(bf16[64,2688]{1,0:T(8,128)(2,1)S(1)} %slice.204), channel_id=1, source_target_pairs={{0,48},{1,17},{2,50},{3,19},{4,52},{5,21},{6,54},{7,23},{8,56},{9,... | collective-permute-start | bytes 1032200 | tf_op jit(solution)/shard_map/ppermute | solution.py:54
  113.3 3.2 %collective-permute-start.32 = (bf16[128,2688]{1,0:T(8,128)(2,1)S(1)}, bf16[128,2688]{1,0:T(8,128)(2,1)S(1)}, u32[]{:S(2)}, u32[]{:S(2)}) collective-permute-start(bf16[128,2688]{1,0:T(8,128)(2,1)S(1)} %pad_maximum_fusion.5.refs_0_.refs_13_), channel_id=1, source_target_pairs={{0,48},{1,17},{2,50},{3,19},{4,52},{5,21},{6,54},{7,23},{8,56},{9,... | collective-permute-start | bytes 2064392 | tf_op jit(solution)/shard_map/ppermute | solution.py:54
  116.5 4.0 %collective-permute-done.27.refs_4_.refs_8_ = bf16[64,2688]{1,0:T(8,128)(2,1)S(1)} collective-permute-done((bf16[64,2688]{1,0:T(8,128)(2,1)S(1)}, bf16[64,2688]{1,0:T(8,128)(2,1)S(1)}, u32[]{:S(2)}, u32[]{:S(2)}) %collective-permute-start.27) | collective-permute-done | bytes 344096 | tf_op jit(solution)/shard_map/ppermute | solution.py:54
  120.7 3.2 %backward.2 = (bf16[4,64,1024]{2,1,0:T(8,128)(2,1)S(1)}, bf16[4,64,1024]{2,1,0:T(8,128)(2,1)S(1)}, bf16[4,64,1024]{2,1,0:T(8,128)(2,1)S(1)}, bf16[4,64,1024]{2,1,0:T(8,128)(2,1)S(1)}) custom-call(bf16[128,2688]{1,0:T(8,128)(2,1)S(1)} %pad_maximum_fusion.3.refs_0_.refs_4_, bf16[128,2688]{1,0:T(8,128)(2,1)S(1)} %collective-permute-done.22.refs_1_.refs_5_, ...), custom_call_target="tpu_custom_call" | custom-call | flops 2818572288 | bytes 22020096 | tf_op jit(solution)/shard_map/backward/pallas_call | solution.py:186
  124.5 10.6 %collective-permute-done.31.refs_2_.refs_15_ = bf16[128,2688]{1,0:T(8,128)(2,1)S(1)} collective-permute-done((bf16[128,2688]{1,0:T(8,128)(2,1)S(1)}, bf16[128,2688]{1,0:T(8,128)(2,1)S(1)}, u32[]{:S(2)}, u32[]{:S(2)}) %collective-permute-start.31) | collective-permute-done | bytes 688160 | tf_op jit(solution)/shard_map/ppermute | solution.py:54
  135.2 3.3 %collective-permute-start.37 = (bf16[64,2688]{1,0:T(8,128)(2,1)S(1)}, bf16[64,2688]{1,0:T(8,128)(2,1)S(1)}, u32[]{:S(2)}, u32[]{:S(2)}) collective-permute-start(bf16[64,2688]{1,0:T(8,128)(2,1)S(1)} %slice.209), channel_id=1, source_target_pairs={{0,48},{1,17},{2,50},{3,19},{4,52},{5,21},{6,54},{7,23},{8,56},{9,... | collective-permute-start | bytes 1032200 | tf_op jit(solution)/shard_map/ppermute | solution.py:54
  139.6 2.8 %collective-permute-start.34 = (bf16[64,2048]{1,0:T(8,128)(2,1)S(1)}, bf16[64,2048]{1,0:T(8,128)(2,1)S(1)}, u32[]{:S(2)}, u32[]{:S(2)}) collective-permute-start(bf16[64,2048]{1,0:T(8,128)(2,1)S(1)} %get-tuple-element.217), channel_id=1, source_target_pairs={{0,8},{1,9},{2,10},{3,11},{4,12},{5,13},{6,14},{7,15},{8,0},{9,1},... | collective-permute-start | bytes 786440 | tf_op jit(solution)/shard_map/ppermute | solution.py:54
  142.3 2.5 %collective-permute-start.35 = (bf16[64,2048]{1,0:T(8,128)(2,1)S(1)}, bf16[64,2048]{1,0:T(8,128)(2,1)S(1)}, u32[]{:S(2)}, u32[]{:S(2)}) collective-permute-start(bf16[64,2048]{1,0:T(8,128)(2,1)S(1)} %get-tuple-element.215), channel_id=1, source_target_pairs={{0,12},{1,13},{2,14},{3,15},{4,0},{5,1},{6,2},{7,3},{8,4},{9,5},{1... | collective-permute-start | bytes 786440 | tf_op jit(solution)/shard_map/ppermute | solution.py:54
  144.9 1.2 collective-permute-done.36.refs_3_.refs_16_
  146.0 3.2 %backward.3 = (bf16[4,64,1024]{2,1,0:T(8,128)(2,1)S(1)}, bf16[4,64,1024]{2,1,0:T(8,128)(2,1)S(1)}, bf16[4,64,1024]{2,1,0:T(8,128)(2,1)S(1)}, bf16[4,64,1024]{2,1,0:T(8,128)(2,1)S(1)}) custom-call(bf16[128,2688]{1,0:T(8,128)(2,1)S(1)} %pad_maximum_fusion.5.refs_0_.refs_13_, bf16[128,2688]{1,0:T(8,128)(2,1)S(1)} %collective-permute-done.32.refs_1_.refs_14_, ...), custom_call_target="tpu_custom_call" | custom-call | flops 2818572288 | bytes 22020096 | tf_op jit(solution)/shard_map/backward/pallas_call | solution.py:186
  151.3 0.8 collective-permute-start.38
  152.7 1.8 %collective-permute-start.41 = (bf16[64,2048]{1,0:T(8,128)(2,1)S(1)}, bf16[64,2048]{1,0:T(8,128)(2,1)S(1)}, u32[]{:S(2)}, u32[]{:S(2)}) collective-permute-start(bf16[64,2048]{1,0:T(8,128)(2,1)S(1)} %get-tuple-element.212), channel_id=1, source_target_pairs={{0,4},{1,5},{2,6},{3,7},{4,8},{5,9},{6,10},{7,11},{8,12},{9,13},{1... | collective-permute-start | bytes 786440 | tf_op jit(solution)/shard_map/ppermute | solution.py:54
  154.5 2.4 %collective-permute-start.42 = (bf16[64,2048]{1,0:T(8,128)(2,1)S(1)}, bf16[64,2048]{1,0:T(8,128)(2,1)S(1)}, u32[]{:S(2)}, u32[]{:S(2)}) collective-permute-start(bf16[64,2048]{1,0:T(8,128)(2,1)S(1)} %get-tuple-element.213), channel_id=1, source_target_pairs={{0,8},{1,9},{2,10},{3,11},{4,12},{5,13},{6,14},{7,15},{8,0},{9,1},... | collective-permute-start | bytes 786440 | tf_op jit(solution)/shard_map/ppermute | solution.py:54
  156.9 1.0 collective-permute-start.43
  157.9 9.6 %weight_grads.1 = (bf16[1024,896]{1,0:T(8,128)(2,1)}, bf16[1024,896]{1,0:T(8,128)(2,1)}, bf16[896,1024]{1,0:T(8,128)(2,1)}) custom-call(bf16[4,64,1024]{2,1,0:T(8,128)(2,1)S(1)} %pad_maximum_fusion.6.refs_0_, bf16[4,64,1024]{2,1,0:T(8,128)(2,1)S(1)} %pad_maximum_fusion.7.refs_1_, bf16[4,64,1024]{2,1,0:T(8,128)(2,1)S(1)} %collective-permute-done.8.refs_2_, ...), custom_call_target="tpu_custom_call" | custom-call | flops 5637144576 | bytes 44040192 | tf_op jit(solution)/shard_map/weight_grads/pallas_call | solution.py:245
  168.6 1.9 %collective-permute-start.44 = (bf16[32,2048]{1,0:T(8,128)(2,1)S(1)}, bf16[32,2048]{1,0:T(8,128)(2,1)S(1)}, u32[]{:S(2)}, u32[]{:S(2)}) collective-permute-start(bf16[32,2048]{1,0:T(8,128)(2,1)S(1)} %slice.257), channel_id=1, source_target_pairs={{0,2},{1,3},{2,0},{3,1},{4,6},{5,7},{6,4},{7,5},{8,10},{9,11},{10,... | collective-permute-start | bytes 393224 | tf_op jit(solution)/shard_map/ppermute | solution.py:54
  170.5 4.6 %collective-permute-done.44 = bf16[32,2048]{1,0:T(8,128)(2,1)S(1)} collective-permute-done((bf16[32,2048]{1,0:T(8,128)(2,1)S(1)}, bf16[32,2048]{1,0:T(8,128)(2,1)S(1)}, u32[]{:S(2)}, u32[]{:S(2)}) %collective-permute-start.44) | collective-permute-done | bytes 131104 | tf_op jit(solution)/shard_map/ppermute | solution.py:54
  (121 shorter events, 16.2 us)
Async XLA Ops:
  1.6 10.3 %collective-permute-start.7 = (bf16[2,32,1024]{2,1,0:T(8,128)(2,1)S(1)}, bf16[2,32,1024]{2,1,0:T(8,128)(2,1)S(1)}, u32[]{:S(2)}, u32[]{:S(2)}) collective-permute-start(bf16[2,32,1024]{2,1,0:T(8,128)(2,1)S(1)} %pad_maximum_fusion.13), channel_id=1, source_target_pairs={{0,2},{1,3},{2,0},{3,1},{4,6},{5,7},{6,4},{7,5},{8,10},{9,11},{10,... | collective-permute-start | bytes 393224 | tf_op jit(solution)/shard_map/ppermute | solution.py:54
  4.8 10.5 %collective-permute-start = (bf16[2,32,1024]{2,1,0:T(8,128)(2,1)S(1)}, bf16[2,32,1024]{2,1,0:T(8,128)(2,1)S(1)}, u32[]{:S(2)}, u32[]{:S(2)}) collective-permute-start(bf16[2,32,1024]{2,1,0:T(8,128)(2,1)S(1)} %pad_maximum_fusion.12), channel_id=1, source_target_pairs={{0,2},{1,3},{2,0},{3,1},{4,6},{5,7},{6,4},{7,5},{8,10},{9,11},{10,... | collective-permute-start | bytes 393224 | tf_op jit(solution)/shard_map/ppermute | solution.py:54
  5.3 11.1 %collective-permute-start.1 = (bf16[2,32,1024]{2,1,0:T(8,128)(2,1)S(1)}, bf16[2,32,1024]{2,1,0:T(8,128)(2,1)S(1)}, u32[]{:S(2)}, u32[]{:S(2)}) collective-permute-start(bf16[2,32,1024]{2,1,0:T(8,128)(2,1)S(1)} %pad_maximum_fusion.12), channel_id=1, source_target_pairs={{0,12},{1,13},{2,14},{3,15},{4,0},{5,1},{6,2},{7,3},{8,4},{9,5},{1... | collective-permute-start | bytes 393224 | tf_op jit(solution)/shard_map/ppermute | solution.py:54
  8.4 19.9 %collective-permute-start.2 = (bf16[2,32,1024]{2,1,0:T(8,128)(2,1)S(1)}, bf16[2,32,1024]{2,1,0:T(8,128)(2,1)S(1)}, u32[]{:S(2)}, u32[]{:S(2)}) collective-permute-start(bf16[2,32,1024]{2,1,0:T(8,128)(2,1)S(1)} %pad_maximum_fusion.12), channel_id=1, source_target_pairs={{0,14},{1,15},{2,12},{3,13},{4,2},{5,3},{6,0},{7,1},{8,6},{9,7},{1... | collective-permute-start | bytes 393224 | tf_op jit(solution)/shard_map/ppermute | solution.py:54
  11.6 16.7 %collective-permute-start.3 = (bf16[2,32,1024]{2,1,0:T(8,128)(2,1)S(1)}, bf16[2,32,1024]{2,1,0:T(8,128)(2,1)S(1)}, u32[]{:S(2)}, u32[]{:S(2)}) collective-permute-start(bf16[2,32,1024]{2,1,0:T(8,128)(2,1)S(1)} %pad_maximum_fusion.12), channel_id=1, source_target_pairs={{0,8},{1,9},{2,10},{3,11},{4,12},{5,13},{6,14},{7,15},{8,0},{9,1},... | collective-permute-start | bytes 393224 | tf_op jit(solution)/shard_map/ppermute | solution.py:54
  12.0 16.4 %collective-permute-start.4 = (bf16[2,32,1024]{2,1,0:T(8,128)(2,1)S(1)}, bf16[2,32,1024]{2,1,0:T(8,128)(2,1)S(1)}, u32[]{:S(2)}, u32[]{:S(2)}) collective-permute-start(bf16[2,32,1024]{2,1,0:T(8,128)(2,1)S(1)} %pad_maximum_fusion.12), channel_id=1, source_target_pairs={{0,10},{1,11},{2,8},{3,9},{4,14},{5,15},{6,12},{7,13},{8,2},{9,3},... | collective-permute-start | bytes 393224 | tf_op jit(solution)/shard_map/ppermute | solution.py:54
  15.3 13.0 %collective-permute-start.5 = (bf16[2,32,1024]{2,1,0:T(8,128)(2,1)S(1)}, bf16[2,32,1024]{2,1,0:T(8,128)(2,1)S(1)}, u32[]{:S(2)}, u32[]{:S(2)}) collective-permute-start(bf16[2,32,1024]{2,1,0:T(8,128)(2,1)S(1)} %pad_maximum_fusion.12), channel_id=1, source_target_pairs={{0,4},{1,5},{2,6},{3,7},{4,8},{5,9},{6,10},{7,11},{8,12},{9,13},{1... | collective-permute-start | bytes 393224 | tf_op jit(solution)/shard_map/ppermute | solution.py:54
  16.4 12.0 %collective-permute-start.6 = (bf16[2,32,1024]{2,1,0:T(8,128)(2,1)S(1)}, bf16[2,32,1024]{2,1,0:T(8,128)(2,1)S(1)}, u32[]{:S(2)}, u32[]{:S(2)}) collective-permute-start(bf16[2,32,1024]{2,1,0:T(8,128)(2,1)S(1)} %pad_maximum_fusion.12), channel_id=1, source_target_pairs={{0,6},{1,7},{2,4},{3,5},{4,10},{5,11},{6,8},{7,9},{8,14},{9,15},{1... | collective-permute-start | bytes 393224 | tf_op jit(solution)/shard_map/ppermute | solution.py:54
  28.7 2.0 %collective-permute-start.9 = (bf16[4,64,1024]{2,1,0:T(8,128)(2,1)S(1)}, bf16[4,64,1024]{2,1,0:T(8,128)(2,1)S(1)}, u32[]{:S(2)}, u32[]{:S(2)}) collective-permute-start(bf16[4,64,1024]{2,1,0:T(8,128)(2,1)S(1)} %pad_maximum_fusion.7.refs_1_), channel_id=1, source_target_pairs={{0,1},{1,0},{2,3},{3,2},{4,5},{5,4},{6,7},{7,6},{8,9},{9,8},{10,11... | collective-permute-start | bytes 1572872 | tf_op jit(solution)/shard_map/ppermute | solution.py:54
  28.9 2.6 %collective-permute-start.8 = (bf16[4,64,1024]{2,1,0:T(8,128)(2,1)S(1)}, bf16[4,64,1024]{2,1,0:T(8,128)(2,1)S(1)}, u32[]{:S(2)}, u32[]{:S(2)}) collective-permute-start(bf16[4,64,1024]{2,1,0:T(8,128)(2,1)S(1)} %pad_maximum_fusion.6.refs_0_), channel_id=1, source_target_pairs={{0,1},{1,0},{2,3},{3,2},{4,5},{5,4},{6,7},{7,6},{8,9},{9,8},{10,11... | collective-permute-start | bytes 1572872 | tf_op jit(solution)/shard_map/ppermute | solution.py:54
  34.9 13.0 %collective-permute-start.10 = (bf16[128,2688]{1,0:T(8,128)(2,1)S(1)}, bf16[128,2688]{1,0:T(8,128)(2,1)S(1)}, u32[]{:S(2)}, u32[]{:S(2)}) collective-permute-start(bf16[128,2688]{1,0:T(8,128)(2,1)S(1)} %get-tuple-element.119), channel_id=1, source_target_pairs={{0,16},{1,49},{2,18},{3,51},{4,20},{5,53},{6,22},{7,55},{8,24},{9,... | collective-permute-start | bytes 2064392 | tf_op jit(solution)/shard_map/ppermute | solution.py:54
  36.8 19.8 %collective-permute-start.14 = (bf16[2,64,1024]{2,1,0:T(8,128)(2,1)S(1)}, bf16[2,64,1024]{2,1,0:T(8,128)(2,1)S(1)}, u32[]{:S(2)}, u32[]{:S(2)}) collective-permute-start(bf16[2,64,1024]{2,1,0:T(8,128)(2,1)S(1)} %pad_maximum_fusion.10), channel_id=1, source_target_pairs={{0,12},{1,13},{2,14},{3,15},{4,0},{5,1},{6,2},{7,3},{8,4},{9,5},{1... | collective-permute-start | bytes 786440 | tf_op jit(solution)/shard_map/ppermute | solution.py:54
  42.1 14.5 %collective-permute-start.15 = (bf16[2,64,1024]{2,1,0:T(8,128)(2,1)S(1)}, bf16[2,64,1024]{2,1,0:T(8,128)(2,1)S(1)}, u32[]{:S(2)}, u32[]{:S(2)}) collective-permute-start(bf16[2,64,1024]{2,1,0:T(8,128)(2,1)S(1)} %pad_maximum_fusion.10), channel_id=1, source_target_pairs={{0,8},{1,9},{2,10},{3,11},{4,12},{5,13},{6,14},{7,15},{8,0},{9,1},... | collective-permute-start | bytes 786440 | tf_op jit(solution)/shard_map/ppermute | solution.py:54
  44.2 14.2 %collective-permute-start.16 = (bf16[2,64,1024]{2,1,0:T(8,128)(2,1)S(1)}, bf16[2,64,1024]{2,1,0:T(8,128)(2,1)S(1)}, u32[]{:S(2)}, u32[]{:S(2)}) collective-permute-start(bf16[2,64,1024]{2,1,0:T(8,128)(2,1)S(1)} %pad_maximum_fusion.10), channel_id=1, source_target_pairs={{0,4},{1,5},{2,6},{3,7},{4,8},{5,9},{6,10},{7,11},{8,12},{9,13},{1... | collective-permute-start | bytes 786440 | tf_op jit(solution)/shard_map/ppermute | solution.py:54
  45.6 10.9 %collective-permute-start.12 = (bf16[128,2688]{1,0:T(8,128)(2,1)S(1)}, bf16[128,2688]{1,0:T(8,128)(2,1)S(1)}, u32[]{:S(2)}, u32[]{:S(2)}) collective-permute-start(bf16[128,2688]{1,0:T(8,128)(2,1)S(1)} %get-tuple-element.122), channel_id=1, source_target_pairs={{0,48},{1,17},{2,50},{3,19},{4,52},{5,21},{6,54},{7,23},{8,56},{9,... | collective-permute-start | bytes 2064392 | tf_op jit(solution)/shard_map/ppermute | solution.py:54
  58.5 2.8 %collective-permute-start.18 = (bf16[4,64,1024]{2,1,0:T(8,128)(2,1)S(1)}, bf16[4,64,1024]{2,1,0:T(8,128)(2,1)S(1)}, u32[]{:S(2)}, u32[]{:S(2)}) collective-permute-start(bf16[4,64,1024]{2,1,0:T(8,128)(2,1)S(1)} %pad_maximum_fusion.9.refs_1_.refs_10_), channel_id=1, source_target_pairs={{0,1},{1,0},{2,3},{3,2},{4,5},{5,4},{6,7},{7,6},{8,9},{9,8},{10,11... | collective-permute-start | bytes 1572872 | tf_op jit(solution)/shard_map/ppermute | solution.py:54
  58.8 2.5 %collective-permute-start.17 = (bf16[4,64,1024]{2,1,0:T(8,128)(2,1)S(1)}, bf16[4,64,1024]{2,1,0:T(8,128)(2,1)S(1)}, u32[]{:S(2)}, u32[]{:S(2)}) collective-permute-start(bf16[4,64,1024]{2,1,0:T(8,128)(2,1)S(1)} %pad_maximum_fusion.8.refs_0_.refs_9_), channel_id=1, source_target_pairs={{0,1},{1,0},{2,3},{3,2},{4,5},{5,4},{6,7},{7,6},{8,9},{9,8},{10,11... | collective-permute-start | bytes 1572872 | tf_op jit(solution)/shard_map/ppermute | solution.py:54
  59.3 10.9 %collective-permute-start.13 = (bf16[64,2688]{1,0:T(8,128)(2,1)S(1)}, bf16[64,2688]{1,0:T(8,128)(2,1)S(1)}, u32[]{:S(2)}, u32[]{:S(2)}) collective-permute-start(bf16[64,2688]{1,0:T(8,128)(2,1)S(1)} %slice_add_fusion.2), channel_id=1, source_target_pairs={{0,48},{1,17},{2,50},{3,19},{4,52},{5,21},{6,54},{7,23},{8,56},{9,... | collective-permute-start | bytes 1032200 | tf_op jit(solution)/shard_map/ppermute | solution.py:54
  61.0 9.6 %collective-permute-start.11 = (bf16[64,2688]{1,0:T(8,128)(2,1)S(1)}, bf16[64,2688]{1,0:T(8,128)(2,1)S(1)}, u32[]{:S(2)}, u32[]{:S(2)}) collective-permute-start(bf16[64,2688]{1,0:T(8,128)(2,1)S(1)} %slice_add_fusion.3), channel_id=1, source_target_pairs={{0,16},{1,49},{2,18},{3,51},{4,20},{5,53},{6,22},{7,55},{8,24},{9,... | collective-permute-start | bytes 1032200 | tf_op jit(solution)/shard_map/ppermute | solution.py:54
  64.8 17.3 %collective-permute-start.20 = (bf16[128,2688]{1,0:T(8,128)(2,1)S(1)}, bf16[128,2688]{1,0:T(8,128)(2,1)S(1)}, u32[]{:S(2)}, u32[]{:S(2)}) collective-permute-start(bf16[128,2688]{1,0:T(8,128)(2,1)S(1)} %get-tuple-element.133), channel_id=1, source_target_pairs={{0,16},{1,49},{2,18},{3,51},{4,20},{5,53},{6,22},{7,55},{8,24},{9,... | collective-permute-start | bytes 2064392 | tf_op jit(solution)/shard_map/ppermute | solution.py:54
  70.6 14.7 %collective-permute-start.21 = (bf16[128,2688]{1,0:T(8,128)(2,1)S(1)}, bf16[128,2688]{1,0:T(8,128)(2,1)S(1)}, u32[]{:S(2)}, u32[]{:S(2)}) collective-permute-start(bf16[128,2688]{1,0:T(8,128)(2,1)S(1)} %get-tuple-element.139), channel_id=1, source_target_pairs={{0,48},{1,17},{2,50},{3,19},{4,52},{5,21},{6,54},{7,23},{8,56},{9,... | collective-permute-start | bytes 2064392 | tf_op jit(solution)/shard_map/ppermute | solution.py:54
  73.1 15.3 %collective-permute-start.19 = (bf16[128,2688]{1,0:T(8,128)(2,1)S(1)}, bf16[128,2688]{1,0:T(8,128)(2,1)S(1)}, u32[]{:S(2)}, u32[]{:S(2)}) collective-permute-start(bf16[128,2688]{1,0:T(8,128)(2,1)S(1)} %pad_maximum_fusion.2), channel_id=1, source_target_pairs={{0,64},{1,65},{2,66},{3,67},{4,68},{5,69},{6,70},{7,71},{8,72},{9,... | collective-permute-start | bytes 2064392 | tf_op jit(solution)/shard_map/ppermute | solution.py:54
  82.1 13.9 %collective-permute-start.24 = (bf16[64,2688]{1,0:T(8,128)(2,1)S(1)}, bf16[64,2688]{1,0:T(8,128)(2,1)S(1)}, u32[]{:S(2)}, u32[]{:S(2)}) collective-permute-start(bf16[64,2688]{1,0:T(8,128)(2,1)S(1)} %slice_add_fusion.1), channel_id=1, source_target_pairs={{0,16},{1,49},{2,18},{3,51},{4,20},{5,53},{6,22},{7,55},{8,24},{9,... | collective-permute-start | bytes 1032200 | tf_op jit(solution)/shard_map/ppermute | solution.py:54
  85.3 10.7 %collective-permute-start.25 = (bf16[64,2688]{1,0:T(8,128)(2,1)S(1)}, bf16[64,2688]{1,0:T(8,128)(2,1)S(1)}, u32[]{:S(2)}, u32[]{:S(2)}) collective-permute-start(bf16[64,2688]{1,0:T(8,128)(2,1)S(1)} %slice_add_fusion), channel_id=1, source_target_pairs={{0,48},{1,17},{2,50},{3,19},{4,52},{5,21},{6,54},{7,23},{8,56},{9,... | collective-permute-start | bytes 1032200 | tf_op jit(solution)/shard_map/ppermute | solution.py:54
  88.9 19.7 %collective-permute-start.23 = (bf16[128,2688]{1,0:T(8,128)(2,1)S(1)}, bf16[128,2688]{1,0:T(8,128)(2,1)S(1)}, u32[]{:S(2)}, u32[]{:S(2)}) collective-permute-start(bf16[128,2688]{1,0:T(8,128)(2,1)S(1)} %pad_maximum_fusion.3.refs_0_.refs_4_), channel_id=1, source_target_pairs={{0,16},{1,49},{2,18},{3,51},{4,20},{5,53},{6,22},{7,55},{8,24},{9,... | collective-permute-start | bytes 2064392 | tf_op jit(solution)/shard_map/ppermute | solution.py:54
  90.2 18.5 %collective-permute-start.22 = (bf16[128,2688]{1,0:T(8,128)(2,1)S(1)}, bf16[128,2688]{1,0:T(8,128)(2,1)S(1)}, u32[]{:S(2)}, u32[]{:S(2)}) collective-permute-start(bf16[128,2688]{1,0:T(8,128)(2,1)S(1)} %pad_maximum_fusion.3.refs_0_.refs_4_), channel_id=1, source_target_pairs={{0,48},{1,17},{2,50},{3,19},{4,52},{5,21},{6,54},{7,23},{8,56},{9,... | collective-permute-start | bytes 2064392 | tf_op jit(solution)/shard_map/ppermute | solution.py:54
  96.3 16.4 %collective-permute-start.28 = (bf16[128,2688]{1,0:T(8,128)(2,1)S(1)}, bf16[128,2688]{1,0:T(8,128)(2,1)S(1)}, u32[]{:S(2)}, u32[]{:S(2)}) collective-permute-start(bf16[128,2688]{1,0:T(8,128)(2,1)S(1)} %pad_maximum_fusion.4), channel_id=1, source_target_pairs={{0,64},{1,65},{2,66},{3,67},{4,68},{5,69},{6,70},{7,71},{8,72},{9,... | collective-permute-start | bytes 2064392 | tf_op jit(solution)/shard_map/ppermute | solution.py:54
  108.6 12.1 %collective-permute-start.26 = (bf16[64,2688]{1,0:T(8,128)(2,1)S(1)}, bf16[64,2688]{1,0:T(8,128)(2,1)S(1)}, u32[]{:S(2)}, u32[]{:S(2)}) collective-permute-start(bf16[64,2688]{1,0:T(8,128)(2,1)S(1)} %slice.203), channel_id=1, source_target_pairs={{0,16},{1,49},{2,18},{3,51},{4,20},{5,53},{6,22},{7,55},{8,24},{9,... | collective-permute-start | bytes 1032200 | tf_op jit(solution)/shard_map/ppermute | solution.py:54
  108.7 11.8 %collective-permute-start.27 = (bf16[64,2688]{1,0:T(8,128)(2,1)S(1)}, bf16[64,2688]{1,0:T(8,128)(2,1)S(1)}, u32[]{:S(2)}, u32[]{:S(2)}) collective-permute-start(bf16[64,2688]{1,0:T(8,128)(2,1)S(1)} %slice.204), channel_id=1, source_target_pairs={{0,48},{1,17},{2,50},{3,19},{4,52},{5,21},{6,54},{7,23},{8,56},{9,... | collective-permute-start | bytes 1032200 | tf_op jit(solution)/shard_map/ppermute | solution.py:54
  113.2 21.9 %collective-permute-start.31 = (bf16[128,2688]{1,0:T(8,128)(2,1)S(1)}, bf16[128,2688]{1,0:T(8,128)(2,1)S(1)}, u32[]{:S(2)}, u32[]{:S(2)}) collective-permute-start(bf16[128,2688]{1,0:T(8,128)(2,1)S(1)} %pad_maximum_fusion.5.refs_0_.refs_13_), channel_id=1, source_target_pairs={{0,16},{1,49},{2,18},{3,51},{4,20},{5,53},{6,22},{7,55},{8,24},{9,... | collective-permute-start | bytes 2064392 | tf_op jit(solution)/shard_map/ppermute | solution.py:54
  113.3 21.9 %collective-permute-start.32 = (bf16[128,2688]{1,0:T(8,128)(2,1)S(1)}, bf16[128,2688]{1,0:T(8,128)(2,1)S(1)}, u32[]{:S(2)}, u32[]{:S(2)}) collective-permute-start(bf16[128,2688]{1,0:T(8,128)(2,1)S(1)} %pad_maximum_fusion.5.refs_0_.refs_13_), channel_id=1, source_target_pairs={{0,48},{1,17},{2,50},{3,19},{4,52},{5,21},{6,54},{7,23},{8,56},{9,... | collective-permute-start | bytes 2064392 | tf_op jit(solution)/shard_map/ppermute | solution.py:54
  123.9 14.6 %collective-permute-start.29 = (bf16[256,1024]{1,0:T(8,128)(2,1)S(1)}, bf16[256,1024]{1,0:T(8,128)(2,1)S(1)}, u32[]{:S(2)}, u32[]{:S(2)}) collective-permute-start(bf16[256,1024]{1,0:T(8,128)(2,1)S(1)} %bitcast.27), channel_id=1, source_target_pairs={{0,1},{1,0},{2,3},{3,2},{4,5},{5,4},{6,7},{7,6},{8,9},{9,8},{10,11... | collective-permute-start | bytes 1572872 | tf_op jit(solution)/shard_map/ppermute | solution.py:54
  124.0 14.5 %collective-permute-start.30 = (bf16[256,1024]{1,0:T(8,128)(2,1)S(1)}, bf16[256,1024]{1,0:T(8,128)(2,1)S(1)}, u32[]{:S(2)}, u32[]{:S(2)}) collective-permute-start(bf16[256,1024]{1,0:T(8,128)(2,1)S(1)} %bitcast.26), channel_id=1, source_target_pairs={{0,1},{1,0},{2,3},{3,2},{4,5},{5,4},{6,7},{7,6},{8,9},{9,8},{10,11... | collective-permute-start | bytes 1572872 | tf_op jit(solution)/shard_map/ppermute | solution.py:54
  135.1 11.0 %collective-permute-start.36 = (bf16[64,2688]{1,0:T(8,128)(2,1)S(1)}, bf16[64,2688]{1,0:T(8,128)(2,1)S(1)}, u32[]{:S(2)}, u32[]{:S(2)}) collective-permute-start(bf16[64,2688]{1,0:T(8,128)(2,1)S(1)} %slice.208), channel_id=1, source_target_pairs={{0,16},{1,49},{2,18},{3,51},{4,20},{5,53},{6,22},{7,55},{8,24},{9,... | collective-permute-start | bytes 1032200 | tf_op jit(solution)/shard_map/ppermute | solution.py:54
  135.2 9.6 %collective-permute-start.37 = (bf16[64,2688]{1,0:T(8,128)(2,1)S(1)}, bf16[64,2688]{1,0:T(8,128)(2,1)S(1)}, u32[]{:S(2)}, u32[]{:S(2)}) collective-permute-start(bf16[64,2688]{1,0:T(8,128)(2,1)S(1)} %slice.209), channel_id=1, source_target_pairs={{0,48},{1,17},{2,50},{3,19},{4,52},{5,21},{6,54},{7,23},{8,56},{9,... | collective-permute-start | bytes 1032200 | tf_op jit(solution)/shard_map/ppermute | solution.py:54
  139.0 11.5 %collective-permute-start.33 = (bf16[64,2048]{1,0:T(8,128)(2,1)S(1)}, bf16[64,2048]{1,0:T(8,128)(2,1)S(1)}, u32[]{:S(2)}, u32[]{:S(2)}) collective-permute-start(bf16[64,2048]{1,0:T(8,128)(2,1)S(1)} %get-tuple-element.216), channel_id=1, source_target_pairs={{0,4},{1,5},{2,6},{3,7},{4,8},{5,9},{6,10},{7,11},{8,12},{9,13},{1... | collective-permute-start | bytes 786440 | tf_op jit(solution)/shard_map/ppermute | solution.py:54
  139.6 11.0 %collective-permute-start.34 = (bf16[64,2048]{1,0:T(8,128)(2,1)S(1)}, bf16[64,2048]{1,0:T(8,128)(2,1)S(1)}, u32[]{:S(2)}, u32[]{:S(2)}) collective-permute-start(bf16[64,2048]{1,0:T(8,128)(2,1)S(1)} %get-tuple-element.217), channel_id=1, source_target_pairs={{0,8},{1,9},{2,10},{3,11},{4,12},{5,13},{6,14},{7,15},{8,0},{9,1},... | collective-permute-start | bytes 786440 | tf_op jit(solution)/shard_map/ppermute | solution.py:54
  142.3 8.9 %collective-permute-start.35 = (bf16[64,2048]{1,0:T(8,128)(2,1)S(1)}, bf16[64,2048]{1,0:T(8,128)(2,1)S(1)}, u32[]{:S(2)}, u32[]{:S(2)}) collective-permute-start(bf16[64,2048]{1,0:T(8,128)(2,1)S(1)} %get-tuple-element.215), channel_id=1, source_target_pairs={{0,12},{1,13},{2,14},{3,15},{4,0},{5,1},{6,2},{7,3},{8,4},{9,5},{1... | collective-permute-start | bytes 786440 | tf_op jit(solution)/shard_map/ppermute | solution.py:54
  149.2 2.9 %collective-permute-start.39 = (bf16[256,1024]{1,0:T(8,128)(2,1)S(1)}, bf16[256,1024]{1,0:T(8,128)(2,1)S(1)}, u32[]{:S(2)}, u32[]{:S(2)}) collective-permute-start(bf16[256,1024]{1,0:T(8,128)(2,1)S(1)} %bitcast.25), channel_id=1, source_target_pairs={{0,1},{1,0},{2,3},{3,2},{4,5},{5,4},{6,7},{7,6},{8,9},{9,8},{10,11... | collective-permute-start | bytes 1572872 | tf_op jit(solution)/shard_map/ppermute | solution.py:54
  149.3 2.8 %collective-permute-start.40 = (bf16[256,1024]{1,0:T(8,128)(2,1)S(1)}, bf16[256,1024]{1,0:T(8,128)(2,1)S(1)}, u32[]{:S(2)}, u32[]{:S(2)}) collective-permute-start(bf16[256,1024]{1,0:T(8,128)(2,1)S(1)} %bitcast.24), channel_id=1, source_target_pairs={{0,1},{1,0},{2,3},{3,2},{4,5},{5,4},{6,7},{7,6},{8,9},{9,8},{10,11... | collective-permute-start | bytes 1572872 | tf_op jit(solution)/shard_map/ppermute | solution.py:54
  151.3 19.1 %collective-permute-start.38 = (bf16[32,2048]{1,0:T(8,128)(2,1)S(1)}, bf16[32,2048]{1,0:T(8,128)(2,1)S(1)}, u32[]{:S(2)}, u32[]{:S(2)}) collective-permute-start(bf16[32,2048]{1,0:T(8,128)(2,1)S(1)} %slice.247), channel_id=1, source_target_pairs={{0,2},{1,3},{2,0},{3,1},{4,6},{5,7},{6,4},{7,5},{8,10},{9,11},{10,... | collective-permute-start | bytes 393224 | tf_op jit(solution)/shard_map/ppermute | solution.py:54
  152.6 5.3 %copy-start.4 = (s32[8,7]{1,0:T(8,128)S(1)}, s32[8,7]{1,0:T(8,128)}, u32[]{:S(2)}) copy-start(s32[8,7]{1,0:T(8,128)} %refs_18_.1) | copy-start | bytes 676
  152.6 5.3 %copy-start.6 = (s32[8,7]{1,0:T(8,128)S(1)}, s32[8,7]{1,0:T(8,128)}, u32[]{:S(2)}) copy-start(s32[8,7]{1,0:T(8,128)} %refs_19_.1) | copy-start | bytes 676
  152.6 5.3 %copy-start.8 = (s32[7,8]{1,0:T(8,128)S(1)}, s32[7,8]{1,0:T(8,128)}, u32[]{:S(2)}) copy-start(s32[7,8]{1,0:T(8,128)} %refs_20_.1) | copy-start | bytes 676
  152.7 15.1 %collective-permute-start.41 = (bf16[64,2048]{1,0:T(8,128)(2,1)S(1)}, bf16[64,2048]{1,0:T(8,128)(2,1)S(1)}, u32[]{:S(2)}, u32[]{:S(2)}) collective-permute-start(bf16[64,2048]{1,0:T(8,128)(2,1)S(1)} %get-tuple-element.212), channel_id=1, source_target_pairs={{0,4},{1,5},{2,6},{3,7},{4,8},{5,9},{6,10},{7,11},{8,12},{9,13},{1... | collective-permute-start | bytes 786440 | tf_op jit(solution)/shard_map/ppermute | solution.py:54
  154.5 13.3 %collective-permute-start.42 = (bf16[64,2048]{1,0:T(8,128)(2,1)S(1)}, bf16[64,2048]{1,0:T(8,128)(2,1)S(1)}, u32[]{:S(2)}, u32[]{:S(2)}) collective-permute-start(bf16[64,2048]{1,0:T(8,128)(2,1)S(1)} %get-tuple-element.213), channel_id=1, source_target_pairs={{0,8},{1,9},{2,10},{3,11},{4,12},{5,13},{6,14},{7,15},{8,0},{9,1},... | collective-permute-start | bytes 786440 | tf_op jit(solution)/shard_map/ppermute | solution.py:54
  156.9 11.5 %collective-permute-start.43 = (bf16[64,2048]{1,0:T(8,128)(2,1)S(1)}, bf16[64,2048]{1,0:T(8,128)(2,1)S(1)}, u32[]{:S(2)}, u32[]{:S(2)}) collective-permute-start(bf16[64,2048]{1,0:T(8,128)(2,1)S(1)} %get-tuple-element.211), channel_id=1, source_target_pairs={{0,12},{1,13},{2,14},{3,15},{4,0},{5,1},{6,2},{7,3},{8,4},{9,5},{1... | collective-permute-start | bytes 786440 | tf_op jit(solution)/shard_map/ppermute | solution.py:54
  168.6 6.6 %collective-permute-start.44 = (bf16[32,2048]{1,0:T(8,128)(2,1)S(1)}, bf16[32,2048]{1,0:T(8,128)(2,1)S(1)}, u32[]{:S(2)}, u32[]{:S(2)}) collective-permute-start(bf16[32,2048]{1,0:T(8,128)(2,1)S(1)} %slice.257), channel_id=1, source_target_pairs={{0,2},{1,3},{2,0},{3,1},{4,6},{5,7},{6,4},{7,5},{8,10},{9,11},{10,... | collective-permute-start | bytes 393224 | tf_op jit(solution)/shard_map/ppermute | solution.py:54
  (6 other events, 6.6 us)
